TPU v7x, 512 devices: a whole 4x8x8 slice. The times are simulated.
512 devices in a mesh: dp: 64 (over y, z), vocab: 8 (over x, core).
Axes of the slice: x: 4, y: 8, z: 8, core: 2. Of those that a mesh axis runs over, the one named last changes fastest.
Arguments:
- hidden: bfloat16 [16384, 5120], P('dp'), may hold values from -40 to 40
- head_weight: bfloat16 [5120, 6144], P('dp', 'vocab'), may hold values from -1 to 1, as said below
- targets: int32 [16384], P('dp'), may hold values from 0 to 6143
- kept_mask: int32 [16384], P('dp'), may hold values from 0 to 1, as said below
- old_logprob: float32 [16384], P('dp'), as said below
- advantage: float32 [16384], P('dp'), may hold values from -3 to 3
Outputs:
- entropy: float32 [16384], P('dp')
- grad_hidden: float32 [16384, 5120], P('dp', 'vocab')
- grad_head: float32 [5120, 6144], P('dp', 'vocab')
Inputs may be any that keep to these rules, and one draw needn't show every extreme that they name: `kept_mask`: among the 256 tokens of one index of dp at most 80 are kept, and one such block keeps exactly 80; every block keeps at least one. Entries of head_weight lie within 6 / sqrt(5120) of zero. `old_logprob`: within 1.5 of -(log(6144) + 0.5).
All inputs are finite; a program needn't handle non-finite values.
Results may differ from a plain program's by a relative error of at most 0.015.
Values may be sent and summed in bfloat16 or wider, within the bound.
No kernel may reach another device: no remote copies, remote signals or barrier semaphores. Data moves between devices by JAX's collectives and lax.ppermute only.
A program may use at most 64 MiB of HBM per device.

v0:
```python
import jax
import jax.numpy as jnp
from jax import lax
from jax.sharding import PartitionSpec as P

KEEP_MOST = 80


clip_eps = 0.2
loss_scale = 8192.0


def surrogate_slope(logprob, old_logprob, advantage, keep_float, kept_total):
    importance = jnp.exp(logprob - old_logprob)
    bent_term = jnp.tanh((importance - 1.0) / clip_eps)
    clipped = 1.0 + clip_eps * bent_term
    choose_grad = jnp.where(
        importance * advantage <= clipped * advantage,
        advantage,
        advantage * (1.0 - bent_term * bent_term),
    )
    return -(loss_scale / kept_total) * keep_float * choose_grad * importance


def per_device(hidden, head_weight, targets, kept_mask, old_logprob, advantage):
    vocab_cols = head_weight.shape[1]
    offset = lax.axis_index("vocab") * vocab_cols
    assembled = lax.all_gather(head_weight, "dp", axis=0, tiled=True)
    logits = jnp.dot(hidden, assembled, preferred_element_type=jnp.float32)
    local_target = targets - offset
    positions = jnp.arange(vocab_cols, dtype=jnp.int32)
    onehot = (positions[None, :] == local_target[:, None]).astype(jnp.float32)
    local_pick = jnp.sum(logits * onehot, axis=1)
    row_top = lax.pmax(jnp.max(logits, axis=1), "vocab")
    shifted = logits - row_top[:, None]
    weights = jnp.exp(shifted)
    row_total, row_moment, picked = lax.psum(
        (jnp.sum(weights, axis=1), jnp.sum(weights * shifted, axis=1), local_pick), "vocab"
    )
    entropy = jnp.log(row_total) - row_moment / row_total
    logprob = picked - row_top - jnp.log(row_total)
    keep_float = kept_mask.astype(jnp.float32)
    kept_total = lax.psum(jnp.sum(keep_float), "dp")
    logprob_grad = surrogate_slope(logprob, old_logprob, advantage, keep_float, kept_total)
    slot_index = jnp.cumsum(kept_mask) - 1
    capacity_ids = jnp.arange(KEEP_MOST, dtype=jnp.int32)
    selector = ((slot_index[None, :] == capacity_ids[:, None]) & (kept_mask[None, :] == 1)).astype(
        jnp.float32
    )
    softmax_rows = jnp.exp(logits - row_top[:, None]) / row_total[:, None]
    logit_grads = (logprob_grad[:, None] * (onehot - softmax_rows)).astype(jnp.bfloat16)
    partial_rows = lax.dot_general(
        logit_grads, assembled, (((1,), (1,)), ((), ())), preferred_element_type=jnp.float32
    ).astype(jnp.bfloat16)
    grad_hidden = lax.psum_scatter(partial_rows, "vocab", scatter_dimension=1, tiled=True).astype(
        jnp.float32
    )
    compact = jnp.dot(
        selector.astype(jnp.bfloat16), logit_grads, preferred_element_type=jnp.float32
    ).astype(jnp.bfloat16)
    kept_hidden = jnp.dot(
        selector.astype(jnp.bfloat16), hidden, preferred_element_type=jnp.float32
    ).astype(jnp.bfloat16)
    columns_in = lax.all_to_all(kept_hidden, "dp", split_axis=1, concat_axis=0, tiled=True)
    grad_head = lax.dot_general(
        columns_in,
        lax.all_gather(compact, "dp", axis=0, tiled=True),
        (((0,), (0,)), ((), ())),
        preferred_element_type=jnp.float32,
    )
    return (entropy, grad_hidden, grad_head)


def solution(mesh):
    placed = (P("dp", None), P("dp", "vocab"), P("dp"), P("dp"), P("dp"), P("dp"))
    return jax.shard_map(
        per_device,
        mesh=mesh,
        in_specs=placed,
        out_specs=(P("dp"), P("dp", "vocab"), P("dp", "vocab")),
        check_vma=False,
    )
```

profile of v0, /device:TPU:6, one launch (start us, length us, event | category | flops | bytes accessed | tf_op | source)
XLA Modules:
  0.0 349.1 jit_solution(4053650728160083324)
XLA Ops:
  7.2 0.0 copy-start
  7.2 0.0 all-gather.3.cloned.1.call-start
  7.2 0.7 all-gather.3.cloned.1.call-update
  7.9 0.0 reduce-scatter.4.cloned.1.call-start
  8.0 1.3 convert_reduce_fusion
  9.2 151.3 %psum.30 = f32[]{:T(128)} all-reduce(f32[]{:T(128)} %convert_reduce_fusion), channel_id=1, replica_groups=mesh['dp'=64,'vocab'=8] {'dp'}, use_global_device_ids=true, to_apply=%region_7.0 | all-reduce | flops 1 | bytes 8 | tf_op jit(solution)/shard_map/psum | solution.py:43
  161.3 0.7 broadcast_subtract_fusion
  161.9 0.0 copy-start.3
  162.0 0.0 copy-start.4
  162.0 0.0 copy-start.5
  162.0 0.0 all-gather.3.cloned.1.call-done
  162.0 0.0 copy-done
  162.0 5.5 %fusion.11 = (f32[256]{0:T(256)S(1)}, f32[256,768]{1,0:T(8,128)S(1)}) fusion(bf16[256,5120]{1,0:T(8,128)(2,1)S(1)} %copy-done, bf16[5120,768]{1,0:T(8,128)(2,1)} %all-gather.3.cloned.1.call-done), kind=kOutput, calls=%fused_computation.28 | convolution fusion | flops 2013462272 | bytes 11273216 | tf_op jit(solution)/shard_map/dot_general | solution.py:29
  167.5 10.0 %pmax.7 = f32[256]{0:T(256)S(1)} all-reduce(f32[256]{0:T(256)S(1)} %get-tuple-element.11), channel_id=1, replica_groups=mesh['dp'=64,'vocab'=8] {'vocab'}, use_global_device_ids=true, to_apply=%region_1.0 | all-reduce | flops 256 | bytes 2048 | tf_op jit(solution)/shard_map/pmax | solution.py:34
  177.5 0.4 exponential_reduce_fusion
  178.0 11.4 %all-reduce = (f32[256]{0:T(256)S(1)}, f32[256]{0:T(256)S(1)}, f32[256]{0:T(256)S(1)}) all-reduce(f32[256]{0:T(256)S(1)} %get-tuple-element.4, f32[256]{0:T(256)S(1)} %get-tuple-element.3, f32[256]{0:T(256)S(1)} %get-tuple-element.5), channel_id=1, replica_groups=mesh['dp'=64,'vocab'=8] {'vocab'}, use_global_device_ids=true, to_apply=%region_5.0 | all-reduce | flops 768 | bytes 6144 | tf_op jit(solution)/shard_map/psum | solution.py:37
  189.3 0.0 copy-done.3
  189.3 0.0 copy-done.4
  189.4 0.0 copy-done.5
  189.4 0.6 fusion.10
  189.9 0.3 fusion.3
  190.3 0.0 copy-start.1
  190.3 0.7 copy-done.1
  191.0 7.0 %convolution_convert_fusion = bf16[256,5120]{1,0:T(8,128)(2,1)} fusion(bf16[256,768]{1,0:T(8,128)(2,1)S(1)} %fusion.3, bf16[5120,768]{1,0:T(8,128)(2,1)} %all-gather.3.cloned.1.call-done), kind=kOutput, calls=%fused_computation | convolution fusion | flops 2014576640 | bytes 10878976 | tf_op jit(solution)/shard_map/dot_general | solution.py:52
  198.0 4.4 %copy.13 = bf16[256,5120]{0,1:T(8,128)(2,1)} copy(bf16[256,5120]{1,0:T(8,128)(2,1)} %convolution_convert_fusion) | data formatting | bytes 5242880
  202.4 0.0 copy-start.2
  202.4 0.0 reduce-scatter.4.cloned.1.call-update
  202.5 0.0 all-gather.5.cloned.1.call-start
  202.5 0.3 reduce-window.9
  202.8 0.1 slice.7
  202.9 0.1 slice_reduce_fusion
  203.1 0.1 add_bitcast_fusion
  203.1 0.3 copy-done.2
  203.4 0.9 convolution_convert_fusion.2
  204.3 0.0 all-gather.5.cloned.1.call-update
  204.3 0.6 convolution_convert_fusion.1
  204.9 1.4 copy.12
  206.3 40.3 %all_to_all.19 = bf16[80,64,80]{0,2,1:T(8,128)(2,1)S(1)} all-to-all(bf16[80,64,80]{0,2,1:T(8,128)(2,1)} %bitcast.18), channel_id=1, replica_groups=mesh['dp'=64,'vocab'=8] {'dp'}, dimensions={1} | all-to-all | bytes 1638400 | tf_op jit(solution)/shard_map/all_to_all | solution.py:64
  246.6 1.4 copy.11
  248.0 3.2 all_to_all.17
  251.2 0.0 reduce-scatter.4.cloned.1.call-done
  251.3 1.9 copy.14
  253.1 1.9 convert_element_type.32
  255.0 82.2 %all-gather.5.cloned.1.call-done = bf16[5120,768]{1,0:T(8,128)(2,1)} async-done(((bf16[80,768]{1,0:T(8,128)(2,1)}), bf16[5120,768]{1,0:T(8,128)(2,1)}) %all-gather.5.cloned.1.call-update) | async-done | bytes 7864336 | tf_op jit(solution)/shard_map/all_gather | solution.py:67
  337.2 5.4 %fusion.12 = f32[80,768]{1,0:T(8,128)} fusion(bf16[5120,80]{0,1:T(8,128)(2,1)S(1)} %all_to_all.17, bf16[5120,768]{1,0:T(8,128)(2,1)} %all-gather.5.cloned.1.call-done), kind=kOutput, calls=%fused_computation.29 | convolution fusion | flops 629145600 | bytes 8929280 | tf_op jit(solution)/shard_map/dot_general | solution.py:65
  (2 shorter events, 0.0 us)
Async XLA Ops:
  7.2 154.8 %copy-start = (bf16[256,5120]{1,0:T(8,128)(2,1)S(1)}, bf16[256,5120]{1,0:T(8,128)(2,1)}, u32[]{:S(2)}) copy-start(bf16[256,5120]{1,0:T(8,128)(2,1)} %param.6) | copy-start | bytes 7864324
  7.2 154.8 %all-gather.3.cloned.1.call-start = ((), (), s32[]{:S(2)}) async-start(), calls=%async_computation.2 | async-start | bytes 7987200 | tf_op jit(solution)/shard_map/all_gather | solution.py:28
  7.9 243.3 %reduce-scatter.4.cloned.1.call-start = ((), (), s32[]{:S(2)}) async-start(), calls=%async_computation.4 | async-start | bytes 2949120
  161.9 27.4 %copy-start.3 = (s32[256]{0:T(256)S(1)}, s32[256]{0:T(256)}, u32[]{:S(2)}) copy-start(s32[256]{0:T(256)} %param.9) | copy-start | bytes 3076
  162.0 27.4 %copy-start.4 = (f32[256]{0:T(256)S(1)}, f32[256]{0:T(256)}, u32[]{:S(2)}) copy-start(f32[256]{0:T(256)} %param.11) | copy-start | bytes 3076
  162.0 27.4 %copy-start.5 = (f32[256]{0:T(256)S(1)}, f32[256]{0:T(256)}, u32[]{:S(2)}) copy-start(f32[256]{0:T(256)} %param.10) | copy-start | bytes 3076
  190.3 0.7 copy-start.1
  202.4 1.0 copy-start.2
  202.5 134.7 %all-gather.5.cloned.1.call-start = ((), (), s32[]{:S(2)}) async-start(), calls=%async_computation.3 | async-start | bytes 7987200 | tf_op jit(solution)/shard_map/all_gather | solution.py:67
Sparse Core Ops, SparseCore 0:
  11.1 102.4 all-gather.2
  202.6 31.4 reduce-scatter.3
  237.7 99.4 all-gather.4
where the time goes:
time: 350 us; the launch traced here: 349 us
  blocking collectives  213 us (61%)
  waiting for transfers between devices  83 us (24%)
  matrix products  19.3 us (6%)
  between operations  14.5 us (4%)
  local copies, waits for them, and re-layouts  13.5 us (4%)
  other arithmetic  5.58 us (2%)
    psum x1, blocking collectives, per_device(): kept_total = lax.psum(jnp.sum(keep_float), 'dp')  151 us
    all_gather x1, waiting for transfers between devices, per_device(): lax.all_gather(compact, 'dp', axis=0, tiled=True)  82.2 us
    all_to_all x1, blocking collectives, per_device(): lax.all_to_all(kept_hidden, 'dp', split_axis=1, concat_axis=0, tiled=True)  40.3 us
    psum x1, blocking collectives, per_device(): lax.psum((jnp.sum(weights, axis=1), jnp.sum(weights * shifted, axis=1), l...  11.4 us
    pmax x1, blocking collectives, per_device(): row_top = lax.pmax(jnp.max(logits, axis=1), 'vocab')  10 us
    unnamed x14, local copies, waits for them, and re-layouts  7.36 us
    dot_general x1, matrix products, per_device(): lax.dot_general(logit_grads, assembled, (((1,), (1,)), ((), ())), preferr...  7.01 us
  transfers between devices with their start and end apart: 3, of which 1 were waited for; matrix products, arithmetic and copies ran while one was open for 3% of the time, Pallas kernels for 0%

commit v1 on v0

v1 whole, which is shorter than its diff:
```python
import jax
import jax.numpy as jnp
from jax import lax
from jax.sharding import Mesh, PartitionSpec as P

Y, Z, X, C = 8, 8, 4, 2
V = X * C
SLOTS = 96
CLIP_EPS = 0.2
LOSS_SCALE = 8192.0


def surrogate_slope(logprob, old_logprob, advantage, keep_float):
    importance = jnp.exp(logprob - old_logprob)
    bent_term = jnp.tanh((importance - 1.0) / CLIP_EPS)
    clipped = 1.0 + CLIP_EPS * bent_term
    choose_grad = jnp.where(
        importance * advantage <= clipped * advantage,
        advantage,
        advantage * (1.0 - bent_term * bent_term),
    )
    return keep_float * choose_grad * importance


def to_all(values, axes, n):
    return lax.all_to_all(
        jnp.broadcast_to(values[None], (n,) + values.shape), axes, split_axis=0, concat_axis=0
    )


def per_device(hidden, head_weight, targets, kept_mask, old_logprob, advantage):
    tokens, width = hidden.shape
    rows, cols = head_weight.shape
    offset = (lax.axis_index("x") * C + lax.axis_index("c")) * cols
    assembled = lax.all_gather(head_weight, ("y", "z"), axis=0, tiled=True)

    keep_float = kept_mask.astype(jnp.float32)
    slot_index = jnp.cumsum(kept_mask) - 1
    ids = jnp.arange(SLOTS, dtype=jnp.int32)
    selector = ((slot_index[None, :] == ids[:, None]) & (kept_mask[None, :] == 1)).astype(jnp.bfloat16)
    kept_hidden = jnp.dot(selector, hidden, preferred_element_type=jnp.float32).astype(jnp.bfloat16)
    kept_hidden = kept_hidden.reshape(SLOTS, Y, Z, rows).transpose(2, 0, 1, 3).reshape(Z, SLOTS, Y * rows)
    kept_hidden = lax.all_to_all(kept_hidden, "z", split_axis=0, concat_axis=0)
    kept_hidden = kept_hidden.reshape(Z * SLOTS, Y * rows)
    kept_here = jnp.broadcast_to(jnp.sum(keep_float), (8, 128))
    kept_y = jnp.sum(to_all(kept_here, "y", Y), axis=0)
    kept_total = jnp.sum(to_all(kept_y, "z", Z), axis=0)[0, 0]
    scale = -(LOSS_SCALE / kept_total)

    logits = jnp.dot(hidden, assembled, preferred_element_type=jnp.float32)
    local_target = targets - offset
    positions = jnp.arange(cols, dtype=jnp.int32)
    onehot = (positions[None, :] == local_target[:, None]).astype(jnp.float32)
    local_pick = jnp.sum(logits * onehot, axis=1)
    local_top = jnp.max(logits, axis=1)
    shifted = logits - local_top[:, None]
    weights = jnp.exp(shifted)
    stats = jnp.stack(
        [local_top, jnp.sum(weights, axis=1), jnp.sum(weights * shifted, axis=1), local_pick]
    )
    stats = to_all(stats, ("x", "c"), V)
    tops, totals, moments, picks = (stats[:, i] for i in range(4))
    row_top = jnp.max(tops, axis=0)
    lower = tops - row_top[None]
    factor = jnp.exp(lower)
    row_total = jnp.sum(totals * factor, axis=0)
    row_moment = jnp.sum((moments + lower * totals) * factor, axis=0)
    picked = jnp.sum(picks, axis=0)
    entropy = jnp.log(row_total) - row_moment / row_total
    logprob = picked - row_top - jnp.log(row_total)
    slope = surrogate_slope(logprob, old_logprob, advantage, keep_float)
    softmax_rows = jnp.exp(logits - row_top[:, None]) / row_total[:, None]
    logit_grads = (slope[:, None] * (onehot - softmax_rows)).astype(jnp.bfloat16)
    compact = jnp.dot(selector, logit_grads, preferred_element_type=jnp.float32).astype(jnp.bfloat16)

    all_slots = lax.all_gather(compact, "z", axis=0, tiled=True)
    partial_head = lax.dot_general(
        kept_hidden, all_slots, (((0,), (0,)), ((), ())), preferred_element_type=jnp.float32
    ).astype(jnp.bfloat16)
    parts = lax.all_to_all(partial_head.reshape(Y, rows, cols), "y", split_axis=0, concat_axis=0)
    grad_head = scale * jnp.sum(parts.astype(jnp.float32), axis=0)

    hidden_part = lax.dot_general(
        compact, assembled, (((1,), (1,)), ((), ())), preferred_element_type=jnp.float32
    ).astype(jnp.bfloat16)
    mine = width // V
    hidden_part = hidden_part.reshape(SLOTS, V, mine).transpose(1, 0, 2)
    hidden_part = lax.all_to_all(hidden_part, ("x", "c"), split_axis=0, concat_axis=0)
    spread = jnp.tile(selector, (V, 1))
    grad_hidden = scale * lax.dot_general(
        spread, hidden_part.reshape(V * SLOTS, mine), (((0,), (0,)), ((), ())),
        preferred_element_type=jnp.float32,
    )
    return (entropy, grad_hidden, grad_head)


def solution(mesh):
    grid = Mesh(mesh.devices.reshape(Y, Z, X, C), ("y", "z", "x", "c"))
    dp, vocab = ("y", "z"), ("x", "c")
    placed = (P(dp, None), P(dp, vocab), P(dp), P(dp), P(dp), P(dp))
    return jax.shard_map(
        per_device,
        mesh=grid,
        in_specs=placed,
        out_specs=(P(dp), P(dp, vocab), P(dp, vocab)),
        check_vma=False,
    )
```

time: 350 us -> 256 us (0.73)
  blocking collectives: 213 us -> 0 us
  waiting for transfers between devices: 83 us -> 166 us
  starting transfers between devices: 0.12 us -> 34.5 us
    psum x2 -> x0, blocking collectives: 163 us -> none  [the longest x1 151 us: per_device(): kept_total = lax.psum(jnp.sum(keep_float), 'dp')]
    all_to_all x0 -> x6, waiting for transfers between devices: none -> 60 us  [the longest x1 24.5 us: per_device(): kept_hidden = lax.all_to_all(kept_hidden, 'z', split_axis=0, concat_axis=0)]
    all_to_all x1 -> x0, blocking collectives: 40.3 us -> none  [per_device(): lax.all_to_all(kept_hidden, 'dp', split_axis=1, concat_axis=0, tiled=True)]
    all_to_all x0 -> x6, starting transfers between devices: none -> 34.4 us  [the longest x3 16.4 us: to_all(): lax.all_to_all(jnp.broadcast_to(values[None], (n,) + values.shape), axes,...]
    all_gather x2, waiting for transfers between devices: 82.2 us -> 105 us  [the longest x1 103 us: per_device(): assembled = lax.all_gather(head_weight, ('y', 'z'), axis=0, tiled=True)]
    pmax x1 -> x0, blocking collectives: 10 us -> none  [per_device(): row_top = lax.pmax(jnp.max(logits, axis=1), 'vocab')]
    unnamed x14 -> x8, local copies, waits for them, and re-layouts: 7.36 us -> 0.02 us
    all_to_all x3 -> x0, local copies, waits for them, and re-layouts: 5.98 us -> none  [per_device(): lax.all_to_all(kept_hidden, 'dp', split_axis=1, concat_axis=0, tiled=True)]
  transfers between devices with their start and end apart: 3 -> 8, of which waited for: 1 -> 7; matrix products, arithmetic and copies ran while one was open for 3% -> 10% of each run, Pallas kernels for 0% -> 0%
where the time goes in v1:
time: 256 us; the launch traced here: 252 us
  waiting for transfers between devices  166 us (65%)
  starting transfers between devices  34.5 us (13%)
  matrix products  20 us (8%)
  between operations  14.8 us (6%)
  local copies, waits for them, and re-layouts  11.5 us (4%)
  other arithmetic  5.63 us (2%)
    all_gather x1, waiting for transfers between devices, per_device(): assembled = lax.all_gather(head_weight, ('y', 'z'), axis=0, tiled=True)  103 us
    all_to_all x1, waiting for transfers between devices, per_device(): kept_hidden = lax.all_to_all(kept_hidden, 'z', split_axis=0, concat_axis=0)  24.5 us
    all_to_all x1, waiting for transfers between devices, per_device(): lax.all_to_all(partial_head.reshape(Y, rows, cols), 'y', split_axis=0, co...  23.4 us
    all_to_all x3, starting transfers between devices, to_all(): lax.all_to_all(jnp.broadcast_to(values[None], (n,) + values.shape), axes,...  16.4 us
    all_to_all x1, starting transfers between devices, per_device(): lax.all_to_all(partial_head.reshape(Y, rows, cols), 'y', split_axis=0, co...  7.41 us
    all_to_all x1, waiting for transfers between devices, per_device(): lax.all_to_all(hidden_part, ('x', 'c'), split_axis=0, concat_axis=0)  7.39 us
    all_to_all x1, starting transfers between devices, per_device(): lax.all_to_all(hidden_part, ('x', 'c'), split_axis=0, concat_axis=0)  6.34 us
    dot_general x1, matrix products, per_device(): lax.dot_general(compact, assembled, (((1,), (1,)), ((), ())), preferred_e...  5.82 us
  transfers between devices with their start and end apart: 8, of which 7 were waited for; matrix products, arithmetic and copies ran while one was open for 10% of the time, Pallas kernels for 0%

profile of v1, /device:TPU:6, one launch (start us, length us, event | category | flops | bytes accessed | tf_op | source)
XLA Modules:
  0.0 252.5 jit_solution(5245884751713318101)
XLA Ops:
  7.2 0.0 copy-start
  7.2 0.0 all-gather.3.cloned.1.call-start
  7.2 0.7 all-gather.3.cloned.1.call-update
  7.9 1.0 reduce-window.9
  8.9 0.1 slice.26
  9.1 0.1 slice_reduce_fusion.1
  9.2 0.7 broadcast_subtract_fusion
  9.9 0.1 add_bitcast_fusion
  9.9 0.0 copy-start.1
  9.9 0.0 copy-start.2
  9.9 0.0 copy-start.3
  9.9 102.9 %all-gather.3.cloned.1.call-done = bf16[5120,768]{1,0:T(8,128)(2,1)} async-done(((bf16[80,768]{1,0:T(8,128)(2,1)}), bf16[5120,768]{1,0:T(8,128)(2,1)}) %all-gather.3.cloned.1.call-update) | async-done | bytes 7864336 | tf_op jit(solution)/shard_map/all_gather | solution.py:35
  112.9 0.0 copy-done
  112.9 5.5 %fusion.17 = (f32[256]{0:T(256)S(1)}, f32[256,768]{1,0:T(8,128)S(1)}) fusion(bf16[256,5120]{1,0:T(8,128)(2,1)S(1)} %copy-done, bf16[5120,768]{1,0:T(8,128)(2,1)} %all-gather.3.cloned.1.call-done), kind=kOutput, calls=%fused_computation.43 | convolution fusion | flops 2013462272 | bytes 11273216 | tf_op jit(solution)/shard_map/dot_general | solution.py:50
  118.4 0.5 exponential_reduce_fusion
  118.8 0.6 broadcast_in_dim.4
  119.5 4.8 %all-to-all-start = ((f32[8,4,256]{2,1,0:T(4,128)}), f32[8,4,256]{2,1,0:T(4,128)S(1)}, u32[]{:S(2)}, u32[]{:S(2)}) async-start(f32[8,4,256]{2,1,0:T(4,128)} %broadcast_in_dim.4), calls=%async_computation | async-start | bytes 65536 | tf_op jit(solution)/shard_map/all_to_all | solution.py:26
  124.3 0.0 copy-done.1
  124.3 3.4 %all-to-all-done = f32[8,4,256]{2,1,0:T(4,128)S(1)} async-done(((f32[8,4,256]{2,1,0:T(4,128)}), f32[8,4,256]{2,1,0:T(4,128)S(1)}, u32[]{:S(2)}, u32[]{:S(2)}) %all-to-all-start) | async-done | bytes 32800 | tf_op jit(solution)/shard_map/all_to_all | solution.py:26
  127.7 0.0 copy-done.2
  127.7 0.0 copy-done.3
  127.7 1.2 convert_reduce_fusion.1
  128.9 1.3 broadcast_in_dim_broadcast_in_dim_broadcast_in_dim.3
  130.2 6.4 %all-to-all-start.1 = ((f32[8,8,128]{2,1,0:T(8,128)}), f32[8,8,128]{2,1,0:T(8,128)S(1)}, u32[]{:S(2)}, u32[]{:S(2)}) async-start(f32[8,8,128]{2,1,0:T(8,128)} %broadcast_in_dim_broadcast_in_dim_broadcast_in_dim.3), calls=%async_computation.1 | async-start | bytes 65536 | tf_op jit(solution)/shard_map/all_to_all | solution.py:26
  136.6 1.5 convolution_convert_fusion
  138.1 2.4 copy.37
  140.5 2.5 copy.38
  143.0 2.4 copy.39
  145.3 0.0 all-to-all-done.1
  145.3 4.2 %all-to-all-start.4 = ((bf16[8,96,640]{2,1,0:T(8,128)(2,1)}), bf16[8,96,640]{2,1,0:T(8,128)(2,1)}, u32[]{:S(2)}, u32[]{:S(2)}) async-start(bf16[8,96,640]{2,1,0:T(8,128)(2,1)} %copy.39), calls=%async_computation.4 | async-start | bytes 1966080 | tf_op jit(solution)/shard_map/all_to_all | solution.py:43
  149.6 0.0 all-gather.5.cloned.1.call-start
  149.6 1.1 convolution_convert_fusion.3
  150.8 0.0 all-gather.5.cloned.1.call-update
  150.8 24.5 %all-to-all-done.4 = bf16[8,96,640]{2,1,0:T(8,128)(2,1)} async-done(((bf16[8,96,640]{2,1,0:T(8,128)(2,1)}), bf16[8,96,640]{2,1,0:T(8,128)(2,1)}, u32[]{:S(2)}, u32[]{:S(2)}) %all-to-all-start.4) | async-done | bytes 983072 | tf_op jit(solution)/shard_map/all_to_all | solution.py:43
  175.3 0.6 broadcast_in_dim.5
  175.9 5.2 %all-to-all-start.2 = ((f32[8,8,128]{2,1,0:T(8,128)}), f32[8,8,128]{2,1,0:T(8,128)S(1)}, u32[]{:S(2)}, u32[]{:S(2)}) async-start(f32[8,8,128]{2,1,0:T(8,128)} %broadcast_in_dim.5), calls=%async_computation.2 | async-start | bytes 65536 | tf_op jit(solution)/shard_map/all_to_all | solution.py:26
  181.1 5.8 %convolution_convert_fusion.1 = bf16[96,5120]{1,0:T(8,128)(2,1)S(1)} fusion(bf16[96,768]{1,0:T(8,128)(2,1)} %convolution_convert_fusion.3, bf16[5120,768]{1,0:T(8,128)(2,1)} %all-gather.3.cloned.1.call-done), kind=kOutput, calls=%fused_computation.1 | convolution fusion | flops 755466240 | bytes 8994816 | tf_op jit(solution)/shard_map/dot_general | solution.py:83
  186.9 1.1 copy.60
  188.0 1.3 all-to-all-done.2
  189.3 6.3 %all-to-all-start.3 = ((bf16[8,96,640]{2,1,0:T(8,128)(2,1)}), bf16[8,96,640]{2,1,0:T(8,128)(2,1)}, u32[]{:S(2)}, u32[]{:S(2)}) async-start(bf16[8,96,640]{2,1,0:T(8,128)(2,1)} %bitcast.55), calls=%async_computation.3 | async-start | bytes 1966080 | tf_op jit(solution)/shard_map/all_to_all | solution.py:88
  195.7 2.4 all-gather.5.cloned.1.call-done
  198.0 3.5 %convolution_convert_fusion.2 = bf16[640,768]{1,0:T(8,128)(2,1)} fusion(bf16[768,640]{1,0:T(8,128)(2,1)} %bitcast.14, bf16[768,768]{1,0:T(8,128)(2,1)} %all-gather.5.cloned.1.call-done), kind=kOutput, calls=%fused_computation.3 | convolution fusion | flops 755466240 | bytes 3145728 | tf_op jit(solution)/shard_map/dot_general | solution.py:77
  201.5 7.4 %all-to-all-done.3 = bf16[8,96,640]{2,1,0:T(8,128)(2,1)} async-done(((bf16[8,96,640]{2,1,0:T(8,128)(2,1)}), bf16[8,96,640]{2,1,0:T(8,128)(2,1)}, u32[]{:S(2)}, u32[]{:S(2)}) %all-to-all-start.3) | async-done | bytes 983072 | tf_op jit(solution)/shard_map/all_to_all | solution.py:88
  208.9 7.4 %all-to-all-start.5 = ((bf16[8,80,768]{2,1,0:T(8,128)(2,1)}), bf16[8,80,768]{2,1,0:T(8,128)(2,1)}, u32[]{:S(2)}, u32[]{:S(2)}) async-start(bf16[8,80,768]{2,1,0:T(8,128)(2,1)} %bitcast.57), calls=%async_computation.5 | async-start | bytes 1966080 | tf_op jit(solution)/shard_map/all_to_all | solution.py:80
  216.4 0.5 slice.25
  217.6 2.6 %fusion = f32[256,640]{1,0:T(8,128)} fusion(bf16[8,96,640]{2,1,0:T(8,128)(2,1)} %all-to-all-done.3, f32[]{:T(128)} %bitcast.6, bf16[96,256]{1,0:T(8,128)(2,1)S(1)} %fusion.6), kind=kOutput, calls=%fused_computation.5 | convolution fusion | flops 251822080 | bytes 1687556 | tf_op jit(solution)/shard_map/dot_general | solution.py:90
  220.1 23.4 %all-to-all-done.5 = bf16[8,80,768]{2,1,0:T(8,128)(2,1)} async-done(((bf16[8,80,768]{2,1,0:T(8,128)(2,1)}), bf16[8,80,768]{2,1,0:T(8,128)(2,1)}, u32[]{:S(2)}, u32[]{:S(2)}) %all-to-all-start.5) | async-done | bytes 983072 | tf_op jit(solution)/shard_map/all_to_all | solution.py:80
  243.6 1.4 convert_reduce_fusion
  244.9 0.7 broadcast_multiply_fusion
  (8 shorter events, 0.2 us)
Async XLA Ops:
  7.2 105.7 %copy-start = (bf16[256,5120]{1,0:T(8,128)(2,1)S(1)}, bf16[256,5120]{1,0:T(8,128)(2,1)}, u32[]{:S(2)}) copy-start(bf16[256,5120]{1,0:T(8,128)(2,1)} %param.6) | copy-start | bytes 7864324
  7.2 105.7 %all-gather.3.cloned.1.call-start = ((), (), s32[]{:S(2)}) async-start(), calls=%async_computation.6 | async-start | bytes 7987200 | tf_op jit(solution)/shard_map/all_gather | solution.py:35
  9.9 114.3 %copy-start.1 = (s32[256]{0:T(256)S(1)}, s32[256]{0:T(256)}, u32[]{:S(2)}) copy-start(s32[256]{0:T(256)} %param.9) | copy-start | bytes 3076
  9.9 117.8 %copy-start.2 = (f32[256]{0:T(256)S(1)}, f32[256]{0:T(256)}, u32[]{:S(2)}) copy-start(f32[256]{0:T(256)} %param.11) | copy-start | bytes 3076
  9.9 117.8 %copy-start.3 = (f32[256]{0:T(256)S(1)}, f32[256]{0:T(256)}, u32[]{:S(2)}) copy-start(f32[256]{0:T(256)} %param.10) | copy-start | bytes 3076
  119.5 8.2 %all-to-all-start = ((f32[8,4,256]{2,1,0:T(4,128)}), f32[8,4,256]{2,1,0:T(4,128)S(1)}, u32[]{:S(2)}, u32[]{:S(2)}) async-start(f32[8,4,256]{2,1,0:T(4,128)} %broadcast_in_dim.4), calls=%async_computation | async-start | bytes 65536 | tf_op jit(solution)/shard_map/all_to_all | solution.py:26
  130.2 15.2 %all-to-all-start.1 = ((f32[8,8,128]{2,1,0:T(8,128)}), f32[8,8,128]{2,1,0:T(8,128)S(1)}, u32[]{:S(2)}, u32[]{:S(2)}) async-start(f32[8,8,128]{2,1,0:T(8,128)} %broadcast_in_dim_broadcast_in_dim_broadcast_in_dim.3), calls=%async_computation.1 | async-start | bytes 65536 | tf_op jit(solution)/shard_map/all_to_all | solution.py:26
  145.3 30.0 %all-to-all-start.4 = ((bf16[8,96,640]{2,1,0:T(8,128)(2,1)}), bf16[8,96,640]{2,1,0:T(8,128)(2,1)}, u32[]{:S(2)}, u32[]{:S(2)}) async-start(bf16[8,96,640]{2,1,0:T(8,128)(2,1)} %copy.39), calls=%async_computation.4 | async-start | bytes 1966080 | tf_op jit(solution)/shard_map/all_to_all | solution.py:43
  149.6 48.4 %all-gather.5.cloned.1.call-start = ((), (), s32[]{:S(2)}) async-start(), calls=%async_computation.7 | async-start | bytes 1327104 | tf_op jit(solution)/shard_map/all_gather | solution.py:76
  175.9 13.4 %all-to-all-start.2 = ((f32[8,8,128]{2,1,0:T(8,128)}), f32[8,8,128]{2,1,0:T(8,128)S(1)}, u32[]{:S(2)}, u32[]{:S(2)}) async-start(f32[8,8,128]{2,1,0:T(8,128)} %broadcast_in_dim.5), calls=%async_computation.2 | async-start | bytes 65536 | tf_op jit(solution)/shard_map/all_to_all | solution.py:26
  189.3 19.6 %all-to-all-start.3 = ((bf16[8,96,640]{2,1,0:T(8,128)(2,1)}), bf16[8,96,640]{2,1,0:T(8,128)(2,1)}, u32[]{:S(2)}, u32[]{:S(2)}) async-start(bf16[8,96,640]{2,1,0:T(8,128)(2,1)} %bitcast.55), calls=%async_computation.3 | async-start | bytes 1966080 | tf_op jit(solution)/shard_map/all_to_all | solution.py:88
  208.9 34.6 %all-to-all-start.5 = ((bf16[8,80,768]{2,1,0:T(8,128)(2,1)}), bf16[8,80,768]{2,1,0:T(8,128)(2,1)}, u32[]{:S(2)}, u32[]{:S(2)}) async-start(bf16[8,80,768]{2,1,0:T(8,128)(2,1)} %bitcast.57), calls=%async_computation.5 | async-start | bytes 1966080 | tf_op jit(solution)/shard_map/all_to_all | solution.py:80
Sparse Core Ops, SparseCore 0:
  11.1 101.7 all-gather.2
  153.1 44.8 all-gather.4

commit v2 on v1

--- a/solution.py
+++ b/solution.py
@@ -46,6 +46,7 @@
     kept_y = jnp.sum(to_all(kept_here, "y", Y), axis=0)
     kept_total = jnp.sum(to_all(kept_y, "z", Z), axis=0)[0, 0]
     scale = -(LOSS_SCALE / kept_total)
+    hidden, kept_hidden, scale = lax.optimization_barrier((hidden, kept_hidden, scale))
 
     logits = jnp.dot(hidden, assembled, preferred_element_type=jnp.float32)
     local_target = targets - offset

time: 256 us -> 215 us (0.84); the launches traced: 252 us -> 214 us
  waiting for transfers between devices: 166 us -> 117 us
  blocking collectives: 0 us -> 7.98 us
  starting transfers between devices: 34.5 us -> 37.7 us
    all_gather x1, waiting for transfers between devices: 103 us -> 38.2 us  [per_device(): assembled = lax.all_gather(head_weight, ('y', 'z'), axis=0, tiled=True)]
    all_gather x1, waiting for transfers between devices: 2.37 us -> 27 us  [per_device(): all_slots = lax.all_gather(compact, 'z', axis=0, tiled=True)]
    all_to_all x0 -> x1, blocking collectives: none -> 7.98 us  [to_all(): lax.all_to_all(jnp.broadcast_to(values[None], (n,) + values.shape), axes,...]
    all_to_all x1, waiting for transfers between devices: 7.39 us -> 0.01 us  [per_device(): lax.all_to_all(hidden_part, ('x', 'c'), split_axis=0, concat_axis=0)]
    all_to_all x1, starting transfers between devices: 4.24 us -> 7.21 us  [per_device(): kept_hidden = lax.all_to_all(kept_hidden, 'z', split_axis=0, concat_axis=0)]
    all_to_all x3 -> x2, waiting for transfers between devices: 4.72 us -> 6.06 us  [to_all(): lax.all_to_all(jnp.broadcast_to(values[None], (n,) + values.shape), axes,...]
    all_to_all x3 -> x2, starting transfers between devices: 16.4 us -> 17.4 us  [to_all(): lax.all_to_all(jnp.broadcast_to(values[None], (n,) + values.shape), axes,...]
  transfers between devices with their start and end apart: 8 -> 7, of which waited for: 7 -> 5; matrix products, arithmetic and copies ran while one was open for 10% -> 13% of each run, Pallas kernels for 0% -> 0%
where the time goes in v2:
time: 215 us; the launch traced here: 214 us
  waiting for transfers between devices  117 us (54%)
  starting transfers between devices  37.7 us (18%)
  matrix products  20 us (9%)
  between operations  14.8 us (7%)
  local copies, waits for them, and re-layouts  11 us (5%)
  blocking collectives  7.98 us (4%)
  other arithmetic  6.35 us (3%)
    all_gather x1, waiting for transfers between devices, per_device(): assembled = lax.all_gather(head_weight, ('y', 'z'), axis=0, tiled=True)  38.2 us
    all_gather x1, waiting for transfers between devices, per_device(): all_slots = lax.all_gather(compact, 'z', axis=0, tiled=True)  27 us
    all_to_all x1, waiting for transfers between devices, per_device(): kept_hidden = lax.all_to_all(kept_hidden, 'z', split_axis=0, concat_axis=0)  23.7 us
    all_to_all x1, waiting for transfers between devices, per_device(): lax.all_to_all(partial_head.reshape(Y, rows, cols), 'y', split_axis=0, co...  21.1 us
    all_to_all x2, starting transfers between devices, to_all(): lax.all_to_all(jnp.broadcast_to(values[None], (n,) + values.shape), axes,...  17.4 us
    all_to_all x1, blocking collectives, to_all(): lax.all_to_all(jnp.broadcast_to(values[None], (n,) + values.shape), axes,...  7.98 us
    all_to_all x1, starting transfers between devices, per_device(): kept_hidden = lax.all_to_all(kept_hidden, 'z', split_axis=0, concat_axis=0)  7.21 us
    all_to_all x1, starting transfers between devices, per_device(): lax.all_to_all(partial_head.reshape(Y, rows, cols), 'y', split_axis=0, co...  6.76 us
  transfers between devices with their start and end apart: 7, of which 5 were waited for; matrix products, arithmetic and copies ran while one was open for 13% of the time, Pallas kernels for 0%

profile of v2, /device:TPU:6, one launch (start us, length us, event | category | flops | bytes accessed | tf_op | source)
XLA Modules:
  0.0 214.5 jit_solution(9993046085650656112)
XLA Ops:
  7.2 0.0 copy-start
  7.2 0.0 all-gather.3.cloned.1.call-start
  7.2 0.7 all-gather.3.cloned.1.call-update
  7.9 1.3 convert_reduce_fusion.1
  9.2 1.3 broadcast_in_dim_broadcast_in_dim_broadcast_in_dim.3
  10.5 7.1 %all-to-all-start.1 = ((f32[8,8,128]{2,1,0:T(8,128)}), f32[8,8,128]{2,1,0:T(8,128)S(1)}, u32[]{:S(2)}, u32[]{:S(2)}) async-start(f32[8,8,128]{2,1,0:T(8,128)} %broadcast_in_dim_broadcast_in_dim_broadcast_in_dim.3), calls=%async_computation.1 | async-start | bytes 65536 | tf_op jit(solution)/shard_map/all_to_all | solution.py:26
  17.6 1.0 reduce-window.9
  18.6 0.1 slice.22
  18.7 0.1 slice_reduce_fusion.1
  18.8 0.1 add_bitcast_fusion
  18.9 0.7 broadcast_compare_fusion
  19.6 6.1 %all-to-all-done.1 = f32[8,8,128]{2,1,0:T(8,128)S(1)} async-done(((f32[8,8,128]{2,1,0:T(8,128)}), f32[8,8,128]{2,1,0:T(8,128)S(1)}, u32[]{:S(2)}, u32[]{:S(2)}) %all-to-all-start.1) | async-done | bytes 32800 | tf_op jit(solution)/shard_map/all_to_all | solution.py:26
  25.6 0.6 broadcast_in_dim.4
  26.3 10.3 %all-to-all-start.2 = ((f32[8,8,128]{2,1,0:T(8,128)}), f32[8,8,128]{2,1,0:T(8,128)S(1)}, u32[]{:S(2)}, u32[]{:S(2)}) async-start(f32[8,8,128]{2,1,0:T(8,128)} %broadcast_in_dim.4), calls=%async_computation.2 | async-start | bytes 65536 | tf_op jit(solution)/shard_map/all_to_all | solution.py:26
  36.6 0.0 copy-done
  36.6 1.5 convolution_convert_fusion.1
  38.1 2.4 %copy.33 = bf16[96,5120]{0,1:T(8,128)(2,1)} copy(bf16[96,5120]{1,0:T(8,128)(2,1)} %convolution_convert_fusion.1) | data formatting | bytes 1966080 | tf_op jit(solution)/shard_map/convert_element_type | solution.py:41
  40.5 2.5 %copy.34 = bf16[8,96,8,80]{1,3,2,0:T(8,128)(2,1)} copy(bf16[8,96,8,80]{1,3,0,2:T(8,128)(2,1)} %bitcast.53) | data formatting | bytes 1966080 | tf_op jit(solution)/shard_map/transpose | solution.py:42
  43.0 0.0 copy-start.4
  43.0 2.4 %copy.35 = bf16[8,96,640]{2,1,0:T(8,128)(2,1)} copy(bf16[8,96,640]{1,2,0:T(8,128)(2,1)} %bitcast.54) | data formatting | bytes 1966080 | tf_op jit(solution)/shard_map/reshape | solution.py:42
  45.4 0.0 all-to-all-done.2
  45.4 7.2 %all-to-all-start = ((bf16[8,96,640]{2,1,0:T(8,128)(2,1)}), bf16[8,96,640]{2,1,0:T(8,128)(2,1)}, u32[]{:S(2)}, u32[]{:S(2)}) async-start(bf16[8,96,640]{2,1,0:T(8,128)(2,1)} %copy.35), calls=%async_computation | async-start | bytes 1966080 | tf_op jit(solution)/shard_map/all_to_all | solution.py:43
  52.6 0.0 all-gather.5.cloned.1.call-start
  52.7 0.0 copy-done.4
  52.7 0.5 slice.24
  53.9 23.7 %all-to-all-done = bf16[8,96,640]{2,1,0:T(8,128)(2,1)} async-done(((bf16[8,96,640]{2,1,0:T(8,128)(2,1)}), bf16[8,96,640]{2,1,0:T(8,128)(2,1)}, u32[]{:S(2)}, u32[]{:S(2)}) %all-to-all-start) | async-done | bytes 983072 | tf_op jit(solution)/shard_map/all_to_all | solution.py:43
  77.6 0.0 copy-start.1
  77.6 0.0 copy-start.2
  77.6 0.0 copy-start.3
  77.6 38.2 %all-gather.3.cloned.1.call-done = bf16[5120,768]{1,0:T(8,128)(2,1)} async-done(((bf16[80,768]{1,0:T(8,128)(2,1)}), bf16[5120,768]{1,0:T(8,128)(2,1)}) %all-gather.3.cloned.1.call-update) | async-done | bytes 7864336 | tf_op jit(solution)/shard_map/all_gather | solution.py:35
  115.8 5.5 %fusion.17 = (f32[256]{0:T(256)S(1)}, f32[256,768]{1,0:T(8,128)S(1)}) fusion(bf16[256,5120]{1,0:T(8,128)(2,1)S(1)} %copy-done, bf16[5120,768]{1,0:T(8,128)(2,1)} %all-gather.3.cloned.1.call-done), kind=kOutput, calls=%fused_computation.43 | convolution fusion | flops 2013462272 | bytes 11273216 | tf_op jit(solution)/shard_map/dot_general | solution.py:51
  121.3 0.5 exponential_reduce_fusion
  121.8 8.0 %all_to_all.30 = f32[8,4,256]{2,1,0:T(4,128)S(1)} all-to-all(f32[8,4,256]{2,1,0:T(4,128)S(1)} %broadcast_in_dim.5), channel_id=1, replica_groups=mesh['y'=8,'z'=8,'x'=4,'c'=2] {'x','c'}, dimensions={0} | all-to-all | bytes 65536 | tf_op jit(solution)/shard_map/all_to_all | solution.py:26
  129.9 0.0 copy-done.1
  129.9 0.0 copy-done.2
  129.9 0.0 copy-done.3
  129.9 0.6 fusion.15
  130.5 1.1 convolution_convert_fusion.3
  131.6 0.0 all-gather.5.cloned.1.call-update
  131.6 5.8 %convolution_convert_fusion = bf16[96,5120]{1,0:T(8,128)(2,1)S(1)} fusion(bf16[96,768]{1,0:T(8,128)(2,1)} %convolution_convert_fusion.3, bf16[5120,768]{1,0:T(8,128)(2,1)} %all-gather.3.cloned.1.call-done), kind=kOutput, calls=%fused_computation | convolution fusion | flops 755466240 | bytes 8994816 | tf_op jit(solution)/shard_map/dot_general | solution.py:84
  137.4 1.1 copy.60
  138.5 6.2 %all-to-all-start.4 = ((bf16[8,96,640]{2,1,0:T(8,128)(2,1)}), bf16[8,96,640]{2,1,0:T(8,128)(2,1)}, u32[]{:S(2)}, u32[]{:S(2)}) async-start(bf16[8,96,640]{2,1,0:T(8,128)(2,1)} %bitcast.55), calls=%async_computation.4 | async-start | bytes 1966080 | tf_op jit(solution)/shard_map/all_to_all | solution.py:89
  144.7 27.0 %all-gather.5.cloned.1.call-done = bf16[768,768]{1,0:T(8,128)(2,1)} async-done(((bf16[96,768]{1,0:T(8,128)(2,1)}), bf16[768,768]{1,0:T(8,128)(2,1)}) %all-gather.5.cloned.1.call-update) | async-done | bytes 1179664 | tf_op jit(solution)/shard_map/all_gather | solution.py:77
  171.7 3.5 %convolution_convert_fusion.2 = bf16[640,768]{1,0:T(8,128)(2,1)} fusion(bf16[768,640]{1,0:T(8,128)(2,1)} %bitcast.5, bf16[768,768]{1,0:T(8,128)(2,1)} %all-gather.5.cloned.1.call-done), kind=kOutput, calls=%fused_computation.3 | convolution fusion | flops 755466240 | bytes 3145728 | tf_op jit(solution)/shard_map/dot_general | solution.py:78
  175.2 0.0 all-to-all-done.4
  175.2 6.8 %all-to-all-start.5 = ((bf16[8,80,768]{2,1,0:T(8,128)(2,1)}), bf16[8,80,768]{2,1,0:T(8,128)(2,1)}, u32[]{:S(2)}, u32[]{:S(2)}) async-start(bf16[8,80,768]{2,1,0:T(8,128)(2,1)} %bitcast.57), calls=%async_computation.5 | async-start | bytes 1966080 | tf_op jit(solution)/shard_map/all_to_all | solution.py:81
  182.0 2.6 %fusion = f32[256,640]{1,0:T(8,128)} fusion(bf16[8,96,640]{2,1,0:T(8,128)(2,1)} %all-to-all-done.4, f32[]{:T(128)} %bitcast.6, bf16[96,256]{1,0:T(8,128)(2,1)S(1)} %fusion.5), kind=kOutput, calls=%fused_computation.5 | convolution fusion | flops 251822080 | bytes 1687556 | tf_op jit(solution)/shard_map/dot_general | solution.py:91
  184.5 21.1 %all-to-all-done.5 = bf16[8,80,768]{2,1,0:T(8,128)(2,1)} async-done(((bf16[8,80,768]{2,1,0:T(8,128)(2,1)}), bf16[8,80,768]{2,1,0:T(8,128)(2,1)}, u32[]{:S(2)}, u32[]{:S(2)}) %all-to-all-start.5) | async-done | bytes 983072 | tf_op jit(solution)/shard_map/all_to_all | solution.py:81
  205.6 1.4 convert_reduce_fusion
  206.9 0.7 broadcast_multiply_fusion
  (9 shorter events, 0.2 us)
Async XLA Ops:
  7.2 29.4 %copy-start = (bf16[256,5120]{1,0:T(8,128)(2,1)S(1)}, bf16[256,5120]{1,0:T(8,128)(2,1)}, u32[]{:S(2)}) copy-start(bf16[256,5120]{1,0:T(8,128)(2,1)} %param.6) | copy-start | bytes 7864324
  7.2 108.6 %all-gather.3.cloned.1.call-start = ((), (), s32[]{:S(2)}) async-start(), calls=%async_computation.6 | async-start | bytes 7987200 | tf_op jit(solution)/shard_map/all_gather | solution.py:35
  10.5 15.1 %all-to-all-start.1 = ((f32[8,8,128]{2,1,0:T(8,128)}), f32[8,8,128]{2,1,0:T(8,128)S(1)}, u32[]{:S(2)}, u32[]{:S(2)}) async-start(f32[8,8,128]{2,1,0:T(8,128)} %broadcast_in_dim_broadcast_in_dim_broadcast_in_dim.3), calls=%async_computation.1 | async-start | bytes 65536 | tf_op jit(solution)/shard_map/all_to_all | solution.py:26
  26.3 19.1 %all-to-all-start.2 = ((f32[8,8,128]{2,1,0:T(8,128)}), f32[8,8,128]{2,1,0:T(8,128)S(1)}, u32[]{:S(2)}, u32[]{:S(2)}) async-start(f32[8,8,128]{2,1,0:T(8,128)} %broadcast_in_dim.4), calls=%async_computation.2 | async-start | bytes 65536 | tf_op jit(solution)/shard_map/all_to_all | solution.py:26
  43.0 9.7 %copy-start.4 = (s32[256]{0:T(256)S(1)}, s32[256]{0:T(256)}, u32[]{:S(2)}) copy-start(s32[256]{0:T(256)} %param.8) | copy-start | bytes 3076
  45.4 32.2 %all-to-all-start = ((bf16[8,96,640]{2,1,0:T(8,128)(2,1)}), bf16[8,96,640]{2,1,0:T(8,128)(2,1)}, u32[]{:S(2)}, u32[]{:S(2)}) async-start(bf16[8,96,640]{2,1,0:T(8,128)(2,1)} %copy.35), calls=%async_computation | async-start | bytes 1966080 | tf_op jit(solution)/shard_map/all_to_all | solution.py:43
  52.6 119.1 %all-gather.5.cloned.1.call-start = ((), (), s32[]{:S(2)}) async-start(), calls=%async_computation.7 | async-start | bytes 1327104 | tf_op jit(solution)/shard_map/all_gather | solution.py:77
  77.6 52.2 %copy-start.1 = (s32[256]{0:T(256)S(1)}, s32[256]{0:T(256)}, u32[]{:S(2)}) copy-start(s32[256]{0:T(256)} %param.9) | copy-start | bytes 3076
  77.6 52.2 %copy-start.2 = (f32[256]{0:T(256)S(1)}, f32[256]{0:T(256)}, u32[]{:S(2)}) copy-start(f32[256]{0:T(256)} %param.11) | copy-start | bytes 3076
  77.6 52.2 %copy-start.3 = (f32[256]{0:T(256)S(1)}, f32[256]{0:T(256)}, u32[]{:S(2)}) copy-start(f32[256]{0:T(256)} %param.10) | copy-start | bytes 3076
  138.5 36.7 %all-to-all-start.4 = ((bf16[8,96,640]{2,1,0:T(8,128)(2,1)}), bf16[8,96,640]{2,1,0:T(8,128)(2,1)}, u32[]{:S(2)}, u32[]{:S(2)}) async-start(bf16[8,96,640]{2,1,0:T(8,128)(2,1)} %bitcast.55), calls=%async_computation.4 | async-start | bytes 1966080 | tf_op jit(solution)/shard_map/all_to_all | solution.py:89
  175.2 30.4 %all-to-all-start.5 = ((bf16[8,80,768]{2,1,0:T(8,128)(2,1)}), bf16[8,80,768]{2,1,0:T(8,128)(2,1)}, u32[]{:S(2)}, u32[]{:S(2)}) async-start(bf16[8,80,768]{2,1,0:T(8,128)(2,1)} %bitcast.57), calls=%async_computation.5 | async-start | bytes 1966080 | tf_op jit(solution)/shard_map/all_to_all | solution.py:81
Sparse Core Ops, SparseCore 0:
  11.1 104.6 all-gather.2
  131.7 39.9 all-gather.4

commit v3 on v2

--- a/solution.py
+++ b/solution.py
@@ -5,6 +5,7 @@
 
 Y, Z, X, C = 8, 8, 4, 2
 V = X * C
+KEEP_MOST = 80
 SLOTS = 96
 CLIP_EPS = 0.2
 LOSS_SCALE = 8192.0
@@ -22,33 +23,67 @@
     return keep_float * choose_grad * importance
 
 
+def exchange(parts, axes):
+    return lax.all_to_all(parts, axes, split_axis=0, concat_axis=0)
+
+
 def to_all(values, axes, n):
-    return lax.all_to_all(
-        jnp.broadcast_to(values[None], (n,) + values.shape), axes, split_axis=0, concat_axis=0
-    )
+    return exchange(jnp.broadcast_to(values[None], (n,) + values.shape), axes)
+
+
+def shift(block, step):
+    return lax.ppermute(block, "z", [(i, (i + step) % Z) for i in range(Z)])
+
+
+def ring_over_z(own):
+    here = lax.axis_index("z")
+    whole = jnp.zeros((Y, Z) + own.shape[1:], own.dtype)
+
+    def put(whole, block, away, first=0):
+        at = lax.rem(here + away + Z, Z)
+        return lax.dynamic_update_slice(whole, block[:, None], (first, at, 0, 0))
+
+    whole = put(whole, own, 0)
+    up = down = own
+    for hop in range(1, Z // 2):
+        up, down = shift(up, 1), shift(down, -1)
+        whole = put(put(whole, up, -hop), down, hop)
+    half = Y // 2
+    up, down = shift(up[:half], 1), shift(down[half:], -1)
+    whole = put(whole, up, -(Z // 2))
+    return put(whole, down, Z // 2, half)
 
 
 def per_device(hidden, head_weight, targets, kept_mask, old_logprob, advantage):
     tokens, width = hidden.shape
     rows, cols = head_weight.shape
+    half = cols // 2
     offset = (lax.axis_index("x") * C + lax.axis_index("c")) * cols
-    assembled = lax.all_gather(head_weight, ("y", "z"), axis=0, tiled=True)
+
+    head_a = lax.all_gather(head_weight[:, :half], ("y", "z"), axis=0, tiled=True)
+    small_b = to_all(head_weight[:, half:], "y", Y)
 
     keep_float = kept_mask.astype(jnp.float32)
     slot_index = jnp.cumsum(kept_mask) - 1
     ids = jnp.arange(SLOTS, dtype=jnp.int32)
     selector = ((slot_index[None, :] == ids[:, None]) & (kept_mask[None, :] == 1)).astype(jnp.bfloat16)
-    kept_hidden = jnp.dot(selector, hidden, preferred_element_type=jnp.float32).astype(jnp.bfloat16)
-    kept_hidden = kept_hidden.reshape(SLOTS, Y, Z, rows).transpose(2, 0, 1, 3).reshape(Z, SLOTS, Y * rows)
-    kept_hidden = lax.all_to_all(kept_hidden, "z", split_axis=0, concat_axis=0)
-    kept_hidden = kept_hidden.reshape(Z * SLOTS, Y * rows)
-    kept_here = jnp.broadcast_to(jnp.sum(keep_float), (8, 128))
-    kept_y = jnp.sum(to_all(kept_here, "y", Y), axis=0)
-    kept_total = jnp.sum(to_all(kept_y, "z", Z), axis=0)[0, 0]
+    hidden_early, small_b = lax.optimization_barrier((hidden, small_b))
+    head_b = ring_over_z(small_b).reshape(width, half)
+    kept_hidden = jnp.dot(selector, hidden_early, preferred_element_type=jnp.float32)
+    kept_hidden = jnp.where(ids[:, None] < KEEP_MOST, kept_hidden, jnp.sum(keep_float)).astype(jnp.bfloat16)
+    kept_hidden = exchange(kept_hidden.reshape(SLOTS, Y, Z * rows).transpose(1, 0, 2), "y")
+    kept_y = jnp.sum(kept_hidden[:, KEEP_MOST, :128].astype(jnp.float32), axis=0)
+    kept_total = jnp.sum(to_all(jnp.broadcast_to(kept_y, (8, 128)), "z", Z), axis=0)[0, 0]
     scale = -(LOSS_SCALE / kept_total)
     hidden, kept_hidden, scale = lax.optimization_barrier((hidden, kept_hidden, scale))
 
-    logits = jnp.dot(hidden, assembled, preferred_element_type=jnp.float32)
+    logits = jnp.concatenate(
+        [
+            jnp.dot(hidden, head_a, preferred_element_type=jnp.float32),
+            jnp.dot(hidden, head_b, preferred_element_type=jnp.float32),
+        ],
+        axis=1,
+    )
     local_target = targets - offset
     positions = jnp.arange(cols, dtype=jnp.int32)
     onehot = (positions[None, :] == local_target[:, None]).astype(jnp.float32)
@@ -74,19 +109,21 @@
     logit_grads = (slope[:, None] * (onehot - softmax_rows)).astype(jnp.bfloat16)
     compact = jnp.dot(selector, logit_grads, preferred_element_type=jnp.float32).astype(jnp.bfloat16)
 
-    all_slots = lax.all_gather(compact, "z", axis=0, tiled=True)
-    partial_head = lax.dot_general(
-        kept_hidden, all_slots, (((0,), (0,)), ((), ())), preferred_element_type=jnp.float32
+    all_slots = lax.all_gather(compact, "y", axis=0, tiled=True)
+    part_head = lax.dot_general(
+        kept_hidden.reshape(Y * SLOTS, Z * rows), all_slots, (((0,), (0,)), ((), ())),
+        preferred_element_type=jnp.float32,
     ).astype(jnp.bfloat16)
-    parts = lax.all_to_all(partial_head.reshape(Y, rows, cols), "y", split_axis=0, concat_axis=0)
-    grad_head = scale * jnp.sum(parts.astype(jnp.float32), axis=0)
+    sums = exchange(part_head.reshape(Z, rows, cols), "z")
+    grad_head = scale * jnp.sum(sums.astype(jnp.float32), axis=0)
 
-    hidden_part = lax.dot_general(
-        compact, assembled, (((1,), (1,)), ((), ())), preferred_element_type=jnp.float32
+    over_cols = (((1,), (1,)), ((), ()))
+    hidden_part = (
+        lax.dot_general(compact[:, :half], head_a, over_cols, preferred_element_type=jnp.float32)
+        + lax.dot_general(compact[:, half:], head_b, over_cols, preferred_element_type=jnp.float32)
     ).astype(jnp.bfloat16)
     mine = width // V
-    hidden_part = hidden_part.reshape(SLOTS, V, mine).transpose(1, 0, 2)
-    hidden_part = lax.all_to_all(hidden_part, ("x", "c"), split_axis=0, concat_axis=0)
+    hidden_part = exchange(hidden_part.reshape(SLOTS, V, mine).transpose(1, 0, 2), ("x", "c"))
     spread = jnp.tile(selector, (V, 1))
     grad_hidden = scale * lax.dot_general(
         spread, hidden_part.reshape(V * SLOTS, mine), (((0,), (0,)), ((), ())),

time: 215 us -> 223 us (1.037)
  waiting for transfers between devices: 117 us -> 86.3 us
  starting transfers between devices: 37.7 us -> 63.4 us
  local copies, waits for them, and re-layouts: 11 us -> 18.6 us
  matrix products: 20 us -> 22.8 us
    all_gather x2, waiting for transfers between devices: 65.2 us -> 22.3 us  [the longest x1 22.3 us: per_device(): all_slots = lax.all_gather(compact, 'y', axis=0, tiled=True)]
    ppermute x0 -> x8, starting transfers between devices: none -> 34.7 us  [shift(): return lax.ppermute(block, 'z', [(i, (i + step) % Z) for i in range(Z)])]
    ppermute x0 -> x8, waiting for transfers between devices: none -> 23.3 us  [shift(): return lax.ppermute(block, 'z', [(i, (i + step) % Z) for i in range(Z)])]
    all_to_all x5, waiting for transfers between devices: 50.8 us -> 40.7 us  [exchange(): return lax.all_to_all(parts, axes, split_axis=0, concat_axis=0)]
    dynamic_update_slice x0 -> x9, local copies, waits for them, and re-layouts: none -> 9.54 us  [put(): return lax.dynamic_update_slice(whole, block[:, None], (first, at, 0, 0))]
    all_to_all x5, starting transfers between devices: 37.6 us -> 28.7 us  [exchange(): return lax.all_to_all(parts, axes, split_axis=0, concat_axis=0)]
    dot_general x4 -> x6, matrix products: 16.3 us -> 19.2 us  [the longest x1 3.77 us: per_device(): jnp.dot(hidden, head_a, preferred_element_type=jnp.float32)]
    broadcast_in_dim x2 -> x3, local copies, waits for them, and re-layouts: 0.63 us -> 3.13 us  [the longest x1 2.3 us: ring_over_z(): whole = jnp.zeros((Y, Z) + own.shape[1:], own.dtype)]
  transfers between devices with their start and end apart: 7 -> 15, of which waited for: 5 -> 8; matrix products, arithmetic and copies ran while one was open for 13% -> 18% of each run, Pallas kernels for 0% -> 0%
where the time goes in v3:
time: 223 us; the launch traced here: 222 us
  waiting for transfers between devices  86.3 us (39%)
  starting transfers between devices  63.4 us (28%)
  matrix products  22.8 us (10%)
  local copies, waits for them, and re-layouts  18.6 us (8%)
  between operations  15 us (7%)
  blocking collectives  7.95 us (4%)
  other arithmetic  7.72 us (3%)
    all_to_all x5, waiting for transfers between devices, exchange(): return lax.all_to_all(parts, axes, split_axis=0, concat_axis=0)  40.7 us
    ppermute x8, starting transfers between devices, shift(): return lax.ppermute(block, 'z', [(i, (i + step) % Z) for i in range(Z)])  34.7 us
    all_to_all x5, starting transfers between devices, exchange(): return lax.all_to_all(parts, axes, split_axis=0, concat_axis=0)  28.7 us
    ppermute x8, waiting for transfers between devices, shift(): return lax.ppermute(block, 'z', [(i, (i + step) % Z) for i in range(Z)])  23.3 us
    all_gather x1, waiting for transfers between devices, per_device(): all_slots = lax.all_gather(compact, 'y', axis=0, tiled=True)  22.3 us
    dynamic_update_slice x9, local copies, waits for them, and re-layouts, put(): return lax.dynamic_update_slice(whole, block[:, None], (first, at, 0, 0))  9.54 us
    all_to_all x1, blocking collectives, exchange(): return lax.all_to_all(parts, axes, split_axis=0, concat_axis=0)  7.95 us
  transfers between devices with their start and end apart: 15, of which 8 were waited for; matrix products, arithmetic and copies ran while one was open for 18% of the time, Pallas kernels for 0%

profile of v3, /device:TPU:6, one launch (start us, length us, event | category | flops | bytes accessed | tf_op | source)
XLA Modules:
  0.0 221.8 jit_solution(10148988999055360891)
XLA Ops:
  7.2 0.0 all-gather.3.cloned.1.call-start
  7.2 1.6 fusion.23
  8.9 0.0 all-gather.3.cloned.1.call-update
  8.9 0.8 broadcast_in_dim.66
  9.7 7.1 %all-to-all-start = ((bf16[8,80,384]{2,1,0:T(8,128)(2,1)}), bf16[8,80,384]{2,1,0:T(8,128)(2,1)S(1)}, u32[]{:S(2)}, u32[]{:S(2)}) async-start(bf16[8,80,384]{2,1,0:T(8,128)(2,1)} %broadcast_in_dim.66), calls=%async_computation | async-start | bytes 983040 | tf_op jit(solution)/shard_map/all_to_all | solution.py:27
  16.8 1.0 reduce-window.9
  17.8 0.1 slice.43
  17.9 1.3 convert_reduce_fusion.1
  19.2 0.1 slice_reduce_fusion.1
  19.3 0.7 broadcast_compare_fusion
  20.0 0.7 broadcast_subtract_fusion
  20.7 0.1 add_bitcast_fusion
  20.8 12.8 %all-to-all-done = bf16[8,80,384]{2,1,0:T(8,128)(2,1)S(1)} async-done(((bf16[8,80,384]{2,1,0:T(8,128)(2,1)}), bf16[8,80,384]{2,1,0:T(8,128)(2,1)S(1)}, u32[]{:S(2)}, u32[]{:S(2)}) %all-to-all-start) | async-done | bytes 491552 | tf_op jit(solution)/shard_map/all_to_all | solution.py:27
  33.6 4.3 %collective-permute-start = (bf16[8,80,384]{2,1,0:T(8,128)(2,1)S(1)}, bf16[8,80,384]{2,1,0:T(8,128)(2,1)}, u32[]{:S(2)}, u32[]{:S(2)}) collective-permute-start(bf16[8,80,384]{2,1,0:T(8,128)(2,1)S(1)} %all-to-all-done), channel_id=1, source_target_pairs={{0,8},{8,16},{16,24},{24,32},{32,40},{40,48},{48,56},{56,0},{1,9},... | collective-permute-start | bytes 1474568 | tf_op jit(solution)/shard_map/ppermute | solution.py:35
  37.9 8.9 %collective-permute-start.1 = (bf16[8,80,384]{2,1,0:T(8,128)(2,1)S(1)}, bf16[8,80,384]{2,1,0:T(8,128)(2,1)}, u32[]{:S(2)}, u32[]{:S(2)}) collective-permute-start(bf16[8,80,384]{2,1,0:T(8,128)(2,1)S(1)} %all-to-all-done), channel_id=1, source_target_pairs={{0,56},{8,0},{16,8},{24,16},{32,24},{40,32},{48,40},{56,48},{1,57}... | collective-permute-start | bytes 1474568 | tf_op jit(solution)/shard_map/ppermute | solution.py:35
  46.8 1.2 fusion.1
  48.0 1.1 copy.70
  49.1 4.2 %all-to-all-start.1 = ((bf16[8,96,640]{2,1,0:T(8,128)(2,1)}), bf16[8,96,640]{2,1,0:T(8,128)(2,1)}, u32[]{:S(2)}, u32[]{:S(2)}) async-start(bf16[8,96,640]{2,1,0:T(8,128)(2,1)} %bitcast.93), calls=%async_computation.1 | async-start | bytes 1966080 | tf_op jit(solution)/shard_map/all_to_all | solution.py:27
  53.4 2.3 %broadcast_in_dim.68 = bf16[8,8,80,384]{3,2,1,0:T(8,128)(2,1)} broadcast(bf16[]{:T(256)} %constant.70.clone.1), dimensions={} | broadcast | bytes 3932162 | tf_op jit(solution)/shard_map/broadcast_in_dim | solution.py:40
  55.7 0.8 bitcast_dynamic-update-slice_fusion.6
  56.5 0.9 collective-permute-done
  57.4 1.9 collective-permute-start.2
  59.3 5.1 %collective-permute-start.3 = (bf16[8,80,384]{2,1,0:T(8,128)(2,1)}, bf16[8,80,384]{2,1,0:T(8,128)(2,1)S(1)}, u32[]{:S(2)}, u32[]{:S(2)}) collective-permute-start(bf16[8,80,384]{2,1,0:T(8,128)(2,1)} %collective-permute-done.1), channel_id=1, source_target_pairs={{0,56},{8,0},{16,8},{24,16},{32,24},{40,32},{48,40},{56,48},{1,57}... | collective-permute-start | bytes 1474568 | tf_op jit(solution)/shard_map/ppermute | solution.py:35
  64.5 1.9 bitcast_dynamic-update-slice_fusion.5
  66.3 1.9 bitcast_dynamic-update-slice_fusion.4
  68.3 5.0 %collective-permute-done.2 = bf16[8,80,384]{2,1,0:T(8,128)(2,1)S(1)} collective-permute-done((bf16[8,80,384]{2,1,0:T(8,128)(2,1)}, bf16[8,80,384]{2,1,0:T(8,128)(2,1)S(1)}, u32[]{:S(2)}, u32[]{:S(2)}) %collective-permute-start.2) | collective-permute-done | bytes 491552 | tf_op jit(solution)/shard_map/ppermute | solution.py:35
  73.2 1.9 collective-permute-start.4
  75.1 0.8 collective-permute-done.3
  75.9 5.5 %collective-permute-start.5 = (bf16[8,80,384]{2,1,0:T(8,128)(2,1)S(1)}, bf16[8,80,384]{2,1,0:T(8,128)(2,1)S(1)}, u32[]{:S(2)}, u32[]{:S(2)}) collective-permute-start(bf16[8,80,384]{2,1,0:T(8,128)(2,1)S(1)} %collective-permute-done.3), channel_id=1, source_target_pairs={{0,56},{8,0},{16,8},{24,16},{32,24},{40,32},{48,40},{56,48},{1,57}... | collective-permute-start | bytes 1474568 | tf_op jit(solution)/shard_map/ppermute | solution.py:35
  81.4 0.9 bitcast_dynamic-update-slice_fusion.3
  82.3 0.8 bitcast_dynamic-update-slice_fusion.2
  83.1 16.6 %collective-permute-done.4 = bf16[8,80,384]{2,1,0:T(8,128)(2,1)S(1)} collective-permute-done((bf16[8,80,384]{2,1,0:T(8,128)(2,1)S(1)}, bf16[8,80,384]{2,1,0:T(8,128)(2,1)S(1)}, u32[]{:S(2)}, u32[]{:S(2)}) %collective-permute-start.4) | collective-permute-done | bytes 491552 | tf_op jit(solution)/shard_map/ppermute | solution.py:35
  99.8 1.9 collective-permute-start.6
  101.7 0.7 slice.59
  102.4 5.1 %collective-permute-start.7 = (bf16[4,80,384]{2,1,0:T(8,128)(2,1)}, bf16[4,80,384]{2,1,0:T(8,128)(2,1)S(1)}, u32[]{:S(2)}, u32[]{:S(2)}) collective-permute-start(bf16[4,80,384]{2,1,0:T(8,128)(2,1)} %slice.59), channel_id=1, source_target_pairs={{0,56},{8,0},{16,8},{24,16},{32,24},{40,32},{48,40},{56,48},{1,57}... | collective-permute-start | bytes 737288 | tf_op jit(solution)/shard_map/ppermute | solution.py:35
  107.5 0.9 bitcast_dynamic-update-slice_fusion.1
  108.4 0.8 bitcast_dynamic-update-slice_fusion
  109.3 0.7 fusion.19
  110.0 0.6 broadcast_in_dim_broadcast_in_dim_broadcast_in_dim.3
  110.6 3.7 %all-to-all-start.2 = ((f32[8,8,128]{2,1,0:T(8,128)}), f32[8,8,128]{2,1,0:T(8,128)S(1)}, u32[]{:S(2)}, u32[]{:S(2)}) async-start(f32[8,8,128]{2,1,0:T(8,128)} %broadcast_in_dim_broadcast_in_dim_broadcast_in_dim.3), calls=%async_computation.2 | async-start | bytes 65536 | tf_op jit(solution)/shard_map/all_to_all | solution.py:27
  114.3 0.0 all-gather.5.cloned.1.call-start
  114.4 0.7 bitcast_dynamic-update-slice_fusion.7
  115.1 0.8 bitcast_dynamic-update-slice_fusion.8
  115.9 6.5 %all-to-all-done.2 = f32[8,8,128]{2,1,0:T(8,128)S(1)} async-done(((f32[8,8,128]{2,1,0:T(8,128)}), f32[8,8,128]{2,1,0:T(8,128)S(1)}, u32[]{:S(2)}, u32[]{:S(2)}) %all-to-all-start.2) | async-done | bytes 32800 | tf_op jit(solution)/shard_map/all_to_all | solution.py:27
  122.4 0.5 slice.47
  123.6 3.7 %fusion.26 = (f32[256]{0:T(256)S(1)}, f32[256,384]{1,0:T(8,128)S(1)}) fusion(bf16[256,5120]{1,0:T(8,128)(2,1)S(1)} %copy-done, bf16[5120,384]{1,0:T(8,128)(2,1)} %bitcast.21), kind=kOutput, calls=%fused_computation.65 | convolution fusion | flops 1006731008 | bytes 6947840 | tf_op jit(solution)/shard_map/dot_general | solution.py:83
  127.3 0.0 all-gather.3.cloned.1.call-done
  127.4 3.8 %fusion.25 = (f32[256]{0:T(256)S(1)}, f32[256,384]{1,0:T(8,128)S(1)}) fusion(bf16[256,5120]{1,0:T(8,128)(2,1)S(1)} %copy-done, bf16[5120,384]{1,0:T(8,128)(2,1)} %all-gather.3.cloned.1.call-done), kind=kOutput, calls=%fused_computation.64 | convolution fusion | flops 1006731008 | bytes 6947840 | tf_op jit(solution)/shard_map/dot_general | solution.py:82
  131.1 0.5 exponential_reduce_fusion
  131.7 7.9 %all_to_all.30 = f32[8,4,256]{2,1,0:T(4,128)S(1)} all-to-all(f32[8,4,256]{2,1,0:T(4,128)S(1)} %broadcast_in_dim.78), channel_id=1, replica_groups=mesh['y'=8,'z'=8,'x'=4,'c'=2] {'x','c'}, dimensions={0} | all-to-all | bytes 65536 | tf_op jit(solution)/shard_map/all_to_all | solution.py:27
  139.7 0.6 fusion.21
  140.3 1.1 convolution_convert_fusion.1
  141.4 0.0 all-gather.5.cloned.1.call-update
  141.4 3.5 %fusion.10 = f32[96,5120]{1,0:T(8,128)S(1)} fusion(bf16[5120,384]{1,0:T(8,128)(2,1)} %all-gather.3.cloned.1.call-done, bf16[96,768]{1,0:T(8,128)(2,1)} %convolution_convert_fusion.1), kind=kOutput, calls=%fused_computation.33 | convolution fusion | flops 377487360 | bytes 5971968 | tf_op jit(solution)/shard_map/dot_general | solution.py:122
  145.0 3.4 %fusion = bf16[96,5120]{1,0:T(8,128)(2,1)S(1)} fusion(f32[96,5120]{1,0:T(8,128)S(1)} %fusion.10, bf16[5120,384]{1,0:T(8,128)(2,1)} %bitcast.21, bf16[96,768]{1,0:T(8,128)(2,1)S(1)} %copy-done.1), kind=kOutput, calls=%fused_computation.2 | convolution fusion | flops 378470400 | bytes 6955008 | tf_op jit(solution)/shard_map/dot_general | solution.py:123
  148.4 1.0 copy.69
  149.4 6.2 %all-to-all-start.4 = ((bf16[8,96,640]{2,1,0:T(8,128)(2,1)}), bf16[8,96,640]{2,1,0:T(8,128)(2,1)}, u32[]{:S(2)}, u32[]{:S(2)}) async-start(bf16[8,96,640]{2,1,0:T(8,128)(2,1)} %bitcast.94), calls=%async_computation.4 | async-start | bytes 1966080 | tf_op jit(solution)/shard_map/all_to_all | solution.py:27
  155.7 22.3 %all-gather.5.cloned.1.call-done = bf16[768,768]{1,0:T(8,128)(2,1)} async-done(((bf16[96,768]{1,0:T(8,128)(2,1)}), bf16[768,768]{1,0:T(8,128)(2,1)}) %all-gather.5.cloned.1.call-update) | async-done | bytes 1179664 | tf_op jit(solution)/shard_map/all_gather | solution.py:112
  178.0 3.5 %convolution_convert_fusion = bf16[640,768]{1,0:T(8,128)(2,1)} fusion(bf16[768,640]{1,0:T(8,128)(2,1)} %bitcast.30, bf16[768,768]{1,0:T(8,128)(2,1)} %all-gather.5.cloned.1.call-done), kind=kOutput, calls=%fused_computation.5 | convolution fusion | flops 755466240 | bytes 3145728 | tf_op jit(solution)/shard_map/dot_general | solution.py:113
  181.5 7.4 %all-to-all-start.5 = ((bf16[8,80,768]{2,1,0:T(8,128)(2,1)}), bf16[8,80,768]{2,1,0:T(8,128)(2,1)}, u32[]{:S(2)}, u32[]{:S(2)}) async-start(bf16[8,80,768]{2,1,0:T(8,128)(2,1)} %bitcast.97), calls=%async_computation.5 | async-start | bytes 1966080 | tf_op jit(solution)/shard_map/all_to_all | solution.py:27
  188.9 2.6 %fusion.2 = f32[256,640]{1,0:T(8,128)} fusion(bf16[8,96,640]{2,1,0:T(8,128)(2,1)} %all-to-all-done.4, f32[]{:T(128)} %bitcast.3, bf16[96,256]{1,0:T(8,128)(2,1)S(1)} %fusion.7), kind=kOutput, calls=%fused_computation.7 | convolution fusion | flops 251822080 | bytes 1687556 | tf_op jit(solution)/shard_map/dot_general | solution.py:128
  191.5 21.4 %all-to-all-done.5 = bf16[8,80,768]{2,1,0:T(8,128)(2,1)} async-done(((bf16[8,80,768]{2,1,0:T(8,128)(2,1)}), bf16[8,80,768]{2,1,0:T(8,128)(2,1)}, u32[]{:S(2)}, u32[]{:S(2)}) %all-to-all-start.5) | async-done | bytes 983072 | tf_op jit(solution)/shard_map/all_to_all | solution.py:27
  212.9 1.4 convert_reduce_fusion
  214.2 0.7 broadcast_multiply_fusion
  (26 shorter events, 0.2 us)
Async XLA Ops:
  7.2 39.6 %copy-start = (bf16[256,5120]{1,0:T(8,128)(2,1)S(1)}, bf16[256,5120]{1,0:T(8,128)(2,1)}, u32[]{:S(2)}) copy-start(bf16[256,5120]{1,0:T(8,128)(2,1)} %param.6) | copy-start | bytes 7864324
  7.2 120.2 %all-gather.3.cloned.1.call-start = ((), (), s32[]{:S(2)}) async-start(), calls=%async_computation.6 | async-start | bytes 3993600 | tf_op jit(solution)/shard_map/all_gather | solution.py:63
  9.7 23.9 %all-to-all-start = ((bf16[8,80,384]{2,1,0:T(8,128)(2,1)}), bf16[8,80,384]{2,1,0:T(8,128)(2,1)S(1)}, u32[]{:S(2)}, u32[]{:S(2)}) async-start(bf16[8,80,384]{2,1,0:T(8,128)(2,1)} %broadcast_in_dim.66), calls=%async_computation | async-start | bytes 983040 | tf_op jit(solution)/shard_map/all_to_all | solution.py:27
  33.6 23.8 %collective-permute-start = (bf16[8,80,384]{2,1,0:T(8,128)(2,1)S(1)}, bf16[8,80,384]{2,1,0:T(8,128)(2,1)}, u32[]{:S(2)}, u32[]{:S(2)}) collective-permute-start(bf16[8,80,384]{2,1,0:T(8,128)(2,1)S(1)} %all-to-all-done), channel_id=1, source_target_pairs={{0,8},{8,16},{16,24},{24,32},{32,40},{40,48},{48,56},{56,0},{1,9},... | collective-permute-start | bytes 1474568 | tf_op jit(solution)/shard_map/ppermute | solution.py:35
  37.9 21.4 %collective-permute-start.1 = (bf16[8,80,384]{2,1,0:T(8,128)(2,1)S(1)}, bf16[8,80,384]{2,1,0:T(8,128)(2,1)}, u32[]{:S(2)}, u32[]{:S(2)}) collective-permute-start(bf16[8,80,384]{2,1,0:T(8,128)(2,1)S(1)} %all-to-all-done), channel_id=1, source_target_pairs={{0,56},{8,0},{16,8},{24,16},{32,24},{40,32},{48,40},{56,48},{1,57}... | collective-permute-start | bytes 1474568 | tf_op jit(solution)/shard_map/ppermute | solution.py:35
  49.1 60.1 %all-to-all-start.1 = ((bf16[8,96,640]{2,1,0:T(8,128)(2,1)}), bf16[8,96,640]{2,1,0:T(8,128)(2,1)}, u32[]{:S(2)}, u32[]{:S(2)}) async-start(bf16[8,96,640]{2,1,0:T(8,128)(2,1)} %bitcast.93), calls=%async_computation.1 | async-start | bytes 1966080 | tf_op jit(solution)/shard_map/all_to_all | solution.py:27
  57.4 15.8 %collective-permute-start.2 = (bf16[8,80,384]{2,1,0:T(8,128)(2,1)}, bf16[8,80,384]{2,1,0:T(8,128)(2,1)S(1)}, u32[]{:S(2)}, u32[]{:S(2)}) collective-permute-start(bf16[8,80,384]{2,1,0:T(8,128)(2,1)} %collective-permute-done), channel_id=1, source_target_pairs={{0,8},{8,16},{16,24},{24,32},{32,40},{40,48},{48,56},{56,0},{1,9},... | collective-permute-start | bytes 1474568 | tf_op jit(solution)/shard_map/ppermute | solution.py:35
  59.3 16.6 %collective-permute-start.3 = (bf16[8,80,384]{2,1,0:T(8,128)(2,1)}, bf16[8,80,384]{2,1,0:T(8,128)(2,1)S(1)}, u32[]{:S(2)}, u32[]{:S(2)}) collective-permute-start(bf16[8,80,384]{2,1,0:T(8,128)(2,1)} %collective-permute-done.1), channel_id=1, source_target_pairs={{0,56},{8,0},{16,8},{24,16},{32,24},{40,32},{48,40},{56,48},{1,57}... | collective-permute-start | bytes 1474568 | tf_op jit(solution)/shard_map/ppermute | solution.py:35
  73.2 26.5 %collective-permute-start.4 = (bf16[8,80,384]{2,1,0:T(8,128)(2,1)S(1)}, bf16[8,80,384]{2,1,0:T(8,128)(2,1)S(1)}, u32[]{:S(2)}, u32[]{:S(2)}) collective-permute-start(bf16[8,80,384]{2,1,0:T(8,128)(2,1)S(1)} %collective-permute-done.2), channel_id=1, source_target_pairs={{0,8},{8,16},{16,24},{24,32},{32,40},{40,48},{48,56},{56,0},{1,9},... | collective-permute-start | bytes 1474568 | tf_op jit(solution)/shard_map/ppermute | solution.py:35
  75.9 25.8 %collective-permute-start.5 = (bf16[8,80,384]{2,1,0:T(8,128)(2,1)S(1)}, bf16[8,80,384]{2,1,0:T(8,128)(2,1)S(1)}, u32[]{:S(2)}, u32[]{:S(2)}) collective-permute-start(bf16[8,80,384]{2,1,0:T(8,128)(2,1)S(1)} %collective-permute-done.3), channel_id=1, source_target_pairs={{0,56},{8,0},{16,8},{24,16},{32,24},{40,32},{48,40},{56,48},{1,57}... | collective-permute-start | bytes 1474568 | tf_op jit(solution)/shard_map/ppermute | solution.py:35
  99.8 14.6 %collective-permute-start.6 = (bf16[4,80,384]{2,1,0:T(8,128)(2,1)S(1)}, bf16[4,80,384]{2,1,0:T(8,128)(2,1)S(1)}, u32[]{:S(2)}, u32[]{:S(2)}) collective-permute-start(bf16[4,80,384]{2,1,0:T(8,128)(2,1)S(1)} %slice.58), channel_id=1, source_target_pairs={{0,8},{8,16},{16,24},{24,32},{32,40},{40,48},{48,56},{56,0},{1,9},... | collective-permute-start | bytes 737288 | tf_op jit(solution)/shard_map/ppermute | solution.py:35
  102.4 12.7 %collective-permute-start.7 = (bf16[4,80,384]{2,1,0:T(8,128)(2,1)}, bf16[4,80,384]{2,1,0:T(8,128)(2,1)S(1)}, u32[]{:S(2)}, u32[]{:S(2)}) collective-permute-start(bf16[4,80,384]{2,1,0:T(8,128)(2,1)} %slice.59), channel_id=1, source_target_pairs={{0,56},{8,0},{16,8},{24,16},{32,24},{40,32},{48,40},{56,48},{1,57}... | collective-permute-start | bytes 737288 | tf_op jit(solution)/shard_map/ppermute | solution.py:35
  110.6 11.7 %all-to-all-start.2 = ((f32[8,8,128]{2,1,0:T(8,128)}), f32[8,8,128]{2,1,0:T(8,128)S(1)}, u32[]{:S(2)}, u32[]{:S(2)}) async-start(f32[8,8,128]{2,1,0:T(8,128)} %broadcast_in_dim_broadcast_in_dim_broadcast_in_dim.3), calls=%async_computation.2 | async-start | bytes 65536 | tf_op jit(solution)/shard_map/all_to_all | solution.py:27
  114.3 63.6 %all-gather.5.cloned.1.call-start = ((), (), s32[]{:S(2)}) async-start(), calls=%async_computation.7 | async-start | bytes 1327104 | tf_op jit(solution)/shard_map/all_gather | solution.py:112
  127.3 12.4 %copy-start.2 = (s32[256]{0:T(256)S(1)}, s32[256]{0:T(256)}, u32[]{:S(2)}) copy-start(s32[256]{0:T(256)} %param.9) | copy-start | bytes 3076
  127.3 12.4 %copy-start.3 = (f32[256]{0:T(256)S(1)}, f32[256]{0:T(256)}, u32[]{:S(2)}) copy-start(f32[256]{0:T(256)} %param.11) | copy-start | bytes 3076
  127.3 12.4 %copy-start.4 = (f32[256]{0:T(256)S(1)}, f32[256]{0:T(256)}, u32[]{:S(2)}) copy-start(f32[256]{0:T(256)} %param.10) | copy-start | bytes 3076
  141.4 3.6 %copy-start.1 = (bf16[96,768]{1,0:T(8,128)(2,1)S(1)}, bf16[96,768]{1,0:T(8,128)(2,1)}, u32[]{:S(2)}) copy-start(bf16[96,768]{1,0:T(8,128)(2,1)} %convolution_convert_fusion.1) | copy-start | bytes 442372
  149.4 32.1 %all-to-all-start.4 = ((bf16[8,96,640]{2,1,0:T(8,128)(2,1)}), bf16[8,96,640]{2,1,0:T(8,128)(2,1)}, u32[]{:S(2)}, u32[]{:S(2)}) async-start(bf16[8,96,640]{2,1,0:T(8,128)(2,1)} %bitcast.94), calls=%async_computation.4 | async-start | bytes 1966080 | tf_op jit(solution)/shard_map/all_to_all | solution.py:27
  181.5 31.4 %all-to-all-start.5 = ((bf16[8,80,768]{2,1,0:T(8,128)(2,1)}), bf16[8,80,768]{2,1,0:T(8,128)(2,1)}, u32[]{:S(2)}, u32[]{:S(2)}) async-start(bf16[8,80,768]{2,1,0:T(8,128)(2,1)} %bitcast.97), calls=%async_computation.5 | async-start | bytes 1966080 | tf_op jit(solution)/shard_map/all_to_all | solution.py:27
Sparse Core Ops, SparseCore 0:
  11.1 100.4 all-gather.2
  141.5 36.3 all-gather.4

commit v4 on v3

--- a/solution.py
+++ b/solution.py
@@ -6,6 +6,7 @@
 Y, Z, X, C = 8, 8, 4, 2
 V = X * C
 KEEP_MOST = 80
+SPARE = 8
 SLOTS = 96
 CLIP_EPS = 0.2
 LOSS_SCALE = 8192.0
@@ -60,20 +61,26 @@
     half = cols // 2
     offset = (lax.axis_index("x") * C + lax.axis_index("c")) * cols
 
-    head_a = lax.all_gather(head_weight[:, :half], ("y", "z"), axis=0, tiled=True)
+    keep_float = kept_mask.astype(jnp.float32)
+    count_rows = jnp.broadcast_to(jnp.sum(keep_float).astype(jnp.bfloat16), (SPARE, cols))
+    over_z = lax.all_gather(jnp.concatenate([head_weight, count_rows], axis=0), "z")
     small_b = to_all(head_weight[:, half:], "y", Y)
+    head_b = ring_over_z(small_b).reshape(width, half)
+    over_z, _ = lax.optimization_barrier((over_z, small_b))
+    small_a = over_z[:, :rows, :half].reshape(Z * rows, half)
+    head_a = lax.all_gather(small_a, "y", axis=0, tiled=True)
+    kept_z = jnp.sum(over_z[:, rows, :128].astype(jnp.float32), axis=0)[0]
 
-    keep_float = kept_mask.astype(jnp.float32)
     slot_index = jnp.cumsum(kept_mask) - 1
     ids = jnp.arange(SLOTS, dtype=jnp.int32)
     selector = ((slot_index[None, :] == ids[:, None]) & (kept_mask[None, :] == 1)).astype(jnp.bfloat16)
-    hidden_early, small_b = lax.optimization_barrier((hidden, small_b))
-    head_b = ring_over_z(small_b).reshape(width, half)
-    kept_hidden = jnp.dot(selector, hidden_early, preferred_element_type=jnp.float32)
-    kept_hidden = jnp.where(ids[:, None] < KEEP_MOST, kept_hidden, jnp.sum(keep_float)).astype(jnp.bfloat16)
+    kept_hidden = jnp.dot(selector, hidden, preferred_element_type=jnp.float32)
+    high = jnp.floor(kept_z / 64.0)
+    count_pair = jnp.where(ids == KEEP_MOST, high, kept_z - 64.0 * high)
+    kept_hidden = jnp.where(ids[:, None] < KEEP_MOST, kept_hidden, count_pair[:, None]).astype(jnp.bfloat16)
     kept_hidden = exchange(kept_hidden.reshape(SLOTS, Y, Z * rows).transpose(1, 0, 2), "y")
-    kept_y = jnp.sum(kept_hidden[:, KEEP_MOST, :128].astype(jnp.float32), axis=0)
-    kept_total = jnp.sum(to_all(jnp.broadcast_to(kept_y, (8, 128)), "z", Z), axis=0)[0, 0]
+    pairs = jnp.sum(kept_hidden[:, KEEP_MOST:KEEP_MOST + 2, 0].astype(jnp.float32), axis=0)
+    kept_total = 64.0 * pairs[0] + pairs[1]
     scale = -(LOSS_SCALE / kept_total)
     hidden, kept_hidden, scale = lax.optimization_barrier((hidden, kept_hidden, scale))
 

time: 223 us -> 233 us (1.045)
  blocking collectives: 7.95 us -> 31.7 us
  starting transfers between devices: 63.4 us -> 48.8 us
    all_gather x1 -> x2, waiting for transfers between devices: 0.02 us -> 24.4 us  [the longest x1 22.2 us: per_device(): lax.all_gather(jnp.concatenate([head_weight, count_rows], axis=0), 'z')]
    all_to_all x1 -> x2, blocking collectives: 7.95 us -> 31.7 us  [exchange(): return lax.all_to_all(parts, axes, split_axis=0, concat_axis=0)]
    ppermute x8, waiting for transfers between devices: 23.3 us -> 7.47 us  [shift(): return lax.ppermute(block, 'z', [(i, (i + step) % Z) for i in range(Z)])]
    all_to_all x5 -> x3, waiting for transfers between devices: 40.7 us -> 26.7 us  [exchange(): return lax.all_to_all(parts, axes, split_axis=0, concat_axis=0)]
    all_to_all x5 -> x3, starting transfers between devices: 28.7 us -> 20.8 us  [exchange(): return lax.all_to_all(parts, axes, split_axis=0, concat_axis=0)]
    ppermute x8, starting transfers between devices: 34.7 us -> 27.9 us  [shift(): return lax.ppermute(block, 'z', [(i, (i + step) % Z) for i in range(Z)])]
    all_gather x1, waiting for transfers between devices: 22.3 us -> 25.8 us  [per_device(): all_slots = lax.all_gather(compact, 'y', axis=0, tiled=True)]
  transfers between devices with their start and end apart: 15 -> 14, of which waited for: 8 -> 10; matrix products, arithmetic and copies ran while one was open for 18% -> 16% of each run, Pallas kernels for 0% -> 0%
where the time goes in v4:
time: 233 us; the launch traced here: 232 us
  waiting for transfers between devices  84.4 us (36%)
  starting transfers between devices  48.8 us (21%)
  blocking collectives  31.7 us (14%)
  matrix products  22.2 us (10%)
  local copies, waits for them, and re-layouts  20.8 us (9%)
  between operations  15.5 us (7%)
  other arithmetic  8.71 us (4%)
    all_to_all x2, blocking collectives, exchange(): return lax.all_to_all(parts, axes, split_axis=0, concat_axis=0)  31.7 us
    ppermute x8, starting transfers between devices, shift(): return lax.ppermute(block, 'z', [(i, (i + step) % Z) for i in range(Z)])  27.9 us
    all_to_all x3, waiting for transfers between devices, exchange(): return lax.all_to_all(parts, axes, split_axis=0, concat_axis=0)  26.7 us
    all_gather x1, waiting for transfers between devices, per_device(): all_slots = lax.all_gather(compact, 'y', axis=0, tiled=True)  25.8 us
    all_gather x1, waiting for transfers between devices, per_device(): lax.all_gather(jnp.concatenate([head_weight, count_rows], axis=0), 'z')  22.2 us
    all_to_all x3, starting transfers between devices, exchange(): return lax.all_to_all(parts, axes, split_axis=0, concat_axis=0)  20.8 us
    dynamic_update_slice x9, local copies, waits for them, and re-layouts, put(): return lax.dynamic_update_slice(whole, block[:, None], (first, at, 0, 0))  10.5 us
    ppermute x8, waiting for transfers between devices, shift(): return lax.ppermute(block, 'z', [(i, (i + step) % Z) for i in range(Z)])  7.47 us
  transfers between devices with their start and end apart: 14, of which 10 were waited for; matrix products, arithmetic and copies ran while one was open for 16% of the time, Pallas kernels for 0%

profile of v4, /device:TPU:6, one launch (start us, length us, event | category | flops | bytes accessed | tf_op | source)
XLA Modules:
  0.0 232.1 jit_solution(3651639845877411422)
XLA Ops:
  7.2 0.0 all-gather.9.cloned.1.call-start
  7.2 1.4 convert_reduce_fusion.3
  8.7 2.2 concatenate.6
  10.9 0.0 all-gather.5.cloned.1.call-start
  10.9 0.8 slice.54
  11.8 23.7 %all_to_all.25 = bf16[8,80,384]{2,1,0:T(8,128)(2,1)S(1)} all-to-all(bf16[8,80,384]{2,1,0:T(8,128)(2,1)S(1)} %broadcast_in_dim.80), channel_id=1, replica_groups=mesh['y'=8,'z'=8,'x'=4,'c'=2] {'y'}, dimensions={0} | all-to-all | bytes 983040 | tf_op jit(solution)/shard_map/all_to_all | solution.py:28
  35.5 22.2 %all-gather.9.cloned.1.call-done = bf16[704,768]{1,0:T(8,128)(2,1)} async-done(((bf16[88,768]{1,0:T(8,128)(2,1)}), bf16[704,768]{1,0:T(8,128)(2,1)}) %all-gather.9.cloned.1.call-update) | async-done | bytes 1081360 | tf_op jit(solution)/shard_map/all_gather | solution.py:66
  57.7 1.9 slice.60
  59.6 0.0 all-gather.5.cloned.1.call-update
  59.6 1.0 reduce-window.9
  60.6 0.1 slice.52
  60.7 0.1 slice_reduce_fusion.1
  60.8 0.7 broadcast_compare_fusion
  61.5 0.7 broadcast_subtract_fusion
  62.2 2.9 %collective-permute-start = (bf16[8,80,384]{2,1,0:T(8,128)(2,1)S(1)}, bf16[8,80,384]{2,1,0:T(8,128)(2,1)}, u32[]{:S(2)}, u32[]{:S(2)}) collective-permute-start(bf16[8,80,384]{2,1,0:T(8,128)(2,1)S(1)} %all_to_all.25), channel_id=1, source_target_pairs={{0,8},{8,16},{16,24},{24,32},{32,40},{40,48},{48,56},{56,0},{1,9},... | collective-permute-start | bytes 1474568 | tf_op jit(solution)/shard_map/ppermute | solution.py:36
  65.1 4.2 %collective-permute-start.1 = (bf16[8,80,384]{2,1,0:T(8,128)(2,1)S(1)}, bf16[8,80,384]{2,1,0:T(8,128)(2,1)}, u32[]{:S(2)}, u32[]{:S(2)}) collective-permute-start(bf16[8,80,384]{2,1,0:T(8,128)(2,1)S(1)} %all_to_all.25), channel_id=1, source_target_pairs={{0,56},{8,0},{16,8},{24,16},{32,24},{40,32},{48,40},{56,48},{1,57}... | collective-permute-start | bytes 1474568 | tf_op jit(solution)/shard_map/ppermute | solution.py:36
  69.3 0.1 add_bitcast_fusion
  69.4 2.3 broadcast_in_dim.84
  71.6 0.8 bitcast_dynamic-update-slice_fusion.6
  72.5 1.7 collective-permute-done
  74.2 2.0 collective-permute-start.2
  76.2 0.3 collective-permute-done.1
  76.5 4.8 %collective-permute-start.3 = (bf16[8,80,384]{2,1,0:T(8,128)(2,1)}, bf16[8,80,384]{2,1,0:T(8,128)(2,1)S(1)}, u32[]{:S(2)}, u32[]{:S(2)}) collective-permute-start(bf16[8,80,384]{2,1,0:T(8,128)(2,1)} %collective-permute-done.1), channel_id=1, source_target_pairs={{0,56},{8,0},{16,8},{24,16},{32,24},{40,32},{48,40},{56,48},{1,57}... | collective-permute-start | bytes 1474568 | tf_op jit(solution)/shard_map/ppermute | solution.py:36
  81.3 0.7 convert_reduce_fusion.2
  82.1 0.5 fusion.1
  82.7 1.1 copy.70
  83.8 7.2 %all-to-all-start.1 = ((bf16[8,96,640]{2,1,0:T(8,128)(2,1)}), bf16[8,96,640]{2,1,0:T(8,128)(2,1)}, u32[]{:S(2)}, u32[]{:S(2)}) async-start(bf16[8,96,640]{2,1,0:T(8,128)(2,1)} %bitcast.97), calls=%async_computation.1 | async-start | bytes 1966080 | tf_op jit(solution)/shard_map/all_to_all | solution.py:28
  91.0 0.0 all-gather.7.cloned.1.call-start
  91.1 1.9 bitcast_dynamic-update-slice_fusion.5
  92.9 1.9 bitcast_dynamic-update-slice_fusion.4
  94.8 1.9 collective-permute-start.4
  96.7 5.1 %collective-permute-start.5 = (bf16[8,80,384]{2,1,0:T(8,128)(2,1)S(1)}, bf16[8,80,384]{2,1,0:T(8,128)(2,1)S(1)}, u32[]{:S(2)}, u32[]{:S(2)}) collective-permute-start(bf16[8,80,384]{2,1,0:T(8,128)(2,1)S(1)} %collective-permute-done.3), channel_id=1, source_target_pairs={{0,56},{8,0},{16,8},{24,16},{32,24},{40,32},{48,40},{56,48},{1,57}... | collective-permute-start | bytes 1474568 | tf_op jit(solution)/shard_map/ppermute | solution.py:36
  101.8 1.9 bitcast_dynamic-update-slice_fusion.3
  103.7 0.9 bitcast_dynamic-update-slice_fusion.2
  104.6 4.2 %collective-permute-done.4 = bf16[8,80,384]{2,1,0:T(8,128)(2,1)S(1)} collective-permute-done((bf16[8,80,384]{2,1,0:T(8,128)(2,1)}, bf16[8,80,384]{2,1,0:T(8,128)(2,1)S(1)}, u32[]{:S(2)}, u32[]{:S(2)}) %collective-permute-start.4) | collective-permute-done | bytes 491552 | tf_op jit(solution)/shard_map/ppermute | solution.py:36
  108.9 1.9 collective-permute-start.6
  110.8 5.1 %collective-permute-start.7 = (bf16[4,80,384]{2,1,0:T(8,128)(2,1)S(1)}, bf16[4,80,384]{2,1,0:T(8,128)(2,1)S(1)}, u32[]{:S(2)}, u32[]{:S(2)}) collective-permute-start(bf16[4,80,384]{2,1,0:T(8,128)(2,1)S(1)} %slice.71), channel_id=1, source_target_pairs={{0,56},{8,0},{16,8},{24,16},{32,24},{40,32},{48,40},{56,48},{1,57}... | collective-permute-start | bytes 737288 | tf_op jit(solution)/shard_map/ppermute | solution.py:36
  116.0 0.9 bitcast_dynamic-update-slice_fusion.1
  116.8 0.8 bitcast_dynamic-update-slice_fusion
  117.7 0.5 collective-permute-done.6
  118.2 0.8 bitcast_dynamic-update-slice_fusion.7
  118.9 0.8 collective-permute-done.7
  119.7 0.7 bitcast_dynamic-update-slice_fusion.8
  120.4 5.3 %all-to-all-done.1 = bf16[8,96,640]{2,1,0:T(8,128)(2,1)} async-done(((bf16[8,96,640]{2,1,0:T(8,128)(2,1)}), bf16[8,96,640]{2,1,0:T(8,128)(2,1)}, u32[]{:S(2)}, u32[]{:S(2)}) %all-to-all-start.1) | async-done | bytes 983072 | tf_op jit(solution)/shard_map/all_to_all | solution.py:28
  125.7 0.8 convert_reduce_fusion.1
  126.6 0.6 fusion.23
  128.5 3.8 %fusion.25 = (f32[256]{0:T(256)S(1)}, f32[256,384]{1,0:T(8,128)S(1)}) fusion(bf16[256,5120]{1,0:T(8,128)(2,1)S(1)} %copy-done, bf16[5120,384]{1,0:T(8,128)(2,1)} %bitcast.24), kind=kOutput, calls=%fused_computation.66 | convolution fusion | flops 1006731008 | bytes 6947840 | tf_op jit(solution)/shard_map/dot_general | solution.py:90
  132.3 2.2 all-gather.5.cloned.1.call-done
  134.5 3.8 %fusion.24 = (f32[256]{0:T(256)S(1)}, f32[256,384]{1,0:T(8,128)S(1)}) fusion(bf16[256,5120]{1,0:T(8,128)(2,1)S(1)} %copy-done, bf16[5120,384]{1,0:T(8,128)(2,1)} %all-gather.5.cloned.1.call-done), kind=kOutput, calls=%fused_computation.65 | convolution fusion | flops 1006731008 | bytes 6947840 | tf_op jit(solution)/shard_map/dot_general | solution.py:89
  138.3 0.5 exponential_reduce_fusion
  138.8 8.0 %all_to_all.26 = f32[8,4,256]{2,1,0:T(4,128)S(1)} all-to-all(f32[8,4,256]{2,1,0:T(4,128)S(1)} %broadcast_in_dim.94), channel_id=1, replica_groups=mesh['y'=8,'z'=8,'x'=4,'c'=2] {'x','c'}, dimensions={0} | all-to-all | bytes 65536 | tf_op jit(solution)/shard_map/all_to_all | solution.py:28
  146.9 0.6 fusion.20
  147.4 1.1 convolution_convert_fusion.1
  148.6 3.5 %fusion.10 = f32[96,5120]{1,0:T(8,128)S(1)} fusion(bf16[5120,384]{1,0:T(8,128)(2,1)} %all-gather.5.cloned.1.call-done, bf16[96,768]{1,0:T(8,128)(2,1)} %convolution_convert_fusion.1), kind=kOutput, calls=%fused_computation.33 | convolution fusion | flops 377487360 | bytes 5971968 | tf_op jit(solution)/shard_map/dot_general | solution.py:129
  152.1 3.4 %fusion = bf16[96,5120]{1,0:T(8,128)(2,1)S(1)} fusion(f32[96,5120]{1,0:T(8,128)S(1)} %fusion.10, bf16[5120,384]{1,0:T(8,128)(2,1)} %bitcast.24, bf16[96,768]{1,0:T(8,128)(2,1)S(1)} %copy-done.1), kind=kOutput, calls=%fused_computation.2 | convolution fusion | flops 378470400 | bytes 6955008 | tf_op jit(solution)/shard_map/dot_general | solution.py:130
  155.6 1.1 copy.69
  156.6 6.2 %all-to-all-start.3 = ((bf16[8,96,640]{2,1,0:T(8,128)(2,1)}), bf16[8,96,640]{2,1,0:T(8,128)(2,1)}, u32[]{:S(2)}, u32[]{:S(2)}) async-start(bf16[8,96,640]{2,1,0:T(8,128)(2,1)} %bitcast.98), calls=%async_computation.3 | async-start | bytes 1966080 | tf_op jit(solution)/shard_map/all_to_all | solution.py:28
  162.8 25.8 %all-gather.7.cloned.1.call-done = bf16[768,768]{1,0:T(8,128)(2,1)} async-done(((bf16[96,768]{1,0:T(8,128)(2,1)}), bf16[768,768]{1,0:T(8,128)(2,1)}) %all-gather.7.cloned.1.call-update) | async-done | bytes 1179664 | tf_op jit(solution)/shard_map/all_gather | solution.py:119
  188.7 3.5 %convolution_convert_fusion = bf16[640,768]{1,0:T(8,128)(2,1)} fusion(bf16[768,640]{1,0:T(8,128)(2,1)} %bitcast.33, bf16[768,768]{1,0:T(8,128)(2,1)} %all-gather.7.cloned.1.call-done), kind=kOutput, calls=%fused_computation.5 | convolution fusion | flops 755466240 | bytes 3145728 | tf_op jit(solution)/shard_map/dot_general | solution.py:120
  192.2 7.4 %all-to-all-start.4 = ((bf16[8,80,768]{2,1,0:T(8,128)(2,1)}), bf16[8,80,768]{2,1,0:T(8,128)(2,1)}, u32[]{:S(2)}, u32[]{:S(2)}) async-start(bf16[8,80,768]{2,1,0:T(8,128)(2,1)} %bitcast.102), calls=%async_computation.4 | async-start | bytes 1966080 | tf_op jit(solution)/shard_map/all_to_all | solution.py:28
  199.6 2.6 %fusion.2 = f32[256,640]{1,0:T(8,128)} fusion(bf16[8,96,640]{2,1,0:T(8,128)(2,1)} %all-to-all-done.3, f32[]{:T(128)} %bitcast.5, bf16[96,256]{1,0:T(8,128)(2,1)S(1)} %fusion.7), kind=kOutput, calls=%fused_computation.7 | convolution fusion | flops 251822080 | bytes 1687556 | tf_op jit(solution)/shard_map/dot_general | solution.py:135
  202.1 21.4 %all-to-all-done.4 = bf16[8,80,768]{2,1,0:T(8,128)(2,1)} async-done(((bf16[8,80,768]{2,1,0:T(8,128)(2,1)}), bf16[8,80,768]{2,1,0:T(8,128)(2,1)}, u32[]{:S(2)}, u32[]{:S(2)}) %all-to-all-start.4) | async-done | bytes 983072 | tf_op jit(solution)/shard_map/all_to_all | solution.py:28
  223.5 1.4 convert_reduce_fusion
  224.9 0.7 broadcast_multiply_fusion
  (28 shorter events, 0.3 us)
Async XLA Ops:
  7.2 75.0 %copy-start = (bf16[256,5120]{1,0:T(8,128)(2,1)S(1)}, bf16[256,5120]{1,0:T(8,128)(2,1)}, u32[]{:S(2)}) copy-start(bf16[256,5120]{1,0:T(8,128)(2,1)} %param.6) | copy-start | bytes 7864324
  7.2 50.5 %all-gather.9.cloned.1.call-start = ((), (), s32[]{:S(2)}) async-start(), calls=%async_computation.7 | async-start | bytes 1216512 | tf_op jit(solution)/shard_map/all_gather | solution.py:66
  10.9 123.6 %all-gather.5.cloned.1.call-start = ((), (), s32[]{:S(2)}) async-start(), calls=%async_computation.5 | async-start | bytes 4423680 | tf_op jit(solution)/shard_map/all_gather | solution.py:71
  62.2 12.0 %collective-permute-start = (bf16[8,80,384]{2,1,0:T(8,128)(2,1)S(1)}, bf16[8,80,384]{2,1,0:T(8,128)(2,1)}, u32[]{:S(2)}, u32[]{:S(2)}) collective-permute-start(bf16[8,80,384]{2,1,0:T(8,128)(2,1)S(1)} %all_to_all.25), channel_id=1, source_target_pairs={{0,8},{8,16},{16,24},{24,32},{32,40},{40,48},{48,56},{56,0},{1,9},... | collective-permute-start | bytes 1474568 | tf_op jit(solution)/shard_map/ppermute | solution.py:36
  65.1 11.4 %collective-permute-start.1 = (bf16[8,80,384]{2,1,0:T(8,128)(2,1)S(1)}, bf16[8,80,384]{2,1,0:T(8,128)(2,1)}, u32[]{:S(2)}, u32[]{:S(2)}) collective-permute-start(bf16[8,80,384]{2,1,0:T(8,128)(2,1)S(1)} %all_to_all.25), channel_id=1, source_target_pairs={{0,56},{8,0},{16,8},{24,16},{32,24},{40,32},{48,40},{56,48},{1,57}... | collective-permute-start | bytes 1474568 | tf_op jit(solution)/shard_map/ppermute | solution.py:36
  74.2 20.6 %collective-permute-start.2 = (bf16[8,80,384]{2,1,0:T(8,128)(2,1)}, bf16[8,80,384]{2,1,0:T(8,128)(2,1)}, u32[]{:S(2)}, u32[]{:S(2)}) collective-permute-start(bf16[8,80,384]{2,1,0:T(8,128)(2,1)} %collective-permute-done), channel_id=1, source_target_pairs={{0,8},{8,16},{16,24},{24,32},{32,40},{40,48},{48,56},{56,0},{1,9},... | collective-permute-start | bytes 1474568 | tf_op jit(solution)/shard_map/ppermute | solution.py:36
  76.5 20.2 %collective-permute-start.3 = (bf16[8,80,384]{2,1,0:T(8,128)(2,1)}, bf16[8,80,384]{2,1,0:T(8,128)(2,1)S(1)}, u32[]{:S(2)}, u32[]{:S(2)}) collective-permute-start(bf16[8,80,384]{2,1,0:T(8,128)(2,1)} %collective-permute-done.1), channel_id=1, source_target_pairs={{0,56},{8,0},{16,8},{24,16},{32,24},{40,32},{48,40},{56,48},{1,57}... | collective-permute-start | bytes 1474568 | tf_op jit(solution)/shard_map/ppermute | solution.py:36
  83.8 41.9 %all-to-all-start.1 = ((bf16[8,96,640]{2,1,0:T(8,128)(2,1)}), bf16[8,96,640]{2,1,0:T(8,128)(2,1)}, u32[]{:S(2)}, u32[]{:S(2)}) async-start(bf16[8,96,640]{2,1,0:T(8,128)(2,1)} %bitcast.97), calls=%async_computation.1 | async-start | bytes 1966080 | tf_op jit(solution)/shard_map/all_to_all | solution.py:28
  91.0 97.7 %all-gather.7.cloned.1.call-start = ((), (), s32[]{:S(2)}) async-start(), calls=%async_computation.6 | async-start | bytes 1327104 | tf_op jit(solution)/shard_map/all_gather | solution.py:119
  94.8 14.1 %collective-permute-start.4 = (bf16[8,80,384]{2,1,0:T(8,128)(2,1)}, bf16[8,80,384]{2,1,0:T(8,128)(2,1)S(1)}, u32[]{:S(2)}, u32[]{:S(2)}) collective-permute-start(bf16[8,80,384]{2,1,0:T(8,128)(2,1)} %collective-permute-done.2), channel_id=1, source_target_pairs={{0,8},{8,16},{16,24},{24,32},{32,40},{40,48},{48,56},{56,0},{1,9},... | collective-permute-start | bytes 1474568 | tf_op jit(solution)/shard_map/ppermute | solution.py:36
  96.7 14.1 %collective-permute-start.5 = (bf16[8,80,384]{2,1,0:T(8,128)(2,1)S(1)}, bf16[8,80,384]{2,1,0:T(8,128)(2,1)S(1)}, u32[]{:S(2)}, u32[]{:S(2)}) collective-permute-start(bf16[8,80,384]{2,1,0:T(8,128)(2,1)S(1)} %collective-permute-done.3), channel_id=1, source_target_pairs={{0,56},{8,0},{16,8},{24,16},{32,24},{40,32},{48,40},{56,48},{1,57}... | collective-permute-start | bytes 1474568 | tf_op jit(solution)/shard_map/ppermute | solution.py:36
  108.9 9.3 %collective-permute-start.6 = (bf16[4,80,384]{2,1,0:T(8,128)(2,1)S(1)}, bf16[4,80,384]{2,1,0:T(8,128)(2,1)S(1)}, u32[]{:S(2)}, u32[]{:S(2)}) collective-permute-start(bf16[4,80,384]{2,1,0:T(8,128)(2,1)S(1)} %slice.70), channel_id=1, source_target_pairs={{0,8},{8,16},{16,24},{24,32},{32,40},{40,48},{48,56},{56,0},{1,9},... | collective-permute-start | bytes 737288 | tf_op jit(solution)/shard_map/ppermute | solution.py:36
  110.8 8.8 %collective-permute-start.7 = (bf16[4,80,384]{2,1,0:T(8,128)(2,1)S(1)}, bf16[4,80,384]{2,1,0:T(8,128)(2,1)S(1)}, u32[]{:S(2)}, u32[]{:S(2)}) collective-permute-start(bf16[4,80,384]{2,1,0:T(8,128)(2,1)S(1)} %slice.71), channel_id=1, source_target_pairs={{0,56},{8,0},{16,8},{24,16},{32,24},{40,32},{48,40},{56,48},{1,57}... | collective-permute-start | bytes 737288 | tf_op jit(solution)/shard_map/ppermute | solution.py:36
  132.2 14.6 %copy-start.2 = (s32[256]{0:T(256)S(1)}, s32[256]{0:T(256)}, u32[]{:S(2)}) copy-start(s32[256]{0:T(256)} %param.9) | copy-start | bytes 3076
  132.3 14.6 %copy-start.3 = (f32[256]{0:T(256)S(1)}, f32[256]{0:T(256)}, u32[]{:S(2)}) copy-start(f32[256]{0:T(256)} %param.11) | copy-start | bytes 3076
  132.3 14.6 %copy-start.4 = (f32[256]{0:T(256)S(1)}, f32[256]{0:T(256)}, u32[]{:S(2)}) copy-start(f32[256]{0:T(256)} %param.10) | copy-start | bytes 3076
  148.6 3.6 %copy-start.1 = (bf16[96,768]{1,0:T(8,128)(2,1)S(1)}, bf16[96,768]{1,0:T(8,128)(2,1)}, u32[]{:S(2)}) copy-start(bf16[96,768]{1,0:T(8,128)(2,1)} %convolution_convert_fusion.1) | copy-start | bytes 442372
  156.6 35.6 %all-to-all-start.3 = ((bf16[8,96,640]{2,1,0:T(8,128)(2,1)}), bf16[8,96,640]{2,1,0:T(8,128)(2,1)}, u32[]{:S(2)}, u32[]{:S(2)}) async-start(bf16[8,96,640]{2,1,0:T(8,128)(2,1)} %bitcast.98), calls=%async_computation.3 | async-start | bytes 1966080 | tf_op jit(solution)/shard_map/all_to_all | solution.py:28
  192.2 31.3 %all-to-all-start.4 = ((bf16[8,80,768]{2,1,0:T(8,128)(2,1)}), bf16[8,80,768]{2,1,0:T(8,128)(2,1)}, u32[]{:S(2)}, u32[]{:S(2)}) async-start(bf16[8,80,768]{2,1,0:T(8,128)(2,1)} %bitcast.102), calls=%async_computation.4 | async-start | bytes 1966080 | tf_op jit(solution)/shard_map/all_to_all | solution.py:28
Sparse Core Ops, SparseCore 0:
  11.0 46.6 all-gather.8
  60.4 74.0 all-gather.4
  148.7 39.9 all-gather.6

commit v5 on v2

v5 whole, which is shorter than its diff:
```python
import jax
import jax.numpy as jnp
from jax import lax
from jax.sharding import Mesh, PartitionSpec as P

Y, Z, X, C = 8, 8, 4, 2
V = X * C
KEEP_MOST = 80
SLOTS = 96
CLIP_EPS = 0.2
LOSS_SCALE = 8192.0


def surrogate_slope(logprob, old_logprob, advantage, keep_float):
    importance = jnp.exp(logprob - old_logprob)
    bent_term = jnp.tanh((importance - 1.0) / CLIP_EPS)
    clipped = 1.0 + CLIP_EPS * bent_term
    choose_grad = jnp.where(
        importance * advantage <= clipped * advantage,
        advantage,
        advantage * (1.0 - bent_term * bent_term),
    )
    return keep_float * choose_grad * importance


def exchange(parts, axes):
    return lax.all_to_all(parts, axes, split_axis=0, concat_axis=0)


def to_all(values, axes, n):
    return exchange(jnp.broadcast_to(values[None], (n,) + values.shape), axes)


def rows_of(weights, factors):
    positions = lax.broadcasted_iota(jnp.int32, weights.shape, weights.ndim - 1).astype(jnp.float32)
    scale, entry, target = (factors[..., i, :, None] for i in range(3))
    return jnp.where(positions == target, entry, -scale * weights.astype(jnp.float32)).astype(jnp.bfloat16)


def per_device(hidden, head_weight, targets, kept_mask, old_logprob, advantage):
    tokens, width = hidden.shape
    rows, cols = head_weight.shape
    offset = (lax.axis_index("x") * C + lax.axis_index("c")) * cols
    head = lax.all_gather(head_weight, ("y", "z"), axis=0, tiled=True)

    keep_float = kept_mask.astype(jnp.float32)
    slot_index = jnp.cumsum(kept_mask) - 1
    ids = jnp.arange(SLOTS, dtype=jnp.int32)
    chosen = (slot_index[None, :] == ids[:, None]) & (kept_mask[None, :] == 1)
    selector = chosen.astype(jnp.bfloat16)
    kept_hidden = jnp.dot(selector, hidden, preferred_element_type=jnp.float32)
    kept_hidden = jnp.where(ids[:, None] < KEEP_MOST, kept_hidden, jnp.sum(keep_float)).astype(jnp.bfloat16)
    kept_hidden = exchange(kept_hidden.reshape(SLOTS, Y, Z * rows).transpose(1, 0, 2), "y")
    kept_y = jnp.sum(kept_hidden[:, KEEP_MOST, :128].astype(jnp.float32), axis=0)
    kept_total = jnp.sum(to_all(jnp.broadcast_to(kept_y, (8, 128)), "z", Z), axis=0)[0, 0]
    scale = -(LOSS_SCALE / kept_total)
    hidden, kept_hidden, scale = lax.optimization_barrier((hidden, kept_hidden, scale))

    logits = jnp.dot(hidden, head, preferred_element_type=jnp.float32)
    local_target = targets - offset
    positions = jnp.arange(cols, dtype=jnp.int32)
    hit = positions[None, :] == local_target[:, None]
    local_top = jnp.max(logits, axis=1)
    shifted = logits - local_top[:, None]
    weights = jnp.exp(shifted)

    compact = jnp.dot(
        selector, jnp.where(hit, 0.0, weights).astype(jnp.bfloat16), preferred_element_type=jnp.float32
    ).astype(jnp.bfloat16)
    all_slots = lax.all_gather(compact, "y")

    stats = jnp.stack(
        [
            local_top,
            jnp.sum(weights, axis=1),
            jnp.sum(weights * shifted, axis=1),
            jnp.sum(jnp.where(hit, logits, 0.0), axis=1),
        ]
    )
    stats = to_all(stats, ("x", "c"), V)
    tops, totals, moments, picks = (stats[:, i] for i in range(4))
    row_top = jnp.max(tops, axis=0)
    lower = tops - row_top[None]
    factor = jnp.exp(lower)
    row_total = jnp.sum(totals * factor, axis=0)
    row_moment = jnp.sum((moments + lower * totals) * factor, axis=0)
    picked = jnp.sum(picks, axis=0)
    entropy = jnp.log(row_total) - row_moment / row_total
    logprob = picked - row_top - jnp.log(row_total)
    slope = surrogate_slope(logprob, old_logprob, advantage, keep_float)
    row_scale = slope * (jnp.exp(local_top - row_top) / row_total)
    row_entry = slope * (1.0 - jnp.exp(picked - row_top) / row_total)
    of_slots = jnp.stack([row_scale, row_entry, local_target.astype(jnp.float32)])
    of_slots = jnp.sum(jnp.where(chosen[None], of_slots[:, None, :], 0.0), axis=2)

    own_rows = rows_of(compact, of_slots)
    hidden_part = lax.dot_general(
        own_rows, head, (((1,), (1,)), ((), ())), preferred_element_type=jnp.float32
    ).astype(jnp.bfloat16)
    mine = width // V
    hidden_part = hidden_part.reshape(SLOTS, V, mine).transpose(1, 0, 2)
    hidden_part, of_slots = lax.optimization_barrier((hidden_part, of_slots))
    hidden_part = exchange(hidden_part, ("x", "c"))

    all_factors = lax.all_gather(jnp.pad(of_slots, ((0, 5), (0, 128 - SLOTS))), "y")
    all_rows = rows_of(all_slots, all_factors[:, :3, :SLOTS])
    part_head = lax.dot_general(
        kept_hidden.reshape(Y * SLOTS, Z * rows), all_rows.reshape(Y * SLOTS, cols), (((0,), (0,)), ((), ())),
        preferred_element_type=jnp.float32,
    ).astype(jnp.bfloat16)
    sums = exchange(part_head.reshape(Z, rows, cols), "z")
    grad_head = scale * jnp.sum(sums.astype(jnp.float32), axis=0)

    spread = jnp.tile(selector, (V, 1))
    grad_hidden = scale * lax.dot_general(
        spread, hidden_part.reshape(V * SLOTS, mine), (((0,), (0,)), ((), ())),
        preferred_element_type=jnp.float32,
    )
    return (entropy, grad_hidden, grad_head)


def solution(mesh):
    grid = Mesh(mesh.devices.reshape(Y, Z, X, C), ("y", "z", "x", "c"))
    dp, vocab = ("y", "z"), ("x", "c")
    placed = (P(dp, None), P(dp, vocab), P(dp), P(dp), P(dp), P(dp))
    return jax.shard_map(
        per_device,
        mesh=grid,
        in_specs=placed,
        out_specs=(P(dp), P(dp, vocab), P(dp, vocab)),
        check_vma=False,
    )
```

time: 215 us -> 215 us (level)
  blocking collectives: 7.98 us -> 25.2 us
  waiting for transfers between devices: 117 us -> 106 us
  local copies, waits for them, and re-layouts: 11 us -> 4.19 us
    all_gather x0 -> x1, blocking collectives: none -> 25.2 us  [per_device(): lax.all_gather(jnp.pad(of_slots, ((0, 5), (0, 128 - SLOTS))), 'y')]
    all_gather x2, waiting for transfers between devices: 65.2 us -> 44.7 us  [the longest x1 44.6 us: per_device(): head = lax.all_gather(head_weight, ('y', 'z'), axis=0, tiled=True)]
    all_to_all x5, waiting for transfers between devices: 50.8 us -> 61 us  [exchange(): return lax.all_to_all(parts, axes, split_axis=0, concat_axis=0)]
    all_to_all x1 -> x0, blocking collectives: 7.98 us -> none  [to_all(): lax.all_to_all(jnp.broadcast_to(values[None], (n,) + values.shape), axes,...]
    transpose x1 -> x0, local copies, waits for them, and re-layouts: 2.47 us -> none  [per_device(): kept_hidden.reshape(SLOTS, Y, Z, rows).transpose(2, 0, 1, 3)]
    convert_element_type x1 -> x0, local copies, waits for them, and re-layouts: 2.44 us -> none  [per_device(): jnp.dot(selector, hidden, preferred_element_type=jnp.float32)]
  transfers between devices with their start and end apart: 7 -> 7, of which waited for: 5 -> 5; matrix products, arithmetic and copies ran while one was open for 13% -> 11% of each run, Pallas kernels for 0% -> 0%
where the time goes in v5:
time: 215 us
  waiting for transfers between devices  106 us (49%)
  starting transfers between devices  36.9 us (17%)
  blocking collectives  25.2 us (12%)
  matrix products  19.9 us (9%)
  between operations  14.9 us (7%)
  other arithmetic  7.27 us (3%)
  local copies, waits for them, and re-layouts  4.19 us (2%)
    all_to_all x5, waiting for transfers between devices, exchange(): return lax.all_to_all(parts, axes, split_axis=0, concat_axis=0)  61 us
    all_gather x1, waiting for transfers between devices, per_device(): head = lax.all_gather(head_weight, ('y', 'z'), axis=0, tiled=True)  44.6 us
    all_to_all x5, starting transfers between devices, exchange(): return lax.all_to_all(parts, axes, split_axis=0, concat_axis=0)  36.9 us
    all_gather x1, blocking collectives, per_device(): lax.all_gather(jnp.pad(of_slots, ((0, 5), (0, 128 - SLOTS))), 'y')  25.2 us
    dot_general x1, matrix products, per_device(): lax.dot_general(own_rows, head, (((1,), (1,)), ((), ())), preferred_eleme...  5.82 us
    dot_general x1, matrix products, per_device(): logits = jnp.dot(hidden, head, preferred_element_type=jnp.float32)  5.5 us
  transfers between devices with their start and end apart: 7, of which 5 were waited for; matrix products, arithmetic and copies ran while one was open for 11% of the time, Pallas kernels for 0%

profile of v5, /device:TPU:6, one launch (start us, length us, event | category | flops | bytes accessed | tf_op | source)
XLA Modules:
  0.0 214.7 jit_solution(1374303564925415536)
XLA Ops:
  7.2 0.0 copy-start
  7.2 0.0 all-gather.5.cloned.1.call-start
  7.2 0.7 all-gather.5.cloned.1.call-update
  7.9 1.0 reduce-window.9
  8.9 0.1 slice.47
  9.1 1.3 convert_reduce_fusion.1
  10.3 0.1 slice_reduce_fusion.1
  10.5 0.7 broadcast_compare_fusion
  11.1 0.1 add_bitcast_fusion
  11.2 0.0 copy-done
  11.2 1.2 fusion
  12.4 0.0 copy-start.2
  12.4 1.1 copy.47
  13.6 7.1 %all-to-all-start = ((bf16[8,96,640]{2,1,0:T(8,128)(2,1)}), bf16[8,96,640]{2,1,0:T(8,128)(2,1)}, u32[]{:S(2)}, u32[]{:S(2)}) async-start(bf16[8,96,640]{2,1,0:T(8,128)(2,1)} %bitcast.70), calls=%async_computation | async-start | bytes 1966080 | tf_op jit(solution)/shard_map/all_to_all | solution.py:27
  20.7 0.0 copy-done.2
  20.7 29.3 %all-to-all-done = bf16[8,96,640]{2,1,0:T(8,128)(2,1)} async-done(((bf16[8,96,640]{2,1,0:T(8,128)(2,1)}), bf16[8,96,640]{2,1,0:T(8,128)(2,1)}, u32[]{:S(2)}, u32[]{:S(2)}) %all-to-all-start) | async-done | bytes 983072 | tf_op jit(solution)/shard_map/all_to_all | solution.py:27
  50.0 0.7 fusion.24
  50.8 0.6 broadcast_in_dim_broadcast_in_dim_broadcast_in_dim.3
  51.4 11.5 %all-to-all-start.1 = ((f32[8,8,128]{2,1,0:T(8,128)}), f32[8,8,128]{2,1,0:T(8,128)S(1)}, u32[]{:S(2)}, u32[]{:S(2)}) async-start(f32[8,8,128]{2,1,0:T(8,128)} %broadcast_in_dim_broadcast_in_dim_broadcast_in_dim.3), calls=%async_computation.1 | async-start | bytes 65536 | tf_op jit(solution)/shard_map/all_to_all | solution.py:27
  62.9 8.0 %all-to-all-done.1 = f32[8,8,128]{2,1,0:T(8,128)S(1)} async-done(((f32[8,8,128]{2,1,0:T(8,128)}), f32[8,8,128]{2,1,0:T(8,128)S(1)}, u32[]{:S(2)}, u32[]{:S(2)}) %all-to-all-start.1) | async-done | bytes 32800 | tf_op jit(solution)/shard_map/all_to_all | solution.py:27
  70.9 0.5 slice.50
  72.1 0.0 copy-start.1
  72.1 0.0 copy-start.3
  72.1 0.0 copy-start.4
  72.2 44.6 %all-gather.5.cloned.1.call-done = bf16[5120,768]{1,0:T(8,128)(2,1)} async-done(((bf16[80,768]{1,0:T(8,128)(2,1)}), bf16[5120,768]{1,0:T(8,128)(2,1)}) %all-gather.5.cloned.1.call-update) | async-done | bytes 7864336 | tf_op jit(solution)/shard_map/all_gather | solution.py:44
  116.8 5.5 %fusion.35 = (f32[256]{0:T(256)S(1)}, f32[256,768]{1,0:T(8,128)S(1)}) fusion(bf16[256,5120]{1,0:T(8,128)(2,1)S(1)} %copy-done, bf16[5120,768]{1,0:T(8,128)(2,1)} %all-gather.5.cloned.1.call-done), kind=kOutput, calls=%fused_computation.73 | convolution fusion | flops 2013462272 | bytes 11273216 | tf_op jit(solution)/shard_map/dot_general | solution.py:59
  122.3 0.5 exponential_reduce_fusion
  122.8 0.6 broadcast_in_dim.77
  123.4 4.8 %all-to-all-start.2 = ((f32[8,4,256]{2,1,0:T(4,128)}), f32[8,4,256]{2,1,0:T(4,128)S(1)}, u32[]{:S(2)}, u32[]{:S(2)}) async-start(f32[8,4,256]{2,1,0:T(4,128)} %broadcast_in_dim.77), calls=%async_computation.2 | async-start | bytes 65536 | tf_op jit(solution)/shard_map/all_to_all | solution.py:27
  128.2 0.0 all-gather.7.cloned.1.call-start
  128.2 1.0 convolution_convert_fusion.1
  129.2 0.0 all-gather.7.cloned.1.call-update
  129.2 2.3 %all-to-all-done.2 = f32[8,4,256]{2,1,0:T(4,128)S(1)} async-done(((f32[8,4,256]{2,1,0:T(4,128)}), f32[8,4,256]{2,1,0:T(4,128)S(1)}, u32[]{:S(2)}, u32[]{:S(2)}) %all-to-all-start.2) | async-done | bytes 32800 | tf_op jit(solution)/shard_map/all_to_all | solution.py:27
  131.6 0.0 copy-done.1
  131.6 0.0 copy-done.3
  131.7 0.0 copy-done.4
  131.7 0.6 subtract_multiply_fusion
  132.3 0.1 select_reduce_fusion.1
  132.5 5.8 %convolution_convert_fusion = bf16[96,5120]{1,0:T(8,128)(2,1)S(1)} fusion(bf16[5120,768]{1,0:T(8,128)(2,1)} %all-gather.5.cloned.1.call-done, bf16[96,768]{1,0:T(8,128)(2,1)} %convolution_convert_fusion.1, f32[96]{0:T(128)S(1)} %get-tuple-element.33, bf16[96]{0:T(256)(128)(2,1)S(1)} %slice_bitcast_fusion, f32[768]{0:T(1024)S(1)} %iota_convert_fusion, ...), kind=kOutput, calls=%fused_computation.1 | convolution fusion | flops 755761152 | bytes 8998848 | tf_op jit(solution)/shard_map/dot_general | solution.py:97
  138.3 1.1 copy.46
  139.3 6.2 %all-to-all-start.3 = ((bf16[8,96,640]{2,1,0:T(8,128)(2,1)}), bf16[8,96,640]{2,1,0:T(8,128)(2,1)}, u32[]{:S(2)}, u32[]{:S(2)}) async-start(bf16[8,96,640]{2,1,0:T(8,128)(2,1)} %bitcast.71), calls=%async_computation.3 | async-start | bytes 1966080 | tf_op jit(solution)/shard_map/all_to_all | solution.py:27
  145.5 25.2 %all-gather = f32[64,128]{1,0:T(8,128)S(1)} all-gather(f32[8,128]{1,0:T(8,128)S(1)} %pad.4), channel_id=2, replica_groups=mesh['y'=8,'z'=8,'x'=4,'c'=2] {'y'}, dimensions={0}, use_global_device_ids=true | all-gather | bytes 36864 | tf_op jit(solution)/shard_map/all_gather | solution.py:105
  170.7 0.0 all-gather.7.cloned.1.call-done
  170.8 3.8 %bitcast_convert_fusion = bf16[640,768]{1,0:T(8,128)(2,1)} fusion(bf16[8,96,640]{2,1,0:T(8,128)(2,1)} %all-to-all-done, bf16[8,96,768]{2,1,0:T(8,128)(2,1)} %bitcast.87, f32[8,96]{1,0:T(8,128)S(1)} %bitcast.85, f32[8,96]{1,0:T(8,128)S(1)} %bitcast.86, f32[8,96]{1,0:T(8,128)S(1)} %bitcast.84, f32[768]{0:T(1024)S(1)} %iota_convert_fusion), kind=kOutput, calls=%fused_computation.6 | convolution fusion | flops 757825536 | bytes 3158016 | tf_op jit(solution)/shard_map/dot_general | solution.py:107
  174.5 0.0 all-to-all-done.3
  174.5 7.3 %all-to-all-start.4 = ((bf16[8,80,768]{2,1,0:T(8,128)(2,1)}), bf16[8,80,768]{2,1,0:T(8,128)(2,1)}, u32[]{:S(2)}, u32[]{:S(2)}) async-start(bf16[8,80,768]{2,1,0:T(8,128)(2,1)} %bitcast.74), calls=%async_computation.4 | async-start | bytes 1966080 | tf_op jit(solution)/shard_map/all_to_all | solution.py:27
  181.8 2.5 %fusion.3 = f32[256,640]{1,0:T(8,128)} fusion(bf16[8,96,640]{2,1,0:T(8,128)(2,1)} %all-to-all-done.3, f32[]{:T(128)} %bitcast.3, bf16[96,256]{1,0:T(8,128)(2,1)S(1)} %get-tuple-element.34), kind=kOutput, calls=%fused_computation.9 | convolution fusion | flops 251822080 | bytes 1687556 | tf_op jit(solution)/shard_map/dot_general | solution.py:115
  184.4 21.4 %all-to-all-done.4 = bf16[8,80,768]{2,1,0:T(8,128)(2,1)} async-done(((bf16[8,80,768]{2,1,0:T(8,128)(2,1)}), bf16[8,80,768]{2,1,0:T(8,128)(2,1)}, u32[]{:S(2)}, u32[]{:S(2)}) %all-to-all-start.4) | async-done | bytes 983072 | tf_op jit(solution)/shard_map/all_to_all | solution.py:27
  205.8 1.4 convert_reduce_fusion
  207.1 0.7 broadcast_multiply_fusion
  (15 shorter events, 0.2 us)
Async XLA Ops:
  7.2 4.0 %copy-start = (bf16[256,5120]{1,0:T(8,128)(2,1)S(1)}, bf16[256,5120]{1,0:T(8,128)(2,1)}, u32[]{:S(2)}) copy-start(bf16[256,5120]{1,0:T(8,128)(2,1)} %param.6) | copy-start | bytes 7864324
  7.2 109.6 %all-gather.5.cloned.1.call-start = ((), (), s32[]{:S(2)}) async-start(), calls=%async_computation.5 | async-start | bytes 7987200 | tf_op jit(solution)/shard_map/all_gather | solution.py:44
  12.4 8.3 %copy-start.2 = (s32[256]{0:T(256)S(1)}, s32[256]{0:T(256)}, u32[]{:S(2)}) copy-start(s32[256]{0:T(256)} %param.8) | copy-start | bytes 3076
  13.6 36.5 %all-to-all-start = ((bf16[8,96,640]{2,1,0:T(8,128)(2,1)}), bf16[8,96,640]{2,1,0:T(8,128)(2,1)}, u32[]{:S(2)}, u32[]{:S(2)}) async-start(bf16[8,96,640]{2,1,0:T(8,128)(2,1)} %bitcast.70), calls=%async_computation | async-start | bytes 1966080 | tf_op jit(solution)/shard_map/all_to_all | solution.py:27
  51.4 19.5 %all-to-all-start.1 = ((f32[8,8,128]{2,1,0:T(8,128)}), f32[8,8,128]{2,1,0:T(8,128)S(1)}, u32[]{:S(2)}, u32[]{:S(2)}) async-start(f32[8,8,128]{2,1,0:T(8,128)} %broadcast_in_dim_broadcast_in_dim_broadcast_in_dim.3), calls=%async_computation.1 | async-start | bytes 65536 | tf_op jit(solution)/shard_map/all_to_all | solution.py:27
  72.1 59.5 %copy-start.1 = (s32[256]{0:T(256)S(1)}, s32[256]{0:T(256)}, u32[]{:S(2)}) copy-start(s32[256]{0:T(256)} %param.9) | copy-start | bytes 3076
  72.1 59.5 %copy-start.3 = (f32[256]{0:T(256)S(1)}, f32[256]{0:T(256)}, u32[]{:S(2)}) copy-start(f32[256]{0:T(256)} %param.11) | copy-start | bytes 3076
  72.1 59.5 %copy-start.4 = (f32[256]{0:T(256)S(1)}, f32[256]{0:T(256)}, u32[]{:S(2)}) copy-start(f32[256]{0:T(256)} %param.10) | copy-start | bytes 3076
  123.4 8.2 %all-to-all-start.2 = ((f32[8,4,256]{2,1,0:T(4,128)}), f32[8,4,256]{2,1,0:T(4,128)S(1)}, u32[]{:S(2)}, u32[]{:S(2)}) async-start(f32[8,4,256]{2,1,0:T(4,128)} %broadcast_in_dim.77), calls=%async_computation.2 | async-start | bytes 65536 | tf_op jit(solution)/shard_map/all_to_all | solution.py:27
  128.2 42.6 %all-gather.7.cloned.1.call-start = ((), (), s32[]{:S(2)}) async-start(), calls=%async_computation.6 | async-start | bytes 1327104 | tf_op jit(solution)/shard_map/all_gather | solution.py:70
  139.3 35.2 %all-to-all-start.3 = ((bf16[8,96,640]{2,1,0:T(8,128)(2,1)}), bf16[8,96,640]{2,1,0:T(8,128)(2,1)}, u32[]{:S(2)}, u32[]{:S(2)}) async-start(bf16[8,96,640]{2,1,0:T(8,128)(2,1)} %bitcast.71), calls=%async_computation.3 | async-start | bytes 1966080 | tf_op jit(solution)/shard_map/all_to_all | solution.py:27
  174.5 31.2 %all-to-all-start.4 = ((bf16[8,80,768]{2,1,0:T(8,128)(2,1)}), bf16[8,80,768]{2,1,0:T(8,128)(2,1)}, u32[]{:S(2)}, u32[]{:S(2)}) async-start(bf16[8,80,768]{2,1,0:T(8,128)(2,1)} %bitcast.74), calls=%async_computation.4 | async-start | bytes 1966080 | tf_op jit(solution)/shard_map/all_to_all | solution.py:27
Sparse Core Ops, SparseCore 0:
  11.1 105.6 all-gather.4
  131.7 38.8 all-gather.6

commit v6 on v4

--- a/solution.py
+++ b/solution.py
@@ -6,8 +6,7 @@
 Y, Z, X, C = 8, 8, 4, 2
 V = X * C
 KEEP_MOST = 80
-SPARE = 8
-SLOTS = 96
+SPARE = 16
 CLIP_EPS = 0.2
 LOSS_SCALE = 8192.0
 
@@ -40,19 +39,19 @@
     here = lax.axis_index("z")
     whole = jnp.zeros((Y, Z) + own.shape[1:], own.dtype)
 
-    def put(whole, block, away, first=0):
-        at = lax.rem(here + away + Z, Z)
-        return lax.dynamic_update_slice(whole, block[:, None], (first, at, 0, 0))
+    def put(whole, block, away):
+        at = lax.rem(here + (away + Z), Z)
+        return lax.dynamic_update_slice(whole, block[:, None], (0, at, 0, 0))
 
     whole = put(whole, own, 0)
     up = down = own
-    for hop in range(1, Z // 2):
-        up, down = shift(up, 1), shift(down, -1)
-        whole = put(put(whole, up, -hop), down, hop)
-    half = Y // 2
-    up, down = shift(up[:half], 1), shift(down[half:], -1)
-    whole = put(whole, up, -(Z // 2))
-    return put(whole, down, Z // 2, half)
+    for hop in range(1, Z // 2 + 1):
+        down = shift(down, -1)
+        whole = put(whole, down, hop)
+        if hop < Z // 2:
+            up = shift(up, 1)
+            whole = put(whole, up, -hop)
+    return whole
 
 
 def per_device(hidden, head_weight, targets, kept_mask, old_logprob, advantage):
@@ -62,25 +61,27 @@
     offset = (lax.axis_index("x") * C + lax.axis_index("c")) * cols
 
     keep_float = kept_mask.astype(jnp.float32)
-    count_rows = jnp.broadcast_to(jnp.sum(keep_float).astype(jnp.bfloat16), (SPARE, cols))
-    over_z = lax.all_gather(jnp.concatenate([head_weight, count_rows], axis=0), "z")
-    small_b = to_all(head_weight[:, half:], "y", Y)
+    count_rows = jnp.broadcast_to(jnp.sum(keep_float).astype(jnp.bfloat16), (SPARE, half))
+    over_z = to_all(jnp.concatenate([head_weight[:, :half], count_rows], axis=0), "z", Z)
+    head_a = lax.all_gather(over_z[:, :rows].reshape(Z * rows, half), "y", axis=0, tiled=True)
+    kept_z = jnp.sum(over_z[:, rows, :128].astype(jnp.float32), axis=0)[0]
+    head_of_b, _ = lax.optimization_barrier((head_weight[:, half:], over_z))
+    small_b = to_all(head_of_b, "y", Y)
     head_b = ring_over_z(small_b).reshape(width, half)
-    over_z, _ = lax.optimization_barrier((over_z, small_b))
-    small_a = over_z[:, :rows, :half].reshape(Z * rows, half)
-    head_a = lax.all_gather(small_a, "y", axis=0, tiled=True)
-    kept_z = jnp.sum(over_z[:, rows, :128].astype(jnp.float32), axis=0)[0]
 
     slot_index = jnp.cumsum(kept_mask) - 1
-    ids = jnp.arange(SLOTS, dtype=jnp.int32)
+    ids = jnp.arange(KEEP_MOST, dtype=jnp.int32)
     selector = ((slot_index[None, :] == ids[:, None]) & (kept_mask[None, :] == 1)).astype(jnp.bfloat16)
-    kept_hidden = jnp.dot(selector, hidden, preferred_element_type=jnp.float32)
+    kept_hidden = jnp.dot(selector, hidden, preferred_element_type=jnp.float32).astype(jnp.bfloat16)
+    kept_hidden = kept_hidden.reshape(KEEP_MOST, Y, Z * rows).transpose(1, 0, 2)
     high = jnp.floor(kept_z / 64.0)
-    count_pair = jnp.where(ids == KEEP_MOST, high, kept_z - 64.0 * high)
-    kept_hidden = jnp.where(ids[:, None] < KEEP_MOST, kept_hidden, count_pair[:, None]).astype(jnp.bfloat16)
-    kept_hidden = exchange(kept_hidden.reshape(SLOTS, Y, Z * rows).transpose(1, 0, 2), "y")
-    pairs = jnp.sum(kept_hidden[:, KEEP_MOST:KEEP_MOST + 2, 0].astype(jnp.float32), axis=0)
+    count_pair = jnp.where(jnp.arange(SPARE) == 0, high, kept_z - 64.0 * high).astype(jnp.bfloat16)
+    count_pair = jnp.broadcast_to(count_pair[None, :, None], (Y, SPARE, Z * rows))
+    kept_hidden, _ = lax.optimization_barrier((kept_hidden, small_b))
+    kept_hidden = exchange(jnp.concatenate([kept_hidden, count_pair], axis=1), "y")
+    pairs = jnp.sum(kept_hidden[:, KEEP_MOST:, 0].astype(jnp.float32), axis=0)
     kept_total = 64.0 * pairs[0] + pairs[1]
+    kept_hidden = kept_hidden[:, :KEEP_MOST]
     scale = -(LOSS_SCALE / kept_total)
     hidden, kept_hidden, scale = lax.optimization_barrier((hidden, kept_hidden, scale))
 
@@ -116,10 +117,10 @@
     logit_grads = (slope[:, None] * (onehot - softmax_rows)).astype(jnp.bfloat16)
     compact = jnp.dot(selector, logit_grads, preferred_element_type=jnp.float32).astype(jnp.bfloat16)
 
-    all_slots = lax.all_gather(compact, "y", axis=0, tiled=True)
+    all_slots = to_all(compact, "y", Y)
     part_head = lax.dot_general(
-        kept_hidden.reshape(Y * SLOTS, Z * rows), all_slots, (((0,), (0,)), ((), ())),
-        preferred_element_type=jnp.float32,
+        kept_hidden.reshape(Y * KEEP_MOST, Z * rows), all_slots.reshape(Y * KEEP_MOST, cols),
+        (((0,), (0,)), ((), ())), preferred_element_type=jnp.float32,
     ).astype(jnp.bfloat16)
     sums = exchange(part_head.reshape(Z, rows, cols), "z")
     grad_head = scale * jnp.sum(sums.astype(jnp.float32), axis=0)
@@ -130,11 +131,10 @@
         + lax.dot_general(compact[:, half:], head_b, over_cols, preferred_element_type=jnp.float32)
     ).astype(jnp.bfloat16)
     mine = width // V
-    hidden_part = exchange(hidden_part.reshape(SLOTS, V, mine).transpose(1, 0, 2), ("x", "c"))
-    spread = jnp.tile(selector, (V, 1))
+    hidden_part = hidden_part.reshape(KEEP_MOST, V, mine).transpose(1, 0, 2)
+    hidden_part = lax.psum_scatter(hidden_part, ("x", "c"), scatter_dimension=0)
     grad_hidden = scale * lax.dot_general(
-        spread, hidden_part.reshape(V * SLOTS, mine), (((0,), (0,)), ((), ())),
-        preferred_element_type=jnp.float32,
+        selector, hidden_part, (((0,), (0,)), ((), ())), preferred_element_type=jnp.float32
     )
     return (entropy, grad_hidden, grad_head)
 

time: 233 us -> 230 us (0.987); the launches traced: 232 us -> 226 us
  waiting for transfers between devices: 84.4 us -> 74.7 us
  blocking collectives: 31.7 us -> 37.1 us
  starting transfers between devices: 48.8 us -> 44.8 us
  local copies, waits for them, and re-layouts: 20.8 us -> 24.1 us
    all_gather x3 -> x1, waiting for transfers between devices: 50.2 us -> 0.01 us  [per_device(): lax.all_gather(over_z[:, :rows].reshape(Z * rows, half), 'y', axis=0, til...]
    all_to_all x3 -> x4, waiting for transfers between devices: 26.7 us -> 58.8 us  [exchange(): return lax.all_to_all(parts, axes, split_axis=0, concat_axis=0)]
    ppermute x8 -> x7, starting transfers between devices: 27.9 us -> 19.2 us  [shift(): return lax.ppermute(block, 'z', [(i, (i + step) % Z) for i in range(Z)])]
    all_to_all x2, blocking collectives: 31.7 us -> 37.1 us  [exchange(): return lax.all_to_all(parts, axes, split_axis=0, concat_axis=0)]
    reduce_scatter x0 -> x1, waiting for transfers between devices: none -> 5.47 us  [per_device(): hidden_part = lax.psum_scatter(hidden_part, ('x', 'c'), scatter_dimension=0)]
    all_to_all x3 -> x4, starting transfers between devices: 20.8 us -> 25.5 us  [exchange(): return lax.all_to_all(parts, axes, split_axis=0, concat_axis=0)]
    ppermute x8 -> x7, waiting for transfers between devices: 7.47 us -> 10.4 us  [shift(): return lax.ppermute(block, 'z', [(i, (i + step) % Z) for i in range(Z)])]
    dynamic_update_slice x9 -> x8, local copies, waits for them, and re-layouts: 10.5 us -> 12 us  [put(): return lax.dynamic_update_slice(whole, block[:, None], (0, at, 0, 0))]
  transfers between devices with their start and end apart: 14 -> 13, of which waited for: 10 -> 9; matrix products, arithmetic and copies ran while one was open for 16% -> 17% of each run, Pallas kernels for 0% -> 0%
where the time goes in v6:
time: 230 us; the launch traced here: 226 us
  waiting for transfers between devices  74.7 us (32%)
  starting transfers between devices  44.8 us (19%)
  blocking collectives  37.1 us (16%)
  local copies, waits for them, and re-layouts  24.1 us (10%)
  matrix products  21.3 us (9%)
  between operations  15.8 us (7%)
  other arithmetic  7.8 us (3%)
    all_to_all x4, waiting for transfers between devices, exchange(): return lax.all_to_all(parts, axes, split_axis=0, concat_axis=0)  58.8 us
    all_to_all x2, blocking collectives, exchange(): return lax.all_to_all(parts, axes, split_axis=0, concat_axis=0)  37.1 us
    all_to_all x4, starting transfers between devices, exchange(): return lax.all_to_all(parts, axes, split_axis=0, concat_axis=0)  25.5 us
    ppermute x7, starting transfers between devices, shift(): return lax.ppermute(block, 'z', [(i, (i + step) % Z) for i in range(Z)])  19.2 us
    dynamic_update_slice x8, local copies, waits for them, and re-layouts, put(): return lax.dynamic_update_slice(whole, block[:, None], (0, at, 0, 0))  12 us
    ppermute x7, waiting for transfers between devices, shift(): return lax.ppermute(block, 'z', [(i, (i + step) % Z) for i in range(Z)])  10.4 us
    reduce_scatter x1, waiting for transfers between devices, per_device(): hidden_part = lax.psum_scatter(hidden_part, ('x', 'c'), scatter_dimension=0)  5.47 us
  transfers between devices with their start and end apart: 13, of which 9 were waited for; matrix products, arithmetic and copies ran while one was open for 17% of the time, Pallas kernels for 0%

profile of v6, /device:TPU:6, one launch (start us, length us, event | category | flops | bytes accessed | tf_op | source)
XLA Modules:
  0.0 225.7 jit_solution(15168101341722374112)
XLA Ops:
  7.2 1.0 fusion.23
  8.3 1.3 convert_reduce_fusion.3
  9.6 0.7 concatenate.9
  10.2 0.1 broadcast_in_dim.36
  10.3 29.0 %all_to_all.30 = bf16[8,96,384]{2,1,0:T(8,128)(2,1)S(1)} all-to-all(bf16[8,96,384]{2,1,0:T(8,128)(2,1)S(1)} %broadcast_in_dim.36), channel_id=1, replica_groups=mesh['y'=8,'z'=8,'x'=4,'c'=2] {'z'}, dimensions={0} | all-to-all | bytes 1179648 | tf_op jit(solution)/shard_map/all_to_all | solution.py:27
  39.3 0.8 copy-done.1
  40.1 0.8 slice.72
  41.0 1.0 reduce-window.9
  41.9 0.1 slice.52
  42.0 0.1 slice_reduce_fusion.1
  42.2 0.1 add_bitcast_fusion
  42.2 0.8 broadcast_in_dim.37
  43.1 7.1 %all-to-all-start.1 = ((bf16[8,80,384]{2,1,0:T(8,128)(2,1)}), bf16[8,80,384]{2,1,0:T(8,128)(2,1)}, u32[]{:S(2)}, u32[]{:S(2)}) async-start(bf16[8,80,384]{2,1,0:T(8,128)(2,1)} %broadcast_in_dim.37), calls=%async_computation.1 | async-start | bytes 983040 | tf_op jit(solution)/shard_map/all_to_all | solution.py:27
  50.3 0.6 convolution_convert_fusion
  50.8 0.1 copy.79
  51.0 0.7 slice.69
  51.8 0.1 pad.8.clone
  51.9 18.7 %all-to-all-done.1 = bf16[8,80,384]{2,1,0:T(8,128)(2,1)} async-done(((bf16[8,80,384]{2,1,0:T(8,128)(2,1)}), bf16[8,80,384]{2,1,0:T(8,128)(2,1)}, u32[]{:S(2)}, u32[]{:S(2)}) %all-to-all-start.1) | async-done | bytes 491552 | tf_op jit(solution)/shard_map/all_to_all | solution.py:27
  70.6 1.9 collective-permute-start
  72.5 3.9 %collective-permute-start.1 = (bf16[8,80,384]{2,1,0:T(8,128)(2,1)}, bf16[8,80,384]{2,1,0:T(8,128)(2,1)}, u32[]{:S(2)}, u32[]{:S(2)}) collective-permute-start(bf16[8,80,384]{2,1,0:T(8,128)(2,1)} %all-to-all-done.1), channel_id=1, source_target_pairs={{0,8},{8,16},{16,24},{24,32},{32,40},{40,48},{48,56},{56,0},{1,9},... | collective-permute-start | bytes 1474568 | tf_op jit(solution)/shard_map/ppermute | solution.py:35
  76.5 1.3 pad_maximum_fusion
  77.8 4.2 %all-to-all-start.2 = ((bf16[8,96,640]{2,1,0:T(8,128)(2,1)}), bf16[8,96,640]{2,1,0:T(8,128)(2,1)}, u32[]{:S(2)}, u32[]{:S(2)}) async-start(bf16[8,96,640]{2,1,0:T(8,128)(2,1)} %pad_maximum_fusion), calls=%async_computation.2 | async-start | bytes 1966080 | tf_op jit(solution)/shard_map/all_to_all | solution.py:27
  82.0 2.3 %broadcast_in_dim.41 = bf16[8,8,80,384]{3,2,1,0:T(8,128)(2,1)} broadcast(bf16[]{:T(256)} %constant.65.clone.1), dimensions={} | broadcast | bytes 3932162 | tf_op jit(solution)/shard_map/broadcast_in_dim | solution.py:40
  84.3 1.9 bitcast_dynamic-update-slice_fusion.6
  86.1 3.1 %collective-permute-start.2 = (bf16[8,80,384]{2,1,0:T(8,128)(2,1)}, bf16[8,80,384]{2,1,0:T(8,128)(2,1)S(1)}, u32[]{:S(2)}, u32[]{:S(2)}) collective-permute-start(bf16[8,80,384]{2,1,0:T(8,128)(2,1)} %collective-permute-done), channel_id=1, source_target_pairs={{0,56},{8,0},{16,8},{24,16},{32,24},{40,32},{48,40},{56,48},{1,57}... | collective-permute-start | bytes 1474568 | tf_op jit(solution)/shard_map/ppermute | solution.py:35
  89.3 2.7 %collective-permute-start.3 = (bf16[8,80,384]{2,1,0:T(8,128)(2,1)}, bf16[8,80,384]{2,1,0:T(8,128)(2,1)S(1)}, u32[]{:S(2)}, u32[]{:S(2)}) collective-permute-start(bf16[8,80,384]{2,1,0:T(8,128)(2,1)} %collective-permute-done.1), channel_id=1, source_target_pairs={{0,8},{8,16},{16,24},{24,32},{32,40},{40,48},{48,56},{56,0},{1,9},... | collective-permute-start | bytes 1474568 | tf_op jit(solution)/shard_map/ppermute | solution.py:35
  92.0 1.9 bitcast_dynamic-update-slice_fusion.5
  93.9 1.9 bitcast_dynamic-update-slice_fusion.4
  95.7 3.1 %collective-permute-done.2 = bf16[8,80,384]{2,1,0:T(8,128)(2,1)S(1)} collective-permute-done((bf16[8,80,384]{2,1,0:T(8,128)(2,1)}, bf16[8,80,384]{2,1,0:T(8,128)(2,1)S(1)}, u32[]{:S(2)}, u32[]{:S(2)}) %collective-permute-start.2) | collective-permute-done | bytes 491552 | tf_op jit(solution)/shard_map/ppermute | solution.py:35
  98.8 2.6 %collective-permute-start.4 = (bf16[8,80,384]{2,1,0:T(8,128)(2,1)S(1)}, bf16[8,80,384]{2,1,0:T(8,128)(2,1)}, u32[]{:S(2)}, u32[]{:S(2)}) collective-permute-start(bf16[8,80,384]{2,1,0:T(8,128)(2,1)S(1)} %collective-permute-done.2), channel_id=1, source_target_pairs={{0,56},{8,0},{16,8},{24,16},{32,24},{40,32},{48,40},{56,48},{1,57}... | collective-permute-start | bytes 1474568 | tf_op jit(solution)/shard_map/ppermute | solution.py:35
  101.4 0.3 collective-permute-done.3
  101.7 3.0 %collective-permute-start.5 = (bf16[8,80,384]{2,1,0:T(8,128)(2,1)S(1)}, bf16[8,80,384]{2,1,0:T(8,128)(2,1)S(1)}, u32[]{:S(2)}, u32[]{:S(2)}) collective-permute-start(bf16[8,80,384]{2,1,0:T(8,128)(2,1)S(1)} %collective-permute-done.3), channel_id=1, source_target_pairs={{0,8},{8,16},{16,24},{24,32},{32,40},{40,48},{48,56},{56,0},{1,9},... | collective-permute-start | bytes 1474568 | tf_op jit(solution)/shard_map/ppermute | solution.py:35
  104.7 0.9 bitcast_dynamic-update-slice_fusion.3
  105.6 0.9 bitcast_dynamic-update-slice_fusion.2
  106.4 5.4 %collective-permute-done.4 = bf16[8,80,384]{2,1,0:T(8,128)(2,1)} collective-permute-done((bf16[8,80,384]{2,1,0:T(8,128)(2,1)S(1)}, bf16[8,80,384]{2,1,0:T(8,128)(2,1)}, u32[]{:S(2)}, u32[]{:S(2)}) %collective-permute-start.4) | collective-permute-done | bytes 491552 | tf_op jit(solution)/shard_map/ppermute | solution.py:35
  111.9 2.0 collective-permute-start.6
  113.9 1.9 bitcast_dynamic-update-slice_fusion.1
  115.8 0.8 bitcast_dynamic-update-slice_fusion
  116.6 0.7 all-to-all-done.2
  117.3 0.9 convert_reduce_fusion.1
  118.2 0.6 fusion.25
  120.1 1.2 slice.70
  121.3 1.6 collective-permute-done.6
  122.9 1.9 bitcast_dynamic-update-slice_fusion.7
  124.8 4.4 %fusion.27 = (f32[256]{0:T(256)S(1)}, f32[256,384]{1,0:T(8,128)}) fusion(bf16[256,5120]{1,0:T(8,128)(2,1)S(1)} %copy-done, bf16[5120,384]{1,0:T(8,128)(2,1)} %bitcast.21), kind=kOutput, calls=%fused_computation.66 | convolution fusion | flops 1006731008 | bytes 6947840 | tf_op jit(solution)/shard_map/dot_general | solution.py:91
  129.2 3.8 %fusion.26 = (f32[256]{0:T(256)S(1)}, f32[256,384]{1,0:T(8,128)S(1)}) fusion(bf16[256,5120]{1,0:T(8,128)(2,1)S(1)} %copy-done, bf16[5120,384]{1,0:T(8,128)(2,1)} %all-gather.2.cloned.1.call-done), kind=kOutput, calls=%fused_computation.65 | convolution fusion | flops 1006731008 | bytes 6947840 | tf_op jit(solution)/shard_map/dot_general | solution.py:90
  133.1 0.5 exponential_reduce_fusion
  133.6 8.1 %all_to_all.31 = f32[8,4,256]{2,1,0:T(4,128)S(1)} all-to-all(f32[8,4,256]{2,1,0:T(4,128)S(1)} %broadcast_in_dim.90), channel_id=1, replica_groups=mesh['y'=8,'z'=8,'x'=4,'c'=2] {'x','c'}, dimensions={0} | all-to-all | bytes 65536 | tf_op jit(solution)/shard_map/all_to_all | solution.py:27
  141.8 0.6 fusion.20
  142.3 0.4 convolution_convert_fusion.1
  142.8 0.6 copy-done.2
  143.5 1.1 broadcast_in_dim.91
  144.5 7.7 %all-to-all-start.4 = ((bf16[8,80,768]{2,1,0:T(8,128)(2,1)}), bf16[8,80,768]{2,1,0:T(8,128)(2,1)}, u32[]{:S(2)}, u32[]{:S(2)}) async-start(bf16[8,80,768]{2,1,0:T(8,128)(2,1)} %broadcast_in_dim.91), calls=%async_computation.5 | async-start | bytes 1966080 | tf_op jit(solution)/shard_map/all_to_all | solution.py:27
  152.3 3.5 %fusion.8 = f32[80,5120]{1,0:T(8,128)S(1)} fusion(bf16[5120,384]{1,0:T(8,128)(2,1)} %all-gather.2.cloned.1.call-done, bf16[80,768]{1,0:T(8,128)(2,1)} %copy-done.2), kind=kOutput, calls=%fused_computation.31 | convolution fusion | flops 314572800 | bytes 5632000 | tf_op jit(solution)/shard_map/dot_general | solution.py:130
  155.8 3.4 %fusion = bf16[80,5120]{1,0:T(8,128)(2,1)S(1)} fusion(f32[80,5120]{1,0:T(8,128)S(1)} %fusion.8, bf16[5120,384]{1,0:T(8,128)(2,1)} %bitcast.21, bf16[80,768]{1,0:T(8,128)(2,1)S(1)} %copy-done.3), kind=kOutput, calls=%fused_computation.1 | convolution fusion | flops 315392000 | bytes 6451200 | tf_op jit(solution)/shard_map/dot_general | solution.py:131
  159.2 1.0 copy.78
  160.2 19.3 %all-to-all-done.4 = bf16[8,80,768]{2,1,0:T(8,128)(2,1)} async-done(((bf16[8,80,768]{2,1,0:T(8,128)(2,1)}), bf16[8,80,768]{2,1,0:T(8,128)(2,1)}, u32[]{:S(2)}, u32[]{:S(2)}) %all-to-all-start.4) | async-done | bytes 983072 | tf_op jit(solution)/shard_map/all_to_all | solution.py:27
  179.6 3.1 %bitcast_convert_fusion = bf16[640,768]{1,0:T(8,128)(2,1)} fusion(bf16[8,80,640]{2,1,0:T(8,128)(2,1)S(1)} %slice.70, bf16[8,80,768]{2,1,0:T(8,128)(2,1)} %all-to-all-done.4), kind=kOutput, calls=%fused_computation.3 | convolution fusion | flops 629637120 | bytes 2785280 | tf_op jit(solution)/shard_map/dot_general | solution.py:121
  182.7 6.5 %all-to-all-start.5 = ((bf16[8,80,768]{2,1,0:T(8,128)(2,1)}), bf16[8,80,768]{2,1,0:T(8,128)(2,1)}, u32[]{:S(2)}, u32[]{:S(2)}) async-start(bf16[8,80,768]{2,1,0:T(8,128)(2,1)} %bitcast.96), calls=%async_computation.6 | async-start | bytes 1966080 | tf_op jit(solution)/shard_map/all_to_all | solution.py:27
  189.2 5.5 %reduce-scatter.2.cloned.1.call-done = bf16[1,80,640]{2,1,0:T(8,128)(2,1)} async-done(((bf16[8,80,640]{2,1,0:T(8,128)(2,1)}), bf16[1,80,640]{2,1,0:T(8,128)(2,1)}) %reduce-scatter.2.cloned.1.call-update) | async-done | bytes 102416 | tf_op jit(solution)/shard_map/reduce_scatter | solution.py:135
  194.7 2.0 convolution_multiply_fusion
  196.7 20.1 %all-to-all-done.5 = bf16[8,80,768]{2,1,0:T(8,128)(2,1)} async-done(((bf16[8,80,768]{2,1,0:T(8,128)(2,1)}), bf16[8,80,768]{2,1,0:T(8,128)(2,1)}, u32[]{:S(2)}, u32[]{:S(2)}) %all-to-all-start.5) | async-done | bytes 983072 | tf_op jit(solution)/shard_map/all_to_all | solution.py:27
  216.8 1.4 convert_reduce_fusion
  218.2 0.7 broadcast_multiply_fusion
  (34 shorter events, 0.3 us)
Async XLA Ops:
  7.2 43.1 %copy-start = (bf16[256,5120]{1,0:T(8,128)(2,1)S(1)}, bf16[256,5120]{1,0:T(8,128)(2,1)}, u32[]{:S(2)}) copy-start(bf16[256,5120]{1,0:T(8,128)(2,1)} %param.6) | copy-start | bytes 7864324
  7.2 43.0 %copy-start.5 = (s32[256]{0:T(256)S(1)}, s32[256]{0:T(256)}, u32[]{:S(2)}) copy-start(s32[256]{0:T(256)} %param.9) | copy-start | bytes 3076
  7.2 122.0 %all-gather.2.cloned.1.call-start = ((), (), s32[]{:S(2)}) async-start(), calls=%async_computation.7 | async-start | bytes 4423680 | tf_op jit(solution)/shard_map/all_gather | solution.py:66
  39.3 0.8 copy-start.1
  40.1 10.9 %copy-start.8 = (s32[256]{0:T(256)S(1)}, s32[256]{0:T(256)}, u32[]{:S(2)}) copy-start(s32[256]{0:T(256)} %param.8) | copy-start | bytes 3076
  43.1 27.5 %all-to-all-start.1 = ((bf16[8,80,384]{2,1,0:T(8,128)(2,1)}), bf16[8,80,384]{2,1,0:T(8,128)(2,1)}, u32[]{:S(2)}, u32[]{:S(2)}) async-start(bf16[8,80,384]{2,1,0:T(8,128)(2,1)} %broadcast_in_dim.37), calls=%async_computation.1 | async-start | bytes 983040 | tf_op jit(solution)/shard_map/all_to_all | solution.py:27
  70.6 15.5 %collective-permute-start = (bf16[8,80,384]{2,1,0:T(8,128)(2,1)}, bf16[8,80,384]{2,1,0:T(8,128)(2,1)}, u32[]{:S(2)}, u32[]{:S(2)}) collective-permute-start(bf16[8,80,384]{2,1,0:T(8,128)(2,1)} %all-to-all-done.1), channel_id=1, source_target_pairs={{0,56},{8,0},{16,8},{24,16},{32,24},{40,32},{48,40},{56,48},{1,57}... | collective-permute-start | bytes 1474568 | tf_op jit(solution)/shard_map/ppermute | solution.py:35
  72.5 16.7 %collective-permute-start.1 = (bf16[8,80,384]{2,1,0:T(8,128)(2,1)}, bf16[8,80,384]{2,1,0:T(8,128)(2,1)}, u32[]{:S(2)}, u32[]{:S(2)}) collective-permute-start(bf16[8,80,384]{2,1,0:T(8,128)(2,1)} %all-to-all-done.1), channel_id=1, source_target_pairs={{0,8},{8,16},{16,24},{24,32},{32,40},{40,48},{48,56},{56,0},{1,9},... | collective-permute-start | bytes 1474568 | tf_op jit(solution)/shard_map/ppermute | solution.py:35
  77.8 39.5 %all-to-all-start.2 = ((bf16[8,96,640]{2,1,0:T(8,128)(2,1)}), bf16[8,96,640]{2,1,0:T(8,128)(2,1)}, u32[]{:S(2)}, u32[]{:S(2)}) async-start(bf16[8,96,640]{2,1,0:T(8,128)(2,1)} %pad_maximum_fusion), calls=%async_computation.2 | async-start | bytes 1966080 | tf_op jit(solution)/shard_map/all_to_all | solution.py:27
  86.1 12.7 %collective-permute-start.2 = (bf16[8,80,384]{2,1,0:T(8,128)(2,1)}, bf16[8,80,384]{2,1,0:T(8,128)(2,1)S(1)}, u32[]{:S(2)}, u32[]{:S(2)}) collective-permute-start(bf16[8,80,384]{2,1,0:T(8,128)(2,1)} %collective-permute-done), channel_id=1, source_target_pairs={{0,56},{8,0},{16,8},{24,16},{32,24},{40,32},{48,40},{56,48},{1,57}... | collective-permute-start | bytes 1474568 | tf_op jit(solution)/shard_map/ppermute | solution.py:35
  89.3 12.4 %collective-permute-start.3 = (bf16[8,80,384]{2,1,0:T(8,128)(2,1)}, bf16[8,80,384]{2,1,0:T(8,128)(2,1)S(1)}, u32[]{:S(2)}, u32[]{:S(2)}) collective-permute-start(bf16[8,80,384]{2,1,0:T(8,128)(2,1)} %collective-permute-done.1), channel_id=1, source_target_pairs={{0,8},{8,16},{16,24},{24,32},{32,40},{40,48},{48,56},{56,0},{1,9},... | collective-permute-start | bytes 1474568 | tf_op jit(solution)/shard_map/ppermute | solution.py:35
  98.8 13.1 %collective-permute-start.4 = (bf16[8,80,384]{2,1,0:T(8,128)(2,1)S(1)}, bf16[8,80,384]{2,1,0:T(8,128)(2,1)}, u32[]{:S(2)}, u32[]{:S(2)}) collective-permute-start(bf16[8,80,384]{2,1,0:T(8,128)(2,1)S(1)} %collective-permute-done.2), channel_id=1, source_target_pairs={{0,56},{8,0},{16,8},{24,16},{32,24},{40,32},{48,40},{56,48},{1,57}... | collective-permute-start | bytes 1474568 | tf_op jit(solution)/shard_map/ppermute | solution.py:35
  101.7 14.1 %collective-permute-start.5 = (bf16[8,80,384]{2,1,0:T(8,128)(2,1)S(1)}, bf16[8,80,384]{2,1,0:T(8,128)(2,1)S(1)}, u32[]{:S(2)}, u32[]{:S(2)}) collective-permute-start(bf16[8,80,384]{2,1,0:T(8,128)(2,1)S(1)} %collective-permute-done.3), channel_id=1, source_target_pairs={{0,8},{8,16},{16,24},{24,32},{32,40},{40,48},{48,56},{56,0},{1,9},... | collective-permute-start | bytes 1474568 | tf_op jit(solution)/shard_map/ppermute | solution.py:35
  111.9 11.0 %collective-permute-start.6 = (bf16[8,80,384]{2,1,0:T(8,128)(2,1)}, bf16[8,80,384]{2,1,0:T(8,128)(2,1)}, u32[]{:S(2)}, u32[]{:S(2)}) collective-permute-start(bf16[8,80,384]{2,1,0:T(8,128)(2,1)} %collective-permute-done.4), channel_id=1, source_target_pairs={{0,56},{8,0},{16,8},{24,16},{32,24},{40,32},{48,40},{56,48},{1,57}... | collective-permute-start | bytes 1474568 | tf_op jit(solution)/shard_map/ppermute | solution.py:35
  129.2 12.6 %copy-start.6 = (f32[256]{0:T(256)S(1)}, f32[256]{0:T(256)}, u32[]{:S(2)}) copy-start(f32[256]{0:T(256)} %param.11) | copy-start | bytes 3076
  129.2 12.6 %copy-start.7 = (f32[256]{0:T(256)S(1)}, f32[256]{0:T(256)}, u32[]{:S(2)}) copy-start(f32[256]{0:T(256)} %param.10) | copy-start | bytes 3076
  129.2 3.8 %copy-start.4 = (f32[256,384]{1,0:T(8,128)S(1)}, f32[256,384]{1,0:T(8,128)}, u32[]{:S(2)}) copy-start(f32[256,384]{1,0:T(8,128)} %get-tuple-element.34) | copy-start | bytes 1179652
  142.8 0.7 copy-start.2
  144.5 35.0 %all-to-all-start.4 = ((bf16[8,80,768]{2,1,0:T(8,128)(2,1)}), bf16[8,80,768]{2,1,0:T(8,128)(2,1)}, u32[]{:S(2)}, u32[]{:S(2)}) async-start(bf16[8,80,768]{2,1,0:T(8,128)(2,1)} %broadcast_in_dim.91), calls=%async_computation.5 | async-start | bytes 1966080 | tf_op jit(solution)/shard_map/all_to_all | solution.py:27
  152.2 42.5 %reduce-scatter.2.cloned.1.call-start = ((), (), s32[]{:S(2)}) async-start(), calls=%async_computation.8 | async-start | bytes 921600 | tf_op jit(solution)/shard_map/reduce_scatter | solution.py:135
  152.3 3.5 %copy-start.3 = (bf16[80,768]{1,0:T(8,128)(2,1)S(1)}, bf16[80,768]{1,0:T(8,128)(2,1)}, u32[]{:S(2)}) copy-start(bf16[80,768]{1,0:T(8,128)(2,1)} %copy-done.2) | copy-start | bytes 368644
  182.7 34.1 %all-to-all-start.5 = ((bf16[8,80,768]{2,1,0:T(8,128)(2,1)}), bf16[8,80,768]{2,1,0:T(8,128)(2,1)}, u32[]{:S(2)}, u32[]{:S(2)}) async-start(bf16[8,80,768]{2,1,0:T(8,128)(2,1)} %bitcast.96), calls=%async_computation.6 | async-start | bytes 1966080 | tf_op jit(solution)/shard_map/all_to_all | solution.py:27
Sparse Core Ops, SparseCore 0:
  41.1 79.9 all-gather.1
  160.4 34.2 reduce-scatter.1

commit v7 on v5

--- a/solution.py
+++ b/solution.py
@@ -6,7 +6,9 @@
 Y, Z, X, C = 8, 8, 4, 2
 V = X * C
 KEEP_MOST = 80
-SLOTS = 96
+SPARE = 16
+SLOTS = KEEP_MOST + SPARE
+SENT = 512
 CLIP_EPS = 0.2
 LOSS_SCALE = 8192.0
 
@@ -31,6 +33,28 @@
     return exchange(jnp.broadcast_to(values[None], (n,) + values.shape), axes)
 
 
+def shift(block, step):
+    return lax.ppermute(block, "y", [(i, (i + step) % Y) for i in range(Y)])
+
+
+def ring_over_y(own):
+    here = lax.axis_index("y")
+    whole = jnp.zeros((Y,) + own.shape, own.dtype)
+
+    def put(whole, block, away):
+        return lax.dynamic_update_slice(whole, block[None], (lax.rem(here + (away + Y), Y), 0, 0))
+
+    whole = put(whole, own, 0)
+    up = down = own
+    for hop in range(1, Y // 2 + 1):
+        down = shift(down, -1)
+        whole = put(whole, down, hop)
+        if hop < Y // 2:
+            up = shift(up, 1)
+            whole = put(whole, up, -hop)
+    return whole
+
+
 def rows_of(weights, factors):
     positions = lax.broadcasted_iota(jnp.int32, weights.shape, weights.ndim - 1).astype(jnp.float32)
     scale, entry, target = (factors[..., i, :, None] for i in range(3))
@@ -41,22 +65,36 @@
     tokens, width = hidden.shape
     rows, cols = head_weight.shape
     offset = (lax.axis_index("x") * C + lax.axis_index("c")) * cols
-    head = lax.all_gather(head_weight, ("y", "z"), axis=0, tiled=True)
 
+    head_a = lax.all_gather(head_weight[:, :SENT], ("y", "z"), axis=0, tiled=True)
     keep_float = kept_mask.astype(jnp.float32)
+    count_rows = jnp.broadcast_to(jnp.sum(keep_float).astype(jnp.bfloat16), (SPARE, cols - SENT))
+    over_z = to_all(jnp.concatenate([head_weight[:, SENT:], count_rows], axis=0), "z", Z)
+    kept_z = jnp.sum(over_z[:, rows, :128].astype(jnp.float32), axis=0)[0]
+    small_b = over_z[:, :rows].reshape(Z * rows, cols - SENT)
+    head_b = ring_over_y(small_b).reshape(width, cols - SENT)
+
     slot_index = jnp.cumsum(kept_mask) - 1
     ids = jnp.arange(SLOTS, dtype=jnp.int32)
     chosen = (slot_index[None, :] == ids[:, None]) & (kept_mask[None, :] == 1)
     selector = chosen.astype(jnp.bfloat16)
     kept_hidden = jnp.dot(selector, hidden, preferred_element_type=jnp.float32)
-    kept_hidden = jnp.where(ids[:, None] < KEEP_MOST, kept_hidden, jnp.sum(keep_float)).astype(jnp.bfloat16)
+    high = jnp.floor(kept_z / 64.0)
+    count_pair = jnp.where(ids == KEEP_MOST, high, kept_z - 64.0 * high)
+    kept_hidden = jnp.where(ids[:, None] < KEEP_MOST, kept_hidden, count_pair[:, None]).astype(jnp.bfloat16)
     kept_hidden = exchange(kept_hidden.reshape(SLOTS, Y, Z * rows).transpose(1, 0, 2), "y")
-    kept_y = jnp.sum(kept_hidden[:, KEEP_MOST, :128].astype(jnp.float32), axis=0)
-    kept_total = jnp.sum(to_all(jnp.broadcast_to(kept_y, (8, 128)), "z", Z), axis=0)[0, 0]
+    pairs = jnp.sum(kept_hidden[:, KEEP_MOST:KEEP_MOST + 2, 0].astype(jnp.float32), axis=0)
+    kept_total = 64.0 * pairs[0] + pairs[1]
     scale = -(LOSS_SCALE / kept_total)
     hidden, kept_hidden, scale = lax.optimization_barrier((hidden, kept_hidden, scale))
 
-    logits = jnp.dot(hidden, head, preferred_element_type=jnp.float32)
+    logits = jnp.concatenate(
+        [
+            jnp.dot(hidden, head_a, preferred_element_type=jnp.float32),
+            jnp.dot(hidden, head_b, preferred_element_type=jnp.float32),
+        ],
+        axis=1,
+    )
     local_target = targets - offset
     positions = jnp.arange(cols, dtype=jnp.int32)
     hit = positions[None, :] == local_target[:, None]
@@ -77,6 +115,7 @@
             jnp.sum(jnp.where(hit, logits, 0.0), axis=1),
         ]
     )
+    stats, compact = lax.optimization_barrier((stats, compact))
     stats = to_all(stats, ("x", "c"), V)
     tops, totals, moments, picks = (stats[:, i] for i in range(4))
     row_top = jnp.max(tops, axis=0)
@@ -93,16 +132,19 @@
     of_slots = jnp.stack([row_scale, row_entry, local_target.astype(jnp.float32)])
     of_slots = jnp.sum(jnp.where(chosen[None], of_slots[:, None, :], 0.0), axis=2)
 
+    all_factors = to_all(jnp.pad(of_slots, ((0, 5), (0, 128 - SLOTS))), "y", Y)
+
     own_rows = rows_of(compact, of_slots)
-    hidden_part = lax.dot_general(
-        own_rows, head, (((1,), (1,)), ((), ())), preferred_element_type=jnp.float32
+    over_cols = (((1,), (1,)), ((), ()))
+    hidden_part = (
+        lax.dot_general(own_rows[:, :SENT], head_a, over_cols, preferred_element_type=jnp.float32)
+        + lax.dot_general(own_rows[:, SENT:], head_b, over_cols, preferred_element_type=jnp.float32)
     ).astype(jnp.bfloat16)
     mine = width // V
     hidden_part = hidden_part.reshape(SLOTS, V, mine).transpose(1, 0, 2)
-    hidden_part, of_slots = lax.optimization_barrier((hidden_part, of_slots))
+    hidden_part, all_factors = lax.optimization_barrier((hidden_part, all_factors))
     hidden_part = exchange(hidden_part, ("x", "c"))
 
-    all_factors = lax.all_gather(jnp.pad(of_slots, ((0, 5), (0, 128 - SLOTS))), "y")
     all_rows = rows_of(all_slots, all_factors[:, :3, :SLOTS])
     part_head = lax.dot_general(
         kept_hidden.reshape(Y * SLOTS, Z * rows), all_rows.reshape(Y * SLOTS, cols), (((0,), (0,)), ((), ())),

time: 215 us -> 223 us (1.037)
  starting transfers between devices: 36.9 us -> 63.4 us
  blocking collectives: 25.2 us -> 0 us
  local copies, waits for them, and re-layouts: 4.19 us -> 18 us
  waiting for transfers between devices: 106 us -> 93.3 us
    all_gather x1, waiting for transfers between devices: 44.6 us -> 0.02 us  [per_device(): lax.all_gather(head_weight[:, :SENT], ('y', 'z'), axis=0, tiled=True)]
    ppermute x0 -> x7, waiting for transfers between devices: none -> 43.5 us  [shift(): return lax.ppermute(block, 'y', [(i, (i + step) % Y) for i in range(Y)])]
    all_to_all x5 -> x6, waiting for transfers between devices: 61 us -> 35.6 us  [exchange(): return lax.all_to_all(parts, axes, split_axis=0, concat_axis=0)]
    all_gather x1 -> x0, blocking collectives: 25.2 us -> none  [per_device(): lax.all_gather(jnp.pad(of_slots, ((0, 5), (0, 128 - SLOTS))), 'y')]
    ppermute x0 -> x7, starting transfers between devices: none -> 23 us  [shift(): return lax.ppermute(block, 'y', [(i, (i + step) % Y) for i in range(Y)])]
    all_gather x1, waiting for transfers between devices: 0.02 us -> 13.5 us  [per_device(): all_slots = lax.all_gather(compact, 'y')]
    dynamic_update_slice x0 -> x8, local copies, waits for them, and re-layouts: none -> 8.01 us  [put(): lax.dynamic_update_slice(whole, block[None], (lax.rem(here + (away + Y),...]
    all_to_all x5 -> x6, starting transfers between devices: 36.9 us -> 40.4 us  [exchange(): return lax.all_to_all(parts, axes, split_axis=0, concat_axis=0)]
  transfers between devices with their start and end apart: 7 -> 15, of which waited for: 5 -> 7; matrix products, arithmetic and copies ran while one was open for 11% -> 18% of each run, Pallas kernels for 0% -> 0%
where the time goes in v7:
time: 223 us; the launch traced here: 221 us
  waiting for transfers between devices  93.3 us (42%)
  starting transfers between devices  63.4 us (28%)
  matrix products  21.7 us (10%)
  local copies, waits for them, and re-layouts  18 us (8%)
  between operations  15.7 us (7%)
  other arithmetic  9.06 us (4%)
    ppermute x7, waiting for transfers between devices, shift(): return lax.ppermute(block, 'y', [(i, (i + step) % Y) for i in range(Y)])  43.5 us
    all_to_all x6, starting transfers between devices, exchange(): return lax.all_to_all(parts, axes, split_axis=0, concat_axis=0)  40.4 us
    all_to_all x6, waiting for transfers between devices, exchange(): return lax.all_to_all(parts, axes, split_axis=0, concat_axis=0)  35.6 us
    ppermute x7, starting transfers between devices, shift(): return lax.ppermute(block, 'y', [(i, (i + step) % Y) for i in range(Y)])  23 us
    all_gather x1, waiting for transfers between devices, per_device(): all_slots = lax.all_gather(compact, 'y')  13.5 us
    dynamic_update_slice x8, local copies, waits for them, and re-layouts, put(): lax.dynamic_update_slice(whole, block[None], (lax.rem(here + (away + Y),...  8.01 us
  transfers between devices with their start and end apart: 15, of which 7 were waited for; matrix products, arithmetic and copies ran while one was open for 18% of the time, Pallas kernels for 0%

profile of v7, /device:TPU:6, one launch (start us, length us, event | category | flops | bytes accessed | tf_op | source)
XLA Modules:
  0.0 221.3 jit_solution(18113785770441360964)
XLA Ops:
  7.2 0.0 all-gather.4.cloned.1.call-start
  7.2 1.7 slice.79
  8.9 0.8 slice.73
  9.7 1.3 convert_reduce_fusion.3
  11.0 0.6 concatenate.6
  11.7 0.8 broadcast_in_dim.125
  12.4 10.3 %all-to-all-start = ((bf16[8,96,256]{2,1,0:T(8,128)(2,1)}), bf16[8,96,256]{2,1,0:T(8,128)(2,1)S(1)}, u32[]{:S(2)}, u32[]{:S(2)}) async-start(bf16[8,96,256]{2,1,0:T(8,128)(2,1)} %broadcast_in_dim.125), calls=%async_computation | async-start | bytes 786432 | tf_op jit(solution)/shard_map/all_to_all | solution.py:29
  22.7 1.0 reduce-window.9
  23.7 0.1 slice.71
  23.8 0.1 slice_reduce_fusion.1
  24.0 0.7 broadcast_compare_fusion
  24.6 0.1 add_bitcast_fusion
  24.7 0.7 fusion.32
  25.4 12.0 %all-to-all-done = bf16[8,96,256]{2,1,0:T(8,128)(2,1)S(1)} async-done(((bf16[8,96,256]{2,1,0:T(8,128)(2,1)}), bf16[8,96,256]{2,1,0:T(8,128)(2,1)S(1)}, u32[]{:S(2)}, u32[]{:S(2)}) %all-to-all-start) | async-done | bytes 393248 | tf_op jit(solution)/shard_map/all_to_all | solution.py:29
  37.5 5.4 %collective-permute-start = (bf16[640,256]{1,0:T(8,128)(2,1)S(1)}, bf16[640,256]{1,0:T(8,128)(2,1)}, u32[]{:S(2)}, u32[]{:S(2)}) collective-permute-start(bf16[640,256]{1,0:T(8,128)(2,1)S(1)} %bitcast.97), channel_id=1, source_target_pairs={{0,448},{64,0},{128,64},{192,128},{256,192},{320,256},{384,320},{4... | collective-permute-start | bytes 983048 | tf_op jit(solution)/shard_map/ppermute | solution.py:37
  42.9 1.9 collective-permute-start.1
  44.9 0.5 fusion.1
  45.5 1.1 copy.62
  46.6 5.7 %all-to-all-start.1 = ((bf16[8,96,640]{2,1,0:T(8,128)(2,1)}), bf16[8,96,640]{2,1,0:T(8,128)(2,1)}, u32[]{:S(2)}, u32[]{:S(2)}) async-start(bf16[8,96,640]{2,1,0:T(8,128)(2,1)} %bitcast.93), calls=%async_computation.1 | async-start | bytes 1966080 | tf_op jit(solution)/shard_map/all_to_all | solution.py:29
  52.3 1.7 broadcast_in_dim.129
  54.0 0.7 bitcast_dynamic-update-slice_fusion.7
  54.7 5.2 %collective-permute-start.2 = (bf16[640,256]{1,0:T(8,128)(2,1)}, bf16[640,256]{1,0:T(8,128)(2,1)S(1)}, u32[]{:S(2)}, u32[]{:S(2)}) collective-permute-start(bf16[640,256]{1,0:T(8,128)(2,1)} %collective-permute-done), channel_id=1, source_target_pairs={{0,448},{64,0},{128,64},{192,128},{256,192},{320,256},{384,320},{4... | collective-permute-start | bytes 983048 | tf_op jit(solution)/shard_map/ppermute | solution.py:37
  59.9 1.9 collective-permute-start.3
  61.9 1.7 bitcast_dynamic-update-slice_fusion.6
  63.6 1.8 bitcast_dynamic-update-slice_fusion.5
  65.3 24.3 %collective-permute-done.2 = bf16[640,256]{1,0:T(8,128)(2,1)S(1)} collective-permute-done((bf16[640,256]{1,0:T(8,128)(2,1)}, bf16[640,256]{1,0:T(8,128)(2,1)S(1)}, u32[]{:S(2)}, u32[]{:S(2)}) %collective-permute-start.2) | collective-permute-done | bytes 327712 | tf_op jit(solution)/shard_map/ppermute | solution.py:37
  89.6 1.9 collective-permute-start.4
  91.6 3.9 %collective-permute-start.5 = (bf16[640,256]{1,0:T(8,128)(2,1)S(1)}, bf16[640,256]{1,0:T(8,128)(2,1)S(1)}, u32[]{:S(2)}, u32[]{:S(2)}) collective-permute-start(bf16[640,256]{1,0:T(8,128)(2,1)S(1)} %collective-permute-done.3), channel_id=1, source_target_pairs={{0,64},{64,128},{128,192},{192,256},{256,320},{320,384},{384,448},... | collective-permute-start | bytes 983048 | tf_op jit(solution)/shard_map/ppermute | solution.py:37
  95.5 0.7 bitcast_dynamic-update-slice_fusion.4
  96.2 0.8 bitcast_dynamic-update-slice_fusion.3
  97.0 10.2 %collective-permute-done.4 = bf16[640,256]{1,0:T(8,128)(2,1)S(1)} collective-permute-done((bf16[640,256]{1,0:T(8,128)(2,1)S(1)}, bf16[640,256]{1,0:T(8,128)(2,1)S(1)}, u32[]{:S(2)}, u32[]{:S(2)}) %collective-permute-start.4) | collective-permute-done | bytes 327712 | tf_op jit(solution)/shard_map/ppermute | solution.py:37
  107.2 2.8 %collective-permute-start.6 = (bf16[640,256]{1,0:T(8,128)(2,1)S(1)}, bf16[640,256]{1,0:T(8,128)(2,1)S(1)}, u32[]{:S(2)}, u32[]{:S(2)}) collective-permute-start(bf16[640,256]{1,0:T(8,128)(2,1)S(1)} %collective-permute-done.4), channel_id=1, source_target_pairs={{0,448},{64,0},{128,64},{192,128},{256,192},{320,256},{384,320},{4... | collective-permute-start | bytes 983048 | tf_op jit(solution)/shard_map/ppermute | solution.py:37
  110.0 0.8 bitcast_dynamic-update-slice_fusion.2
  110.8 0.7 bitcast_dynamic-update-slice_fusion.1
  111.5 9.0 %collective-permute-done.6 = bf16[640,256]{1,0:T(8,128)(2,1)S(1)} collective-permute-done((bf16[640,256]{1,0:T(8,128)(2,1)S(1)}, bf16[640,256]{1,0:T(8,128)(2,1)S(1)}, u32[]{:S(2)}, u32[]{:S(2)}) %collective-permute-start.6) | collective-permute-done | bytes 327712 | tf_op jit(solution)/shard_map/ppermute | solution.py:37
  120.5 0.7 bitcast_dynamic-update-slice_fusion
  121.3 0.8 convert_reduce_fusion.1
  122.1 0.6 fusion.35
  124.0 2.9 %fusion.37 = (f32[256]{0:T(256)S(1)}, f32[256,256]{0,1:T(8,128)S(1)}) fusion(bf16[256,5120]{1,0:T(8,128)(2,1)S(1)} %copy-done, bf16[5120,256]{1,0:T(8,128)(2,1)} %bitcast.14), kind=kOutput, calls=%fused_computation.86 | convolution fusion | flops 671153920 | bytes 5506048 | tf_op jit(solution)/shard_map/dot_general | solution.py:94
  126.9 0.1 copy.33
  127.0 0.0 all-gather.4.cloned.1.call-done
  127.1 4.1 %fusion.36 = (f32[256]{0:T(256)S(1)}, f32[256,512]{1,0:T(8,128)S(1)}) fusion(bf16[256,5120]{1,0:T(8,128)(2,1)S(1)} %copy-done, bf16[5120,512]{1,0:T(8,128)(2,1)} %all-gather.4.cloned.1.call-done), kind=kOutput, calls=%fused_computation.85 | convolution fusion | flops 1342308096 | bytes 8389632 | tf_op jit(solution)/shard_map/dot_general | solution.py:93
  131.2 1.0 convolution_convert_fusion
  132.2 0.4 exponential_reduce_fusion
  132.7 0.6 broadcast_in_dim.138
  133.3 4.8 %all-to-all-start.2 = ((f32[8,4,256]{2,1,0:T(4,128)}), f32[8,4,256]{2,1,0:T(4,128)S(1)}, u32[]{:S(2)}, u32[]{:S(2)}) async-start(f32[8,4,256]{2,1,0:T(4,128)} %broadcast_in_dim.138), calls=%async_computation.2 | async-start | bytes 65536 | tf_op jit(solution)/shard_map/all_to_all | solution.py:29
  138.1 0.7 all-gather.6.cloned.1.call-update
  138.8 2.6 %all-to-all-done.2 = f32[8,4,256]{2,1,0:T(4,128)S(1)} async-done(((f32[8,4,256]{2,1,0:T(4,128)}), f32[8,4,256]{2,1,0:T(4,128)S(1)}, u32[]{:S(2)}, u32[]{:S(2)}) %all-to-all-start.2) | async-done | bytes 32800 | tf_op jit(solution)/shard_map/all_to_all | solution.py:29
  141.6 0.6 subtract_multiply_fusion
  142.2 0.1 select_reduce_fusion.1
  142.4 0.6 broadcast_in_dim.144
  143.0 5.8 %all-to-all-start.3 = ((f32[8,8,128]{2,1,0:T(8,128)}), f32[8,8,128]{2,1,0:T(8,128)S(1)}, u32[]{:S(2)}, u32[]{:S(2)}) async-start(f32[8,8,128]{2,1,0:T(8,128)} %broadcast_in_dim.144), calls=%async_computation.3 | async-start | bytes 65536 | tf_op jit(solution)/shard_map/all_to_all | solution.py:29
  148.8 1.0 select_convert_fusion
  149.8 4.2 %fusion.17 = f32[96,5120]{1,0:T(8,128)S(1)} fusion(bf16[5120,512]{1,0:T(8,128)(2,1)} %all-gather.4.cloned.1.call-done, bf16[96,768]{1,0:T(8,128)(2,1)S(1)} %select_convert_fusion), kind=kOutput, calls=%fused_computation.41 | convolution fusion | flops 503316480 | bytes 7307264 | tf_op jit(solution)/shard_map/dot_general | solution.py:140
  154.1 2.7 %fusion = bf16[96,5120]{1,0:T(8,128)(2,1)S(1)} fusion(f32[96,5120]{1,0:T(8,128)S(1)} %fusion.17, bf16[5120,256]{1,0:T(8,128)(2,1)} %bitcast.14, bf16[96,768]{1,0:T(8,128)(2,1)S(1)} %select_convert_fusion), kind=kOutput, calls=%fused_computation.2 | convolution fusion | flops 252641280 | bytes 5619712 | tf_op jit(solution)/shard_map/dot_general | solution.py:141
  156.8 1.0 copy.61
  157.8 6.2 %all-to-all-start.4 = ((bf16[8,96,640]{2,1,0:T(8,128)(2,1)}), bf16[8,96,640]{2,1,0:T(8,128)(2,1)}, u32[]{:S(2)}, u32[]{:S(2)}) async-start(bf16[8,96,640]{2,1,0:T(8,128)(2,1)} %bitcast.94), calls=%async_computation.4 | async-start | bytes 1966080 | tf_op jit(solution)/shard_map/all_to_all | solution.py:29
  164.0 13.5 %all-gather.6.cloned.1.call-done = bf16[768,768]{1,0:T(8,128)(2,1)} async-done(((bf16[96,768]{1,0:T(8,128)(2,1)}), bf16[768,768]{1,0:T(8,128)(2,1)}) %all-gather.6.cloned.1.call-update) | async-done | bytes 1179664 | tf_op jit(solution)/shard_map/all_gather | solution.py:108
  177.5 3.7 %bitcast_convert_fusion = bf16[640,768]{1,0:T(8,128)(2,1)} fusion(bf16[8,96,640]{2,1,0:T(8,128)(2,1)} %all-to-all-done.1, bf16[8,96,768]{2,1,0:T(8,128)(2,1)} %bitcast.114, f32[8,96]{1,0:T(8,128)S(1)} %bitcast.110, f32[8,96]{1,0:T(8,128)S(1)} %bitcast.111, f32[8,96]{1,0:T(8,128)S(1)} %bitcast.109, f32[768]{0:T(1024)S(1)} %iota_convert_fusion), kind=kOutput, calls=%fused_computation.7 | convolution fusion | flops 757825536 | bytes 3158016 | tf_op jit(solution)/shard_map/dot_general | solution.py:149
  181.2 7.6 %all-to-all-start.5 = ((bf16[8,80,768]{2,1,0:T(8,128)(2,1)}), bf16[8,80,768]{2,1,0:T(8,128)(2,1)}, u32[]{:S(2)}, u32[]{:S(2)}) async-start(bf16[8,80,768]{2,1,0:T(8,128)(2,1)} %bitcast.100), calls=%async_computation.5 | async-start | bytes 1966080 | tf_op jit(solution)/shard_map/all_to_all | solution.py:29
  188.9 2.6 %fusion.4 = f32[256,640]{1,0:T(8,128)} fusion(bf16[8,96,640]{2,1,0:T(8,128)(2,1)} %all-to-all-done.4, f32[]{:T(128)} %bitcast.4, bf16[96,256]{1,0:T(8,128)(2,1)S(1)} %get-tuple-element.38), kind=kOutput, calls=%fused_computation.10 | convolution fusion | flops 251822080 | bytes 1687556 | tf_op jit(solution)/shard_map/dot_general | solution.py:157
  191.4 20.9 %all-to-all-done.5 = bf16[8,80,768]{2,1,0:T(8,128)(2,1)} async-done(((bf16[8,80,768]{2,1,0:T(8,128)(2,1)}), bf16[8,80,768]{2,1,0:T(8,128)(2,1)}, u32[]{:S(2)}, u32[]{:S(2)}) %all-to-all-start.5) | async-done | bytes 983072 | tf_op jit(solution)/shard_map/all_to_all | solution.py:29
  212.4 1.4 convert_reduce_fusion
  213.7 0.7 broadcast_multiply_fusion
  (35 shorter events, 0.3 us)
Async XLA Ops:
  7.2 37.8 %copy-start = (bf16[256,5120]{1,0:T(8,128)(2,1)S(1)}, bf16[256,5120]{1,0:T(8,128)(2,1)}, u32[]{:S(2)}) copy-start(bf16[256,5120]{1,0:T(8,128)(2,1)} %param.6) | copy-start | bytes 7864324
  7.2 119.9 %all-gather.4.cloned.1.call-start = ((), (), s32[]{:S(2)}) async-start(), calls=%async_computation.6 | async-start | bytes 5324800 | tf_op jit(solution)/shard_map/all_gather | solution.py:69
  12.4 25.0 %all-to-all-start = ((bf16[8,96,256]{2,1,0:T(8,128)(2,1)}), bf16[8,96,256]{2,1,0:T(8,128)(2,1)S(1)}, u32[]{:S(2)}, u32[]{:S(2)}) async-start(bf16[8,96,256]{2,1,0:T(8,128)(2,1)} %broadcast_in_dim.125), calls=%async_computation | async-start | bytes 786432 | tf_op jit(solution)/shard_map/all_to_all | solution.py:29
  37.5 17.3 %collective-permute-start = (bf16[640,256]{1,0:T(8,128)(2,1)S(1)}, bf16[640,256]{1,0:T(8,128)(2,1)}, u32[]{:S(2)}, u32[]{:S(2)}) collective-permute-start(bf16[640,256]{1,0:T(8,128)(2,1)S(1)} %bitcast.97), channel_id=1, source_target_pairs={{0,448},{64,0},{128,64},{192,128},{256,192},{320,256},{384,320},{4... | collective-permute-start | bytes 983048 | tf_op jit(solution)/shard_map/ppermute | solution.py:37
  42.9 17.1 %collective-permute-start.1 = (bf16[640,256]{1,0:T(8,128)(2,1)S(1)}, bf16[640,256]{1,0:T(8,128)(2,1)}, u32[]{:S(2)}, u32[]{:S(2)}) collective-permute-start(bf16[640,256]{1,0:T(8,128)(2,1)S(1)} %bitcast.98), channel_id=1, source_target_pairs={{0,64},{64,128},{128,192},{192,256},{256,320},{320,384},{384,448},... | collective-permute-start | bytes 983048 | tf_op jit(solution)/shard_map/ppermute | solution.py:37
  46.6 74.6 %all-to-all-start.1 = ((bf16[8,96,640]{2,1,0:T(8,128)(2,1)}), bf16[8,96,640]{2,1,0:T(8,128)(2,1)}, u32[]{:S(2)}, u32[]{:S(2)}) async-start(bf16[8,96,640]{2,1,0:T(8,128)(2,1)} %bitcast.93), calls=%async_computation.1 | async-start | bytes 1966080 | tf_op jit(solution)/shard_map/all_to_all | solution.py:29
  54.7 34.9 %collective-permute-start.2 = (bf16[640,256]{1,0:T(8,128)(2,1)}, bf16[640,256]{1,0:T(8,128)(2,1)S(1)}, u32[]{:S(2)}, u32[]{:S(2)}) collective-permute-start(bf16[640,256]{1,0:T(8,128)(2,1)} %collective-permute-done), channel_id=1, source_target_pairs={{0,448},{64,0},{128,64},{192,128},{256,192},{320,256},{384,320},{4... | collective-permute-start | bytes 983048 | tf_op jit(solution)/shard_map/ppermute | solution.py:37
  59.9 31.6 %collective-permute-start.3 = (bf16[640,256]{1,0:T(8,128)(2,1)}, bf16[640,256]{1,0:T(8,128)(2,1)S(1)}, u32[]{:S(2)}, u32[]{:S(2)}) collective-permute-start(bf16[640,256]{1,0:T(8,128)(2,1)} %collective-permute-done.1), channel_id=1, source_target_pairs={{0,64},{64,128},{128,192},{192,256},{256,320},{320,384},{384,448},... | collective-permute-start | bytes 983048 | tf_op jit(solution)/shard_map/ppermute | solution.py:37
  89.6 17.6 %collective-permute-start.4 = (bf16[640,256]{1,0:T(8,128)(2,1)S(1)}, bf16[640,256]{1,0:T(8,128)(2,1)S(1)}, u32[]{:S(2)}, u32[]{:S(2)}) collective-permute-start(bf16[640,256]{1,0:T(8,128)(2,1)S(1)} %collective-permute-done.2), channel_id=1, source_target_pairs={{0,448},{64,0},{128,64},{192,128},{256,192},{320,256},{384,320},{4... | collective-permute-start | bytes 983048 | tf_op jit(solution)/shard_map/ppermute | solution.py:37
  91.6 19.2 %collective-permute-start.5 = (bf16[640,256]{1,0:T(8,128)(2,1)S(1)}, bf16[640,256]{1,0:T(8,128)(2,1)S(1)}, u32[]{:S(2)}, u32[]{:S(2)}) collective-permute-start(bf16[640,256]{1,0:T(8,128)(2,1)S(1)} %collective-permute-done.3), channel_id=1, source_target_pairs={{0,64},{64,128},{128,192},{192,256},{256,320},{320,384},{384,448},... | collective-permute-start | bytes 983048 | tf_op jit(solution)/shard_map/ppermute | solution.py:37
  107.2 13.3 %collective-permute-start.6 = (bf16[640,256]{1,0:T(8,128)(2,1)S(1)}, bf16[640,256]{1,0:T(8,128)(2,1)S(1)}, u32[]{:S(2)}, u32[]{:S(2)}) collective-permute-start(bf16[640,256]{1,0:T(8,128)(2,1)S(1)} %collective-permute-done.4), channel_id=1, source_target_pairs={{0,448},{64,0},{128,64},{192,128},{256,192},{320,256},{384,320},{4... | collective-permute-start | bytes 983048 | tf_op jit(solution)/shard_map/ppermute | solution.py:37
  131.2 10.4 %copy-start.1 = (s32[256]{0:T(256)S(1)}, s32[256]{0:T(256)}, u32[]{:S(2)}) copy-start(s32[256]{0:T(256)} %param.9) | copy-start | bytes 3076
  131.2 10.4 %copy-start.2 = (f32[256]{0:T(256)S(1)}, f32[256]{0:T(256)}, u32[]{:S(2)}) copy-start(f32[256]{0:T(256)} %param.11) | copy-start | bytes 3076
  131.2 10.4 %copy-start.3 = (f32[256]{0:T(256)S(1)}, f32[256]{0:T(256)}, u32[]{:S(2)}) copy-start(f32[256]{0:T(256)} %param.10) | copy-start | bytes 3076
  133.3 8.2 %all-to-all-start.2 = ((f32[8,4,256]{2,1,0:T(4,128)}), f32[8,4,256]{2,1,0:T(4,128)S(1)}, u32[]{:S(2)}, u32[]{:S(2)}) async-start(f32[8,4,256]{2,1,0:T(4,128)} %broadcast_in_dim.138), calls=%async_computation.2 | async-start | bytes 65536 | tf_op jit(solution)/shard_map/all_to_all | solution.py:29
  138.1 39.4 %all-gather.6.cloned.1.call-start = ((), (), s32[]{:S(2)}) async-start(), calls=%async_computation.7 | async-start | bytes 1327104 | tf_op jit(solution)/shard_map/all_gather | solution.py:108
  143.0 14.8 %all-to-all-start.3 = ((f32[8,8,128]{2,1,0:T(8,128)}), f32[8,8,128]{2,1,0:T(8,128)S(1)}, u32[]{:S(2)}, u32[]{:S(2)}) async-start(f32[8,8,128]{2,1,0:T(8,128)} %broadcast_in_dim.144), calls=%async_computation.3 | async-start | bytes 65536 | tf_op jit(solution)/shard_map/all_to_all | solution.py:29
  157.8 23.4 %all-to-all-start.4 = ((bf16[8,96,640]{2,1,0:T(8,128)(2,1)}), bf16[8,96,640]{2,1,0:T(8,128)(2,1)}, u32[]{:S(2)}, u32[]{:S(2)}) async-start(bf16[8,96,640]{2,1,0:T(8,128)(2,1)} %bitcast.94), calls=%async_computation.4 | async-start | bytes 1966080 | tf_op jit(solution)/shard_map/all_to_all | solution.py:29
  181.2 31.1 %all-to-all-start.5 = ((bf16[8,80,768]{2,1,0:T(8,128)(2,1)}), bf16[8,80,768]{2,1,0:T(8,128)(2,1)}, u32[]{:S(2)}, u32[]{:S(2)}) async-start(bf16[8,80,768]{2,1,0:T(8,128)(2,1)} %bitcast.100), calls=%async_computation.5 | async-start | bytes 1966080 | tf_op jit(solution)/shard_map/all_to_all | solution.py:29
Sparse Core Ops, SparseCore 0:
  11.6 107.7 all-gather.3
  141.6 35.8 all-gather.5

commit v8 on v7

--- a/solution.py
+++ b/solution.py
@@ -8,6 +8,7 @@
 KEEP_MOST = 80
 SPARE = 16
 SLOTS = KEEP_MOST + SPARE
+SHARE = KEEP_MOST // V
 SENT = 512
 CLIP_EPS = 0.2
 LOSS_SCALE = 8192.0
@@ -78,13 +79,19 @@
     ids = jnp.arange(SLOTS, dtype=jnp.int32)
     chosen = (slot_index[None, :] == ids[:, None]) & (kept_mask[None, :] == 1)
     selector = chosen.astype(jnp.bfloat16)
-    kept_hidden = jnp.dot(selector, hidden, preferred_element_type=jnp.float32)
+    share_ids = jnp.arange(SPARE, dtype=jnp.int32)
+    first = (lax.axis_index("x") * C + lax.axis_index("c")) * SHARE
+    own = (slot_index[None, :] == (first + share_ids)[:, None]) & (kept_mask[None, :] == 1) & (share_ids < SHARE)[:, None]
+    kept_hidden = jnp.dot(own.astype(jnp.bfloat16), hidden, preferred_element_type=jnp.float32)
     high = jnp.floor(kept_z / 64.0)
-    count_pair = jnp.where(ids == KEEP_MOST, high, kept_z - 64.0 * high)
-    kept_hidden = jnp.where(ids[:, None] < KEEP_MOST, kept_hidden, count_pair[:, None]).astype(jnp.bfloat16)
-    kept_hidden = exchange(kept_hidden.reshape(SLOTS, Y, Z * rows).transpose(1, 0, 2), "y")
-    pairs = jnp.sum(kept_hidden[:, KEEP_MOST:KEEP_MOST + 2, 0].astype(jnp.float32), axis=0)
+    count_pair = jnp.where(share_ids == SHARE, high, kept_z - 64.0 * high)
+    kept_hidden = jnp.where(share_ids[:, None] < SHARE, kept_hidden, count_pair[:, None]).astype(jnp.bfloat16)
+    kept_hidden = exchange(kept_hidden.reshape(SPARE, Y, Z * rows).transpose(1, 0, 2), "y")
+    pairs = jnp.sum(kept_hidden[:, SHARE:SHARE + 2, 0].astype(jnp.float32), axis=0)
     kept_total = 64.0 * pairs[0] + pairs[1]
+    kept_hidden = to_all(kept_hidden, ("x", "c"), V)[:, :, :SHARE]
+    kept_hidden = kept_hidden.transpose(1, 0, 2, 3).reshape(Y, KEEP_MOST, Z * rows)
+    kept_hidden = jnp.pad(kept_hidden, ((0, 0), (0, SPARE), (0, 0)))
     scale = -(LOSS_SCALE / kept_total)
     hidden, kept_hidden, scale = lax.optimization_barrier((hidden, kept_hidden, scale))
 
@@ -151,7 +158,7 @@
         preferred_element_type=jnp.float32,
     ).astype(jnp.bfloat16)
     sums = exchange(part_head.reshape(Z, rows, cols), "z")
-    grad_head = scale * jnp.sum(sums.astype(jnp.float32), axis=0)
+    grad_head = jnp.sum(scale * sums.astype(jnp.float32), axis=0)
 
     spread = jnp.tile(selector, (V, 1))
     grad_hidden = scale * lax.dot_general(

time: 223 us -> 221 us (level)
  waiting for transfers between devices: 93.3 us -> 77.9 us
  starting transfers between devices: 63.4 us -> 71.9 us
  local copies, waits for them, and re-layouts: 18 us -> 21.1 us
    ppermute x7, waiting for transfers between devices: 43.5 us -> 26.9 us  [shift(): return lax.ppermute(block, 'y', [(i, (i + step) % Y) for i in range(Y)])]
    all_to_all x6 -> x7, starting transfers between devices: 40.4 us -> 45.3 us  [exchange(): return lax.all_to_all(parts, axes, split_axis=0, concat_axis=0)]
    ppermute x7, starting transfers between devices: 23 us -> 26.6 us  [shift(): return lax.ppermute(block, 'y', [(i, (i + step) % Y) for i in range(Y)])]
    all_to_all x6 -> x7, waiting for transfers between devices: 35.6 us -> 36.1 us  [exchange(): return lax.all_to_all(parts, axes, split_axis=0, concat_axis=0)]
  transfers between devices with their start and end apart: 15 -> 16, of which waited for: 7 -> 10; matrix products, arithmetic and copies ran while one was open for 18% -> 19% of each run, Pallas kernels for 0% -> 0%
where the time goes in v8:
time: 221 us; the launch traced here: 219 us
  waiting for transfers between devices  77.9 us (35%)
  starting transfers between devices  71.9 us (33%)
  matrix products  21.3 us (10%)
  local copies, waits for them, and re-layouts  21.1 us (10%)
  between operations  15.8 us (7%)
  other arithmetic  10.9 us (5%)
    all_to_all x7, starting transfers between devices, exchange(): return lax.all_to_all(parts, axes, split_axis=0, concat_axis=0)  45.3 us
    all_to_all x7, waiting for transfers between devices, exchange(): return lax.all_to_all(parts, axes, split_axis=0, concat_axis=0)  36.1 us
    ppermute x7, waiting for transfers between devices, shift(): return lax.ppermute(block, 'y', [(i, (i + step) % Y) for i in range(Y)])  26.9 us
    ppermute x7, starting transfers between devices, shift(): return lax.ppermute(block, 'y', [(i, (i + step) % Y) for i in range(Y)])  26.6 us
    all_gather x1, waiting for transfers between devices, per_device(): all_slots = lax.all_gather(compact, 'y')  14.1 us
    dynamic_update_slice x8, local copies, waits for them, and re-layouts, put(): lax.dynamic_update_slice(whole, block[None], (lax.rem(here + (away + Y),...  7.04 us
  transfers between devices with their start and end apart: 16, of which 10 were waited for; matrix products, arithmetic and copies ran while one was open for 19% of the time, Pallas kernels for 0%

profile of v8, /device:TPU:6, one launch (start us, length us, event | category | flops | bytes accessed | tf_op | source)
XLA Modules:
  0.0 219.0 jit_solution(906869252100526571)
XLA Ops:
  7.2 1.7 slice.83
  8.9 0.8 slice.76
  9.7 1.3 convert_reduce_fusion.2
  11.0 0.6 concatenate.6
  11.7 0.8 broadcast_in_dim.135
  12.4 10.3 %all-to-all-start = ((bf16[8,96,256]{2,1,0:T(8,128)(2,1)}), bf16[8,96,256]{2,1,0:T(8,128)(2,1)S(1)}, u32[]{:S(2)}, u32[]{:S(2)}) async-start(bf16[8,96,256]{2,1,0:T(8,128)(2,1)} %broadcast_in_dim.135), calls=%async_computation | async-start | bytes 786432 | tf_op jit(solution)/shard_map/all_to_all | solution.py:30
  22.7 1.0 reduce-window.9
  24.0 0.7 broadcast_compare_fusion
  24.8 0.6 fusion.35
  25.4 12.1 %all-to-all-done = bf16[8,96,256]{2,1,0:T(8,128)(2,1)S(1)} async-done(((bf16[8,96,256]{2,1,0:T(8,128)(2,1)}), bf16[8,96,256]{2,1,0:T(8,128)(2,1)S(1)}, u32[]{:S(2)}, u32[]{:S(2)}) %all-to-all-start) | async-done | bytes 393248 | tf_op jit(solution)/shard_map/all_to_all | solution.py:30
  37.6 0.5 fusion.1
  38.1 0.7 copy.88
  38.8 7.1 %all-to-all-start.1 = ((bf16[8,16,640]{2,1,0:T(8,128)(2,1)}), bf16[8,16,640]{2,1,0:T(8,128)(2,1)S(1)}, u32[]{:S(2)}, u32[]{:S(2)}) async-start(bf16[8,16,640]{2,1,0:T(8,128)(2,1)} %bitcast.93), calls=%async_computation.1 | async-start | bytes 327680 | tf_op jit(solution)/shard_map/all_to_all | solution.py:30
  45.9 5.1 %collective-permute-start = (bf16[640,256]{1,0:T(8,128)(2,1)S(1)}, bf16[640,256]{1,0:T(8,128)(2,1)}, u32[]{:S(2)}, u32[]{:S(2)}) collective-permute-start(bf16[640,256]{1,0:T(8,128)(2,1)S(1)} %bitcast.99), channel_id=1, source_target_pairs={{0,448},{64,0},{128,64},{192,128},{256,192},{320,256},{384,320},{4... | collective-permute-start | bytes 983048 | tf_op jit(solution)/shard_map/ppermute | solution.py:38
  51.1 1.9 collective-permute-start.1
  53.0 1.7 broadcast_in_dim.140
  54.7 0.7 bitcast_dynamic-update-slice_fusion.7
  55.4 0.4 all-to-all-done.1
  56.0 0.6 fusion.41
  58.0 1.2 broadcast_in_dim.139
  59.1 4.8 %all-to-all-start.2 = ((bf16[8,8,16,640]{3,1,2,0:T(8,128)(2,1)}), bf16[8,8,16,640]{3,1,2,0:T(8,128)(2,1)}, u32[]{:S(2)}, u32[]{:S(2)}) async-start(bf16[8,8,16,640]{3,1,2,0:T(8,128)(2,1)} %broadcast_in_dim.139), calls=%async_computation.2 | async-start | bytes 2621440 | tf_op jit(solution)/shard_map/all_to_all | solution.py:30
  63.9 4.7 %collective-permute-start.2 = (bf16[640,256]{1,0:T(8,128)(2,1)}, bf16[640,256]{1,0:T(8,128)(2,1)S(1)}, u32[]{:S(2)}, u32[]{:S(2)}) collective-permute-start(bf16[640,256]{1,0:T(8,128)(2,1)} %collective-permute-done), channel_id=1, source_target_pairs={{0,448},{64,0},{128,64},{192,128},{256,192},{320,256},{384,320},{4... | collective-permute-start | bytes 983048 | tf_op jit(solution)/shard_map/ppermute | solution.py:38
  68.6 1.9 collective-permute-start.3
  70.5 1.8 bitcast_dynamic-update-slice_fusion.6
  72.3 0.7 bitcast_dynamic-update-slice_fusion.5
  73.1 8.8 %collective-permute-done.2 = bf16[640,256]{1,0:T(8,128)(2,1)S(1)} collective-permute-done((bf16[640,256]{1,0:T(8,128)(2,1)}, bf16[640,256]{1,0:T(8,128)(2,1)S(1)}, u32[]{:S(2)}, u32[]{:S(2)}) %collective-permute-start.2) | collective-permute-done | bytes 327712 | tf_op jit(solution)/shard_map/ppermute | solution.py:38
  81.9 5.5 %collective-permute-start.4 = (bf16[640,256]{1,0:T(8,128)(2,1)S(1)}, bf16[640,256]{1,0:T(8,128)(2,1)S(1)}, u32[]{:S(2)}, u32[]{:S(2)}) collective-permute-start(bf16[640,256]{1,0:T(8,128)(2,1)S(1)} %collective-permute-done.2), channel_id=1, source_target_pairs={{0,448},{64,0},{128,64},{192,128},{256,192},{320,256},{384,320},{4... | collective-permute-start | bytes 983048 | tf_op jit(solution)/shard_map/ppermute | solution.py:38
  87.4 1.1 collective-permute-done.3
  88.5 1.9 collective-permute-start.5
  90.4 0.8 bitcast_dynamic-update-slice_fusion.4
  91.1 0.8 bitcast_dynamic-update-slice_fusion.3
  91.9 8.8 %collective-permute-done.4 = bf16[640,256]{1,0:T(8,128)(2,1)S(1)} collective-permute-done((bf16[640,256]{1,0:T(8,128)(2,1)S(1)}, bf16[640,256]{1,0:T(8,128)(2,1)S(1)}, u32[]{:S(2)}, u32[]{:S(2)}) %collective-permute-start.4) | collective-permute-done | bytes 327712 | tf_op jit(solution)/shard_map/ppermute | solution.py:38
  100.7 5.6 %collective-permute-start.6 = (bf16[640,256]{1,0:T(8,128)(2,1)S(1)}, bf16[640,256]{1,0:T(8,128)(2,1)S(1)}, u32[]{:S(2)}, u32[]{:S(2)}) collective-permute-start(bf16[640,256]{1,0:T(8,128)(2,1)S(1)} %collective-permute-done.4), channel_id=1, source_target_pairs={{0,448},{64,0},{128,64},{192,128},{256,192},{320,256},{384,320},{4... | collective-permute-start | bytes 983048 | tf_op jit(solution)/shard_map/ppermute | solution.py:38
  106.3 0.8 bitcast_dynamic-update-slice_fusion.2
  107.1 1.4 collective-permute-done.5
  108.5 0.7 bitcast_dynamic-update-slice_fusion.1
  109.2 6.8 %collective-permute-done.6 = bf16[640,256]{1,0:T(8,128)(2,1)S(1)} collective-permute-done((bf16[640,256]{1,0:T(8,128)(2,1)S(1)}, bf16[640,256]{1,0:T(8,128)(2,1)S(1)}, u32[]{:S(2)}, u32[]{:S(2)}) %collective-permute-start.6) | collective-permute-done | bytes 327712 | tf_op jit(solution)/shard_map/ppermute | solution.py:38
  116.0 0.8 bitcast_dynamic-update-slice_fusion
  116.8 1.2 slice.98
  118.0 1.1 pad.9
  119.1 2.9 %fusion.43 = (f32[256]{0:T(256)S(1)}, f32[256,256]{0,1:T(8,128)S(1)}) fusion(bf16[256,5120]{1,0:T(8,128)(2,1)S(1)} %copy-done, bf16[5120,256]{1,0:T(8,128)(2,1)} %bitcast.16), kind=kOutput, calls=%fused_computation.93 | convolution fusion | flops 671153920 | bytes 5506048 | tf_op jit(solution)/shard_map/dot_general | solution.py:101
  122.1 4.1 %fusion.42 = (f32[256]{0:T(256)S(1)}, f32[256,512]{1,0:T(8,128)S(1)}) fusion(bf16[256,5120]{1,0:T(8,128)(2,1)S(1)} %copy-done, bf16[5120,512]{1,0:T(8,128)(2,1)} %all-gather.4.cloned.1.call-done), kind=kOutput, calls=%fused_computation.92 | convolution fusion | flops 1342308096 | bytes 8389632 | tf_op jit(solution)/shard_map/dot_general | solution.py:100
  126.3 0.7 copy-done.2
  127.0 1.0 convolution_convert_fusion
  128.0 1.5 exponential_reduce_fusion
  129.5 0.6 broadcast_in_dim.149
  130.2 4.8 %all-to-all-start.3 = ((f32[8,4,256]{2,1,0:T(4,128)}), f32[8,4,256]{2,1,0:T(4,128)S(1)}, u32[]{:S(2)}, u32[]{:S(2)}) async-start(f32[8,4,256]{2,1,0:T(4,128)} %broadcast_in_dim.149), calls=%async_computation.3 | async-start | bytes 65536 | tf_op jit(solution)/shard_map/all_to_all | solution.py:30
  135.0 0.7 all-gather.6.cloned.1.call-update
  135.7 2.6 %all-to-all-done.3 = f32[8,4,256]{2,1,0:T(4,128)S(1)} async-done(((f32[8,4,256]{2,1,0:T(4,128)}), f32[8,4,256]{2,1,0:T(4,128)S(1)}, u32[]{:S(2)}, u32[]{:S(2)}) %all-to-all-start.3) | async-done | bytes 32800 | tf_op jit(solution)/shard_map/all_to_all | solution.py:30
  138.5 0.6 subtract_multiply_fusion
  139.2 0.6 broadcast_in_dim.155
  139.9 5.0 %all-to-all-start.4 = ((f32[8,8,128]{2,1,0:T(8,128)}), f32[8,8,128]{2,1,0:T(8,128)S(1)}, u32[]{:S(2)}, u32[]{:S(2)}) async-start(f32[8,8,128]{2,1,0:T(8,128)} %broadcast_in_dim.155), calls=%async_computation.4 | async-start | bytes 65536 | tf_op jit(solution)/shard_map/all_to_all | solution.py:30
  144.8 1.0 select_convert_fusion
  145.9 4.2 %fusion.17 = f32[96,5120]{1,0:T(8,128)S(1)} fusion(bf16[5120,512]{1,0:T(8,128)(2,1)} %all-gather.4.cloned.1.call-done, bf16[96,768]{1,0:T(8,128)(2,1)S(1)} %select_convert_fusion), kind=kOutput, calls=%fused_computation.40 | convolution fusion | flops 503316480 | bytes 7307264 | tf_op jit(solution)/shard_map/dot_general | solution.py:147
  150.1 2.7 %fusion = bf16[96,5120]{1,0:T(8,128)(2,1)S(1)} fusion(f32[96,5120]{1,0:T(8,128)S(1)} %fusion.17, bf16[5120,256]{1,0:T(8,128)(2,1)} %bitcast.16, bf16[96,768]{1,0:T(8,128)(2,1)S(1)} %select_convert_fusion), kind=kOutput, calls=%fused_computation.1 | convolution fusion | flops 252641280 | bytes 5619712 | tf_op jit(solution)/shard_map/dot_general | solution.py:148
  152.8 1.1 copy.87
  154.2 6.2 %all-to-all-start.5 = ((bf16[8,96,640]{2,1,0:T(8,128)(2,1)}), bf16[8,96,640]{2,1,0:T(8,128)(2,1)}, u32[]{:S(2)}, u32[]{:S(2)}) async-start(bf16[8,96,640]{2,1,0:T(8,128)(2,1)} %bitcast.96), calls=%async_computation.5 | async-start | bytes 1966080 | tf_op jit(solution)/shard_map/all_to_all | solution.py:30
  160.4 14.1 %all-gather.6.cloned.1.call-done = bf16[768,768]{1,0:T(8,128)(2,1)} async-done(((bf16[96,768]{1,0:T(8,128)(2,1)}), bf16[768,768]{1,0:T(8,128)(2,1)}) %all-gather.6.cloned.1.call-update) | async-done | bytes 1179664 | tf_op jit(solution)/shard_map/all_gather | solution.py:115
  174.5 1.6 convert
  176.1 3.4 %bitcast_convert_fusion = bf16[640,768]{1,0:T(8,128)(2,1)} fusion(bf16[8,96,640]{2,0,1:T(8,128)(2,1)S(1)} %copy-done.1, f32[8,96,768]{2,1,0:T(8,128)S(1)} %convert, f32[8,96]{0,1:T(8,128)S(1)} %copy.56, bf16[8,96]{0,1:T(8,128)(2,1)S(1)} %copy.55, f32[8,96]{0,1:T(8,128)S(1)} %copy.54, f32[768]{0:T(1024)S(1)} %iota_convert_fusion), kind=kOutput, calls=%fused_computation.7 | convolution fusion | flops 757235712 | bytes 4336128 | tf_op jit(solution)/shard_map/dot_general | solution.py:156
  179.4 7.1 %all-to-all-start.6 = ((bf16[8,80,768]{2,1,0:T(8,128)(2,1)}), bf16[8,80,768]{2,1,0:T(8,128)(2,1)}, u32[]{:S(2)}, u32[]{:S(2)}) async-start(bf16[8,80,768]{2,1,0:T(8,128)(2,1)} %bitcast.103), calls=%async_computation.6 | async-start | bytes 1966080 | tf_op jit(solution)/shard_map/all_to_all | solution.py:30
  186.6 2.6 %fusion.4 = f32[256,640]{1,0:T(8,128)} fusion(bf16[8,96,640]{2,1,0:T(8,128)(2,1)} %all-to-all-done.5, f32[]{:T(128)} %bitcast.6, bf16[96,256]{1,0:T(8,128)(2,1)S(1)} %copy-done.3), kind=kOutput, calls=%fused_computation.10 | convolution fusion | flops 251822080 | bytes 1687556 | tf_op jit(solution)/shard_map/dot_general | solution.py:164
  189.1 20.9 %all-to-all-done.6 = bf16[8,80,768]{2,1,0:T(8,128)(2,1)} async-done(((bf16[8,80,768]{2,1,0:T(8,128)(2,1)}), bf16[8,80,768]{2,1,0:T(8,128)(2,1)}, u32[]{:S(2)}, u32[]{:S(2)}) %all-to-all-start.6) | async-done | bytes 983072 | tf_op jit(solution)/shard_map/all_to_all | solution.py:30
  210.1 2.1 multiply_reduce_fusion
  (53 shorter events, 1.4 us)
Async XLA Ops:
  7.2 30.5 %copy-start = (bf16[256,5120]{1,0:T(8,128)(2,1)S(1)}, bf16[256,5120]{1,0:T(8,128)(2,1)}, u32[]{:S(2)}) copy-start(bf16[256,5120]{1,0:T(8,128)(2,1)} %param.6) | copy-start | bytes 7864324
  7.2 114.9 %all-gather.4.cloned.1.call-start = ((), (), s32[]{:S(2)}) async-start(), calls=%async_computation.7 | async-start | bytes 5324800 | tf_op jit(solution)/shard_map/all_gather | solution.py:70
  8.9 37.0 %copy-start.5 = (s32[256]{0:T(256)S(1)}, s32[256]{0:T(256)}, u32[]{:S(2)}) copy-start(s32[256]{0:T(256)} %param.8) | copy-start | bytes 3076
  12.4 25.1 %all-to-all-start = ((bf16[8,96,256]{2,1,0:T(8,128)(2,1)}), bf16[8,96,256]{2,1,0:T(8,128)(2,1)S(1)}, u32[]{:S(2)}, u32[]{:S(2)}) async-start(bf16[8,96,256]{2,1,0:T(8,128)(2,1)} %broadcast_in_dim.135), calls=%async_computation | async-start | bytes 786432 | tf_op jit(solution)/shard_map/all_to_all | solution.py:30
  38.8 17.1 %all-to-all-start.1 = ((bf16[8,16,640]{2,1,0:T(8,128)(2,1)}), bf16[8,16,640]{2,1,0:T(8,128)(2,1)S(1)}, u32[]{:S(2)}, u32[]{:S(2)}) async-start(bf16[8,16,640]{2,1,0:T(8,128)(2,1)} %bitcast.93), calls=%async_computation.1 | async-start | bytes 327680 | tf_op jit(solution)/shard_map/all_to_all | solution.py:30
  45.9 18.0 %collective-permute-start = (bf16[640,256]{1,0:T(8,128)(2,1)S(1)}, bf16[640,256]{1,0:T(8,128)(2,1)}, u32[]{:S(2)}, u32[]{:S(2)}) collective-permute-start(bf16[640,256]{1,0:T(8,128)(2,1)S(1)} %bitcast.99), channel_id=1, source_target_pairs={{0,448},{64,0},{128,64},{192,128},{256,192},{320,256},{384,320},{4... | collective-permute-start | bytes 983048 | tf_op jit(solution)/shard_map/ppermute | solution.py:38
  51.1 17.5 %collective-permute-start.1 = (bf16[640,256]{1,0:T(8,128)(2,1)S(1)}, bf16[640,256]{1,0:T(8,128)(2,1)S(1)}, u32[]{:S(2)}, u32[]{:S(2)}) collective-permute-start(bf16[640,256]{1,0:T(8,128)(2,1)S(1)} %bitcast.100), channel_id=1, source_target_pairs={{0,64},{64,128},{128,192},{192,256},{256,320},{320,384},{384,448},... | collective-permute-start | bytes 983048 | tf_op jit(solution)/shard_map/ppermute | solution.py:38
  59.1 57.6 %all-to-all-start.2 = ((bf16[8,8,16,640]{3,1,2,0:T(8,128)(2,1)}), bf16[8,8,16,640]{3,1,2,0:T(8,128)(2,1)}, u32[]{:S(2)}, u32[]{:S(2)}) async-start(bf16[8,8,16,640]{3,1,2,0:T(8,128)(2,1)} %broadcast_in_dim.139), calls=%async_computation.2 | async-start | bytes 2621440 | tf_op jit(solution)/shard_map/all_to_all | solution.py:30
  63.9 18.0 %collective-permute-start.2 = (bf16[640,256]{1,0:T(8,128)(2,1)}, bf16[640,256]{1,0:T(8,128)(2,1)S(1)}, u32[]{:S(2)}, u32[]{:S(2)}) collective-permute-start(bf16[640,256]{1,0:T(8,128)(2,1)} %collective-permute-done), channel_id=1, source_target_pairs={{0,448},{64,0},{128,64},{192,128},{256,192},{320,256},{384,320},{4... | collective-permute-start | bytes 983048 | tf_op jit(solution)/shard_map/ppermute | solution.py:38
  68.6 19.9 %collective-permute-start.3 = (bf16[640,256]{1,0:T(8,128)(2,1)S(1)}, bf16[640,256]{1,0:T(8,128)(2,1)S(1)}, u32[]{:S(2)}, u32[]{:S(2)}) collective-permute-start(bf16[640,256]{1,0:T(8,128)(2,1)S(1)} %collective-permute-done.1), channel_id=1, source_target_pairs={{0,64},{64,128},{128,192},{192,256},{256,320},{320,384},{384,448},... | collective-permute-start | bytes 983048 | tf_op jit(solution)/shard_map/ppermute | solution.py:38
  81.9 18.8 %collective-permute-start.4 = (bf16[640,256]{1,0:T(8,128)(2,1)S(1)}, bf16[640,256]{1,0:T(8,128)(2,1)S(1)}, u32[]{:S(2)}, u32[]{:S(2)}) collective-permute-start(bf16[640,256]{1,0:T(8,128)(2,1)S(1)} %collective-permute-done.2), channel_id=1, source_target_pairs={{0,448},{64,0},{128,64},{192,128},{256,192},{320,256},{384,320},{4... | collective-permute-start | bytes 983048 | tf_op jit(solution)/shard_map/ppermute | solution.py:38
  88.5 20.0 %collective-permute-start.5 = (bf16[640,256]{1,0:T(8,128)(2,1)S(1)}, bf16[640,256]{1,0:T(8,128)(2,1)S(1)}, u32[]{:S(2)}, u32[]{:S(2)}) collective-permute-start(bf16[640,256]{1,0:T(8,128)(2,1)S(1)} %collective-permute-done.3), channel_id=1, source_target_pairs={{0,64},{64,128},{128,192},{192,256},{256,320},{320,384},{384,448},... | collective-permute-start | bytes 983048 | tf_op jit(solution)/shard_map/ppermute | solution.py:38
  100.7 15.3 %collective-permute-start.6 = (bf16[640,256]{1,0:T(8,128)(2,1)S(1)}, bf16[640,256]{1,0:T(8,128)(2,1)S(1)}, u32[]{:S(2)}, u32[]{:S(2)}) collective-permute-start(bf16[640,256]{1,0:T(8,128)(2,1)S(1)} %collective-permute-done.4), channel_id=1, source_target_pairs={{0,448},{64,0},{128,64},{192,128},{256,192},{320,256},{384,320},{4... | collective-permute-start | bytes 983048 | tf_op jit(solution)/shard_map/ppermute | solution.py:38
  126.2 0.8 copy-start.2
  126.2 12.2 %copy-start.4 = (s32[256]{0:T(256)S(1)}, s32[256]{0:T(256)}, u32[]{:S(2)}) copy-start(s32[256]{0:T(256)} %param.9) | copy-start | bytes 3076
  126.2 12.2 %copy-start.6 = (f32[256]{0:T(256)S(1)}, f32[256]{0:T(256)}, u32[]{:S(2)}) copy-start(f32[256]{0:T(256)} %param.11) | copy-start | bytes 3076
  126.2 12.2 %copy-start.7 = (f32[256]{0:T(256)S(1)}, f32[256]{0:T(256)}, u32[]{:S(2)}) copy-start(f32[256]{0:T(256)} %param.10) | copy-start | bytes 3076
  130.2 8.2 %all-to-all-start.3 = ((f32[8,4,256]{2,1,0:T(4,128)}), f32[8,4,256]{2,1,0:T(4,128)S(1)}, u32[]{:S(2)}, u32[]{:S(2)}) async-start(f32[8,4,256]{2,1,0:T(4,128)} %broadcast_in_dim.149), calls=%async_computation.3 | async-start | bytes 65536 | tf_op jit(solution)/shard_map/all_to_all | solution.py:30
  135.0 39.5 %all-gather.6.cloned.1.call-start = ((), (), s32[]{:S(2)}) async-start(), calls=%async_computation.8 | async-start | bytes 1327104 | tf_op jit(solution)/shard_map/all_gather | solution.py:115
  139.9 14.0 %all-to-all-start.4 = ((f32[8,8,128]{2,1,0:T(8,128)}), f32[8,8,128]{2,1,0:T(8,128)S(1)}, u32[]{:S(2)}, u32[]{:S(2)}) async-start(f32[8,8,128]{2,1,0:T(8,128)} %broadcast_in_dim.155), calls=%async_computation.4 | async-start | bytes 65536 | tf_op jit(solution)/shard_map/all_to_all | solution.py:30
  154.2 25.3 %all-to-all-start.5 = ((bf16[8,96,640]{2,1,0:T(8,128)(2,1)}), bf16[8,96,640]{2,1,0:T(8,128)(2,1)}, u32[]{:S(2)}, u32[]{:S(2)}) async-start(bf16[8,96,640]{2,1,0:T(8,128)(2,1)} %bitcast.96), calls=%async_computation.5 | async-start | bytes 1966080 | tf_op jit(solution)/shard_map/all_to_all | solution.py:30
  174.5 1.6 copy-start.1
  176.1 10.5 %copy-start.3 = (bf16[96,256]{1,0:T(8,128)(2,1)S(1)}, bf16[96,256]{1,0:T(8,128)(2,1)}, u32[]{:S(2)}) copy-start(bf16[96,256]{1,0:T(8,128)(2,1)} %get-tuple-element.38) | copy-start | bytes 147460
  179.4 30.6 %all-to-all-start.6 = ((bf16[8,80,768]{2,1,0:T(8,128)(2,1)}), bf16[8,80,768]{2,1,0:T(8,128)(2,1)}, u32[]{:S(2)}, u32[]{:S(2)}) async-start(bf16[8,80,768]{2,1,0:T(8,128)(2,1)} %bitcast.103), calls=%async_computation.6 | async-start | bytes 1966080 | tf_op jit(solution)/shard_map/all_to_all | solution.py:30
Sparse Core Ops, SparseCore 0:
  11.1 104.2 all-gather.3
  138.5 35.9 all-gather.5

commit v9 on v6

v9 whole, which is shorter than its diff:
```python
import jax
import jax.numpy as jnp
from jax import lax
from jax.sharding import Mesh, PartitionSpec as P

Y, Z, X, C = 8, 8, 4, 2
V = X * C
KEEP_MOST = 80
SPARE = 16
SHARE = KEEP_MOST // V
CLIP_EPS = 0.2
LOSS_SCALE = 8192.0


def surrogate_slope(logprob, old_logprob, advantage, keep_float):
    importance = jnp.exp(logprob - old_logprob)
    bent_term = jnp.tanh((importance - 1.0) / CLIP_EPS)
    clipped = 1.0 + CLIP_EPS * bent_term
    choose_grad = jnp.where(
        importance * advantage <= clipped * advantage,
        advantage,
        advantage * (1.0 - bent_term * bent_term),
    )
    return keep_float * choose_grad * importance


def exchange(parts, axes):
    return lax.all_to_all(parts, axes, split_axis=0, concat_axis=0)


def to_all(values, axes, n):
    return exchange(jnp.broadcast_to(values[None], (n,) + values.shape), axes)


def ring(own, axis, n):
    blocks = [(0, own)]
    up = down = own
    for hop in range(1, n // 2 + 1):
        down = lax.ppermute(down, axis, [(i, (i - 1) % n) for i in range(n)])
        blocks.append((hop, down))
        if hop < n // 2:
            up = lax.ppermute(up, axis, [(i, (i + 1) % n) for i in range(n)])
            blocks.append((-hop, up))
    return blocks


def per_device(hidden, head_weight, targets, kept_mask, old_logprob, advantage):
    tokens, width = hidden.shape
    rows, cols = head_weight.shape
    half = cols // 2
    at_y, at_z, at_x, at_c = (lax.axis_index(name) for name in ("y", "z", "x", "c"))
    at_v = at_x * C + at_c
    offset = at_v * cols
    across_rows = (((1,), (0,)), ((), ()))

    keep_float = kept_mask.astype(jnp.float32)
    count_rows = jnp.broadcast_to(jnp.sum(keep_float).astype(jnp.bfloat16), (SPARE, half))
    over_z = to_all(jnp.concatenate([head_weight[:, :half], count_rows], axis=0), "z", Z)
    kept_z = jnp.sum(over_z[:, rows, :128].astype(jnp.float32), axis=0)[0]
    head_of_b, _ = lax.optimization_barrier((head_weight[:, half:], over_z))
    over_y = to_all(head_of_b, "y", Y)
    blocks_a = ring(over_z[:, :rows].reshape(Z * rows, half), "y", Y)
    blocks_b = ring(over_y.reshape(Y * rows, half), "z", Z)

    hidden_a = hidden.reshape(tokens, Y, Z * rows).transpose(1, 0, 2)
    hidden_b = hidden.reshape(tokens, Y, Z, rows).transpose(2, 0, 1, 3).reshape(Z, tokens, Y * rows)

    slot_index = jnp.cumsum(kept_mask) - 1
    ids = jnp.arange(KEEP_MOST, dtype=jnp.int32)
    kept = kept_mask[None, :] == 1
    selector = ((slot_index[None, :] == ids[:, None]) & kept).astype(jnp.bfloat16)
    share_ids = jnp.arange(SPARE, dtype=jnp.int32)
    own = (slot_index[None, :] == (at_v * SHARE + share_ids)[:, None]) & kept & (share_ids < SHARE)[:, None]
    kept_share = jnp.dot(own.astype(jnp.bfloat16), hidden, preferred_element_type=jnp.float32)
    high = jnp.floor(kept_z / 64.0)
    count_pair = jnp.where(share_ids == SHARE, high, kept_z - 64.0 * high)
    kept_share = jnp.where(share_ids[:, None] < SHARE, kept_share, count_pair[:, None]).astype(jnp.bfloat16)
    kept_share, _ = lax.optimization_barrier((kept_share, over_y))
    kept_share = exchange(kept_share.reshape(SPARE, Y, Z * rows).transpose(1, 0, 2), "y")
    pairs = jnp.sum(kept_share[:, SHARE:SHARE + 2, 0].astype(jnp.float32), axis=0)
    scale = -(LOSS_SCALE / (64.0 * pairs[0] + pairs[1]))
    kept_share = kept_share[:, :SHARE].reshape(Y * SHARE, Z * rows)
    kept_hidden = to_all(kept_share, ("x", "c"), V).reshape(V, Y, SHARE, Z * rows)

    def logits_of(features, blocks, here, n):
        total = 0.0
        for away, block in blocks:
            part = lax.dynamic_index_in_dim(features, lax.rem(here + (away + n), n), 0, keepdims=False)
            total = total + lax.dot_general(part, block, across_rows, preferred_element_type=jnp.float32)
        return total

    logits = jnp.concatenate(
        [logits_of(hidden_a, blocks_a, at_y, Y), logits_of(hidden_b, blocks_b, at_z, Z)], axis=1
    )
    logits, kept_hidden, scale = lax.optimization_barrier((logits, kept_hidden, scale))
    local_target = targets - offset
    positions = jnp.arange(cols, dtype=jnp.int32)
    onehot = (positions[None, :] == local_target[:, None]).astype(jnp.float32)
    local_pick = jnp.sum(logits * onehot, axis=1)
    local_top = jnp.max(logits, axis=1)
    shifted = logits - local_top[:, None]
    weights = jnp.exp(shifted)
    stats = jnp.stack(
        [local_top, jnp.sum(weights, axis=1), jnp.sum(weights * shifted, axis=1), local_pick]
    )
    stats = to_all(stats, ("x", "c"), V)
    tops, totals, moments, picks = (stats[:, i] for i in range(4))
    row_top = jnp.max(tops, axis=0)
    lower = tops - row_top[None]
    factor = jnp.exp(lower)
    row_total = jnp.sum(totals * factor, axis=0)
    row_moment = jnp.sum((moments + lower * totals) * factor, axis=0)
    picked = jnp.sum(picks, axis=0)
    entropy = jnp.log(row_total) - row_moment / row_total
    logprob = picked - row_top - jnp.log(row_total)
    slope = surrogate_slope(logprob, old_logprob, advantage, keep_float)
    softmax_rows = jnp.exp(logits - row_top[:, None]) / row_total[:, None]
    logit_grads = (slope[:, None] * (onehot - softmax_rows)).astype(jnp.bfloat16)
    compact = jnp.dot(selector, logit_grads, preferred_element_type=jnp.float32).astype(jnp.bfloat16)

    all_slots = to_all(compact, "y", Y)

    def through(grads, blocks, here, n, dtype):
        parts = jnp.zeros((n, KEEP_MOST, width // n), dtype)
        for away, block in blocks:
            part = lax.dot_general(grads, block, (((1,), (1,)), ((), ())), preferred_element_type=jnp.float32)
            parts = lax.dynamic_update_slice(
                parts, part.astype(dtype)[None], (lax.rem(here + (away + n), n), 0, 0)
            )
        return parts

    parts_a = through(compact[:, :half], blocks_a, at_y, Y, jnp.float32)
    parts_b = through(compact[:, half:], blocks_b, at_z, Z, jnp.bfloat16)
    parts_b = parts_b.reshape(Z, KEEP_MOST, Y, rows).transpose(2, 1, 0, 3).reshape(Y, KEEP_MOST, Z * rows)
    hidden_part = (parts_a + parts_b.astype(jnp.float32)).astype(jnp.bfloat16)

    kept_hidden = kept_hidden.transpose(1, 0, 2, 3).reshape(Y * KEEP_MOST, Z * rows)
    part_head = lax.dot_general(
        kept_hidden, all_slots.reshape(Y * KEEP_MOST, cols),
        (((0,), (0,)), ((), ())), preferred_element_type=jnp.float32,
    ).astype(jnp.bfloat16)
    sums = exchange(part_head.reshape(Z, rows, cols), "z")
    grad_head = jnp.sum(scale * sums.astype(jnp.float32), axis=0)

    hidden_part = hidden_part.reshape(X, C, KEEP_MOST, Z * rows)
    mine = lax.dynamic_index_in_dim(hidden_part, at_c, 1, keepdims=False)
    other = lax.dynamic_index_in_dim(hidden_part, 1 - at_c, 1, keepdims=False)
    pair = mine.astype(jnp.float32) + lax.ppermute(other, "c", [(0, 1), (1, 0)]).astype(jnp.float32)
    total = lax.dynamic_index_in_dim(pair, at_x, 0, keepdims=False)
    for step in range(1, X):
        sent = lax.dynamic_index_in_dim(pair, lax.rem(at_x + step, X), 0, keepdims=False)
        total = total + lax.ppermute(sent, "x", [(i, (i + step) % X) for i in range(X)])
    upper = total.astype(jnp.bfloat16)
    under = (total - upper.astype(jnp.float32)).astype(jnp.bfloat16)
    grad_hidden = scale * lax.dot_general(
        jnp.concatenate([selector, selector]), jnp.concatenate([upper, under]),
        (((0,), (0,)), ((), ())), preferred_element_type=jnp.float32,
    )
    return (entropy, grad_hidden, grad_head)


def solution(mesh):
    grid = Mesh(mesh.devices.reshape(Y, Z, X, C), ("y", "z", "x", "c"))
    dp, vocab = ("y", "z"), ("x", "c")
    placed = (P(dp, None), P(dp, vocab), P(dp), P(dp), P(dp), P(dp))
    return jax.shard_map(
        per_device,
        mesh=grid,
        in_specs=placed,
        out_specs=(P(dp), P(dp, vocab), P(dp, vocab)),
        check_vma=False,
    )
```

time: 230 us -> 249 us (1.083)
  the two profiles are of different devices: /device:TPU:6 before, /device:TPU:1 now
where the time goes in v9:
time: 249 us; the launch traced here: 246 us
  starting transfers between devices  108 us (43%)
  matrix products  59.2 us (24%)
  waiting for transfers between devices  40 us (16%)
  local copies, waits for them, and re-layouts  29.1 us (12%)
  other arithmetic  6.61 us (3%)
  between operations  2.71 us (1%)
    all_to_all x7, starting transfers between devices, exchange(): return lax.all_to_all(parts, axes, split_axis=0, concat_axis=0)  49.3 us
    ppermute x8, starting transfers between devices, ring(): down = lax.ppermute(down, axis, [(i, (i - 1) % n) for i in range(n)])  31.7 us
    dot_general x16, matrix products, logits_of(): lax.dot_general(part, block, across_rows, preferred_element_type=jnp.floa...  27.2 us
    dot_general x16, matrix products, through(): lax.dot_general(grads, block, (((1,), (1,)), ((), ())), preferred_element...  24.5 us
    all_to_all x7, waiting for transfers between devices, exchange(): return lax.all_to_all(parts, axes, split_axis=0, concat_axis=0)  20 us
    ppermute x6, starting transfers between devices, ring(): up = lax.ppermute(up, axis, [(i, (i + 1) % n) for i in range(n)])  15.7 us
    ppermute x3, starting transfers between devices, per_device(): lax.ppermute(sent, 'x', [(i, (i + step) % X) for i in range(X)])  8.6 us
    convert_element_type x3, local copies, waits for them, and re-layouts, per_device(): hidden_part = (parts_a + parts_b.astype(jnp.float32)).astype(jnp.bfloat16)  8.49 us
  transfers between devices with their start and end apart: 25, of which 10 were waited for; matrix products, arithmetic and copies ran while one was open for 32% of the time, Pallas kernels for 0%

profile of v9, /device:TPU:1, one launch (start us, length us, event | category | flops | bytes accessed | tf_op | source)
XLA Modules:
  0.0 246.1 jit_solution(15276957283565288306)
XLA Ops:
  4.3 10.9 %all-to-all-start = ((bf16[8,96,384]{2,1,0:T(8,128)(2,1)}), bf16[8,96,384]{2,1,0:T(8,128)(2,1)}, u32[]{:S(2)}, u32[]{:S(2)}) async-start(bf16[8,96,384]{2,1,0:T(8,128)(2,1)} %broadcast_in_dim.125), calls=%async_computation | async-start | bytes 1179648 | tf_op jit(solution)/shard_map/all_to_all | solution.py:28
  15.2 3.0 %copy.81 = bf16[256,5120]{0,1:T(8,128)(2,1)S(1)} copy(bf16[256,5120]{1,0:T(8,128)(2,1)} %param.6) | data formatting | bytes 5242880 | tf_op args[0]
  18.2 1.7 copy.91
  20.7 14.0 %all-to-all-done = bf16[8,96,384]{2,1,0:T(8,128)(2,1)} async-done(((bf16[8,96,384]{2,1,0:T(8,128)(2,1)}), bf16[8,96,384]{2,1,0:T(8,128)(2,1)}, u32[]{:S(2)}, u32[]{:S(2)}) %all-to-all-start) | async-done | bytes 589856 | tf_op jit(solution)/shard_map/all_to_all | solution.py:28
  35.7 5.1 %collective-permute-start = (bf16[640,384]{1,0:T(8,128)(2,1)S(1)}, bf16[640,384]{1,0:T(8,128)(2,1)}, u32[]{:S(2)}, u32[]{:S(2)}) collective-permute-start(bf16[640,384]{1,0:T(8,128)(2,1)S(1)} %bitcast.243), channel_id=1, source_target_pairs={{0,448},{64,0},{128,64},{192,128},{256,192},{320,256},{384,320},{4... | collective-permute-start | bytes 1474568 | tf_op jit(solution)/shard_map/ppermute | solution.py:39
  40.8 1.9 collective-permute-start.1
  43.6 5.1 %all-to-all-start.1 = ((bf16[8,80,384]{2,1,0:T(8,128)(2,1)}), bf16[8,80,384]{2,1,0:T(8,128)(2,1)}, u32[]{:S(2)}, u32[]{:S(2)}) async-start(bf16[8,80,384]{2,1,0:T(8,128)(2,1)} %broadcast_in_dim.126), calls=%async_computation.1 | async-start | bytes 983040 | tf_op jit(solution)/shard_map/all_to_all | solution.py:28
  50.7 2.3 fusion
  53.0 3.5 %collective-permute-done.1 = bf16[640,384]{1,0:T(8,128)(2,1)} collective-permute-done((bf16[640,384]{1,0:T(8,128)(2,1)S(1)}, bf16[640,384]{1,0:T(8,128)(2,1)}, u32[]{:S(2)}, u32[]{:S(2)}) %collective-permute-start.1) | collective-permute-done | bytes 491552 | tf_op jit(solution)/shard_map/ppermute | solution.py:42
  56.4 1.9 collective-permute-start.3
  58.4 4.6 %collective-permute-start.2 = (bf16[640,384]{1,0:T(8,128)(2,1)}, bf16[640,384]{1,0:T(8,128)(2,1)}, u32[]{:S(2)}, u32[]{:S(2)}) collective-permute-start(bf16[640,384]{1,0:T(8,128)(2,1)} %collective-permute-done), channel_id=1, source_target_pairs={{0,448},{64,0},{128,64},{192,128},{256,192},{320,256},{384,320},{4... | collective-permute-start | bytes 1474568 | tf_op jit(solution)/shard_map/ppermute | solution.py:39
  63.0 1.5 convolution_add_fusion.9
  64.4 2.2 convolution_add_fusion.8
  66.6 1.9 collective-permute-start.7
  68.5 3.4 %collective-permute-start.8 = (bf16[640,384]{1,0:T(8,128)(2,1)}, bf16[640,384]{1,0:T(8,128)(2,1)}, u32[]{:S(2)}, u32[]{:S(2)}) collective-permute-start(bf16[640,384]{1,0:T(8,128)(2,1)} %bitcast.14), channel_id=1, source_target_pairs={{0,8},{8,16},{16,24},{24,32},{32,40},{40,48},{48,56},{56,0},{1,9},... | collective-permute-start | bytes 1474568 | tf_op jit(solution)/shard_map/ppermute | solution.py:42
  72.6 4.6 %all-to-all-start.2 = ((bf16[8,16,640]{2,1,0:T(8,128)(2,1)}), bf16[8,16,640]{2,1,0:T(8,128)(2,1)S(1)}, u32[]{:S(2)}, u32[]{:S(2)}) async-start(bf16[8,16,640]{2,1,0:T(8,128)(2,1)} %bitcast.253), calls=%async_computation.2 | async-start | bytes 327680 | tf_op jit(solution)/shard_map/all_to_all | solution.py:28
  77.2 2.3 fusion.50
  79.5 3.4 %collective-permute-start.5 = (bf16[640,384]{1,0:T(8,128)(2,1)}, bf16[640,384]{1,0:T(8,128)(2,1)}, u32[]{:S(2)}, u32[]{:S(2)}) collective-permute-start(bf16[640,384]{1,0:T(8,128)(2,1)} %collective-permute-done.3), channel_id=1, source_target_pairs={{0,64},{64,128},{128,192},{192,256},{256,320},{320,384},{384,448},... | collective-permute-start | bytes 1474568 | tf_op jit(solution)/shard_map/ppermute | solution.py:42
  82.8 1.4 fusion.34
  84.3 3.1 %collective-permute-start.4 = (bf16[640,384]{1,0:T(8,128)(2,1)}, bf16[640,384]{1,0:T(8,128)(2,1)}, u32[]{:S(2)}, u32[]{:S(2)}) collective-permute-start(bf16[640,384]{1,0:T(8,128)(2,1)} %collective-permute-done.2), channel_id=1, source_target_pairs={{0,448},{64,0},{128,64},{192,128},{256,192},{320,256},{384,320},{4... | collective-permute-start | bytes 1474568 | tf_op jit(solution)/shard_map/ppermute | solution.py:39
  87.4 2.2 fusion.4
  92.7 11.1 %all-to-all-start.3 = ((bf16[8,80,640]{2,1,0:T(8,128)(2,1)}), bf16[8,80,640]{2,1,0:T(8,128)(2,1)}, u32[]{:S(2)}, u32[]{:S(2)}) async-start(bf16[8,80,640]{2,1,0:T(8,128)(2,1)} %broadcast_in_dim.132), calls=%async_computation.3 | async-start | bytes 1638400 | tf_op jit(solution)/shard_map/all_to_all | solution.py:28
  103.8 3.2 %collective-permute-start.10 = (bf16[640,384]{1,0:T(8,128)(2,1)}, bf16[640,384]{1,0:T(8,128)(2,1)}, u32[]{:S(2)}, u32[]{:S(2)}) collective-permute-start(bf16[640,384]{1,0:T(8,128)(2,1)} %collective-permute-done.8), channel_id=1, source_target_pairs={{0,8},{8,16},{16,24},{24,32},{32,40},{40,48},{48,56},{56,0},{1,9},... | collective-permute-start | bytes 1474568 | tf_op jit(solution)/shard_map/ppermute | solution.py:42
  107.1 3.4 %collective-permute-start.9 = (bf16[640,384]{1,0:T(8,128)(2,1)}, bf16[640,384]{1,0:T(8,128)(2,1)}, u32[]{:S(2)}, u32[]{:S(2)}) collective-permute-start(bf16[640,384]{1,0:T(8,128)(2,1)} %collective-permute-done.7), channel_id=1, source_target_pairs={{0,56},{8,0},{16,8},{24,16},{32,24},{40,32},{48,40},{56,48},{1,57}... | collective-permute-start | bytes 1474568 | tf_op jit(solution)/shard_map/ppermute | solution.py:39
  110.5 1.6 convolution_add_fusion.4
  112.1 1.5 convolution_add_fusion.3
  113.7 3.6 %collective-permute-start.6 = (bf16[640,384]{1,0:T(8,128)(2,1)}, bf16[640,384]{1,0:T(8,128)(2,1)}, u32[]{:S(2)}, u32[]{:S(2)}) collective-permute-start(bf16[640,384]{1,0:T(8,128)(2,1)} %collective-permute-done.4), channel_id=1, source_target_pairs={{0,448},{64,0},{128,64},{192,128},{256,192},{320,256},{384,320},{4... | collective-permute-start | bytes 1474568 | tf_op jit(solution)/shard_map/ppermute | solution.py:39
  117.3 1.4 fusion.31
  118.8 2.2 fusion.3
  121.0 1.9 collective-permute-start.12
  122.9 4.6 %collective-permute-start.11 = (bf16[640,384]{1,0:T(8,128)(2,1)}, bf16[640,384]{1,0:T(8,128)(2,1)}, u32[]{:S(2)}, u32[]{:S(2)}) collective-permute-start(bf16[640,384]{1,0:T(8,128)(2,1)} %collective-permute-done.9), channel_id=1, source_target_pairs={{0,56},{8,0},{16,8},{24,16},{32,24},{40,32},{48,40},{56,48},{1,57}... | collective-permute-start | bytes 1474568 | tf_op jit(solution)/shard_map/ppermute | solution.py:39
  127.5 1.5 fusion.45
  129.0 2.3 fusion.2
  131.3 2.3 copy.94
  133.6 1.5 convolution_add_fusion.5
  135.1 2.1 collective-permute-done.11
  137.2 5.3 %collective-permute-start.13 = (bf16[640,384]{1,0:T(8,128)(2,1)}, bf16[640,384]{1,0:T(8,128)(2,1)S(1)}, u32[]{:S(2)}, u32[]{:S(2)}) collective-permute-start(bf16[640,384]{1,0:T(8,128)(2,1)} %collective-permute-done.11), channel_id=1, source_target_pairs={{0,56},{8,0},{16,8},{24,16},{32,24},{40,32},{48,40},{56,48},{1,57}... | collective-permute-start | bytes 1474568 | tf_op jit(solution)/shard_map/ppermute | solution.py:39
  142.5 1.5 fusion.42
  144.0 1.5 fusion.1
  145.6 5.7 %collective-permute-done.13 = bf16[640,384]{1,0:T(8,128)(2,1)S(1)} collective-permute-done((bf16[640,384]{1,0:T(8,128)(2,1)}, bf16[640,384]{1,0:T(8,128)(2,1)S(1)}, u32[]{:S(2)}, u32[]{:S(2)}) %collective-permute-start.13) | collective-permute-done | bytes 491552 | tf_op jit(solution)/shard_map/ppermute | solution.py:39
  153.9 7.1 %all-to-all-start.4 = ((f32[8,4,256]{2,1,0:T(4,128)}), f32[8,4,256]{2,1,0:T(4,128)S(1)}, u32[]{:S(2)}, u32[]{:S(2)}) async-start(f32[8,4,256]{2,1,0:T(4,128)} %broadcast_in_dim.133), calls=%async_computation.4 | async-start | bytes 65536 | tf_op jit(solution)/shard_map/all_to_all | solution.py:28
  163.4 2.3 all-to-all-done.4
  167.9 5.8 %all-to-all-start.5 = ((bf16[8,80,768]{2,1,0:T(8,128)(2,1)}), bf16[8,80,768]{2,1,0:T(8,128)(2,1)}, u32[]{:S(2)}, u32[]{:S(2)}) async-start(bf16[8,80,768]{2,1,0:T(8,128)(2,1)} %broadcast_in_dim.152), calls=%async_computation.5 | async-start | bytes 1966080 | tf_op jit(solution)/shard_map/all_to_all | solution.py:28
  174.6 2.0 fusion.14
  177.0 2.3 fusion.16
  179.3 2.0 fusion.18
  181.2 2.0 fusion.20
  183.2 2.0 fusion.22
  185.2 2.0 fusion.24
  187.1 2.0 fusion.26
  190.0 2.2 reshape.140
  192.2 3.1 %copy.98 = f32[8,80,8,80]{3,2,1,0:T(8,128)} copy(f32[8,80,8,80]{3,0,1,2:T(8,128)S(1)} %bitcast.234) | data formatting | bytes 3276800 | tf_op jit(solution)/shard_map/convert_element_type | solution.py:135
  195.4 3.1 %reshape.138 = f32[8,80,640]{2,1,0:T(8,128)} reshape(f32[8,80,8,80]{3,2,1,0:T(8,128)} %copy.98) | data formatting | bytes 3276800 | tf_op jit(solution)/shard_map/convert_element_type | solution.py:135
  207.8 3.5 %convolution_convert_fusion = bf16[640,768]{1,0:T(8,128)(2,1)} fusion(bf16[640,640]{1,0:T(8,128)(2,1)} %reshape.135, bf16[640,768]{1,0:T(8,128)(2,1)} %bitcast.59), kind=kOutput, calls=%fused_computation.4 | convolution fusion | flops 629637120 | bytes 2785280 | tf_op jit(solution)/shard_map/dot_general | solution.py:138
  211.3 4.8 %all-to-all-start.6 = ((bf16[8,80,768]{2,1,0:T(8,128)(2,1)}), bf16[8,80,768]{2,1,0:T(8,128)(2,1)}, u32[]{:S(2)}, u32[]{:S(2)}) async-start(bf16[8,80,768]{2,1,0:T(8,128)(2,1)} %bitcast.250), calls=%async_computation.6 | async-start | bytes 1966080 | tf_op jit(solution)/shard_map/all_to_all | solution.py:28
  217.2 3.2 %collective-permute-start.14 = (bf16[4,80,640]{2,1,0:T(8,128)(2,1)S(1)}, bf16[4,80,640]{2,1,0:T(8,128)(2,1)S(1)}, u32[]{:S(2)}, u32[]{:S(2)}) collective-permute-start(bf16[4,80,640]{2,1,0:T(8,128)(2,1)S(1)} %dynamic-slice_bitcast_fusion), channel_id=1, source_target_pairs={{0,1},{1,0},{2,3},{3,2},{4,5},{5,4},{6,7},{7,6},{8,9},{9,8},{10,11... | collective-permute-start | bytes 1228808 | tf_op jit(solution)/shard_map/ppermute | solution.py:148
  222.9 2.2 collective-permute-start.15
  225.1 3.7 %collective-permute-start.16 = (f32[80,640]{1,0:T(8,128)S(1)}, f32[80,640]{1,0:T(8,128)S(1)}, u32[]{:S(2)}, u32[]{:S(2)}) collective-permute-start(f32[80,640]{1,0:T(8,128)S(1)} %get-tuple-element.24), channel_id=1, source_target_pairs={{0,4},{2,6},{4,0},{6,2},{1,5},{3,7},{5,1},{7,3},{8,12},{10,14},{12... | collective-permute-start | bytes 614408 | tf_op jit(solution)/shard_map/ppermute | solution.py:152
  228.8 2.7 %collective-permute-start.17 = (f32[80,640]{1,0:T(8,128)S(1)}, f32[80,640]{1,0:T(8,128)S(1)}, u32[]{:S(2)}, u32[]{:S(2)}) collective-permute-start(f32[80,640]{1,0:T(8,128)S(1)} %get-tuple-element.23), channel_id=1, source_target_pairs={{0,6},{2,0},{4,2},{6,4},{1,7},{3,1},{5,3},{7,5},{8,14},{10,8},{12,... | collective-permute-start | bytes 614408 | tf_op jit(solution)/shard_map/ppermute | solution.py:152
  231.6 1.4 collective-permute-done.15
  233.0 3.1 %collective-permute-done.16 = f32[80,640]{1,0:T(8,128)S(1)} collective-permute-done((f32[80,640]{1,0:T(8,128)S(1)}, f32[80,640]{1,0:T(8,128)S(1)}, u32[]{:S(2)}, u32[]{:S(2)}) %collective-permute-start.16) | collective-permute-done | bytes 204832 | tf_op jit(solution)/shard_map/ppermute | solution.py:152
  236.2 2.8 %collective-permute-done.17 = f32[80,640]{1,0:T(8,128)S(1)} collective-permute-done((f32[80,640]{1,0:T(8,128)S(1)}, f32[80,640]{1,0:T(8,128)S(1)}, u32[]{:S(2)}, u32[]{:S(2)}) %collective-permute-start.17) | collective-permute-done | bytes 204832 | tf_op jit(solution)/shard_map/ppermute | solution.py:152
  240.2 3.7 %all-to-all-done.6 = bf16[8,80,768]{2,1,0:T(8,128)(2,1)} async-done(((bf16[8,80,768]{2,1,0:T(8,128)(2,1)}), bf16[8,80,768]{2,1,0:T(8,128)(2,1)}, u32[]{:S(2)}, u32[]{:S(2)}) %all-to-all-start.6) | async-done | bytes 983072 | tf_op jit(solution)/shard_map/all_to_all | solution.py:28
  244.0 2.1 multiply_reduce_fusion
  (95 shorter events, 34.2 us)
Async XLA Ops:
  4.3 30.3 %all-to-all-start = ((bf16[8,96,384]{2,1,0:T(8,128)(2,1)}), bf16[8,96,384]{2,1,0:T(8,128)(2,1)}, u32[]{:S(2)}, u32[]{:S(2)}) async-start(bf16[8,96,384]{2,1,0:T(8,128)(2,1)} %broadcast_in_dim.125), calls=%async_computation | async-start | bytes 1179648 | tf_op jit(solution)/shard_map/all_to_all | solution.py:28
  18.2 1.8 copy-start.8
  18.2 2.4 copy-start.11
  35.7 22.6 %collective-permute-start = (bf16[640,384]{1,0:T(8,128)(2,1)S(1)}, bf16[640,384]{1,0:T(8,128)(2,1)}, u32[]{:S(2)}, u32[]{:S(2)}) collective-permute-start(bf16[640,384]{1,0:T(8,128)(2,1)S(1)} %bitcast.243), channel_id=1, source_target_pairs={{0,448},{64,0},{128,64},{192,128},{256,192},{320,256},{384,320},{4... | collective-permute-start | bytes 1474568 | tf_op jit(solution)/shard_map/ppermute | solution.py:39
  40.8 15.6 %collective-permute-start.1 = (bf16[640,384]{1,0:T(8,128)(2,1)S(1)}, bf16[640,384]{1,0:T(8,128)(2,1)}, u32[]{:S(2)}, u32[]{:S(2)}) collective-permute-start(bf16[640,384]{1,0:T(8,128)(2,1)S(1)} %bitcast.244), channel_id=1, source_target_pairs={{0,64},{64,128},{128,192},{192,256},{256,320},{320,384},{384,448},... | collective-permute-start | bytes 1474568 | tf_op jit(solution)/shard_map/ppermute | solution.py:42
  43.6 23.0 %all-to-all-start.1 = ((bf16[8,80,384]{2,1,0:T(8,128)(2,1)}), bf16[8,80,384]{2,1,0:T(8,128)(2,1)}, u32[]{:S(2)}, u32[]{:S(2)}) async-start(bf16[8,80,384]{2,1,0:T(8,128)(2,1)} %broadcast_in_dim.126), calls=%async_computation.1 | async-start | bytes 983040 | tf_op jit(solution)/shard_map/all_to_all | solution.py:28
  50.7 12.3 %copy-start.6 = (f32[256,384]{1,0:T(8,128)S(1)}, f32[256,384]{1,0:T(8,128)}, u32[]{:S(2)}) copy-start(f32[256,384]{1,0:T(8,128)} %fusion.39) | copy-start | bytes 1179652
  56.4 23.0 %collective-permute-start.3 = (bf16[640,384]{1,0:T(8,128)(2,1)}, bf16[640,384]{1,0:T(8,128)(2,1)}, u32[]{:S(2)}, u32[]{:S(2)}) collective-permute-start(bf16[640,384]{1,0:T(8,128)(2,1)} %collective-permute-done.1), channel_id=1, source_target_pairs={{0,64},{64,128},{128,192},{192,256},{256,320},{320,384},{384,448},... | collective-permute-start | bytes 1474568 | tf_op jit(solution)/shard_map/ppermute | solution.py:42
  58.4 25.9 %collective-permute-start.2 = (bf16[640,384]{1,0:T(8,128)(2,1)}, bf16[640,384]{1,0:T(8,128)(2,1)}, u32[]{:S(2)}, u32[]{:S(2)}) collective-permute-start(bf16[640,384]{1,0:T(8,128)(2,1)} %collective-permute-done), channel_id=1, source_target_pairs={{0,448},{64,0},{128,64},{192,128},{256,192},{320,256},{384,320},{4... | collective-permute-start | bytes 1474568 | tf_op jit(solution)/shard_map/ppermute | solution.py:39
  66.6 40.5 %collective-permute-start.7 = (bf16[640,384]{1,0:T(8,128)(2,1)}, bf16[640,384]{1,0:T(8,128)(2,1)}, u32[]{:S(2)}, u32[]{:S(2)}) collective-permute-start(bf16[640,384]{1,0:T(8,128)(2,1)} %bitcast.14), channel_id=1, source_target_pairs={{0,56},{8,0},{16,8},{24,16},{32,24},{40,32},{48,40},{56,48},{1,57}... | collective-permute-start | bytes 1474568 | tf_op jit(solution)/shard_map/ppermute | solution.py:39
  68.5 35.3 %collective-permute-start.8 = (bf16[640,384]{1,0:T(8,128)(2,1)}, bf16[640,384]{1,0:T(8,128)(2,1)}, u32[]{:S(2)}, u32[]{:S(2)}) collective-permute-start(bf16[640,384]{1,0:T(8,128)(2,1)} %bitcast.14), channel_id=1, source_target_pairs={{0,8},{8,16},{16,24},{24,32},{32,40},{40,48},{48,56},{56,0},{1,9},... | collective-permute-start | bytes 1474568 | tf_op jit(solution)/shard_map/ppermute | solution.py:42
  72.6 17.1 %all-to-all-start.2 = ((bf16[8,16,640]{2,1,0:T(8,128)(2,1)}), bf16[8,16,640]{2,1,0:T(8,128)(2,1)S(1)}, u32[]{:S(2)}, u32[]{:S(2)}) async-start(bf16[8,16,640]{2,1,0:T(8,128)(2,1)} %bitcast.253), calls=%async_computation.2 | async-start | bytes 327680 | tf_op jit(solution)/shard_map/all_to_all | solution.py:28
  77.1 10.3 %copy-start.5 = (f32[256,384]{1,0:T(8,128)S(1)}, f32[256,384]{1,0:T(8,128)}, u32[]{:S(2)}) copy-start(f32[256,384]{1,0:T(8,128)} %convolution_add_fusion.8) | copy-start | bytes 1179652
  79.5 37.9 %collective-permute-start.5 = (bf16[640,384]{1,0:T(8,128)(2,1)}, bf16[640,384]{1,0:T(8,128)(2,1)}, u32[]{:S(2)}, u32[]{:S(2)}) collective-permute-start(bf16[640,384]{1,0:T(8,128)(2,1)} %collective-permute-done.3), channel_id=1, source_target_pairs={{0,64},{64,128},{128,192},{192,256},{256,320},{320,384},{384,448},... | collective-permute-start | bytes 1474568 | tf_op jit(solution)/shard_map/ppermute | solution.py:42
  84.3 29.4 %collective-permute-start.4 = (bf16[640,384]{1,0:T(8,128)(2,1)}, bf16[640,384]{1,0:T(8,128)(2,1)}, u32[]{:S(2)}, u32[]{:S(2)}) collective-permute-start(bf16[640,384]{1,0:T(8,128)(2,1)} %collective-permute-done.2), channel_id=1, source_target_pairs={{0,448},{64,0},{128,64},{192,128},{256,192},{320,256},{384,320},{4... | collective-permute-start | bytes 1474568 | tf_op jit(solution)/shard_map/ppermute | solution.py:39
  92.7 38.6 %all-to-all-start.3 = ((bf16[8,80,640]{2,1,0:T(8,128)(2,1)}), bf16[8,80,640]{2,1,0:T(8,128)(2,1)}, u32[]{:S(2)}, u32[]{:S(2)}) async-start(bf16[8,80,640]{2,1,0:T(8,128)(2,1)} %broadcast_in_dim.132), calls=%async_computation.3 | async-start | bytes 1638400 | tf_op jit(solution)/shard_map/all_to_all | solution.py:28
  103.8 14.9 %copy-start.4 = (f32[256,384]{1,0:T(8,128)S(1)}, f32[256,384]{1,0:T(8,128)}, u32[]{:S(2)}) copy-start(f32[256,384]{1,0:T(8,128)} %fusion.4) | copy-start | bytes 1179652
  103.8 17.1 %collective-permute-start.10 = (bf16[640,384]{1,0:T(8,128)(2,1)}, bf16[640,384]{1,0:T(8,128)(2,1)}, u32[]{:S(2)}, u32[]{:S(2)}) collective-permute-start(bf16[640,384]{1,0:T(8,128)(2,1)} %collective-permute-done.8), channel_id=1, source_target_pairs={{0,8},{8,16},{16,24},{24,32},{32,40},{40,48},{48,56},{56,0},{1,9},... | collective-permute-start | bytes 1474568 | tf_op jit(solution)/shard_map/ppermute | solution.py:42
  107.1 15.8 %collective-permute-start.9 = (bf16[640,384]{1,0:T(8,128)(2,1)}, bf16[640,384]{1,0:T(8,128)(2,1)}, u32[]{:S(2)}, u32[]{:S(2)}) collective-permute-start(bf16[640,384]{1,0:T(8,128)(2,1)} %collective-permute-done.7), channel_id=1, source_target_pairs={{0,56},{8,0},{16,8},{24,16},{32,24},{40,32},{48,40},{56,48},{1,57}... | collective-permute-start | bytes 1474568 | tf_op jit(solution)/shard_map/ppermute | solution.py:39
  113.7 19.9 %collective-permute-start.6 = (bf16[640,384]{1,0:T(8,128)(2,1)}, bf16[640,384]{1,0:T(8,128)(2,1)}, u32[]{:S(2)}, u32[]{:S(2)}) collective-permute-start(bf16[640,384]{1,0:T(8,128)(2,1)} %collective-permute-done.4), channel_id=1, source_target_pairs={{0,448},{64,0},{128,64},{192,128},{256,192},{320,256},{384,320},{4... | collective-permute-start | bytes 1474568 | tf_op jit(solution)/shard_map/ppermute | solution.py:39
  121.0 21.5 %collective-permute-start.12 = (bf16[640,384]{1,0:T(8,128)(2,1)}, bf16[640,384]{1,0:T(8,128)(2,1)}, u32[]{:S(2)}, u32[]{:S(2)}) collective-permute-start(bf16[640,384]{1,0:T(8,128)(2,1)} %collective-permute-done.10), channel_id=1, source_target_pairs={{0,8},{8,16},{16,24},{24,32},{32,40},{40,48},{48,56},{56,0},{1,9},... | collective-permute-start | bytes 1474568 | tf_op jit(solution)/shard_map/ppermute | solution.py:42
  122.9 14.3 %collective-permute-start.11 = (bf16[640,384]{1,0:T(8,128)(2,1)}, bf16[640,384]{1,0:T(8,128)(2,1)}, u32[]{:S(2)}, u32[]{:S(2)}) collective-permute-start(bf16[640,384]{1,0:T(8,128)(2,1)} %collective-permute-done.9), channel_id=1, source_target_pairs={{0,56},{8,0},{16,8},{24,16},{32,24},{40,32},{48,40},{56,48},{1,57}... | collective-permute-start | bytes 1474568 | tf_op jit(solution)/shard_map/ppermute | solution.py:39
  131.3 12.7 %copy-start.7 = (f32[256,384]{1,0:T(8,128)S(1)}, f32[256,384]{1,0:T(8,128)}, u32[]{:S(2)}) copy-start(f32[256,384]{1,0:T(8,128)} %fusion.2) | copy-start | bytes 1179652
  137.2 14.1 %collective-permute-start.13 = (bf16[640,384]{1,0:T(8,128)(2,1)}, bf16[640,384]{1,0:T(8,128)(2,1)S(1)}, u32[]{:S(2)}, u32[]{:S(2)}) collective-permute-start(bf16[640,384]{1,0:T(8,128)(2,1)} %collective-permute-done.11), channel_id=1, source_target_pairs={{0,56},{8,0},{16,8},{24,16},{32,24},{40,32},{48,40},{56,48},{1,57}... | collective-permute-start | bytes 1474568 | tf_op jit(solution)/shard_map/ppermute | solution.py:39
  152.8 13.0 %copy-start.9 = (f32[256]{0:T(256)S(1)}, f32[256]{0:T(256)}, u32[]{:S(2)}) copy-start(f32[256]{0:T(256)} %param.11) | copy-start | bytes 3076
  152.8 13.0 %copy-start.10 = (f32[256]{0:T(256)S(1)}, f32[256]{0:T(256)}, u32[]{:S(2)}) copy-start(f32[256]{0:T(256)} %param.10) | copy-start | bytes 3076
  153.9 11.8 %all-to-all-start.4 = ((f32[8,4,256]{2,1,0:T(4,128)}), f32[8,4,256]{2,1,0:T(4,128)S(1)}, u32[]{:S(2)}, u32[]{:S(2)}) async-start(f32[8,4,256]{2,1,0:T(4,128)} %broadcast_in_dim.133), calls=%async_computation.4 | async-start | bytes 65536 | tf_op jit(solution)/shard_map/all_to_all | solution.py:28
  167.9 39.9 %all-to-all-start.5 = ((bf16[8,80,768]{2,1,0:T(8,128)(2,1)}), bf16[8,80,768]{2,1,0:T(8,128)(2,1)}, u32[]{:S(2)}, u32[]{:S(2)}) async-start(bf16[8,80,768]{2,1,0:T(8,128)(2,1)} %broadcast_in_dim.152), calls=%async_computation.5 | async-start | bytes 1966080 | tf_op jit(solution)/shard_map/all_to_all | solution.py:28
  177.0 12.1 %copy-start = (f32[8,80,640]{2,1,0:T(8,128)}, f32[8,80,640]{2,1,0:T(8,128)S(1)}, u32[]{:S(2)}) copy-start(f32[8,80,640]{2,1,0:T(8,128)S(1)} %fusion.12) | copy-start | bytes 4915204
  195.4 3.1 %copy-start.1 = (f32[8,80,640]{2,1,0:T(8,128)S(1)}, f32[8,80,640]{2,1,0:T(8,128)}, u32[]{:S(2)}) copy-start(f32[8,80,640]{2,1,0:T(8,128)} %copy-done) | copy-start | bytes 4915204
  207.8 8.3 %copy-start.2 = (f32[8,80,640]{2,1,0:T(8,128)S(1)}, f32[8,80,640]{2,1,0:T(8,128)}, u32[]{:S(2)}) copy-start(f32[8,80,640]{2,1,0:T(8,128)} %reshape.138) | copy-start | bytes 4915204
  211.3 32.7 %all-to-all-start.6 = ((bf16[8,80,768]{2,1,0:T(8,128)(2,1)}), bf16[8,80,768]{2,1,0:T(8,128)(2,1)}, u32[]{:S(2)}, u32[]{:S(2)}) async-start(bf16[8,80,768]{2,1,0:T(8,128)(2,1)} %bitcast.250), calls=%async_computation.6 | async-start | bytes 1966080 | tf_op jit(solution)/shard_map/all_to_all | solution.py:28
  216.3 0.9 copy-start.3
  217.2 4.6 %collective-permute-start.14 = (bf16[4,80,640]{2,1,0:T(8,128)(2,1)S(1)}, bf16[4,80,640]{2,1,0:T(8,128)(2,1)S(1)}, u32[]{:S(2)}, u32[]{:S(2)}) collective-permute-start(bf16[4,80,640]{2,1,0:T(8,128)(2,1)S(1)} %dynamic-slice_bitcast_fusion), channel_id=1, source_target_pairs={{0,1},{1,0},{2,3},{3,2},{4,5},{5,4},{6,7},{7,6},{8,9},{9,8},{10,11... | collective-permute-start | bytes 1228808 | tf_op jit(solution)/shard_map/ppermute | solution.py:148
  222.9 10.1 %collective-permute-start.15 = (f32[80,640]{1,0:T(8,128)S(1)}, f32[80,640]{1,0:T(8,128)S(1)}, u32[]{:S(2)}, u32[]{:S(2)}) collective-permute-start(f32[80,640]{1,0:T(8,128)S(1)} %get-tuple-element.22), channel_id=1, source_target_pairs={{0,2},{2,4},{4,6},{6,0},{1,3},{3,5},{5,7},{7,1},{8,10},{10,12},{12... | collective-permute-start | bytes 614408 | tf_op jit(solution)/shard_map/ppermute | solution.py:152
  225.1 11.0 %collective-permute-start.16 = (f32[80,640]{1,0:T(8,128)S(1)}, f32[80,640]{1,0:T(8,128)S(1)}, u32[]{:S(2)}, u32[]{:S(2)}) collective-permute-start(f32[80,640]{1,0:T(8,128)S(1)} %get-tuple-element.24), channel_id=1, source_target_pairs={{0,4},{2,6},{4,0},{6,2},{1,5},{3,7},{5,1},{7,3},{8,12},{10,14},{12... | collective-permute-start | bytes 614408 | tf_op jit(solution)/shard_map/ppermute | solution.py:152
  228.8 10.2 %collective-permute-start.17 = (f32[80,640]{1,0:T(8,128)S(1)}, f32[80,640]{1,0:T(8,128)S(1)}, u32[]{:S(2)}, u32[]{:S(2)}) collective-permute-start(f32[80,640]{1,0:T(8,128)S(1)} %get-tuple-element.23), channel_id=1, source_target_pairs={{0,6},{2,0},{4,2},{6,4},{1,7},{3,1},{5,3},{7,5},{8,14},{10,8},{12,... | collective-permute-start | bytes 614408 | tf_op jit(solution)/shard_map/ppermute | solution.py:152

commit v10 on v9

--- a/solution.py
+++ b/solution.py
@@ -1,6 +1,8 @@
 import jax
 import jax.numpy as jnp
 from jax import lax
+from jax.experimental import pallas as pl
+from jax.experimental.pallas import tpu as pltpu
 from jax.sharding import Mesh, PartitionSpec as P
 
 Y, Z, X, C = 8, 8, 4, 2
@@ -44,6 +46,66 @@
     return blocks
 
 
+def start_copies(blocks, held, sems):
+    copies = [pltpu.make_async_copy(block, held.at[i], sems.at[i]) for i, block in enumerate(blocks)]
+    for copy in copies:
+        copy.start()
+    return copies
+
+
+def logits_kernel(owners, features_a, features_b, *refs):
+    n = (len(refs) - 3) // 2
+    out, held, sems = refs[2 * n:]
+    half = out.shape[1] // 2
+    copies = start_copies(refs[:2 * n], held, sems)
+    for first, features in ((0, features_a), (n, features_b)):
+        columns = pl.ds(half if first else 0, half)
+        for i in range(first, first + n):
+            copies[i].wait()
+            part = jnp.dot(features[owners[i]], held[i], preferred_element_type=jnp.float32)
+            if i == first:
+                out[:, columns] = part
+            else:
+                out[:, columns] += part
+
+
+def parts_kernel(owners, grads, *refs):
+    n = (len(refs) - 4) // 2
+    out, held, total, sems = refs[2 * n:]
+    half = grads.shape[1] // 2
+    rows = out.shape[1] // n
+    copies = start_copies(refs[:2 * n], held, sems)
+    total[...] = jnp.zeros_like(total)
+    over_cols = (((1,), (1,)), ((), ()))
+    for i in range(n):
+        copies[i].wait()
+        total[owners[i]] += lax.dot_general(
+            held[i], grads[:, :half], over_cols, preferred_element_type=jnp.float32
+        )
+    for i in range(n, 2 * n):
+        copies[i].wait()
+        part = lax.dot_general(held[i], grads[:, half:], over_cols, preferred_element_type=jnp.float32)
+        at = pl.ds(pl.multiple_of(owners[i] * rows, rows), rows)
+        for y in range(n):
+            total[y, at, :] += part[y * rows:(y + 1) * rows]
+    out[...] = total[...].astype(out.dtype)
+
+
+def over_blocks(kernel, out_shape, owners, arrays, blocks, scratch, flops):
+    smem, vmem, anywhere = (pl.BlockSpec(memory_space=space) for space in (pltpu.SMEM, pltpu.VMEM, pl.ANY))
+    held = pltpu.VMEM((len(blocks),) + blocks[0].shape, blocks[0].dtype)
+    moved = len(blocks) * blocks[0].size * 2
+    return pl.pallas_call(
+        kernel,
+        out_shape=out_shape,
+        in_specs=[smem] + [vmem] * len(arrays) + [anywhere] * len(blocks),
+        out_specs=vmem,
+        scratch_shapes=[held, *scratch, pltpu.SemaphoreType.DMA((len(blocks),))],
+        compiler_params=pltpu.CompilerParams(vmem_limit_bytes=40 * 1024 * 1024),
+        cost_estimate=pl.CostEstimate(flops=flops, bytes_accessed=moved, transcendentals=0),
+    )(owners, *arrays, *blocks)
+
+
 def per_device(hidden, head_weight, targets, kept_mask, old_logprob, advantage):
     tokens, width = hidden.shape
     rows, cols = head_weight.shape
@@ -51,19 +113,18 @@
     at_y, at_z, at_x, at_c = (lax.axis_index(name) for name in ("y", "z", "x", "c"))
     at_v = at_x * C + at_c
     offset = at_v * cols
-    across_rows = (((1,), (0,)), ((), ()))
 
     keep_float = kept_mask.astype(jnp.float32)
     count_rows = jnp.broadcast_to(jnp.sum(keep_float).astype(jnp.bfloat16), (SPARE, half))
     over_z = to_all(jnp.concatenate([head_weight[:, :half], count_rows], axis=0), "z", Z)
+    hidden_a = hidden.reshape(tokens, Y, Z * rows).transpose(1, 0, 2)
+    hidden_b = hidden.reshape(tokens, Y, Z, rows).transpose(2, 0, 1, 3).reshape(Z, tokens, Y * rows)
+    over_z, hidden_a, hidden_b = lax.optimization_barrier((over_z, hidden_a, hidden_b))
     kept_z = jnp.sum(over_z[:, rows, :128].astype(jnp.float32), axis=0)[0]
     head_of_b, _ = lax.optimization_barrier((head_weight[:, half:], over_z))
     over_y = to_all(head_of_b, "y", Y)
     blocks_a = ring(over_z[:, :rows].reshape(Z * rows, half), "y", Y)
     blocks_b = ring(over_y.reshape(Y * rows, half), "z", Z)
-
-    hidden_a = hidden.reshape(tokens, Y, Z * rows).transpose(1, 0, 2)
-    hidden_b = hidden.reshape(tokens, Y, Z, rows).transpose(2, 0, 1, 3).reshape(Z, tokens, Y * rows)
 
     slot_index = jnp.cumsum(kept_mask) - 1
     ids = jnp.arange(KEEP_MOST, dtype=jnp.int32)
@@ -82,15 +143,13 @@
     kept_share = kept_share[:, :SHARE].reshape(Y * SHARE, Z * rows)
     kept_hidden = to_all(kept_share, ("x", "c"), V).reshape(V, Y, SHARE, Z * rows)
 
-    def logits_of(features, blocks, here, n):
-        total = 0.0
-        for away, block in blocks:
-            part = lax.dynamic_index_in_dim(features, lax.rem(here + (away + n), n), 0, keepdims=False)
-            total = total + lax.dot_general(part, block, across_rows, preferred_element_type=jnp.float32)
-        return total
-
-    logits = jnp.concatenate(
-        [logits_of(hidden_a, blocks_a, at_y, Y), logits_of(hidden_b, blocks_b, at_z, Z)], axis=1
+    owners = jnp.stack(
+        [lax.rem(at_y + (away + Y), Y) for away, _ in blocks_a] + [lax.rem(at_z + (away + Z), Z) for away, _ in blocks_b]
+    ).astype(jnp.int32)
+    blocks = [block for _, block in blocks_a + blocks_b]
+    logits = over_blocks(
+        logits_kernel, jax.ShapeDtypeStruct((tokens, cols), jnp.float32), owners, [hidden_a, hidden_b], blocks, [],
+        2 * tokens * width * cols,
     )
     logits, kept_hidden, scale = lax.optimization_barrier((logits, kept_hidden, scale))
     local_target = targets - offset
@@ -120,19 +179,10 @@
 
     all_slots = to_all(compact, "y", Y)
 
-    def through(grads, blocks, here, n, dtype):
-        parts = jnp.zeros((n, KEEP_MOST, width // n), dtype)
-        for away, block in blocks:
-            part = lax.dot_general(grads, block, (((1,), (1,)), ((), ())), preferred_element_type=jnp.float32)
-            parts = lax.dynamic_update_slice(
-                parts, part.astype(dtype)[None], (lax.rem(here + (away + n), n), 0, 0)
-            )
-        return parts
-
-    parts_a = through(compact[:, :half], blocks_a, at_y, Y, jnp.float32)
-    parts_b = through(compact[:, half:], blocks_b, at_z, Z, jnp.bfloat16)
-    parts_b = parts_b.reshape(Z, KEEP_MOST, Y, rows).transpose(2, 1, 0, 3).reshape(Y, KEEP_MOST, Z * rows)
-    hidden_part = (parts_a + parts_b.astype(jnp.float32)).astype(jnp.bfloat16)
+    hidden_part = over_blocks(
+        parts_kernel, jax.ShapeDtypeStruct((Y, Z * rows, KEEP_MOST), jnp.bfloat16), owners, [compact], blocks,
+        [pltpu.VMEM((Y, Z * rows, KEEP_MOST), jnp.float32)], 2 * KEEP_MOST * width * cols,
+    )
 
     kept_hidden = kept_hidden.transpose(1, 0, 2, 3).reshape(Y * KEEP_MOST, Z * rows)
     part_head = lax.dot_general(
@@ -142,7 +192,7 @@
     sums = exchange(part_head.reshape(Z, rows, cols), "z")
     grad_head = jnp.sum(scale * sums.astype(jnp.float32), axis=0)
 
-    hidden_part = hidden_part.reshape(X, C, KEEP_MOST, Z * rows)
+    hidden_part = hidden_part.reshape(X, C, Z * rows, KEEP_MOST)
     mine = lax.dynamic_index_in_dim(hidden_part, at_c, 1, keepdims=False)
     other = lax.dynamic_index_in_dim(hidden_part, 1 - at_c, 1, keepdims=False)
     pair = mine.astype(jnp.float32) + lax.ppermute(other, "c", [(0, 1), (1, 0)]).astype(jnp.float32)
@@ -153,8 +203,8 @@
     upper = total.astype(jnp.bfloat16)
     under = (total - upper.astype(jnp.float32)).astype(jnp.bfloat16)
     grad_hidden = scale * lax.dot_general(
-        jnp.concatenate([selector, selector]), jnp.concatenate([upper, under]),
-        (((0,), (0,)), ((), ())), preferred_element_type=jnp.float32,
+        jnp.concatenate([selector, selector]), jnp.concatenate([upper, under], axis=1),
+        (((0,), (1,)), ((), ())), preferred_element_type=jnp.float32,
     )
     return (entropy, grad_hidden, grad_head)
 

time: 249 us -> 230 us (0.924)
  the two profiles are of different devices: /device:TPU:1 before, /device:TPU:6 now
where the time goes in v10:
time: 230 us; the launch traced here: 225 us
  starting transfers between devices  101 us (44%)
  waiting for transfers between devices  55.1 us (24%)
  local copies, waits for them, and re-layouts  33.1 us (14%)
  Pallas kernels  13.9 us (6%)
  blocking collectives  7.98 us (3%)
  matrix products  7.01 us (3%)
  other arithmetic  4.89 us (2%)
  between operations  2.56 us (1%)
    all_to_all x6, waiting for transfers between devices, exchange(): return lax.all_to_all(parts, axes, split_axis=0, concat_axis=0)  43.3 us
    all_to_all x6, starting transfers between devices, exchange(): return lax.all_to_all(parts, axes, split_axis=0, concat_axis=0)  39.9 us
    ppermute x8, starting transfers between devices, ring(): down = lax.ppermute(down, axis, [(i, (i - 1) % n) for i in range(n)])  31.7 us
    ppermute x6, starting transfers between devices, ring(): up = lax.ppermute(up, axis, [(i, (i + 1) % n) for i in range(n)])  16.8 us
    pallas_call x2, Pallas kernels, over_blocks(): pl.pallas_call(kernel, out_shape=out_shape, in_specs=[smem] + [vmem] * le...  13.9 us
    ppermute x3, starting transfers between devices, per_device(): lax.ppermute(sent, 'x', [(i, (i + step) % X) for i in range(X)])  10.4 us
    unnamed x28, local copies, waits for them, and re-layouts  9.36 us
    all_to_all x1, blocking collectives, exchange(): return lax.all_to_all(parts, axes, split_axis=0, concat_axis=0)  7.98 us
  transfers between devices with their start and end apart: 24, of which 10 were waited for; matrix products, arithmetic and copies ran while one was open for 13% of the time, Pallas kernels for 3%

profile of v10, /device:TPU:6, one launch (start us, length us, event | category | flops | bytes accessed | tf_op | source)
XLA Modules:
  0.0 225.4 jit_solution(9788984823422237892)
XLA Ops:
  0.6 0.9 fusion.29
  1.5 1.3 convert_reduce_fusion.2
  2.8 0.7 concatenate.12
  3.5 0.9 broadcast_in_dim.36
  4.3 10.3 %all-to-all-start = ((bf16[8,96,384]{2,1,0:T(8,128)(2,1)}), bf16[8,96,384]{2,1,0:T(8,128)(2,1)S(1)}, u32[]{:S(2)}, u32[]{:S(2)}) async-start(bf16[8,96,384]{2,1,0:T(8,128)(2,1)} %broadcast_in_dim.36), calls=%async_computation | async-start | bytes 1179648 | tf_op jit(solution)/shard_map/all_to_all | solution.py:30
  14.6 4.4 %copy.43 = bf16[256,5120]{0,1:T(8,128)(2,1)} copy(bf16[256,5120]{1,0:T(8,128)(2,1)} %param.6) | data formatting | bytes 5242880 | tf_op args[0]
  19.0 3.1 %copy.44 = bf16[256,8,640]{2,0,1:T(8,128)(2,1)S(1)} copy(bf16[256,8,640]{0,2,1:T(8,128)(2,1)} %bitcast.92) | data formatting | bytes 5242880 | tf_op jit(solution)/shard_map/reshape | solution.py:120
  22.2 3.5 %copy.46 = bf16[8,256,8,80]{1,3,2,0:T(8,128)(2,1)} copy(bf16[8,256,8,80]{1,3,0,2:T(8,128)(2,1)} %bitcast.93) | data formatting | bytes 5242880 | tf_op jit(solution)/shard_map/transpose | solution.py:121
  25.7 7.8 %all-to-all-done = bf16[8,96,384]{2,1,0:T(8,128)(2,1)S(1)} async-done(((bf16[8,96,384]{2,1,0:T(8,128)(2,1)}), bf16[8,96,384]{2,1,0:T(8,128)(2,1)S(1)}, u32[]{:S(2)}, u32[]{:S(2)}) %all-to-all-start) | async-done | bytes 589856 | tf_op jit(solution)/shard_map/all_to_all | solution.py:30
  33.5 0.9 broadcast_in_dim.37
  34.5 7.1 %all-to-all-start.1 = ((bf16[8,80,384]{2,1,0:T(8,128)(2,1)}), bf16[8,80,384]{2,1,0:T(8,128)(2,1)S(1)}, u32[]{:S(2)}, u32[]{:S(2)}) async-start(bf16[8,80,384]{2,1,0:T(8,128)(2,1)} %broadcast_in_dim.37), calls=%async_computation.1 | async-start | bytes 983040 | tf_op jit(solution)/shard_map/all_to_all | solution.py:30
  42.2 1.9 slice.47
  44.0 5.1 %collective-permute-start = (bf16[640,384]{1,0:T(8,128)(2,1)}, bf16[640,384]{1,0:T(8,128)(2,1)}, u32[]{:S(2)}, u32[]{:S(2)}) collective-permute-start(bf16[640,384]{1,0:T(8,128)(2,1)} %bitcast.21.refs_0_), channel_id=1, source_target_pairs={{0,448},{64,0},{128,64},{192,128},{256,192},{320,256},{384,320},{4... | collective-permute-start | bytes 1474568 | tf_op jit(solution)/shard_map/ppermute | solution.py:41
  49.2 9.4 %all-to-all-done.1 = bf16[8,80,384]{2,1,0:T(8,128)(2,1)S(1)} async-done(((bf16[8,80,384]{2,1,0:T(8,128)(2,1)}), bf16[8,80,384]{2,1,0:T(8,128)(2,1)S(1)}, u32[]{:S(2)}, u32[]{:S(2)}) %all-to-all-start.1) | async-done | bytes 491552 | tf_op jit(solution)/shard_map/all_to_all | solution.py:30
  58.6 1.9 collective-permute-start.7
  60.6 3.6 %collective-permute-start.1 = (bf16[640,384]{1,0:T(8,128)(2,1)}, bf16[640,384]{1,0:T(8,128)(2,1)}, u32[]{:S(2)}, u32[]{:S(2)}) collective-permute-start(bf16[640,384]{1,0:T(8,128)(2,1)} %bitcast.21.refs_0_), channel_id=1, source_target_pairs={{0,64},{64,128},{128,192},{192,256},{256,320},{320,384},{384,448},... | collective-permute-start | bytes 1474568 | tf_op jit(solution)/shard_map/ppermute | solution.py:44
  64.2 1.1 collective-permute-done.refs_1_
  65.3 3.5 %collective-permute-start.2 = (bf16[640,384]{1,0:T(8,128)(2,1)}, bf16[640,384]{1,0:T(8,128)(2,1)}, u32[]{:S(2)}, u32[]{:S(2)}) collective-permute-start(bf16[640,384]{1,0:T(8,128)(2,1)} %collective-permute-done.refs_1_), channel_id=1, source_target_pairs={{0,448},{64,0},{128,64},{192,128},{256,192},{320,256},{384,320},{4... | collective-permute-start | bytes 1474568 | tf_op jit(solution)/shard_map/ppermute | solution.py:41
  68.8 2.8 %collective-permute-start.8 = (bf16[640,384]{1,0:T(8,128)(2,1)S(1)}, bf16[640,384]{1,0:T(8,128)(2,1)}, u32[]{:S(2)}, u32[]{:S(2)}) collective-permute-start(bf16[640,384]{1,0:T(8,128)(2,1)S(1)} %bitcast.89), channel_id=1, source_target_pairs={{0,8},{8,16},{16,24},{24,32},{32,40},{40,48},{48,56},{56,0},{1,9},... | collective-permute-start | bytes 1474568 | tf_op jit(solution)/shard_map/ppermute | solution.py:44
  71.6 2.1 collective-permute-done.7.refs_9_
  73.7 3.4 %collective-permute-start.9 = (bf16[640,384]{1,0:T(8,128)(2,1)}, bf16[640,384]{1,0:T(8,128)(2,1)}, u32[]{:S(2)}, u32[]{:S(2)}) collective-permute-start(bf16[640,384]{1,0:T(8,128)(2,1)} %collective-permute-done.7.refs_9_), channel_id=1, source_target_pairs={{0,56},{8,0},{16,8},{24,16},{32,24},{40,32},{48,40},{56,48},{1,57}... | collective-permute-start | bytes 1474568 | tf_op jit(solution)/shard_map/ppermute | solution.py:41
  77.1 0.7 convert_reduce_fusion.1
  78.0 2.2 fusion
  80.2 0.7 copy.77
  80.9 5.6 %all-to-all-start.2 = ((bf16[8,16,640]{2,1,0:T(8,128)(2,1)}), bf16[8,16,640]{2,1,0:T(8,128)(2,1)S(1)}, u32[]{:S(2)}, u32[]{:S(2)}) async-start(bf16[8,16,640]{2,1,0:T(8,128)(2,1)} %bitcast.83), calls=%async_computation.2 | async-start | bytes 327680 | tf_op jit(solution)/shard_map/all_to_all | solution.py:30
  86.5 3.9 %collective-permute-start.3 = (bf16[640,384]{1,0:T(8,128)(2,1)}, bf16[640,384]{1,0:T(8,128)(2,1)}, u32[]{:S(2)}, u32[]{:S(2)}) collective-permute-start(bf16[640,384]{1,0:T(8,128)(2,1)} %collective-permute-done.1.refs_2_), channel_id=1, source_target_pairs={{0,64},{64,128},{128,192},{192,256},{256,320},{320,384},{384,448},... | collective-permute-start | bytes 1474568 | tf_op jit(solution)/shard_map/ppermute | solution.py:44
  90.5 3.1 %collective-permute-start.4 = (bf16[640,384]{1,0:T(8,128)(2,1)}, bf16[640,384]{1,0:T(8,128)(2,1)}, u32[]{:S(2)}, u32[]{:S(2)}) collective-permute-start(bf16[640,384]{1,0:T(8,128)(2,1)} %collective-permute-done.2.refs_3_), channel_id=1, source_target_pairs={{0,448},{64,0},{128,64},{192,128},{256,192},{320,256},{384,320},{4... | collective-permute-start | bytes 1474568 | tf_op jit(solution)/shard_map/ppermute | solution.py:41
  93.6 1.9 collective-permute-start.10
  95.5 5.1 %collective-permute-start.11 = (bf16[640,384]{1,0:T(8,128)(2,1)}, bf16[640,384]{1,0:T(8,128)(2,1)}, u32[]{:S(2)}, u32[]{:S(2)}) collective-permute-start(bf16[640,384]{1,0:T(8,128)(2,1)} %collective-permute-done.9.refs_11_), channel_id=1, source_target_pairs={{0,56},{8,0},{16,8},{24,16},{32,24},{40,32},{48,40},{56,48},{1,57}... | collective-permute-start | bytes 1474568 | tf_op jit(solution)/shard_map/ppermute | solution.py:41
  100.8 1.0 broadcast_in_dim.43
  101.7 4.8 %all-to-all-start.3 = ((bf16[8,80,640]{2,1,0:T(8,128)(2,1)}), bf16[8,80,640]{2,1,0:T(8,128)(2,1)}, u32[]{:S(2)}, u32[]{:S(2)}) async-start(bf16[8,80,640]{2,1,0:T(8,128)(2,1)} %broadcast_in_dim.43), calls=%async_computation.3 | async-start | bytes 1638400 | tf_op jit(solution)/shard_map/all_to_all | solution.py:30
  106.5 2.7 %collective-permute-start.5 = (bf16[640,384]{1,0:T(8,128)(2,1)}, bf16[640,384]{1,0:T(8,128)(2,1)S(1)}, u32[]{:S(2)}, u32[]{:S(2)}) collective-permute-start(bf16[640,384]{1,0:T(8,128)(2,1)} %collective-permute-done.3.refs_4_), channel_id=1, source_target_pairs={{0,64},{64,128},{128,192},{192,256},{256,320},{320,384},{384,448},... | collective-permute-start | bytes 1474568 | tf_op jit(solution)/shard_map/ppermute | solution.py:44
  109.2 4.3 %collective-permute-start.6 = (bf16[640,384]{1,0:T(8,128)(2,1)}, bf16[640,384]{1,0:T(8,128)(2,1)}, u32[]{:S(2)}, u32[]{:S(2)}) collective-permute-start(bf16[640,384]{1,0:T(8,128)(2,1)} %collective-permute-done.4.refs_5_), channel_id=1, source_target_pairs={{0,448},{64,0},{128,64},{192,128},{256,192},{320,256},{384,320},{4... | collective-permute-start | bytes 1474568 | tf_op jit(solution)/shard_map/ppermute | solution.py:41
  113.6 1.9 collective-permute-start.12
  115.5 5.1 %collective-permute-start.13 = (bf16[640,384]{1,0:T(8,128)(2,1)}, bf16[640,384]{1,0:T(8,128)(2,1)}, u32[]{:S(2)}, u32[]{:S(2)}) collective-permute-start(bf16[640,384]{1,0:T(8,128)(2,1)} %collective-permute-done.11.refs_13_), channel_id=1, source_target_pairs={{0,56},{8,0},{16,8},{24,16},{32,24},{40,32},{48,40},{56,48},{1,57}... | collective-permute-start | bytes 1474568 | tf_op jit(solution)/shard_map/ppermute | solution.py:41
  120.8 4.4 %copy.47.features_b = bf16[8,256,640]{2,1,0:T(8,128)(2,1)} copy(bf16[8,256,640]{1,2,0:T(8,128)(2,1)} %bitcast.94) | data formatting | bytes 5242880 | tf_op jit(solution)/shard_map/optimization_barrier | solution.py:122
  125.3 0.6 fusion.31
  127.3 2.2 copy.49
  129.5 0.8 copy-done.4
  130.3 0.6 collective-permute-done.13.refs_15_
  130.9 1.7 copy-done
  132.7 1.0 copy-done.2
  133.7 1.0 copy-done.5
  134.7 6.8 %shard_map.85 = f32[256,768]{1,0:T(8,128)S(1)} custom-call(s32[16]{0:T(128)S(1)} %stack.82.owners, bf16[8,256,640]{2,1,0:T(8,128)(2,1)S(1)} %bitcast.86, bf16[8,256,640]{2,1,0:T(8,128)(2,1)S(1)} %copy-done, bf16[640,384]{1,0:T(8,128)(2,1)} %bitcast.21.refs_0_, bf16[640,384]{1,0:T(8,128)(2,1)} %collective-permute-done.refs_1_, ...), custom_call_target="tpu_custom_call" | custom-call | flops 2013265920 | bytes 7864320 | tf_op jit(solution)/shard_map/pallas_call | solution.py:98
  141.6 0.4 exponential_reduce_fusion
  142.1 8.0 %all_to_all.35 = f32[8,4,256]{2,1,0:T(4,128)S(1)} all-to-all(f32[8,4,256]{2,1,0:T(4,128)S(1)} %broadcast_in_dim.44), channel_id=1, replica_groups=mesh['y'=8,'z'=8,'x'=4,'c'=2] {'x','c'}, dimensions={0} | all-to-all | bytes 65536 | tf_op jit(solution)/shard_map/all_to_all | solution.py:30
  150.2 0.6 fusion.25
  150.7 0.4 convolution_convert_fusion.1.grads
  151.2 1.0 broadcast_in_dim.45
  152.2 7.2 %all-to-all-start.5 = ((bf16[8,80,768]{2,1,0:T(8,128)(2,1)}), bf16[8,80,768]{2,1,0:T(8,128)(2,1)S(1)}, u32[]{:S(2)}, u32[]{:S(2)}) async-start(bf16[8,80,768]{2,1,0:T(8,128)(2,1)} %broadcast_in_dim.45), calls=%async_computation.5 | async-start | bytes 1966080 | tf_op jit(solution)/shard_map/all_to_all | solution.py:30
  159.6 1.1 reshape.113
  160.7 26.0 %all-to-all-done.5 = bf16[8,80,768]{2,1,0:T(8,128)(2,1)S(1)} async-done(((bf16[8,80,768]{2,1,0:T(8,128)(2,1)}), bf16[8,80,768]{2,1,0:T(8,128)(2,1)S(1)}, u32[]{:S(2)}, u32[]{:S(2)}) %all-to-all-start.5) | async-done | bytes 983072 | tf_op jit(solution)/shard_map/all_to_all | solution.py:30
  186.7 3.2 %convolution_convert_fusion = bf16[640,768]{1,0:T(8,128)(2,1)} fusion(bf16[640,640]{1,0:T(8,128)(2,1)} %reshape.113, bf16[640,768]{1,0:T(8,128)(2,1)S(1)} %bitcast.96), kind=kOutput, calls=%fused_computation.3 | convolution fusion | flops 629637120 | bytes 2785280 | tf_op jit(solution)/shard_map/dot_general | solution.py:188
  189.8 5.0 %all-to-all-start.6 = ((bf16[8,80,768]{2,1,0:T(8,128)(2,1)}), bf16[8,80,768]{2,1,0:T(8,128)(2,1)S(1)}, u32[]{:S(2)}, u32[]{:S(2)}) async-start(bf16[8,80,768]{2,1,0:T(8,128)(2,1)} %bitcast.44), calls=%async_computation.6 | async-start | bytes 1966080 | tf_op jit(solution)/shard_map/all_to_all | solution.py:30
  194.8 7.2 %shard_map.86 = bf16[8,640,80]{2,1,0:T(8,128)(2,1)S(1)} custom-call(s32[16]{0:T(128)S(1)} %stack.82.owners, bf16[80,768]{1,0:T(8,128)(2,1)S(1)} %convolution_convert_fusion.1.grads, bf16[640,384]{1,0:T(8,128)(2,1)} %bitcast.21.refs_0_, bf16[640,384]{1,0:T(8,128)(2,1)} %collective-permute-done.refs_1_, bf16[640,384]{1,0:T(8,128)(2,1)} %collective-permute-done.1.refs_2_, ...), custom_call_target="tpu_custom_call" | custom-call | flops 629145600 | bytes 7864320 | tf_op jit(solution)/shard_map/pallas_call | solution.py:98
  202.4 1.9 collective-permute-start.14
  204.6 1.4 collective-permute-done.14
  206.2 2.4 %collective-permute-start.17 = (f32[640,80]{0,1:T(8,128)S(1)}, f32[640,80]{0,1:T(8,128)S(1)}, u32[]{:S(2)}, u32[]{:S(2)}) collective-permute-start(f32[640,80]{0,1:T(8,128)S(1)} %get-tuple-element.31), channel_id=1, source_target_pairs={{0,6},{2,0},{4,2},{6,4},{1,7},{3,1},{5,3},{7,5},{8,14},{10,8},{12,... | collective-permute-start | bytes 614408 | tf_op jit(solution)/shard_map/ppermute | solution.py:202
  208.6 5.0 %collective-permute-start.16 = (f32[640,80]{0,1:T(8,128)S(1)}, f32[640,80]{0,1:T(8,128)S(1)}, u32[]{:S(2)}, u32[]{:S(2)}) collective-permute-start(f32[640,80]{0,1:T(8,128)S(1)} %get-tuple-element.32), channel_id=1, source_target_pairs={{0,4},{2,6},{4,0},{6,2},{1,5},{3,7},{5,1},{7,3},{8,12},{10,14},{12... | collective-permute-start | bytes 614408 | tf_op jit(solution)/shard_map/ppermute | solution.py:202
  213.5 3.1 %collective-permute-start.15 = (f32[640,80]{0,1:T(8,128)S(1)}, f32[640,80]{0,1:T(8,128)S(1)}, u32[]{:S(2)}, u32[]{:S(2)}) collective-permute-start(f32[640,80]{0,1:T(8,128)S(1)} %get-tuple-element.30), channel_id=1, source_target_pairs={{0,2},{2,4},{4,6},{6,0},{1,3},{3,5},{5,7},{7,1},{8,10},{10,12},{12... | collective-permute-start | bytes 614408 | tf_op jit(solution)/shard_map/ppermute | solution.py:202
  216.9 4.2 %collective-permute-done.16 = f32[640,80]{0,1:T(8,128)S(1)} collective-permute-done((f32[640,80]{0,1:T(8,128)S(1)}, f32[640,80]{0,1:T(8,128)S(1)}, u32[]{:S(2)}, u32[]{:S(2)}) %collective-permute-start.16) | collective-permute-done | bytes 204832 | tf_op jit(solution)/shard_map/ppermute | solution.py:202
  221.1 2.2 collective-permute-done.15
  223.3 1.2 broadcast_multiply_fusion
  224.5 0.9 multiply_reduce_fusion
  (63 shorter events, 2.6 us)
Async XLA Ops:
  4.3 29.2 %all-to-all-start = ((bf16[8,96,384]{2,1,0:T(8,128)(2,1)}), bf16[8,96,384]{2,1,0:T(8,128)(2,1)S(1)}, u32[]{:S(2)}, u32[]{:S(2)}) async-start(bf16[8,96,384]{2,1,0:T(8,128)(2,1)} %broadcast_in_dim.36), calls=%async_computation | async-start | bytes 1179648 | tf_op jit(solution)/shard_map/all_to_all | solution.py:30
  22.2 19.4 %copy-start.9 = (s32[256]{0:T(256)S(1)}, s32[256]{0:T(256)}, u32[]{:S(2)}) copy-start(s32[256]{0:T(256)} %param.9) | copy-start | bytes 3076
  33.5 1.0 copy-start.8
  34.5 24.1 %all-to-all-start.1 = ((bf16[8,80,384]{2,1,0:T(8,128)(2,1)}), bf16[8,80,384]{2,1,0:T(8,128)(2,1)S(1)}, u32[]{:S(2)}, u32[]{:S(2)}) async-start(bf16[8,80,384]{2,1,0:T(8,128)(2,1)} %broadcast_in_dim.37), calls=%async_computation.1 | async-start | bytes 983040 | tf_op jit(solution)/shard_map/all_to_all | solution.py:30
  44.0 21.3 %collective-permute-start = (bf16[640,384]{1,0:T(8,128)(2,1)}, bf16[640,384]{1,0:T(8,128)(2,1)}, u32[]{:S(2)}, u32[]{:S(2)}) collective-permute-start(bf16[640,384]{1,0:T(8,128)(2,1)} %bitcast.21.refs_0_), channel_id=1, source_target_pairs={{0,448},{64,0},{128,64},{192,128},{256,192},{320,256},{384,320},{4... | collective-permute-start | bytes 1474568 | tf_op jit(solution)/shard_map/ppermute | solution.py:41
  58.6 43.1 %copy-start.1 = (bf16[8,80,384]{2,1,0:T(8,128)(2,1)}, bf16[8,80,384]{2,1,0:T(8,128)(2,1)S(1)}, u32[]{:S(2)}) copy-start(bf16[8,80,384]{2,1,0:T(8,128)(2,1)S(1)} %all-to-all-done.1) | copy-start | bytes 1474564
  58.6 15.1 %collective-permute-start.7 = (bf16[640,384]{1,0:T(8,128)(2,1)S(1)}, bf16[640,384]{1,0:T(8,128)(2,1)}, u32[]{:S(2)}, u32[]{:S(2)}) collective-permute-start(bf16[640,384]{1,0:T(8,128)(2,1)S(1)} %bitcast.88), channel_id=1, source_target_pairs={{0,56},{8,0},{16,8},{24,16},{32,24},{40,32},{48,40},{56,48},{1,57}... | collective-permute-start | bytes 1474568 | tf_op jit(solution)/shard_map/ppermute | solution.py:41
  60.6 25.9 %collective-permute-start.1 = (bf16[640,384]{1,0:T(8,128)(2,1)}, bf16[640,384]{1,0:T(8,128)(2,1)}, u32[]{:S(2)}, u32[]{:S(2)}) collective-permute-start(bf16[640,384]{1,0:T(8,128)(2,1)} %bitcast.21.refs_0_), channel_id=1, source_target_pairs={{0,64},{64,128},{128,192},{192,256},{256,320},{320,384},{384,448},... | collective-permute-start | bytes 1474568 | tf_op jit(solution)/shard_map/ppermute | solution.py:44
  65.3 25.1 %collective-permute-start.2 = (bf16[640,384]{1,0:T(8,128)(2,1)}, bf16[640,384]{1,0:T(8,128)(2,1)}, u32[]{:S(2)}, u32[]{:S(2)}) collective-permute-start(bf16[640,384]{1,0:T(8,128)(2,1)} %collective-permute-done.refs_1_), channel_id=1, source_target_pairs={{0,448},{64,0},{128,64},{192,128},{256,192},{320,256},{384,320},{4... | collective-permute-start | bytes 1474568 | tf_op jit(solution)/shard_map/ppermute | solution.py:41
  68.8 24.8 %collective-permute-start.8 = (bf16[640,384]{1,0:T(8,128)(2,1)S(1)}, bf16[640,384]{1,0:T(8,128)(2,1)}, u32[]{:S(2)}, u32[]{:S(2)}) collective-permute-start(bf16[640,384]{1,0:T(8,128)(2,1)S(1)} %bitcast.89), channel_id=1, source_target_pairs={{0,8},{8,16},{16,24},{24,32},{32,40},{40,48},{48,56},{56,0},{1,9},... | collective-permute-start | bytes 1474568 | tf_op jit(solution)/shard_map/ppermute | solution.py:44
  73.7 21.8 %collective-permute-start.9 = (bf16[640,384]{1,0:T(8,128)(2,1)}, bf16[640,384]{1,0:T(8,128)(2,1)}, u32[]{:S(2)}, u32[]{:S(2)}) collective-permute-start(bf16[640,384]{1,0:T(8,128)(2,1)} %collective-permute-done.7.refs_9_), channel_id=1, source_target_pairs={{0,56},{8,0},{16,8},{24,16},{32,24},{40,32},{48,40},{56,48},{1,57}... | collective-permute-start | bytes 1474568 | tf_op jit(solution)/shard_map/ppermute | solution.py:41
  78.0 42.8 %copy-start.12 = (s32[256]{0:T(256)S(1)}, s32[256]{0:T(256)}, u32[]{:S(2)}) copy-start(s32[256]{0:T(256)} %param.8) | copy-start | bytes 3076
  80.9 19.8 %all-to-all-start.2 = ((bf16[8,16,640]{2,1,0:T(8,128)(2,1)}), bf16[8,16,640]{2,1,0:T(8,128)(2,1)S(1)}, u32[]{:S(2)}, u32[]{:S(2)}) async-start(bf16[8,16,640]{2,1,0:T(8,128)(2,1)} %bitcast.83), calls=%async_computation.2 | async-start | bytes 327680 | tf_op jit(solution)/shard_map/all_to_all | solution.py:30
  86.5 20.0 %collective-permute-start.3 = (bf16[640,384]{1,0:T(8,128)(2,1)}, bf16[640,384]{1,0:T(8,128)(2,1)}, u32[]{:S(2)}, u32[]{:S(2)}) collective-permute-start(bf16[640,384]{1,0:T(8,128)(2,1)} %collective-permute-done.1.refs_2_), channel_id=1, source_target_pairs={{0,64},{64,128},{128,192},{192,256},{256,320},{320,384},{384,448},... | collective-permute-start | bytes 1474568 | tf_op jit(solution)/shard_map/ppermute | solution.py:44
  90.5 18.8 %collective-permute-start.4 = (bf16[640,384]{1,0:T(8,128)(2,1)}, bf16[640,384]{1,0:T(8,128)(2,1)}, u32[]{:S(2)}, u32[]{:S(2)}) collective-permute-start(bf16[640,384]{1,0:T(8,128)(2,1)} %collective-permute-done.2.refs_3_), channel_id=1, source_target_pairs={{0,448},{64,0},{128,64},{192,128},{256,192},{320,256},{384,320},{4... | collective-permute-start | bytes 1474568 | tf_op jit(solution)/shard_map/ppermute | solution.py:41
  93.6 20.0 %collective-permute-start.10 = (bf16[640,384]{1,0:T(8,128)(2,1)}, bf16[640,384]{1,0:T(8,128)(2,1)}, u32[]{:S(2)}, u32[]{:S(2)}) collective-permute-start(bf16[640,384]{1,0:T(8,128)(2,1)} %collective-permute-done.8.refs_10_), channel_id=1, source_target_pairs={{0,8},{8,16},{16,24},{24,32},{32,40},{40,48},{48,56},{56,0},{1,9},... | collective-permute-start | bytes 1474568 | tf_op jit(solution)/shard_map/ppermute | solution.py:44
  95.5 20.0 %collective-permute-start.11 = (bf16[640,384]{1,0:T(8,128)(2,1)}, bf16[640,384]{1,0:T(8,128)(2,1)}, u32[]{:S(2)}, u32[]{:S(2)}) collective-permute-start(bf16[640,384]{1,0:T(8,128)(2,1)} %collective-permute-done.9.refs_11_), channel_id=1, source_target_pairs={{0,56},{8,0},{16,8},{24,16},{32,24},{40,32},{48,40},{56,48},{1,57}... | collective-permute-start | bytes 1474568 | tf_op jit(solution)/shard_map/ppermute | solution.py:41
  101.7 25.5 %all-to-all-start.3 = ((bf16[8,80,640]{2,1,0:T(8,128)(2,1)}), bf16[8,80,640]{2,1,0:T(8,128)(2,1)}, u32[]{:S(2)}, u32[]{:S(2)}) async-start(bf16[8,80,640]{2,1,0:T(8,128)(2,1)} %broadcast_in_dim.43), calls=%async_computation.3 | async-start | bytes 1638400 | tf_op jit(solution)/shard_map/all_to_all | solution.py:30
  106.5 23.0 %collective-permute-start.5 = (bf16[640,384]{1,0:T(8,128)(2,1)}, bf16[640,384]{1,0:T(8,128)(2,1)S(1)}, u32[]{:S(2)}, u32[]{:S(2)}) collective-permute-start(bf16[640,384]{1,0:T(8,128)(2,1)} %collective-permute-done.3.refs_4_), channel_id=1, source_target_pairs={{0,64},{64,128},{128,192},{192,256},{256,320},{320,384},{384,448},... | collective-permute-start | bytes 1474568 | tf_op jit(solution)/shard_map/ppermute | solution.py:44
  109.2 21.1 %collective-permute-start.6 = (bf16[640,384]{1,0:T(8,128)(2,1)}, bf16[640,384]{1,0:T(8,128)(2,1)}, u32[]{:S(2)}, u32[]{:S(2)}) collective-permute-start(bf16[640,384]{1,0:T(8,128)(2,1)} %collective-permute-done.4.refs_5_), channel_id=1, source_target_pairs={{0,448},{64,0},{128,64},{192,128},{256,192},{320,256},{384,320},{4... | collective-permute-start | bytes 1474568 | tf_op jit(solution)/shard_map/ppermute | solution.py:41
  113.6 16.7 %collective-permute-start.12 = (bf16[640,384]{1,0:T(8,128)(2,1)}, bf16[640,384]{1,0:T(8,128)(2,1)}, u32[]{:S(2)}, u32[]{:S(2)}) collective-permute-start(bf16[640,384]{1,0:T(8,128)(2,1)} %collective-permute-done.10.refs_12_), channel_id=1, source_target_pairs={{0,8},{8,16},{16,24},{24,32},{32,40},{40,48},{48,56},{56,0},{1,9},... | collective-permute-start | bytes 1474568 | tf_op jit(solution)/shard_map/ppermute | solution.py:44
  115.5 15.4 %collective-permute-start.13 = (bf16[640,384]{1,0:T(8,128)(2,1)}, bf16[640,384]{1,0:T(8,128)(2,1)}, u32[]{:S(2)}, u32[]{:S(2)}) collective-permute-start(bf16[640,384]{1,0:T(8,128)(2,1)} %collective-permute-done.11.refs_13_), channel_id=1, source_target_pairs={{0,56},{8,0},{16,8},{24,16},{32,24},{40,32},{48,40},{56,48},{1,57}... | collective-permute-start | bytes 1474568 | tf_op jit(solution)/shard_map/ppermute | solution.py:41
  127.3 22.9 %copy-start.10 = (f32[256]{0:T(256)S(1)}, f32[256]{0:T(256)}, u32[]{:S(2)}) copy-start(f32[256]{0:T(256)} %param.11) | copy-start | bytes 3076
  127.3 22.9 %copy-start.11 = (f32[256]{0:T(256)S(1)}, f32[256]{0:T(256)}, u32[]{:S(2)}) copy-start(f32[256]{0:T(256)} %param.10) | copy-start | bytes 3076
  129.5 0.8 copy-start.4
  130.9 1.7 copy-start
  132.7 1.0 copy-start.2
  133.7 1.0 copy-start.5
  150.7 8.7 %copy-start.7 = (bf16[8,80,640]{2,0,1:T(8,128)(2,1)S(1)}, bf16[8,80,640]{2,0,1:T(8,128)(2,1)}, u32[]{:S(2)}) copy-start(bf16[8,80,640]{2,0,1:T(8,128)(2,1)} %copy.49) | copy-start | bytes 2457604
  152.2 34.5 %all-to-all-start.5 = ((bf16[8,80,768]{2,1,0:T(8,128)(2,1)}), bf16[8,80,768]{2,1,0:T(8,128)(2,1)S(1)}, u32[]{:S(2)}, u32[]{:S(2)}) async-start(bf16[8,80,768]{2,1,0:T(8,128)(2,1)} %broadcast_in_dim.45), calls=%async_computation.5 | async-start | bytes 1966080 | tf_op jit(solution)/shard_map/all_to_all | solution.py:30
  186.7 8.1 %copy-start.3 = (bf16[8,80,384]{2,1,0:T(8,128)(2,1)S(1)}, bf16[8,80,384]{2,1,0:T(8,128)(2,1)}, u32[]{:S(2)}) copy-start(bf16[8,80,384]{2,1,0:T(8,128)(2,1)} %copy-done.1) | copy-start | bytes 1474564
  186.7 8.1 %copy-start.6 = (bf16[640,384]{1,0:T(8,128)(2,1)S(1)}, bf16[640,384]{1,0:T(8,128)(2,1)}, u32[]{:S(2)}) copy-start(bf16[640,384]{1,0:T(8,128)(2,1)} %copy-done.4) | copy-start | bytes 1474564
  189.8 34.7 %all-to-all-start.6 = ((bf16[8,80,768]{2,1,0:T(8,128)(2,1)}), bf16[8,80,768]{2,1,0:T(8,128)(2,1)S(1)}, u32[]{:S(2)}, u32[]{:S(2)}) async-start(bf16[8,80,768]{2,1,0:T(8,128)(2,1)} %bitcast.44), calls=%async_computation.6 | async-start | bytes 1966080 | tf_op jit(solution)/shard_map/all_to_all | solution.py:30
  202.4 3.6 %collective-permute-start.14 = (bf16[4,640,80]{1,2,0:T(8,128)(2,1)S(1)}, bf16[4,640,80]{1,2,0:T(8,128)(2,1)S(1)}, u32[]{:S(2)}, u32[]{:S(2)}) collective-permute-start(bf16[4,640,80]{1,2,0:T(8,128)(2,1)S(1)} %bitcast.99), channel_id=1, source_target_pairs={{0,1},{1,0},{2,3},{3,2},{4,5},{5,4},{6,7},{7,6},{8,9},{9,8},{10,11... | collective-permute-start | bytes 1228808 | tf_op jit(solution)/shard_map/ppermute | solution.py:198
  206.2 10.7 %collective-permute-start.17 = (f32[640,80]{0,1:T(8,128)S(1)}, f32[640,80]{0,1:T(8,128)S(1)}, u32[]{:S(2)}, u32[]{:S(2)}) collective-permute-start(f32[640,80]{0,1:T(8,128)S(1)} %get-tuple-element.31), channel_id=1, source_target_pairs={{0,6},{2,0},{4,2},{6,4},{1,7},{3,1},{5,3},{7,5},{8,14},{10,8},{12,... | collective-permute-start | bytes 614408 | tf_op jit(solution)/shard_map/ppermute | solution.py:202
  208.6 12.5 %collective-permute-start.16 = (f32[640,80]{0,1:T(8,128)S(1)}, f32[640,80]{0,1:T(8,128)S(1)}, u32[]{:S(2)}, u32[]{:S(2)}) collective-permute-start(f32[640,80]{0,1:T(8,128)S(1)} %get-tuple-element.32), channel_id=1, source_target_pairs={{0,4},{2,6},{4,0},{6,2},{1,5},{3,7},{5,1},{7,3},{8,12},{10,14},{12... | collective-permute-start | bytes 614408 | tf_op jit(solution)/shard_map/ppermute | solution.py:202
  213.5 9.7 %collective-permute-start.15 = (f32[640,80]{0,1:T(8,128)S(1)}, f32[640,80]{0,1:T(8,128)S(1)}, u32[]{:S(2)}, u32[]{:S(2)}) collective-permute-start(f32[640,80]{0,1:T(8,128)S(1)} %get-tuple-element.30), channel_id=1, source_target_pairs={{0,2},{2,4},{4,6},{6,0},{1,3},{3,5},{5,7},{7,1},{8,10},{10,12},{12... | collective-permute-start | bytes 614408 | tf_op jit(solution)/shard_map/ppermute | solution.py:202

commit v11 on v5

--- a/solution.py
+++ b/solution.py
@@ -6,7 +6,10 @@
 Y, Z, X, C = 8, 8, 4, 2
 V = X * C
 KEEP_MOST = 80
-SLOTS = 96
+SPARE = 8
+SLOTS = KEEP_MOST + SPARE
+SHARE = KEEP_MOST // V
+HELD = 16
 CLIP_EPS = 0.2
 LOSS_SCALE = 8192.0
 
@@ -46,12 +49,18 @@
     keep_float = kept_mask.astype(jnp.float32)
     slot_index = jnp.cumsum(kept_mask) - 1
     ids = jnp.arange(SLOTS, dtype=jnp.int32)
-    chosen = (slot_index[None, :] == ids[:, None]) & (kept_mask[None, :] == 1)
+    kept = kept_mask[None, :] == 1
+    chosen = (slot_index[None, :] == ids[:, None]) & kept
     selector = chosen.astype(jnp.bfloat16)
-    kept_hidden = jnp.dot(selector, hidden, preferred_element_type=jnp.float32)
-    kept_hidden = jnp.where(ids[:, None] < KEEP_MOST, kept_hidden, jnp.sum(keep_float)).astype(jnp.bfloat16)
-    kept_hidden = exchange(kept_hidden.reshape(SLOTS, Y, Z * rows).transpose(1, 0, 2), "y")
-    kept_y = jnp.sum(kept_hidden[:, KEEP_MOST, :128].astype(jnp.float32), axis=0)
+    share_ids = jnp.arange(HELD, dtype=jnp.int32)
+    first = (lax.axis_index("x") * C + lax.axis_index("c")) * SHARE
+    own = (slot_index[None, :] == (first + share_ids)[:, None]) & kept & (share_ids < SHARE)[:, None]
+    kept_hidden = jnp.dot(own.astype(jnp.bfloat16), hidden, preferred_element_type=jnp.float32)
+    kept_hidden = jnp.where(share_ids[:, None] < SHARE, kept_hidden, jnp.sum(keep_float)).astype(jnp.bfloat16)
+    kept_hidden = exchange(kept_hidden.reshape(HELD, Y, Z * rows).transpose(1, 0, 2), "y")
+    kept_y = jnp.sum(kept_hidden[:, SHARE, :128].astype(jnp.float32), axis=0)
+    kept_hidden = to_all(kept_hidden, ("x", "c"), V)[:, :, :SHARE]
+    kept_hidden = kept_hidden.transpose(1, 0, 2, 3).reshape(Y, KEEP_MOST, Z * rows)
     kept_total = jnp.sum(to_all(jnp.broadcast_to(kept_y, (8, 128)), "z", Z), axis=0)[0, 0]
     scale = -(LOSS_SCALE / kept_total)
     hidden, kept_hidden, scale = lax.optimization_barrier((hidden, kept_hidden, scale))
@@ -77,7 +86,8 @@
             jnp.sum(jnp.where(hit, logits, 0.0), axis=1),
         ]
     )
-    stats = to_all(stats, ("x", "c"), V)
+    stats, compact = lax.optimization_barrier((stats, compact))
+    stats = lax.all_gather(stats, ("x", "c"))
     tops, totals, moments, picks = (stats[:, i] for i in range(4))
     row_top = jnp.max(tops, axis=0)
     lower = tops - row_top[None]
@@ -93,27 +103,28 @@
     of_slots = jnp.stack([row_scale, row_entry, local_target.astype(jnp.float32)])
     of_slots = jnp.sum(jnp.where(chosen[None], of_slots[:, None, :], 0.0), axis=2)
 
+    all_factors = to_all(jnp.pad(of_slots, ((0, 5), (0, 128 - SLOTS))), "y", Y)
+
     own_rows = rows_of(compact, of_slots)
     hidden_part = lax.dot_general(
         own_rows, head, (((1,), (1,)), ((), ())), preferred_element_type=jnp.float32
-    ).astype(jnp.bfloat16)
+    ).astype(jnp.bfloat16)[:KEEP_MOST]
     mine = width // V
-    hidden_part = hidden_part.reshape(SLOTS, V, mine).transpose(1, 0, 2)
-    hidden_part, of_slots = lax.optimization_barrier((hidden_part, of_slots))
+    hidden_part = hidden_part.reshape(KEEP_MOST, V, mine).transpose(1, 0, 2)
+    hidden_part, all_factors = lax.optimization_barrier((hidden_part, all_factors))
     hidden_part = exchange(hidden_part, ("x", "c"))
 
-    all_factors = lax.all_gather(jnp.pad(of_slots, ((0, 5), (0, 128 - SLOTS))), "y")
-    all_rows = rows_of(all_slots, all_factors[:, :3, :SLOTS])
+    all_rows = rows_of(all_slots[:, :KEEP_MOST], all_factors[:, :3, :KEEP_MOST])
     part_head = lax.dot_general(
-        kept_hidden.reshape(Y * SLOTS, Z * rows), all_rows.reshape(Y * SLOTS, cols), (((0,), (0,)), ((), ())),
+        kept_hidden.reshape(Y * KEEP_MOST, Z * rows), all_rows.reshape(Y * KEEP_MOST, cols), (((0,), (0,)), ((), ())),
         preferred_element_type=jnp.float32,
     ).astype(jnp.bfloat16)
     sums = exchange(part_head.reshape(Z, rows, cols), "z")
     grad_head = scale * jnp.sum(sums.astype(jnp.float32), axis=0)
 
-    spread = jnp.tile(selector, (V, 1))
+    spread = jnp.tile(selector[:KEEP_MOST], (V, 1))
     grad_hidden = scale * lax.dot_general(
-        spread, hidden_part.reshape(V * SLOTS, mine), (((0,), (0,)), ((), ())),
+        spread, hidden_part.reshape(V * KEEP_MOST, mine), (((0,), (0,)), ((), ())),
         preferred_element_type=jnp.float32,
     )
     return (entropy, grad_hidden, grad_head)

time: 215 us -> 208 us (0.967)
  waiting for transfers between devices: 106 us -> 96.5 us
  starting transfers between devices: 36.9 us -> 31.8 us
  blocking collectives: 25.2 us -> 29.5 us
  local copies, waits for them, and re-layouts: 4.19 us -> 7.62 us
    all_to_all x0 -> x1, blocking collectives: none -> 16.7 us  [exchange(): return lax.all_to_all(parts, axes, split_axis=0, concat_axis=0)]
    all_gather x1, blocking collectives: 25.2 us -> 12.8 us  [per_device(): stats = lax.all_gather(stats, ('x', 'c'))]
    all_to_all x5, waiting for transfers between devices: 61 us -> 50.9 us  [exchange(): return lax.all_to_all(parts, axes, split_axis=0, concat_axis=0)]
    all_to_all x5, starting transfers between devices: 36.9 us -> 31.8 us  [exchange(): return lax.all_to_all(parts, axes, split_axis=0, concat_axis=0)]
    all_gather x1, waiting for transfers between devices: 0.02 us -> 4.19 us  [per_device(): all_slots = lax.all_gather(compact, 'y')]
    all_gather x1, waiting for transfers between devices: 44.6 us -> 40.8 us  [per_device(): head = lax.all_gather(head_weight, ('y', 'z'), axis=0, tiled=True)]
    slice x1 -> x4, local copies, waits for them, and re-layouts: 0.07 us -> 2.61 us  [the longest x1 1.27 us: per_device(): all_rows = rows_of(all_slots[:, :KEEP_MOST], all_factors[:, :3, :KEEP_MOST])]
  transfers between devices with their start and end apart: 7 -> 7, of which waited for: 5 -> 7; matrix products, arithmetic and copies ran while one was open for 11% -> 12% of each run, Pallas kernels for 0% -> 0%
where the time goes in v11:
time: 208 us; the launch traced here: 206 us
  waiting for transfers between devices  96.5 us (46%)
  starting transfers between devices  31.8 us (15%)
  blocking collectives  29.5 us (14%)
  matrix products  19 us (9%)
  between operations  14.9 us (7%)
  local copies, waits for them, and re-layouts  7.62 us (4%)
  other arithmetic  6.59 us (3%)
    all_to_all x5, waiting for transfers between devices, exchange(): return lax.all_to_all(parts, axes, split_axis=0, concat_axis=0)  50.9 us
    all_gather x1, waiting for transfers between devices, per_device(): head = lax.all_gather(head_weight, ('y', 'z'), axis=0, tiled=True)  40.8 us
    all_to_all x5, starting transfers between devices, exchange(): return lax.all_to_all(parts, axes, split_axis=0, concat_axis=0)  31.8 us
    all_to_all x1, blocking collectives, exchange(): return lax.all_to_all(parts, axes, split_axis=0, concat_axis=0)  16.7 us
    all_gather x1, blocking collectives, per_device(): stats = lax.all_gather(stats, ('x', 'c'))  12.8 us
    dot_general x1, matrix products, per_device(): lax.dot_general(own_rows, head, (((1,), (1,)), ((), ())), preferred_eleme...  5.82 us
    dot_general x1, matrix products, per_device(): logits = jnp.dot(hidden, head, preferred_element_type=jnp.float32)  5.5 us
    all_gather x1, waiting for transfers between devices, per_device(): all_slots = lax.all_gather(compact, 'y')  4.19 us
  transfers between devices with their start and end apart: 7, of which 7 were waited for; matrix products, arithmetic and copies ran while one was open for 12% of the time, Pallas kernels for 0%

profile of v11, /device:TPU:6, one launch (start us, length us, event | category | flops | bytes accessed | tf_op | source)
XLA Modules:
  0.0 205.9 jit_solution(10077302029849463178)
XLA Ops:
  7.2 0.0 copy-start
  7.2 0.0 all-gather.6.cloned.1.call-start
  7.2 0.7 all-gather.6.cloned.1.call-update
  7.9 1.0 reduce-window.9
  8.9 0.1 slice.62
  9.1 1.3 convert_reduce_fusion.1
  10.3 0.1 slice_reduce_fusion.1
  10.5 0.7 broadcast_compare_fusion
  11.1 0.1 add_bitcast_fusion
  11.2 0.0 copy-done
  11.2 1.1 fusion
  12.4 0.0 copy-start.2
  12.4 16.7 %all_to_all.30 = bf16[8,16,640]{2,1,0:T(8,128)(2,1)S(1)} all-to-all(bf16[8,16,640]{2,1,0:T(8,128)(2,1)S(1)} %bitcast.77), channel_id=1, replica_groups=mesh['y'=8,'z'=8,'x'=4,'c'=2] {'y'}, dimensions={0} | all-to-all | bytes 327680 | tf_op jit(solution)/shard_map/all_to_all | solution.py:30
  29.1 0.6 broadcast_in_dim_broadcast_in_dim_broadcast_in_dim.3
  29.7 10.3 %all-to-all-start.2 = ((f32[8,8,128]{2,1,0:T(8,128)}), f32[8,8,128]{2,1,0:T(8,128)S(1)}, u32[]{:S(2)}, u32[]{:S(2)}) async-start(f32[8,8,128]{2,1,0:T(8,128)} %broadcast_in_dim_broadcast_in_dim_broadcast_in_dim.3), calls=%async_computation.2 | async-start | bytes 65536 | tf_op jit(solution)/shard_map/all_to_all | solution.py:30
  40.1 8.0 %all-to-all-done.2 = f32[8,8,128]{2,1,0:T(8,128)S(1)} async-done(((f32[8,8,128]{2,1,0:T(8,128)}), f32[8,8,128]{2,1,0:T(8,128)S(1)}, u32[]{:S(2)}, u32[]{:S(2)}) %all-to-all-start.2) | async-done | bytes 32800 | tf_op jit(solution)/shard_map/all_to_all | solution.py:30
  48.1 1.2 broadcast_in_dim.85
  49.2 4.8 %all-to-all-start.1 = ((bf16[8,8,16,640]{3,1,2,0:T(8,128)(2,1)}), bf16[8,8,16,640]{3,1,2,0:T(8,128)(2,1)}, u32[]{:S(2)}, u32[]{:S(2)}) async-start(bf16[8,8,16,640]{3,1,2,0:T(8,128)(2,1)} %broadcast_in_dim.85), calls=%async_computation.1 | async-start | bytes 2621440 | tf_op jit(solution)/shard_map/all_to_all | solution.py:30
  54.0 0.0 all-gather.8.cloned.1.call-start
  54.0 0.0 copy-done.2
  54.1 0.5 slice.66
  55.3 15.5 %all-to-all-done.1 = bf16[8,8,16,640]{3,1,2,0:T(8,128)(2,1)} async-done(((bf16[8,8,16,640]{3,1,2,0:T(8,128)(2,1)}), bf16[8,8,16,640]{3,1,2,0:T(8,128)(2,1)}, u32[]{:S(2)}, u32[]{:S(2)}) %all-to-all-start.1) | async-done | bytes 1310752 | tf_op jit(solution)/shard_map/all_to_all | solution.py:30
  70.8 1.2 slice.81
  72.1 0.0 copy-start.1
  72.1 0.0 copy-start.3
  72.1 0.0 copy-start.4
  72.1 40.8 %all-gather.6.cloned.1.call-done = bf16[5120,768]{1,0:T(8,128)(2,1)} async-done(((bf16[80,768]{1,0:T(8,128)(2,1)}), bf16[5120,768]{1,0:T(8,128)(2,1)}) %all-gather.6.cloned.1.call-update) | async-done | bytes 7864336 | tf_op jit(solution)/shard_map/all_gather | solution.py:47
  112.9 5.5 %fusion.39 = (f32[256]{0:T(256)S(1)}, f32[256,768]{1,0:T(8,128)S(1)}) fusion(bf16[256,5120]{1,0:T(8,128)(2,1)S(1)} %copy-done, bf16[5120,768]{1,0:T(8,128)(2,1)} %all-gather.6.cloned.1.call-done), kind=kOutput, calls=%fused_computation.81 | convolution fusion | flops 2013462272 | bytes 11273216 | tf_op jit(solution)/shard_map/dot_general | solution.py:68
  118.4 0.5 exponential_reduce_fusion
  118.8 1.0 convolution_convert_fusion
  119.9 0.0 all-gather.8.cloned.1.call-update
  119.9 12.8 %all-gather.2 = f32[8,4,256]{2,1,0:T(4,128)S(1)} all-gather(f32[1,4,256]{2,1,0:T(4,128)S(1)} %bitcast.78), channel_id=2, replica_groups=mesh['y'=8,'z'=8,'x'=4,'c'=2] {'x','c'}, dimensions={0}, use_global_device_ids=true | all-gather | bytes 36864 | tf_op jit(solution)/shard_map/all_gather | solution.py:90
  132.8 0.0 copy-done.1
  132.8 0.0 copy-done.3
  132.8 0.0 copy-done.4
  132.8 0.6 subtract_multiply_fusion
  133.4 0.1 select_reduce_fusion.1
  133.6 0.6 broadcast_in_dim.92
  134.2 6.4 %all-to-all-start.3 = ((f32[8,8,128]{2,1,0:T(8,128)}), f32[8,8,128]{2,1,0:T(8,128)S(1)}, u32[]{:S(2)}, u32[]{:S(2)}) async-start(f32[8,8,128]{2,1,0:T(8,128)} %broadcast_in_dim.92), calls=%async_computation.3 | async-start | bytes 65536 | tf_op jit(solution)/shard_map/all_to_all | solution.py:30
  140.6 5.8 %fusion.14 = bf16[88,5120]{1,0:T(8,128)(2,1)S(1)} fusion(bf16[5120,768]{1,0:T(8,128)(2,1)} %all-gather.6.cloned.1.call-done, bf16[88,768]{1,0:T(8,128)(2,1)} %convolution_convert_fusion, f32[88]{0:T(128)S(1)} %get-tuple-element.37, bf16[88]{0:T(256)(128)(2,1)S(1)} %slice_bitcast_fusion, f32[768]{0:T(1024)S(1)} %iota_convert_fusion, f32[88]{0:T(128)S(1)} %get-tuple-element.36), kind=kOutput, calls=%fused_computation.29 | convolution fusion | flops 692330496 | bytes 8904560 | tf_op jit(solution)/shard_map/dot_general | solution.py:109
  146.5 0.1 slice.103
  146.5 1.0 copy.61
  147.5 1.4 all-to-all-done.3
  149.0 4.9 %all-to-all-start.4 = ((bf16[8,80,640]{2,1,0:T(8,128)(2,1)}), bf16[8,80,640]{2,1,0:T(8,128)(2,1)}, u32[]{:S(2)}, u32[]{:S(2)}) async-start(bf16[8,80,640]{2,1,0:T(8,128)(2,1)} %bitcast.69), calls=%async_computation.4 | async-start | bytes 1638400 | tf_op jit(solution)/shard_map/all_to_all | solution.py:30
  153.9 0.1 copy.33
  154.0 0.7 copy.32
  154.7 0.1 copy.31
  154.7 4.2 %all-gather.8.cloned.1.call-done = bf16[704,768]{1,0:T(8,128)(2,1)} async-done(((bf16[88,768]{1,0:T(8,128)(2,1)}), bf16[704,768]{1,0:T(8,128)(2,1)}) %all-gather.8.cloned.1.call-update) | async-done | bytes 1081360 | tf_op jit(solution)/shard_map/all_gather | solution.py:79
  158.9 1.3 slice.89
  160.2 3.1 %bitcast_convert_fusion = bf16[640,768]{1,0:T(8,128)(2,1)} fusion(bf16[8,80,640]{2,0,1:T(8,128)(2,1)S(1)} %bitcast.75, bf16[8,80,768]{2,1,0:T(8,128)(2,1)S(1)} %slice.89, f32[8,80]{0,1:T(8,128)S(1)} %copy.33, bf16[8,80]{0,1:T(8,128)(2,1)} %copy.32, f32[8,80]{0,1:T(8,128)S(1)} %copy.31, f32[768]{0:T(1024)S(1)} %iota_convert_fusion), kind=kOutput, calls=%fused_computation.2 | convolution fusion | flops 631603200 | bytes 2794752 | tf_op jit(solution)/shard_map/dot_general | solution.py:118
  163.3 2.1 %all-to-all-done.4 = bf16[8,80,640]{2,1,0:T(8,128)(2,1)} async-done(((bf16[8,80,640]{2,1,0:T(8,128)(2,1)}), bf16[8,80,640]{2,1,0:T(8,128)(2,1)}, u32[]{:S(2)}, u32[]{:S(2)}) %all-to-all-start.4) | async-done | bytes 819232 | tf_op jit(solution)/shard_map/all_to_all | solution.py:30
  165.4 5.4 %all-to-all-start.5 = ((bf16[8,80,768]{2,1,0:T(8,128)(2,1)}), bf16[8,80,768]{2,1,0:T(8,128)(2,1)}, u32[]{:S(2)}, u32[]{:S(2)}) async-start(bf16[8,80,768]{2,1,0:T(8,128)(2,1)} %bitcast.73), calls=%async_computation.5 | async-start | bytes 1966080 | tf_op jit(solution)/shard_map/all_to_all | solution.py:30
  170.8 2.5 %fusion.1 = f32[256,640]{1,0:T(8,128)} fusion(bf16[8,80,640]{2,1,0:T(8,128)(2,1)} %all-to-all-done.4, f32[]{:T(128)} %bitcast.5, bf16[80,256]{1,0:T(8,128)(2,1)S(1)} %slice_convert_fusion.1), kind=kOutput, calls=%fused_computation.7 | convolution fusion | flops 209879040 | bytes 1515524 | tf_op jit(solution)/shard_map/dot_general | solution.py:126
  173.2 23.8 %all-to-all-done.5 = bf16[8,80,768]{2,1,0:T(8,128)(2,1)} async-done(((bf16[8,80,768]{2,1,0:T(8,128)(2,1)}), bf16[8,80,768]{2,1,0:T(8,128)(2,1)}, u32[]{:S(2)}, u32[]{:S(2)}) %all-to-all-start.5) | async-done | bytes 983072 | tf_op jit(solution)/shard_map/all_to_all | solution.py:30
  197.0 1.4 convert_reduce_fusion
  198.4 0.7 broadcast_multiply_fusion
  (20 shorter events, 0.3 us)
Async XLA Ops:
  7.2 4.1 %copy-start = (bf16[256,5120]{1,0:T(8,128)(2,1)S(1)}, bf16[256,5120]{1,0:T(8,128)(2,1)}, u32[]{:S(2)}) copy-start(bf16[256,5120]{1,0:T(8,128)(2,1)} %param.6) | copy-start | bytes 7864324
  7.2 105.7 %all-gather.6.cloned.1.call-start = ((), (), s32[]{:S(2)}) async-start(), calls=%async_computation.6 | async-start | bytes 7987200 | tf_op jit(solution)/shard_map/all_gather | solution.py:47
  12.4 41.7 %copy-start.2 = (s32[256]{0:T(256)S(1)}, s32[256]{0:T(256)}, u32[]{:S(2)}) copy-start(s32[256]{0:T(256)} %param.8) | copy-start | bytes 3076
  29.7 18.4 %all-to-all-start.2 = ((f32[8,8,128]{2,1,0:T(8,128)}), f32[8,8,128]{2,1,0:T(8,128)S(1)}, u32[]{:S(2)}, u32[]{:S(2)}) async-start(f32[8,8,128]{2,1,0:T(8,128)} %broadcast_in_dim_broadcast_in_dim_broadcast_in_dim.3), calls=%async_computation.2 | async-start | bytes 65536 | tf_op jit(solution)/shard_map/all_to_all | solution.py:30
  49.2 21.6 %all-to-all-start.1 = ((bf16[8,8,16,640]{3,1,2,0:T(8,128)(2,1)}), bf16[8,8,16,640]{3,1,2,0:T(8,128)(2,1)}, u32[]{:S(2)}, u32[]{:S(2)}) async-start(bf16[8,8,16,640]{3,1,2,0:T(8,128)(2,1)} %broadcast_in_dim.85), calls=%async_computation.1 | async-start | bytes 2621440 | tf_op jit(solution)/shard_map/all_to_all | solution.py:30
  54.0 104.9 %all-gather.8.cloned.1.call-start = ((), (), s32[]{:S(2)}) async-start(), calls=%async_computation.7 | async-start | bytes 1216512 | tf_op jit(solution)/shard_map/all_gather | solution.py:79
  72.1 60.7 %copy-start.1 = (s32[256]{0:T(256)S(1)}, s32[256]{0:T(256)}, u32[]{:S(2)}) copy-start(s32[256]{0:T(256)} %param.9) | copy-start | bytes 3076
  72.1 60.7 %copy-start.3 = (f32[256]{0:T(256)S(1)}, f32[256]{0:T(256)}, u32[]{:S(2)}) copy-start(f32[256]{0:T(256)} %param.11) | copy-start | bytes 3076
  72.1 60.7 %copy-start.4 = (f32[256]{0:T(256)S(1)}, f32[256]{0:T(256)}, u32[]{:S(2)}) copy-start(f32[256]{0:T(256)} %param.10) | copy-start | bytes 3076
  134.2 14.8 %all-to-all-start.3 = ((f32[8,8,128]{2,1,0:T(8,128)}), f32[8,8,128]{2,1,0:T(8,128)S(1)}, u32[]{:S(2)}, u32[]{:S(2)}) async-start(f32[8,8,128]{2,1,0:T(8,128)} %broadcast_in_dim.92), calls=%async_computation.3 | async-start | bytes 65536 | tf_op jit(solution)/shard_map/all_to_all | solution.py:30
  149.0 16.4 %all-to-all-start.4 = ((bf16[8,80,640]{2,1,0:T(8,128)(2,1)}), bf16[8,80,640]{2,1,0:T(8,128)(2,1)}, u32[]{:S(2)}, u32[]{:S(2)}) async-start(bf16[8,80,640]{2,1,0:T(8,128)(2,1)} %bitcast.69), calls=%async_computation.4 | async-start | bytes 1638400 | tf_op jit(solution)/shard_map/all_to_all | solution.py:30
  165.4 31.6 %all-to-all-start.5 = ((bf16[8,80,768]{2,1,0:T(8,128)(2,1)}), bf16[8,80,768]{2,1,0:T(8,128)(2,1)}, u32[]{:S(2)}, u32[]{:S(2)}) async-start(bf16[8,80,768]{2,1,0:T(8,128)(2,1)} %bitcast.73), calls=%async_computation.5 | async-start | bytes 1966080 | tf_op jit(solution)/shard_map/all_to_all | solution.py:30
Sparse Core Ops, SparseCore 0:
  11.1 101.7 all-gather.5
  120.0 38.8 all-gather.7

commit v12 on v11

--- a/solution.py
+++ b/solution.py
@@ -109,23 +109,30 @@
     hidden_part = lax.dot_general(
         own_rows, head, (((1,), (1,)), ((), ())), preferred_element_type=jnp.float32
     ).astype(jnp.bfloat16)[:KEEP_MOST]
-    mine = width // V
-    hidden_part = hidden_part.reshape(KEEP_MOST, V, mine).transpose(1, 0, 2)
-    hidden_part, all_factors = lax.optimization_barrier((hidden_part, all_factors))
-    hidden_part = exchange(hidden_part, ("x", "c"))
 
     all_rows = rows_of(all_slots[:, :KEEP_MOST], all_factors[:, :3, :KEEP_MOST])
     part_head = lax.dot_general(
         kept_hidden.reshape(Y * KEEP_MOST, Z * rows), all_rows.reshape(Y * KEEP_MOST, cols), (((0,), (0,)), ((), ())),
         preferred_element_type=jnp.float32,
     ).astype(jnp.bfloat16)
+    hidden_part, part_head = lax.optimization_barrier((hidden_part, part_head))
     sums = exchange(part_head.reshape(Z, rows, cols), "z")
     grad_head = scale * jnp.sum(sums.astype(jnp.float32), axis=0)
 
-    spread = jnp.tile(selector[:KEEP_MOST], (V, 1))
+    hidden_part = hidden_part.reshape(KEEP_MOST, X, C, width // V).transpose(1, 2, 0, 3)
+    at_x, at_c = lax.axis_index("x"), lax.axis_index("c")
+    mine = lax.dynamic_index_in_dim(hidden_part, at_c, 1, keepdims=False)
+    other = lax.dynamic_index_in_dim(hidden_part, 1 - at_c, 1, keepdims=False)
+    pair = mine.astype(jnp.float32) + lax.ppermute(other, "c", [(0, 1), (1, 0)]).astype(jnp.float32)
+    total = lax.dynamic_index_in_dim(pair, at_x, 0, keepdims=False)
+    for step in range(1, X):
+        sent = lax.dynamic_index_in_dim(pair, lax.rem(at_x + step, X), 0, keepdims=False)
+        total = total + lax.ppermute(sent, "x", [(i, (i + step) % X) for i in range(X)])
+    upper = total.astype(jnp.bfloat16)
+    under = (total - upper.astype(jnp.float32)).astype(jnp.bfloat16)
     grad_hidden = scale * lax.dot_general(
-        spread, hidden_part.reshape(V * KEEP_MOST, mine), (((0,), (0,)), ((), ())),
-        preferred_element_type=jnp.float32,
+        jnp.concatenate([selector[:KEEP_MOST]] * 2), jnp.concatenate([upper, under]),
+        (((0,), (0,)), ((), ())), preferred_element_type=jnp.float32,
     )
     return (entropy, grad_hidden, grad_head)
 

time: 208 us -> 215 us (1.034)
  waiting for transfers between devices: 96.5 us -> 84.9 us
  starting transfers between devices: 31.8 us -> 40.7 us
  local copies, waits for them, and re-layouts: 7.62 us -> 14.4 us
  other arithmetic: 6.59 us -> 9.11 us
    all_to_all x5 -> x4, waiting for transfers between devices: 50.9 us -> 25.1 us  [exchange(): return lax.all_to_all(parts, axes, split_axis=0, concat_axis=0)]
    ppermute x0 -> x4, starting transfers between devices: none -> 11.7 us  [the longest x3 9.8 us: per_device(): lax.ppermute(sent, 'x', [(i, (i + step) % X) for i in range(X)])]
    ppermute x0 -> x4, waiting for transfers between devices: none -> 9.26 us  [the longest x3 7.57 us: per_device(): lax.ppermute(sent, 'x', [(i, (i + step) % X) for i in range(X)])]
    all_gather x1, waiting for transfers between devices: 4.19 us -> 9.06 us  [per_device(): all_slots = lax.all_gather(compact, 'y')]
    all_to_all x5 -> x4, starting transfers between devices: 31.8 us -> 29 us  [exchange(): return lax.all_to_all(parts, axes, split_axis=0, concat_axis=0)]
    dynamic_slice x0 -> x1, local copies, waits for them, and re-layouts: none -> 2.59 us  [per_device(): mine = lax.dynamic_index_in_dim(hidden_part, at_c, 1, keepdims=False)]
  transfers between devices with their start and end apart: 7 -> 10, of which waited for: 7 -> 8; matrix products, arithmetic and copies ran while one was open for 12% -> 13% of each run, Pallas kernels for 0% -> 0%
where the time goes in v12:
time: 215 us; the launch traced here: 211 us
  waiting for transfers between devices  84.9 us (39%)
  starting transfers between devices  40.7 us (19%)
  blocking collectives  29.5 us (14%)
  matrix products  17.8 us (8%)
  between operations  15 us (7%)
  local copies, waits for them, and re-layouts  14.4 us (7%)
  other arithmetic  9.11 us (4%)
    all_gather x1, waiting for transfers between devices, per_device(): head = lax.all_gather(head_weight, ('y', 'z'), axis=0, tiled=True)  40.8 us
    all_to_all x4, starting transfers between devices, exchange(): return lax.all_to_all(parts, axes, split_axis=0, concat_axis=0)  29 us
    all_to_all x4, waiting for transfers between devices, exchange(): return lax.all_to_all(parts, axes, split_axis=0, concat_axis=0)  25.1 us
    all_to_all x1, blocking collectives, exchange(): return lax.all_to_all(parts, axes, split_axis=0, concat_axis=0)  16.7 us
    all_gather x1, blocking collectives, per_device(): stats = lax.all_gather(stats, ('x', 'c'))  12.8 us
    ppermute x3, starting transfers between devices, per_device(): lax.ppermute(sent, 'x', [(i, (i + step) % X) for i in range(X)])  9.8 us
    all_gather x1, waiting for transfers between devices, per_device(): all_slots = lax.all_gather(compact, 'y')  9.06 us
    ppermute x3, waiting for transfers between devices, per_device(): lax.ppermute(sent, 'x', [(i, (i + step) % X) for i in range(X)])  7.57 us
  transfers between devices with their start and end apart: 10, of which 8 were waited for; matrix products, arithmetic and copies ran while one was open for 13% of the time, Pallas kernels for 0%

profile of v12, /device:TPU:6, one launch (start us, length us, event | category | flops | bytes accessed | tf_op | source)
XLA Modules:
  0.0 211.4 jit_solution(6002029541181933122)
XLA Ops:
  7.2 0.0 copy-start
  7.2 0.0 all-gather.6.cloned.1.call-start
  7.2 0.7 all-gather.6.cloned.1.call-update
  7.9 1.0 reduce-window.9
  8.9 0.1 slice.60
  9.1 1.3 convert_reduce_fusion.1
  10.3 0.1 slice_reduce_fusion.1
  10.5 0.7 broadcast_compare_fusion
  11.1 0.1 add_bitcast_fusion
  11.2 1.1 fusion
  12.4 16.7 %all_to_all.25 = bf16[8,16,640]{2,1,0:T(8,128)(2,1)S(1)} all-to-all(bf16[8,16,640]{2,1,0:T(8,128)(2,1)S(1)} %bitcast.85), channel_id=1, replica_groups=mesh['y'=8,'z'=8,'x'=4,'c'=2] {'y'}, dimensions={0} | all-to-all | bytes 327680 | tf_op jit(solution)/shard_map/all_to_all | solution.py:30
  29.1 0.6 broadcast_in_dim_broadcast_in_dim_broadcast_in_dim.3
  29.7 10.3 %all-to-all-start.2 = ((f32[8,8,128]{2,1,0:T(8,128)}), f32[8,8,128]{2,1,0:T(8,128)S(1)}, u32[]{:S(2)}, u32[]{:S(2)}) async-start(f32[8,8,128]{2,1,0:T(8,128)} %broadcast_in_dim_broadcast_in_dim_broadcast_in_dim.3), calls=%async_computation.2 | async-start | bytes 65536 | tf_op jit(solution)/shard_map/all_to_all | solution.py:30
  40.1 8.0 %all-to-all-done.2 = f32[8,8,128]{2,1,0:T(8,128)S(1)} async-done(((f32[8,8,128]{2,1,0:T(8,128)}), f32[8,8,128]{2,1,0:T(8,128)S(1)}, u32[]{:S(2)}, u32[]{:S(2)}) %all-to-all-start.2) | async-done | bytes 32800 | tf_op jit(solution)/shard_map/all_to_all | solution.py:30
  48.1 1.2 broadcast_in_dim.85
  49.2 4.8 %all-to-all-start.1 = ((bf16[8,8,16,640]{3,1,2,0:T(8,128)(2,1)}), bf16[8,8,16,640]{3,1,2,0:T(8,128)(2,1)}, u32[]{:S(2)}, u32[]{:S(2)}) async-start(bf16[8,8,16,640]{3,1,2,0:T(8,128)(2,1)} %broadcast_in_dim.85), calls=%async_computation.1 | async-start | bytes 2621440 | tf_op jit(solution)/shard_map/all_to_all | solution.py:30
  54.0 0.0 copy-done.3
  54.1 0.5 slice.64
  55.3 15.5 %all-to-all-done.1 = bf16[8,8,16,640]{3,1,2,0:T(8,128)(2,1)} async-done(((bf16[8,8,16,640]{3,1,2,0:T(8,128)(2,1)}), bf16[8,8,16,640]{3,1,2,0:T(8,128)(2,1)}, u32[]{:S(2)}, u32[]{:S(2)}) %all-to-all-start.1) | async-done | bytes 1310752 | tf_op jit(solution)/shard_map/all_to_all | solution.py:30
  70.8 1.2 slice.78
  72.1 0.0 copy-start.2
  72.1 0.0 copy-start.4
  72.1 0.0 copy-start.5
  72.1 40.8 %all-gather.6.cloned.1.call-done = bf16[5120,768]{1,0:T(8,128)(2,1)} async-done(((bf16[80,768]{1,0:T(8,128)(2,1)}), bf16[5120,768]{1,0:T(8,128)(2,1)}) %all-gather.6.cloned.1.call-update) | async-done | bytes 7864336 | tf_op jit(solution)/shard_map/all_gather | solution.py:47
  112.9 5.5 %fusion.47 = (f32[256]{0:T(256)S(1)}, f32[256,768]{1,0:T(8,128)S(1)}) fusion(bf16[256,5120]{1,0:T(8,128)(2,1)S(1)} %copy-done, bf16[5120,768]{1,0:T(8,128)(2,1)} %all-gather.6.cloned.1.call-done), kind=kOutput, calls=%fused_computation.96 | convolution fusion | flops 2013462272 | bytes 11273216 | tf_op jit(solution)/shard_map/dot_general | solution.py:68
  118.4 0.5 exponential_reduce_fusion
  118.8 1.0 convolution_convert_fusion
  119.9 0.0 all-gather.8.cloned.1.call-update
  119.9 12.8 %all-gather.2 = f32[8,4,256]{2,1,0:T(4,128)S(1)} all-gather(f32[1,4,256]{2,1,0:T(4,128)S(1)} %bitcast.87), channel_id=2, replica_groups=mesh['y'=8,'z'=8,'x'=4,'c'=2] {'x','c'}, dimensions={0}, use_global_device_ids=true | all-gather | bytes 36864 | tf_op jit(solution)/shard_map/all_gather | solution.py:90
  132.8 0.0 copy-done.2
  132.8 0.0 copy-done.4
  132.8 0.6 subtract_multiply_fusion
  133.4 0.1 select_reduce_fusion.1
  133.6 0.6 broadcast_in_dim.92
  134.2 6.4 %all-to-all-start.3 = ((f32[8,8,128]{2,1,0:T(8,128)}), f32[8,8,128]{2,1,0:T(8,128)S(1)}, u32[]{:S(2)}, u32[]{:S(2)}) async-start(f32[8,8,128]{2,1,0:T(8,128)} %broadcast_in_dim.92), calls=%async_computation.3 | async-start | bytes 65536 | tf_op jit(solution)/shard_map/all_to_all | solution.py:30
  140.6 5.8 %fusion.20 = bf16[88,5120]{1,0:T(8,128)(2,1)S(1)} fusion(bf16[5120,768]{1,0:T(8,128)(2,1)} %all-gather.6.cloned.1.call-done, bf16[88,768]{1,0:T(8,128)(2,1)} %convolution_convert_fusion, f32[88]{0:T(128)S(1)} %get-tuple-element.44, bf16[88]{0:T(256)(128)(2,1)S(1)} %slice_bitcast_fusion, f32[768]{0:T(1024)S(1)} %iota_convert_fusion, f32[88]{0:T(128)S(1)} %get-tuple-element.43), kind=kOutput, calls=%fused_computation.41 | convolution fusion | flops 692330496 | bytes 8904560 | tf_op jit(solution)/shard_map/dot_general | solution.py:109
  146.5 1.0 slice.101
  147.4 1.6 all-to-all-done.3
  149.0 0.1 copy.34
  149.1 0.7 copy.33
  149.8 0.1 copy.32
  149.9 9.1 %all-gather.8.cloned.1.call-done = bf16[704,768]{1,0:T(8,128)(2,1)} async-done(((bf16[88,768]{1,0:T(8,128)(2,1)}), bf16[704,768]{1,0:T(8,128)(2,1)}) %all-gather.8.cloned.1.call-update) | async-done | bytes 1081360 | tf_op jit(solution)/shard_map/all_gather | solution.py:79
  158.9 1.3 slice.89
  160.2 3.1 %bitcast_convert_fusion = bf16[640,768]{1,0:T(8,128)(2,1)} fusion(bf16[8,80,640]{2,0,1:T(8,128)(2,1)S(1)} %bitcast.83, bf16[8,80,768]{2,1,0:T(8,128)(2,1)S(1)} %slice.89, f32[8,80]{0,1:T(8,128)S(1)} %copy.34, bf16[8,80]{0,1:T(8,128)(2,1)} %copy.33, f32[8,80]{0,1:T(8,128)S(1)} %copy.32, f32[768]{0:T(1024)S(1)} %iota_convert_fusion), kind=kOutput, calls=%fused_computation.2 | convolution fusion | flops 631603200 | bytes 2794752 | tf_op jit(solution)/shard_map/dot_general | solution.py:114
  163.3 7.5 %all-to-all-start.4 = ((bf16[8,80,768]{2,1,0:T(8,128)(2,1)}), bf16[8,80,768]{2,1,0:T(8,128)(2,1)}, u32[]{:S(2)}, u32[]{:S(2)}) async-start(bf16[8,80,768]{2,1,0:T(8,128)(2,1)} %bitcast.81), calls=%async_computation.4 | async-start | bytes 1966080 | tf_op jit(solution)/shard_map/all_to_all | solution.py:30
  170.8 2.6 %reshape.128 = bf16[80,4,2,640]{3,2,1,0:T(2,128)(2,1)S(1)} reshape(bf16[80,5120]{1,0:T(8,128)(2,1)} %slice.101) | data formatting | bytes 1638400 | tf_op jit(solution)/shard_map/reshape | solution.py:122
  173.4 2.6 %constant_dynamic-slice_fusion.1 = (bf16[80,4,1,640]{3,2,1,0:T(2,128)(2,1)}, bf16[80,4,1,640]{3,2,1,0:T(2,128)(2,1)S(1)}) fusion(bf16[80,4,2,640]{3,2,1,0:T(2,128)(2,1)S(1)} %reshape.128, s32[]{:T(128)S(6)} %select_n.55, s32[]{:T(128)S(6)} %select_n.56), kind=kLoop, calls=%fused_computation.72 | loop fusion | bytes 1638408 | tf_op jit(solution)/shard_map/jit(dynamic_index_in_dim)/dynamic_slice | solution.py:124
  176.0 0.1 copy.66
  176.1 1.9 collective-permute-start
  178.0 1.7 collective-permute-done
  179.7 0.7 copy-done.1
  180.5 1.3 bitcast_add_fusion
  181.8 0.8 dynamic-slice_bitcast_fusion.2
  182.7 2.7 %collective-permute-start.3 = (f32[80,640]{1,0:T(8,128)}, f32[80,640]{1,0:T(8,128)}, u32[]{:S(2)}, u32[]{:S(2)}) collective-permute-start(f32[80,640]{1,0:T(8,128)} %get-tuple-element.31), channel_id=1, source_target_pairs={{0,6},{2,0},{4,2},{6,4},{1,7},{3,1},{5,3},{7,5},{8,14},{10,8},{12,... | collective-permute-start | bytes 614408 | tf_op jit(solution)/shard_map/ppermute | solution.py:130
  185.3 2.9 %collective-permute-start.2 = (f32[80,640]{1,0:T(8,128)}, f32[80,640]{1,0:T(8,128)}, u32[]{:S(2)}, u32[]{:S(2)}) collective-permute-start(f32[80,640]{1,0:T(8,128)} %get-tuple-element.32), channel_id=1, source_target_pairs={{0,4},{2,6},{4,0},{6,2},{1,5},{3,7},{5,1},{7,3},{8,12},{10,14},{12... | collective-permute-start | bytes 614408 | tf_op jit(solution)/shard_map/ppermute | solution.py:130
  188.2 4.3 %collective-permute-start.1 = (f32[80,640]{1,0:T(8,128)}, f32[80,640]{1,0:T(8,128)}, u32[]{:S(2)}, u32[]{:S(2)}) collective-permute-start(f32[80,640]{1,0:T(8,128)} %get-tuple-element.30), channel_id=1, source_target_pairs={{0,2},{2,4},{4,6},{6,0},{1,3},{3,5},{5,7},{7,1},{8,10},{10,12},{12... | collective-permute-start | bytes 614408 | tf_op jit(solution)/shard_map/ppermute | solution.py:130
  192.5 5.1 %collective-permute-done.3 = f32[80,640]{1,0:T(8,128)} collective-permute-done((f32[80,640]{1,0:T(8,128)}, f32[80,640]{1,0:T(8,128)}, u32[]{:S(2)}, u32[]{:S(2)}) %collective-permute-start.3) | collective-permute-done | bytes 204832 | tf_op jit(solution)/shard_map/ppermute | solution.py:130
  197.6 0.0 collective-permute-done.2
  197.6 2.5 %collective-permute-done.1 = f32[80,640]{1,0:T(8,128)} collective-permute-done((f32[80,640]{1,0:T(8,128)}, f32[80,640]{1,0:T(8,128)}, u32[]{:S(2)}, u32[]{:S(2)}) %collective-permute-start.1) | collective-permute-done | bytes 204832 | tf_op jit(solution)/shard_map/ppermute | solution.py:130
  200.1 1.2 subtract_convert_fusion
  201.3 1.2 convolution_multiply_fusion
  202.4 0.0 all-to-all-done.4
  202.4 1.4 convert_reduce_fusion
  203.8 0.7 broadcast_multiply_fusion
  (25 shorter events, 0.3 us)
Async XLA Ops:
  7.2 4.1 %copy-start = (bf16[256,5120]{1,0:T(8,128)(2,1)S(1)}, bf16[256,5120]{1,0:T(8,128)(2,1)}, u32[]{:S(2)}) copy-start(bf16[256,5120]{1,0:T(8,128)(2,1)} %param.6) | copy-start | bytes 7864324
  7.2 105.7 %all-gather.6.cloned.1.call-start = ((), (), s32[]{:S(2)}) async-start(), calls=%async_computation.5 | async-start | bytes 7987200 | tf_op jit(solution)/shard_map/all_gather | solution.py:47
  12.4 41.7 %copy-start.3 = (s32[256]{0:T(256)S(1)}, s32[256]{0:T(256)}, u32[]{:S(2)}) copy-start(s32[256]{0:T(256)} %param.8) | copy-start | bytes 3076
  29.7 18.4 %all-to-all-start.2 = ((f32[8,8,128]{2,1,0:T(8,128)}), f32[8,8,128]{2,1,0:T(8,128)S(1)}, u32[]{:S(2)}, u32[]{:S(2)}) async-start(f32[8,8,128]{2,1,0:T(8,128)} %broadcast_in_dim_broadcast_in_dim_broadcast_in_dim.3), calls=%async_computation.2 | async-start | bytes 65536 | tf_op jit(solution)/shard_map/all_to_all | solution.py:30
  49.2 21.6 %all-to-all-start.1 = ((bf16[8,8,16,640]{3,1,2,0:T(8,128)(2,1)}), bf16[8,8,16,640]{3,1,2,0:T(8,128)(2,1)}, u32[]{:S(2)}, u32[]{:S(2)}) async-start(bf16[8,8,16,640]{3,1,2,0:T(8,128)(2,1)} %broadcast_in_dim.85), calls=%async_computation.1 | async-start | bytes 2621440 | tf_op jit(solution)/shard_map/all_to_all | solution.py:30
  54.0 104.9 %all-gather.8.cloned.1.call-start = ((), (), s32[]{:S(2)}) async-start(), calls=%async_computation.6 | async-start | bytes 1216512 | tf_op jit(solution)/shard_map/all_gather | solution.py:79
  72.1 60.7 %copy-start.2 = (s32[256]{0:T(256)S(1)}, s32[256]{0:T(256)}, u32[]{:S(2)}) copy-start(s32[256]{0:T(256)} %param.9) | copy-start | bytes 3076
  72.1 60.7 %copy-start.4 = (f32[256]{0:T(256)S(1)}, f32[256]{0:T(256)}, u32[]{:S(2)}) copy-start(f32[256]{0:T(256)} %param.11) | copy-start | bytes 3076
  72.1 60.7 %copy-start.5 = (f32[256]{0:T(256)S(1)}, f32[256]{0:T(256)}, u32[]{:S(2)}) copy-start(f32[256]{0:T(256)} %param.10) | copy-start | bytes 3076
  134.2 14.8 %all-to-all-start.3 = ((f32[8,8,128]{2,1,0:T(8,128)}), f32[8,8,128]{2,1,0:T(8,128)S(1)}, u32[]{:S(2)}, u32[]{:S(2)}) async-start(f32[8,8,128]{2,1,0:T(8,128)} %broadcast_in_dim.92), calls=%async_computation.3 | async-start | bytes 65536 | tf_op jit(solution)/shard_map/all_to_all | solution.py:30
  163.3 39.1 %all-to-all-start.4 = ((bf16[8,80,768]{2,1,0:T(8,128)(2,1)}), bf16[8,80,768]{2,1,0:T(8,128)(2,1)}, u32[]{:S(2)}, u32[]{:S(2)}) async-start(bf16[8,80,768]{2,1,0:T(8,128)(2,1)} %bitcast.81), calls=%async_computation.4 | async-start | bytes 1966080 | tf_op jit(solution)/shard_map/all_to_all | solution.py:30
  176.1 3.6 %collective-permute-start = (bf16[4,80,640]{2,1,0:T(8,128)(2,1)S(1)}, bf16[4,80,640]{2,1,0:T(8,128)(2,1)S(1)}, u32[]{:S(2)}, u32[]{:S(2)}) collective-permute-start(bf16[4,80,640]{2,1,0:T(8,128)(2,1)S(1)} %bitcast.86), channel_id=1, source_target_pairs={{0,1},{1,0},{2,3},{3,2},{4,5},{5,4},{6,7},{7,6},{8,9},{9,8},{10,11... | collective-permute-start | bytes 1228808 | tf_op jit(solution)/shard_map/ppermute | solution.py:126
  179.7 0.8 copy-start.1
  182.7 14.9 %collective-permute-start.3 = (f32[80,640]{1,0:T(8,128)}, f32[80,640]{1,0:T(8,128)}, u32[]{:S(2)}, u32[]{:S(2)}) collective-permute-start(f32[80,640]{1,0:T(8,128)} %get-tuple-element.31), channel_id=1, source_target_pairs={{0,6},{2,0},{4,2},{6,4},{1,7},{3,1},{5,3},{7,5},{8,14},{10,8},{12,... | collective-permute-start | bytes 614408 | tf_op jit(solution)/shard_map/ppermute | solution.py:130
  185.3 12.2 %collective-permute-start.2 = (f32[80,640]{1,0:T(8,128)}, f32[80,640]{1,0:T(8,128)}, u32[]{:S(2)}, u32[]{:S(2)}) collective-permute-start(f32[80,640]{1,0:T(8,128)} %get-tuple-element.32), channel_id=1, source_target_pairs={{0,4},{2,6},{4,0},{6,2},{1,5},{3,7},{5,1},{7,3},{8,12},{10,14},{12... | collective-permute-start | bytes 614408 | tf_op jit(solution)/shard_map/ppermute | solution.py:130
  188.2 11.9 %collective-permute-start.1 = (f32[80,640]{1,0:T(8,128)}, f32[80,640]{1,0:T(8,128)}, u32[]{:S(2)}, u32[]{:S(2)}) collective-permute-start(f32[80,640]{1,0:T(8,128)} %get-tuple-element.30), channel_id=1, source_target_pairs={{0,2},{2,4},{4,6},{6,0},{1,3},{3,5},{5,7},{7,1},{8,10},{10,12},{12... | collective-permute-start | bytes 614408 | tf_op jit(solution)/shard_map/ppermute | solution.py:130
Sparse Core Ops, SparseCore 0:
  11.1 101.7 all-gather.5
  120.0 38.8 all-gather.7

commit v13 on v12

--- a/solution.py
+++ b/solution.py
@@ -110,20 +110,23 @@
         own_rows, head, (((1,), (1,)), ((), ())), preferred_element_type=jnp.float32
     ).astype(jnp.bfloat16)[:KEEP_MOST]
 
+    hidden_part, all_factors = lax.optimization_barrier((hidden_part, all_factors))
+    hidden_part = hidden_part.reshape(KEEP_MOST, V, width // V).transpose(1, 0, 2)
+    hidden_part = hidden_part.reshape(X, C, KEEP_MOST, width // V)
+    at_x, at_c = lax.axis_index("x"), lax.axis_index("c")
+    mine = lax.dynamic_index_in_dim(hidden_part, at_c, 1, keepdims=False)
+    other = lax.dynamic_index_in_dim(hidden_part, 1 - at_c, 1, keepdims=False)
+    pair = mine.astype(jnp.float32) + lax.ppermute(other, "c", [(0, 1), (1, 0)]).astype(jnp.float32)
+
     all_rows = rows_of(all_slots[:, :KEEP_MOST], all_factors[:, :3, :KEEP_MOST])
     part_head = lax.dot_general(
         kept_hidden.reshape(Y * KEEP_MOST, Z * rows), all_rows.reshape(Y * KEEP_MOST, cols), (((0,), (0,)), ((), ())),
         preferred_element_type=jnp.float32,
     ).astype(jnp.bfloat16)
-    hidden_part, part_head = lax.optimization_barrier((hidden_part, part_head))
+    pair, part_head = lax.optimization_barrier((pair, part_head))
     sums = exchange(part_head.reshape(Z, rows, cols), "z")
     grad_head = scale * jnp.sum(sums.astype(jnp.float32), axis=0)
 
-    hidden_part = hidden_part.reshape(KEEP_MOST, X, C, width // V).transpose(1, 2, 0, 3)
-    at_x, at_c = lax.axis_index("x"), lax.axis_index("c")
-    mine = lax.dynamic_index_in_dim(hidden_part, at_c, 1, keepdims=False)
-    other = lax.dynamic_index_in_dim(hidden_part, 1 - at_c, 1, keepdims=False)
-    pair = mine.astype(jnp.float32) + lax.ppermute(other, "c", [(0, 1), (1, 0)]).astype(jnp.float32)
     total = lax.dynamic_index_in_dim(pair, at_x, 0, keepdims=False)
     for step in range(1, X):
         sent = lax.dynamic_index_in_dim(pair, lax.rem(at_x + step, X), 0, keepdims=False)

time: 215 us -> 204 us (0.949); the launches traced: 211 us -> 204 us
  local copies, waits for them, and re-layouts: 14.4 us -> 9.34 us
  waiting for transfers between devices: 84.9 us -> 81.9 us
    all_to_all x4, waiting for transfers between devices: 25.1 us -> 32.2 us  [exchange(): return lax.all_to_all(parts, axes, split_axis=0, concat_axis=0)]
    all_gather x1, waiting for transfers between devices: 9.06 us -> 3.95 us  [per_device(): all_slots = lax.all_gather(compact, 'y')]
    ppermute x3, waiting for transfers between devices: 7.57 us -> 4.3 us  [per_device(): lax.ppermute(sent, 'x', [(i, (i + step) % X) for i in range(X)])]
    dynamic_slice x1 -> x0, local copies, waits for them, and re-layouts: 2.59 us -> none  [per_device(): mine = lax.dynamic_index_in_dim(hidden_part, at_c, 1, keepdims=False)]
    reshape x1, local copies, waits for them, and re-layouts: 2.63 us -> 0.07 us  [per_device(): hidden_part.reshape(KEEP_MOST, V, width // V).transpose(1, 0, 2)]
  transfers between devices with their start and end apart: 10 -> 10, of which waited for: 8 -> 9; matrix products, arithmetic and copies ran while one was open for 13% -> 11% of each run, Pallas kernels for 0% -> 0%
where the time goes in v13:
time: 204 us
  waiting for transfers between devices  81.9 us (40%)
  starting transfers between devices  40.7 us (20%)
  blocking collectives  29.5 us (14%)
  matrix products  18.2 us (9%)
  between operations  14.9 us (7%)
  local copies, waits for them, and re-layouts  9.34 us (5%)
  other arithmetic  8.98 us (4%)
    all_gather x1, waiting for transfers between devices, per_device(): head = lax.all_gather(head_weight, ('y', 'z'), axis=0, tiled=True)  39.9 us
    all_to_all x4, waiting for transfers between devices, exchange(): return lax.all_to_all(parts, axes, split_axis=0, concat_axis=0)  32.2 us
    all_to_all x4, starting transfers between devices, exchange(): return lax.all_to_all(parts, axes, split_axis=0, concat_axis=0)  29 us
    all_to_all x1, blocking collectives, exchange(): return lax.all_to_all(parts, axes, split_axis=0, concat_axis=0)  16.7 us
    all_gather x1, blocking collectives, per_device(): stats = lax.all_gather(stats, ('x', 'c'))  12.8 us
    ppermute x3, starting transfers between devices, per_device(): lax.ppermute(sent, 'x', [(i, (i + step) % X) for i in range(X)])  9.8 us
    dot_general x1, matrix products, per_device(): lax.dot_general(own_rows, head, (((1,), (1,)), ((), ())), preferred_eleme...  5.82 us
    dot_general x1, matrix products, per_device(): logits = jnp.dot(hidden, head, preferred_element_type=jnp.float32)  5.5 us
  transfers between devices with their start and end apart: 10, of which 9 were waited for; matrix products, arithmetic and copies ran while one was open for 11% of the time, Pallas kernels for 0%

profile of v13, /device:TPU:6, one launch (start us, length us, event | category | flops | bytes accessed | tf_op | source)
XLA Modules:
  0.0 203.6 jit_solution(16967606814534853700)
XLA Ops:
  7.2 0.0 copy-start
  7.2 0.0 all-gather.6.cloned.1.call-start
  7.2 0.7 all-gather.6.cloned.1.call-update
  7.9 1.0 reduce-window.9
  8.9 0.1 slice.60
  9.1 1.3 convert_reduce_fusion.1
  10.3 0.1 slice_reduce_fusion.1
  10.5 0.7 broadcast_compare_fusion
  11.1 0.1 add_bitcast_fusion
  11.2 0.0 copy-done
  11.2 1.1 fusion
  12.4 0.0 copy-start.3
  12.4 16.7 %all_to_all.25 = bf16[8,16,640]{2,1,0:T(8,128)(2,1)S(1)} all-to-all(bf16[8,16,640]{2,1,0:T(8,128)(2,1)S(1)} %bitcast.91), channel_id=1, replica_groups=mesh['y'=8,'z'=8,'x'=4,'c'=2] {'y'}, dimensions={0} | all-to-all | bytes 327680 | tf_op jit(solution)/shard_map/all_to_all | solution.py:30
  29.1 0.6 broadcast_in_dim_broadcast_in_dim_broadcast_in_dim.3
  29.7 10.3 %all-to-all-start.2 = ((f32[8,8,128]{2,1,0:T(8,128)}), f32[8,8,128]{2,1,0:T(8,128)S(1)}, u32[]{:S(2)}, u32[]{:S(2)}) async-start(f32[8,8,128]{2,1,0:T(8,128)} %broadcast_in_dim_broadcast_in_dim_broadcast_in_dim.3), calls=%async_computation.2 | async-start | bytes 65536 | tf_op jit(solution)/shard_map/all_to_all | solution.py:30
  40.1 8.0 %all-to-all-done.2 = f32[8,8,128]{2,1,0:T(8,128)S(1)} async-done(((f32[8,8,128]{2,1,0:T(8,128)}), f32[8,8,128]{2,1,0:T(8,128)S(1)}, u32[]{:S(2)}, u32[]{:S(2)}) %all-to-all-start.2) | async-done | bytes 32800 | tf_op jit(solution)/shard_map/all_to_all | solution.py:30
  48.1 1.2 broadcast_in_dim.85
  49.2 4.8 %all-to-all-start.1 = ((bf16[8,8,16,640]{3,1,2,0:T(8,128)(2,1)}), bf16[8,8,16,640]{3,1,2,0:T(8,128)(2,1)}, u32[]{:S(2)}, u32[]{:S(2)}) async-start(bf16[8,8,16,640]{3,1,2,0:T(8,128)(2,1)} %broadcast_in_dim.85), calls=%async_computation.1 | async-start | bytes 2621440 | tf_op jit(solution)/shard_map/all_to_all | solution.py:30
  54.0 0.0 all-gather.8.cloned.1.call-start
  54.0 0.0 copy-done.3
  54.1 0.5 slice.64
  55.3 15.5 %all-to-all-done.1 = bf16[8,8,16,640]{3,1,2,0:T(8,128)(2,1)} async-done(((bf16[8,8,16,640]{3,1,2,0:T(8,128)(2,1)}), bf16[8,8,16,640]{3,1,2,0:T(8,128)(2,1)}, u32[]{:S(2)}, u32[]{:S(2)}) %all-to-all-start.1) | async-done | bytes 1310752 | tf_op jit(solution)/shard_map/all_to_all | solution.py:30
  70.8 2.1 %slice.78 = bf16[8,8,10,640]{3,1,2,0:T(8,128)(2,1)} slice(bf16[8,8,16,640]{3,1,2,0:T(8,128)(2,1)} %all-to-all-done.1), slice={[0:8], [0:8], [0:10], [0:640]} | slice | bytes 1638400 | tf_op jit(solution)/shard_map/slice | solution.py:62
  73.0 39.9 %all-gather.6.cloned.1.call-done = bf16[5120,768]{1,0:T(8,128)(2,1)} async-done(((bf16[80,768]{1,0:T(8,128)(2,1)}), bf16[5120,768]{1,0:T(8,128)(2,1)}) %all-gather.6.cloned.1.call-update) | async-done | bytes 7864336 | tf_op jit(solution)/shard_map/all_gather | solution.py:47
  112.9 5.5 %fusion.47 = (f32[256]{0:T(256)S(1)}, f32[256,768]{1,0:T(8,128)S(1)}) fusion(bf16[256,5120]{1,0:T(8,128)(2,1)S(1)} %copy-done, bf16[5120,768]{1,0:T(8,128)(2,1)} %all-gather.6.cloned.1.call-done), kind=kOutput, calls=%fused_computation.95 | convolution fusion | flops 2013462272 | bytes 11273216 | tf_op jit(solution)/shard_map/dot_general | solution.py:68
  118.4 0.5 exponential_reduce_fusion
  118.8 1.0 convolution_convert_fusion
  119.9 0.0 all-gather.8.cloned.1.call-update
  119.9 12.8 %all-gather.2 = f32[8,4,256]{2,1,0:T(4,128)S(1)} all-gather(f32[1,4,256]{2,1,0:T(4,128)S(1)} %bitcast.92), channel_id=2, replica_groups=mesh['y'=8,'z'=8,'x'=4,'c'=2] {'x','c'}, dimensions={0}, use_global_device_ids=true | all-gather | bytes 36864 | tf_op jit(solution)/shard_map/all_gather | solution.py:90
  132.8 0.0 copy-done.2
  132.8 0.0 copy-done.4
  132.8 0.0 copy-done.5
  132.8 0.6 subtract_multiply_fusion
  133.4 0.1 select_reduce_fusion.1
  133.6 0.6 broadcast_in_dim.92
  134.2 6.4 %all-to-all-start.3 = ((f32[8,8,128]{2,1,0:T(8,128)}), f32[8,8,128]{2,1,0:T(8,128)S(1)}, u32[]{:S(2)}, u32[]{:S(2)}) async-start(f32[8,8,128]{2,1,0:T(8,128)} %broadcast_in_dim.92), calls=%async_computation.3 | async-start | bytes 65536 | tf_op jit(solution)/shard_map/all_to_all | solution.py:30
  140.6 5.8 %fusion.20 = bf16[88,5120]{1,0:T(8,128)(2,1)S(1)} fusion(bf16[5120,768]{1,0:T(8,128)(2,1)} %all-gather.6.cloned.1.call-done, bf16[88,768]{1,0:T(8,128)(2,1)} %convolution_convert_fusion, f32[88]{0:T(128)S(1)} %get-tuple-element.46, bf16[88]{0:T(256)(128)(2,1)S(1)} %slice_bitcast_fusion, f32[768]{0:T(1024)S(1)} %iota_convert_fusion, f32[88]{0:T(128)S(1)} %get-tuple-element.45), kind=kOutput, calls=%fused_computation.42 | convolution fusion | flops 692330496 | bytes 8904560 | tf_op jit(solution)/shard_map/dot_general | solution.py:109
  146.5 0.1 slice.98
  146.5 2.5 %all-to-all-done.3 = f32[8,8,128]{2,1,0:T(8,128)S(1)} async-done(((f32[8,8,128]{2,1,0:T(8,128)}), f32[8,8,128]{2,1,0:T(8,128)S(1)}, u32[]{:S(2)}, u32[]{:S(2)}) %all-to-all-start.3) | async-done | bytes 32800 | tf_op jit(solution)/shard_map/all_to_all | solution.py:30
  149.0 0.1 copy.63
  149.0 0.0 copy-start.1
  149.1 0.9 copy-done.1
  150.0 1.9 collective-permute-start
  151.9 0.1 copy.35
  152.0 0.7 copy.34
  152.7 0.1 copy.33
  152.8 1.0 collective-permute-done
  153.8 1.2 convert_add_fusion
  155.0 4.0 %all-gather.8.cloned.1.call-done = bf16[704,768]{1,0:T(8,128)(2,1)} async-done(((bf16[88,768]{1,0:T(8,128)(2,1)}), bf16[704,768]{1,0:T(8,128)(2,1)}) %all-gather.8.cloned.1.call-update) | async-done | bytes 1081360 | tf_op jit(solution)/shard_map/all_gather | solution.py:79
  158.9 1.3 slice.86
  160.2 3.5 %bitcast_convert_fusion = bf16[640,768]{1,0:T(8,128)(2,1)} fusion(bf16[8,80,640]{2,0,1:T(8,128)(2,1)} %bitcast.89, bf16[8,80,768]{2,1,0:T(8,128)(2,1)S(1)} %slice.86, f32[8,80]{0,1:T(8,128)S(1)} %copy.35, bf16[8,80]{0,1:T(8,128)(2,1)} %copy.34, f32[8,80]{0,1:T(8,128)S(1)} %copy.33, f32[768]{0:T(1024)S(1)} %iota_convert_fusion), kind=kOutput, calls=%fused_computation.2 | convolution fusion | flops 631603200 | bytes 2794752 | tf_op jit(solution)/shard_map/dot_general | solution.py:122
  163.7 7.5 %all-to-all-start.4 = ((bf16[8,80,768]{2,1,0:T(8,128)(2,1)}), bf16[8,80,768]{2,1,0:T(8,128)(2,1)}, u32[]{:S(2)}, u32[]{:S(2)}) async-start(bf16[8,80,768]{2,1,0:T(8,128)(2,1)} %bitcast.87), calls=%async_computation.4 | async-start | bytes 1966080 | tf_op jit(solution)/shard_map/all_to_all | solution.py:30
  171.2 0.8 dynamic-slice_bitcast_fusion.3
  172.0 2.7 %collective-permute-start.3 = (f32[80,640]{1,0:T(8,128)}, f32[80,640]{1,0:T(8,128)}, u32[]{:S(2)}, u32[]{:S(2)}) collective-permute-start(f32[80,640]{1,0:T(8,128)} %get-tuple-element.35), channel_id=1, source_target_pairs={{0,6},{2,0},{4,2},{6,4},{1,7},{3,1},{5,3},{7,5},{8,14},{10,8},{12,... | collective-permute-start | bytes 614408 | tf_op jit(solution)/shard_map/ppermute | solution.py:133
  174.7 2.9 %collective-permute-start.2 = (f32[80,640]{1,0:T(8,128)}, f32[80,640]{1,0:T(8,128)}, u32[]{:S(2)}, u32[]{:S(2)}) collective-permute-start(f32[80,640]{1,0:T(8,128)} %get-tuple-element.36), channel_id=1, source_target_pairs={{0,4},{2,6},{4,0},{6,2},{1,5},{3,7},{5,1},{7,3},{8,12},{10,14},{12... | collective-permute-start | bytes 614408 | tf_op jit(solution)/shard_map/ppermute | solution.py:133
  177.6 4.3 %collective-permute-start.1 = (f32[80,640]{1,0:T(8,128)}, f32[80,640]{1,0:T(8,128)}, u32[]{:S(2)}, u32[]{:S(2)}) collective-permute-start(f32[80,640]{1,0:T(8,128)} %get-tuple-element.34), channel_id=1, source_target_pairs={{0,2},{2,4},{4,6},{6,0},{1,3},{3,5},{5,7},{7,1},{8,10},{10,12},{12... | collective-permute-start | bytes 614408 | tf_op jit(solution)/shard_map/ppermute | solution.py:133
  181.8 0.0 collective-permute-done.3
  181.9 2.3 %collective-permute-done.2 = f32[80,640]{1,0:T(8,128)} collective-permute-done((f32[80,640]{1,0:T(8,128)}, f32[80,640]{1,0:T(8,128)}, u32[]{:S(2)}, u32[]{:S(2)}) %collective-permute-start.2) | collective-permute-done | bytes 204832 | tf_op jit(solution)/shard_map/ppermute | solution.py:133
  184.2 2.0 collective-permute-done.1
  186.2 1.2 subtract_convert_fusion
  187.3 1.2 convolution_multiply_fusion
  188.5 6.1 %all-to-all-done.4 = bf16[8,80,768]{2,1,0:T(8,128)(2,1)} async-done(((bf16[8,80,768]{2,1,0:T(8,128)(2,1)}), bf16[8,80,768]{2,1,0:T(8,128)(2,1)}, u32[]{:S(2)}, u32[]{:S(2)}) %all-to-all-start.4) | async-done | bytes 983072 | tf_op jit(solution)/shard_map/all_to_all | solution.py:30
  194.7 1.4 convert_reduce_fusion
  196.0 0.7 broadcast_multiply_fusion
  (24 shorter events, 0.4 us)
Async XLA Ops:
  7.2 4.1 %copy-start = (bf16[256,5120]{1,0:T(8,128)(2,1)S(1)}, bf16[256,5120]{1,0:T(8,128)(2,1)}, u32[]{:S(2)}) copy-start(bf16[256,5120]{1,0:T(8,128)(2,1)} %param.6) | copy-start | bytes 7864324
  7.2 105.7 %all-gather.6.cloned.1.call-start = ((), (), s32[]{:S(2)}) async-start(), calls=%async_computation.5 | async-start | bytes 7987200 | tf_op jit(solution)/shard_map/all_gather | solution.py:47
  12.4 41.7 %copy-start.3 = (s32[256]{0:T(256)S(1)}, s32[256]{0:T(256)}, u32[]{:S(2)}) copy-start(s32[256]{0:T(256)} %param.8) | copy-start | bytes 3076
  29.7 18.4 %all-to-all-start.2 = ((f32[8,8,128]{2,1,0:T(8,128)}), f32[8,8,128]{2,1,0:T(8,128)S(1)}, u32[]{:S(2)}, u32[]{:S(2)}) async-start(f32[8,8,128]{2,1,0:T(8,128)} %broadcast_in_dim_broadcast_in_dim_broadcast_in_dim.3), calls=%async_computation.2 | async-start | bytes 65536 | tf_op jit(solution)/shard_map/all_to_all | solution.py:30
  49.2 21.6 %all-to-all-start.1 = ((bf16[8,8,16,640]{3,1,2,0:T(8,128)(2,1)}), bf16[8,8,16,640]{3,1,2,0:T(8,128)(2,1)}, u32[]{:S(2)}, u32[]{:S(2)}) async-start(bf16[8,8,16,640]{3,1,2,0:T(8,128)(2,1)} %broadcast_in_dim.85), calls=%async_computation.1 | async-start | bytes 2621440 | tf_op jit(solution)/shard_map/all_to_all | solution.py:30
  54.0 104.9 %all-gather.8.cloned.1.call-start = ((), (), s32[]{:S(2)}) async-start(), calls=%async_computation.6 | async-start | bytes 1216512 | tf_op jit(solution)/shard_map/all_gather | solution.py:79
  73.0 59.8 %copy-start.2 = (s32[256]{0:T(256)S(1)}, s32[256]{0:T(256)}, u32[]{:S(2)}) copy-start(s32[256]{0:T(256)} %param.9) | copy-start | bytes 3076
  73.0 59.8 %copy-start.4 = (f32[256]{0:T(256)S(1)}, f32[256]{0:T(256)}, u32[]{:S(2)}) copy-start(f32[256]{0:T(256)} %param.11) | copy-start | bytes 3076
  73.0 59.8 %copy-start.5 = (f32[256]{0:T(256)S(1)}, f32[256]{0:T(256)}, u32[]{:S(2)}) copy-start(f32[256]{0:T(256)} %param.10) | copy-start | bytes 3076
  134.2 14.8 %all-to-all-start.3 = ((f32[8,8,128]{2,1,0:T(8,128)}), f32[8,8,128]{2,1,0:T(8,128)S(1)}, u32[]{:S(2)}, u32[]{:S(2)}) async-start(f32[8,8,128]{2,1,0:T(8,128)} %broadcast_in_dim.92), calls=%async_computation.3 | async-start | bytes 65536 | tf_op jit(solution)/shard_map/all_to_all | solution.py:30
  149.0 0.9 copy-start.1
  150.0 3.8 %collective-permute-start = (bf16[4,80,640]{2,1,0:T(8,128)(2,1)S(1)}, bf16[4,80,640]{2,1,0:T(8,128)(2,1)}, u32[]{:S(2)}, u32[]{:S(2)}) collective-permute-start(bf16[4,80,640]{2,1,0:T(8,128)(2,1)S(1)} %dynamic-slice_bitcast_fusion), channel_id=1, source_target_pairs={{0,1},{1,0},{2,3},{3,2},{4,5},{5,4},{6,7},{7,6},{8,9},{9,8},{10,11... | collective-permute-start | bytes 1228808 | tf_op jit(solution)/shard_map/ppermute | solution.py:119
  163.7 31.0 %all-to-all-start.4 = ((bf16[8,80,768]{2,1,0:T(8,128)(2,1)}), bf16[8,80,768]{2,1,0:T(8,128)(2,1)}, u32[]{:S(2)}, u32[]{:S(2)}) async-start(bf16[8,80,768]{2,1,0:T(8,128)(2,1)} %bitcast.87), calls=%async_computation.4 | async-start | bytes 1966080 | tf_op jit(solution)/shard_map/all_to_all | solution.py:30
  172.0 9.8 %collective-permute-start.3 = (f32[80,640]{1,0:T(8,128)}, f32[80,640]{1,0:T(8,128)}, u32[]{:S(2)}, u32[]{:S(2)}) collective-permute-start(f32[80,640]{1,0:T(8,128)} %get-tuple-element.35), channel_id=1, source_target_pairs={{0,6},{2,0},{4,2},{6,4},{1,7},{3,1},{5,3},{7,5},{8,14},{10,8},{12,... | collective-permute-start | bytes 614408 | tf_op jit(solution)/shard_map/ppermute | solution.py:133
  174.7 9.5 %collective-permute-start.2 = (f32[80,640]{1,0:T(8,128)}, f32[80,640]{1,0:T(8,128)}, u32[]{:S(2)}, u32[]{:S(2)}) collective-permute-start(f32[80,640]{1,0:T(8,128)} %get-tuple-element.36), channel_id=1, source_target_pairs={{0,4},{2,6},{4,0},{6,2},{1,5},{3,7},{5,1},{7,3},{8,12},{10,14},{12... | collective-permute-start | bytes 614408 | tf_op jit(solution)/shard_map/ppermute | solution.py:133
  177.6 8.6 %collective-permute-start.1 = (f32[80,640]{1,0:T(8,128)}, f32[80,640]{1,0:T(8,128)}, u32[]{:S(2)}, u32[]{:S(2)}) collective-permute-start(f32[80,640]{1,0:T(8,128)} %get-tuple-element.34), channel_id=1, source_target_pairs={{0,2},{2,4},{4,6},{6,0},{1,3},{3,5},{5,7},{7,1},{8,10},{10,12},{12... | collective-permute-start | bytes 614408 | tf_op jit(solution)/shard_map/ppermute | solution.py:133
Sparse Core Ops, SparseCore 0:
  11.1 101.7 all-gather.5
  120.0 38.8 all-gather.7

commit v14 on v13

--- a/solution.py
+++ b/solution.py
@@ -10,6 +10,7 @@
 SLOTS = KEEP_MOST + SPARE
 SHARE = KEEP_MOST // V
 HELD = 16
+SENT = 512
 CLIP_EPS = 0.2
 LOSS_SCALE = 8192.0
 
@@ -34,6 +35,28 @@
     return exchange(jnp.broadcast_to(values[None], (n,) + values.shape), axes)
 
 
+def shift(block, step):
+    return lax.ppermute(block, "y", [(i, (i + step) % Y) for i in range(Y)])
+
+
+def ring_over_y(own):
+    here = lax.axis_index("y")
+    whole = jnp.zeros((Y,) + own.shape, own.dtype)
+
+    def put(whole, block, away):
+        return lax.dynamic_update_slice(whole, block[None], (lax.rem(here + (away + Y), Y), 0, 0))
+
+    whole = put(whole, own, 0)
+    up = down = own
+    for hop in range(1, Y // 2 + 1):
+        down = shift(down, -1)
+        whole = put(whole, down, hop)
+        if hop < Y // 2:
+            up = shift(up, 1)
+            whole = put(whole, up, -hop)
+    return whole, down
+
+
 def rows_of(weights, factors):
     positions = lax.broadcasted_iota(jnp.int32, weights.shape, weights.ndim - 1).astype(jnp.float32)
     scale, entry, target = (factors[..., i, :, None] for i in range(3))
@@ -44,9 +67,15 @@
     tokens, width = hidden.shape
     rows, cols = head_weight.shape
     offset = (lax.axis_index("x") * C + lax.axis_index("c")) * cols
-    head = lax.all_gather(head_weight, ("y", "z"), axis=0, tiled=True)
 
+    head_a = lax.all_gather(head_weight[:, :SENT], ("y", "z"), axis=0, tiled=True)
     keep_float = kept_mask.astype(jnp.float32)
+    count_rows = jnp.broadcast_to(jnp.sum(keep_float).astype(jnp.bfloat16), (HELD, cols - SENT))
+    over_z = to_all(jnp.concatenate([head_weight[:, SENT:], count_rows], axis=0), "z", Z)
+    kept_z = jnp.sum(over_z[:, rows, :128].astype(jnp.float32), axis=0)[0]
+    head_b, last = ring_over_y(over_z[:, :rows].reshape(Z * rows, cols - SENT))
+    head_b = head_b.reshape(width, cols - SENT)
+
     slot_index = jnp.cumsum(kept_mask) - 1
     ids = jnp.arange(SLOTS, dtype=jnp.int32)
     kept = kept_mask[None, :] == 1
@@ -56,16 +85,25 @@
     first = (lax.axis_index("x") * C + lax.axis_index("c")) * SHARE
     own = (slot_index[None, :] == (first + share_ids)[:, None]) & kept & (share_ids < SHARE)[:, None]
     kept_hidden = jnp.dot(own.astype(jnp.bfloat16), hidden, preferred_element_type=jnp.float32)
-    kept_hidden = jnp.where(share_ids[:, None] < SHARE, kept_hidden, jnp.sum(keep_float)).astype(jnp.bfloat16)
-    kept_hidden = exchange(kept_hidden.reshape(HELD, Y, Z * rows).transpose(1, 0, 2), "y")
-    kept_y = jnp.sum(kept_hidden[:, SHARE, :128].astype(jnp.float32), axis=0)
-    kept_hidden = to_all(kept_hidden, ("x", "c"), V)[:, :, :SHARE]
+    high = jnp.floor(kept_z / 64.0)
+    count_pair = jnp.where(share_ids == SHARE, high, kept_z - 64.0 * high)
+    kept_hidden = jnp.where(share_ids[:, None] < SHARE, kept_hidden, count_pair[:, None]).astype(jnp.bfloat16)
+    kept_hidden = kept_hidden.reshape(HELD, Y, Z * rows).transpose(1, 0, 2)
+    kept_hidden, _ = lax.optimization_barrier((kept_hidden, last))
+    kept_share = exchange(kept_hidden, "y")
+    pairs = jnp.sum(kept_share[:, SHARE:SHARE + 2, 0].astype(jnp.float32), axis=0)
+    scale = -(LOSS_SCALE / (64.0 * pairs[0] + pairs[1]))
+    kept_hidden = to_all(kept_share, ("x", "c"), V)[:, :, :SHARE]
     kept_hidden = kept_hidden.transpose(1, 0, 2, 3).reshape(Y, KEEP_MOST, Z * rows)
-    kept_total = jnp.sum(to_all(jnp.broadcast_to(kept_y, (8, 128)), "z", Z), axis=0)[0, 0]
-    scale = -(LOSS_SCALE / kept_total)
-    hidden, kept_hidden, scale = lax.optimization_barrier((hidden, kept_hidden, scale))
+    hidden, scale = lax.optimization_barrier((hidden, scale))
 
-    logits = jnp.dot(hidden, head, preferred_element_type=jnp.float32)
+    logits = jnp.concatenate(
+        [
+            jnp.dot(hidden, head_a, preferred_element_type=jnp.float32),
+            jnp.dot(hidden, head_b, preferred_element_type=jnp.float32),
+        ],
+        axis=1,
+    )
     local_target = targets - offset
     positions = jnp.arange(cols, dtype=jnp.int32)
     hit = positions[None, :] == local_target[:, None]
@@ -86,8 +124,8 @@
             jnp.sum(jnp.where(hit, logits, 0.0), axis=1),
         ]
     )
-    stats, compact = lax.optimization_barrier((stats, compact))
-    stats = lax.all_gather(stats, ("x", "c"))
+    stats, compact, kept_hidden = lax.optimization_barrier((stats, compact, kept_hidden))
+    stats = to_all(stats, ("x", "c"), V)
     tops, totals, moments, picks = (stats[:, i] for i in range(4))
     row_top = jnp.max(tops, axis=0)
     lower = tops - row_top[None]
@@ -106,8 +144,10 @@
     all_factors = to_all(jnp.pad(of_slots, ((0, 5), (0, 128 - SLOTS))), "y", Y)
 
     own_rows = rows_of(compact, of_slots)
-    hidden_part = lax.dot_general(
-        own_rows, head, (((1,), (1,)), ((), ())), preferred_element_type=jnp.float32
+    over_cols = (((1,), (1,)), ((), ()))
+    hidden_part = (
+        lax.dot_general(own_rows[:, :SENT], head_a, over_cols, preferred_element_type=jnp.float32)
+        + lax.dot_general(own_rows[:, SENT:], head_b, over_cols, preferred_element_type=jnp.float32)
     ).astype(jnp.bfloat16)[:KEEP_MOST]
 
     hidden_part, all_factors = lax.optimization_barrier((hidden_part, all_factors))

time: 204 us -> 235 us (1.15)
  starting transfers between devices: 40.7 us -> 76.3 us
  blocking collectives: 29.5 us -> 0 us
  local copies, waits for them, and re-layouts: 9.34 us -> 27.4 us
  matrix products: 18.2 us -> 21.5 us
    all_gather x1, waiting for transfers between devices: 39.9 us -> 0.01 us  [per_device(): lax.all_gather(head_weight[:, :SENT], ('y', 'z'), axis=0, tiled=True)]
    ppermute x0 -> x7, starting transfers between devices: none -> 27.9 us  [shift(): return lax.ppermute(block, 'y', [(i, (i + step) % Y) for i in range(Y)])]
    ppermute x0 -> x7, waiting for transfers between devices: none -> 18.4 us  [shift(): return lax.ppermute(block, 'y', [(i, (i + step) % Y) for i in range(Y)])]
    all_to_all x1 -> x0, blocking collectives: 16.7 us -> none  [exchange(): return lax.all_to_all(parts, axes, split_axis=0, concat_axis=0)]
    all_gather x1 -> x0, blocking collectives: 12.8 us -> none  [per_device(): stats = lax.all_gather(stats, ('x', 'c'))]
    all_to_all x4 -> x6, waiting for transfers between devices: 32.2 us -> 44.4 us  [exchange(): return lax.all_to_all(parts, axes, split_axis=0, concat_axis=0)]
    dynamic_update_slice x0 -> x8, local copies, waits for them, and re-layouts: none -> 10.9 us  [put(): lax.dynamic_update_slice(whole, block[None], (lax.rem(here + (away + Y),...]
    all_to_all x4 -> x6, starting transfers between devices: 29 us -> 37.2 us  [exchange(): return lax.all_to_all(parts, axes, split_axis=0, concat_axis=0)]
  transfers between devices with their start and end apart: 10 -> 19, of which waited for: 9 -> 14; matrix products, arithmetic and copies ran while one was open for 11% -> 19% of each run, Pallas kernels for 0% -> 0%
where the time goes in v14:
time: 235 us; the launch traced here: 233 us
  waiting for transfers between devices  81.3 us (35%)
  starting transfers between devices  76.3 us (32%)
  local copies, waits for them, and re-layouts  27.4 us (12%)
  matrix products  21.5 us (9%)
  between operations  15.9 us (7%)
  other arithmetic  10.9 us (5%)
    all_to_all x6, waiting for transfers between devices, exchange(): return lax.all_to_all(parts, axes, split_axis=0, concat_axis=0)  44.4 us
    all_to_all x6, starting transfers between devices, exchange(): return lax.all_to_all(parts, axes, split_axis=0, concat_axis=0)  37.2 us
    ppermute x7, starting transfers between devices, shift(): return lax.ppermute(block, 'y', [(i, (i + step) % Y) for i in range(Y)])  27.9 us
    ppermute x7, waiting for transfers between devices, shift(): return lax.ppermute(block, 'y', [(i, (i + step) % Y) for i in range(Y)])  18.4 us
    dynamic_update_slice x8, local copies, waits for them, and re-layouts, put(): lax.dynamic_update_slice(whole, block[None], (lax.rem(here + (away + Y),...  10.9 us
    all_gather x1, waiting for transfers between devices, per_device(): all_slots = lax.all_gather(compact, 'y')  9.5 us
    ppermute x3, starting transfers between devices, per_device(): lax.ppermute(sent, 'x', [(i, (i + step) % X) for i in range(X)])  9.19 us
    ppermute x3, waiting for transfers between devices, per_device(): lax.ppermute(sent, 'x', [(i, (i + step) % X) for i in range(X)])  7.3 us
  transfers between devices with their start and end apart: 19, of which 14 were waited for; matrix products, arithmetic and copies ran while one was open for 19% of the time, Pallas kernels for 0%

profile of v14, /device:TPU:6, one launch (start us, length us, event | category | flops | bytes accessed | tf_op | source)
XLA Modules:
  0.0 233.1 jit_solution(15784156669426979114)
XLA Ops:
  7.2 1.7 slice.93
  8.9 0.8 slice.86
  9.7 1.3 convert_reduce_fusion.3
  11.6 0.8 broadcast_in_dim.134
  12.4 10.3 %all-to-all-start = ((bf16[8,96,256]{2,1,0:T(8,128)(2,1)}), bf16[8,96,256]{2,1,0:T(8,128)(2,1)S(1)}, u32[]{:S(2)}, u32[]{:S(2)}) async-start(bf16[8,96,256]{2,1,0:T(8,128)(2,1)} %broadcast_in_dim.134), calls=%async_computation | async-start | bytes 786432 | tf_op jit(solution)/shard_map/all_to_all | solution.py:31
  22.7 1.0 reduce-window.9
  25.4 12.1 %all-to-all-done = bf16[8,96,256]{2,1,0:T(8,128)(2,1)S(1)} async-done(((bf16[8,96,256]{2,1,0:T(8,128)(2,1)}), bf16[8,96,256]{2,1,0:T(8,128)(2,1)S(1)}, u32[]{:S(2)}, u32[]{:S(2)}) %all-to-all-start) | async-done | bytes 393248 | tf_op jit(solution)/shard_map/all_to_all | solution.py:31
  37.5 5.4 %collective-permute-start = (bf16[640,256]{1,0:T(8,128)(2,1)S(1)}, bf16[640,256]{1,0:T(8,128)(2,1)}, u32[]{:S(2)}, u32[]{:S(2)}) collective-permute-start(bf16[640,256]{1,0:T(8,128)(2,1)S(1)} %bitcast.110), channel_id=1, source_target_pairs={{0,448},{64,0},{128,64},{192,128},{256,192},{320,256},{384,320},{4... | collective-permute-start | bytes 983048 | tf_op jit(solution)/shard_map/ppermute | solution.py:39
  42.9 7.2 %collective-permute-done = bf16[640,256]{1,0:T(8,128)(2,1)} collective-permute-done((bf16[640,256]{1,0:T(8,128)(2,1)S(1)}, bf16[640,256]{1,0:T(8,128)(2,1)}, u32[]{:S(2)}, u32[]{:S(2)}) %collective-permute-start) | collective-permute-done | bytes 327712 | tf_op jit(solution)/shard_map/ppermute | solution.py:39
  50.2 5.7 %collective-permute-start.1 = (bf16[640,256]{1,0:T(8,128)(2,1)}, bf16[640,256]{1,0:T(8,128)(2,1)}, u32[]{:S(2)}, u32[]{:S(2)}) collective-permute-start(bf16[640,256]{1,0:T(8,128)(2,1)} %collective-permute-done), channel_id=1, source_target_pairs={{0,448},{64,0},{128,64},{192,128},{256,192},{320,256},{384,320},{4... | collective-permute-start | bytes 983048 | tf_op jit(solution)/shard_map/ppermute | solution.py:39
  56.0 1.9 collective-permute-start.4
  58.0 3.7 %collective-permute-done.1 = bf16[640,256]{1,0:T(8,128)(2,1)} collective-permute-done((bf16[640,256]{1,0:T(8,128)(2,1)}, bf16[640,256]{1,0:T(8,128)(2,1)}, u32[]{:S(2)}, u32[]{:S(2)}) %collective-permute-start.1) | collective-permute-done | bytes 327712 | tf_op jit(solution)/shard_map/ppermute | solution.py:39
  61.8 5.6 %collective-permute-start.2 = (bf16[640,256]{1,0:T(8,128)(2,1)}, bf16[640,256]{1,0:T(8,128)(2,1)S(1)}, u32[]{:S(2)}, u32[]{:S(2)}) collective-permute-start(bf16[640,256]{1,0:T(8,128)(2,1)} %collective-permute-done.1), channel_id=1, source_target_pairs={{0,448},{64,0},{128,64},{192,128},{256,192},{320,256},{384,320},{4... | collective-permute-start | bytes 983048 | tf_op jit(solution)/shard_map/ppermute | solution.py:39
  68.5 1.7 broadcast_in_dim.138
  70.2 0.7 bitcast_dynamic-update-slice_fusion.7
  71.0 1.9 collective-permute-start.5
  72.9 2.8 %collective-permute-done.2 = bf16[640,256]{1,0:T(8,128)(2,1)S(1)} collective-permute-done((bf16[640,256]{1,0:T(8,128)(2,1)}, bf16[640,256]{1,0:T(8,128)(2,1)S(1)}, u32[]{:S(2)}, u32[]{:S(2)}) %collective-permute-start.2) | collective-permute-done | bytes 327712 | tf_op jit(solution)/shard_map/ppermute | solution.py:39
  75.7 0.7 copy-done.3
  76.4 5.5 %collective-permute-start.3 = (bf16[640,256]{1,0:T(8,128)(2,1)S(1)}, bf16[640,256]{1,0:T(8,128)(2,1)S(1)}, u32[]{:S(2)}, u32[]{:S(2)}) collective-permute-start(bf16[640,256]{1,0:T(8,128)(2,1)S(1)} %collective-permute-done.2), channel_id=1, source_target_pairs={{0,448},{64,0},{128,64},{192,128},{256,192},{320,256},{384,320},{4... | collective-permute-start | bytes 983048 | tf_op jit(solution)/shard_map/ppermute | solution.py:39
  81.9 1.7 bitcast_dynamic-update-slice_fusion.6
  83.6 1.7 bitcast_dynamic-update-slice_fusion.5
  85.3 4.6 %collective-permute-done.5 = bf16[640,256]{1,0:T(8,128)(2,1)} collective-permute-done((bf16[640,256]{1,0:T(8,128)(2,1)}, bf16[640,256]{1,0:T(8,128)(2,1)}, u32[]{:S(2)}, u32[]{:S(2)}) %collective-permute-start.5) | collective-permute-done | bytes 327712 | tf_op jit(solution)/shard_map/ppermute | solution.py:39
  89.9 1.9 collective-permute-start.6
  91.8 5.0 %all-to-all-start.1 = ((bf16[8,16,640]{2,1,0:T(8,128)(2,1)}), bf16[8,16,640]{2,1,0:T(8,128)(2,1)S(1)}, u32[]{:S(2)}, u32[]{:S(2)}) async-start(bf16[8,16,640]{2,1,0:T(8,128)(2,1)} %bitcast.104), calls=%async_computation.1 | async-start | bytes 327680 | tf_op jit(solution)/shard_map/all_to_all | solution.py:31
  96.8 1.7 bitcast_dynamic-update-slice_fusion.4
  98.6 1.8 bitcast_dynamic-update-slice_fusion.3
  100.3 13.7 %all-to-all-done.1 = bf16[8,16,640]{2,1,0:T(8,128)(2,1)S(1)} async-done(((bf16[8,16,640]{2,1,0:T(8,128)(2,1)}), bf16[8,16,640]{2,1,0:T(8,128)(2,1)S(1)}, u32[]{:S(2)}, u32[]{:S(2)}) %all-to-all-start.1) | async-done | bytes 163872 | tf_op jit(solution)/shard_map/all_to_all | solution.py:31
  114.0 1.2 broadcast_in_dim.147
  115.2 4.8 %all-to-all-start.2 = ((bf16[8,8,16,640]{3,1,2,0:T(8,128)(2,1)}), bf16[8,8,16,640]{3,1,2,0:T(8,128)(2,1)}, u32[]{:S(2)}, u32[]{:S(2)}) async-start(bf16[8,8,16,640]{3,1,2,0:T(8,128)(2,1)} %broadcast_in_dim.147), calls=%async_computation.2 | async-start | bytes 2621440 | tf_op jit(solution)/shard_map/all_to_all | solution.py:31
  120.0 0.7 bitcast_dynamic-update-slice_fusion.2
  120.8 1.7 bitcast_dynamic-update-slice_fusion.1
  122.5 0.8 bitcast_dynamic-update-slice_fusion
  125.3 2.9 %fusion.49 = (f32[256]{0:T(256)S(1)}, f32[256,256]{0,1:T(8,128)S(1)}) fusion(bf16[256,5120]{1,0:T(8,128)(2,1)S(1)} %copy-done, bf16[5120,256]{1,0:T(8,128)(2,1)} %bitcast.14), kind=kOutput, calls=%fused_computation.108 | convolution fusion | flops 671153920 | bytes 5506048 | tf_op jit(solution)/shard_map/dot_general | solution.py:103
  128.3 8.5 %all-to-all-done.2 = bf16[8,8,16,640]{3,1,2,0:T(8,128)(2,1)} async-done(((bf16[8,8,16,640]{3,1,2,0:T(8,128)(2,1)}), bf16[8,8,16,640]{3,1,2,0:T(8,128)(2,1)}, u32[]{:S(2)}, u32[]{:S(2)}) %all-to-all-start.2) | async-done | bytes 1310752 | tf_op jit(solution)/shard_map/all_to_all | solution.py:31
  136.8 2.1 slice.113
  138.9 4.1 %fusion.48 = (f32[256]{0:T(256)S(1)}, f32[256,512]{1,0:T(8,128)S(1)}) fusion(bf16[256,5120]{1,0:T(8,128)(2,1)S(1)} %copy-done, bf16[5120,512]{1,0:T(8,128)(2,1)} %all-gather.4.cloned.1.call-done), kind=kOutput, calls=%fused_computation.107 | convolution fusion | flops 1342308096 | bytes 8389632 | tf_op jit(solution)/shard_map/dot_general | solution.py:102
  143.1 1.0 convolution_convert_fusion
  145.2 5.3 %all-to-all-start.3 = ((f32[8,4,256]{2,1,0:T(4,128)}), f32[8,4,256]{2,1,0:T(4,128)S(1)}, u32[]{:S(2)}, u32[]{:S(2)}) async-start(f32[8,4,256]{2,1,0:T(4,128)} %broadcast_in_dim.148), calls=%async_computation.3 | async-start | bytes 65536 | tf_op jit(solution)/shard_map/all_to_all | solution.py:31
  150.5 0.7 all-gather.6.cloned.1.call-update
  151.3 2.6 %all-to-all-done.3 = f32[8,4,256]{2,1,0:T(4,128)S(1)} async-done(((f32[8,4,256]{2,1,0:T(4,128)}), f32[8,4,256]{2,1,0:T(4,128)S(1)}, u32[]{:S(2)}, u32[]{:S(2)}) %all-to-all-start.3) | async-done | bytes 32800 | tf_op jit(solution)/shard_map/all_to_all | solution.py:31
  154.8 1.0 select_convert_fusion.2
  155.8 4.0 %fusion.24 = f32[88,5120]{1,0:T(8,128)} fusion(bf16[5120,256]{1,0:T(8,128)(2,1)} %bitcast.14, bf16[88,768]{1,0:T(8,128)(2,1)S(1)} %select_convert_fusion.2), kind=kOutput, calls=%fused_computation.57 | convolution fusion | flops 230686720 | bytes 4468736 | tf_op jit(solution)/shard_map/dot_general | solution.py:150
  160.4 4.4 %all-to-all-start.4 = ((f32[8,8,128]{2,1,0:T(8,128)}), f32[8,8,128]{2,1,0:T(8,128)S(1)}, u32[]{:S(2)}, u32[]{:S(2)}) async-start(f32[8,8,128]{2,1,0:T(8,128)} %broadcast_in_dim.154), calls=%async_computation.4 | async-start | bytes 65536 | tf_op jit(solution)/shard_map/all_to_all | solution.py:31
  164.8 4.3 %fusion.21 = f32[88,5120]{1,0:T(8,128)S(1)} fusion(bf16[5120,512]{1,0:T(8,128)(2,1)} %all-gather.4.cloned.1.call-done, bf16[88,768]{1,0:T(8,128)(2,1)S(1)} %select_convert_fusion.2), kind=kOutput, calls=%fused_computation.53 | convolution fusion | flops 461373440 | bytes 7135232 | tf_op jit(solution)/shard_map/dot_general | solution.py:149
  169.3 3.6 %all-to-all-done.4 = f32[8,8,128]{2,1,0:T(8,128)S(1)} async-done(((f32[8,8,128]{2,1,0:T(8,128)}), f32[8,8,128]{2,1,0:T(8,128)S(1)}, u32[]{:S(2)}, u32[]{:S(2)}) %all-to-all-start.4) | async-done | bytes 32800 | tf_op jit(solution)/shard_map/all_to_all | solution.py:31
  173.0 0.9 copy-done.2
  173.9 1.9 collective-permute-start.7
  176.7 1.0 collective-permute-done.7
  177.7 1.2 convert_add_fusion
  178.9 9.5 %all-gather.6.cloned.1.call-done = bf16[704,768]{1,0:T(8,128)(2,1)} async-done(((bf16[88,768]{1,0:T(8,128)(2,1)}), bf16[704,768]{1,0:T(8,128)(2,1)}) %all-gather.6.cloned.1.call-update) | async-done | bytes 1081360 | tf_op jit(solution)/shard_map/all_gather | solution.py:117
  188.4 1.3 slice.123
  189.7 3.5 %bitcast_convert_fusion = bf16[640,768]{1,0:T(8,128)(2,1)} fusion(bf16[8,80,640]{2,0,1:T(8,128)(2,1)} %bitcast.115, bf16[8,80,768]{2,1,0:T(8,128)(2,1)S(1)} %slice.123, f32[8,80]{0,1:T(8,128)S(1)} %copy.59, bf16[8,80]{0,1:T(8,128)(2,1)} %copy.58, f32[8,80]{0,1:T(8,128)S(1)} %copy.57, f32[768]{0:T(1024)S(1)} %iota_convert_fusion), kind=kOutput, calls=%fused_computation.2 | convolution fusion | flops 631603200 | bytes 2794752 | tf_op jit(solution)/shard_map/dot_general | solution.py:162
  193.2 7.4 %all-to-all-start.5 = ((bf16[8,80,768]{2,1,0:T(8,128)(2,1)}), bf16[8,80,768]{2,1,0:T(8,128)(2,1)}, u32[]{:S(2)}, u32[]{:S(2)}) async-start(bf16[8,80,768]{2,1,0:T(8,128)(2,1)} %bitcast.113), calls=%async_computation.5 | async-start | bytes 1966080 | tf_op jit(solution)/shard_map/all_to_all | solution.py:31
  200.5 0.8 dynamic-slice_bitcast_fusion.3
  201.4 3.0 %collective-permute-start.10 = (f32[80,640]{1,0:T(8,128)}, f32[80,640]{1,0:T(8,128)}, u32[]{:S(2)}, u32[]{:S(2)}) collective-permute-start(f32[80,640]{1,0:T(8,128)} %get-tuple-element.37), channel_id=1, source_target_pairs={{0,6},{2,0},{4,2},{6,4},{1,7},{3,1},{5,3},{7,5},{8,14},{10,8},{12,... | collective-permute-start | bytes 614408 | tf_op jit(solution)/shard_map/ppermute | solution.py:173
  204.4 4.0 %collective-permute-start.8 = (f32[80,640]{1,0:T(8,128)}, f32[80,640]{1,0:T(8,128)}, u32[]{:S(2)}, u32[]{:S(2)}) collective-permute-start(f32[80,640]{1,0:T(8,128)} %get-tuple-element.36), channel_id=1, source_target_pairs={{0,2},{2,4},{4,6},{6,0},{1,3},{3,5},{5,7},{7,1},{8,10},{10,12},{12... | collective-permute-start | bytes 614408 | tf_op jit(solution)/shard_map/ppermute | solution.py:173
  208.4 2.1 collective-permute-start.9
  210.6 2.1 collective-permute-done.10
  212.7 5.2 %collective-permute-done.9 = f32[80,640]{1,0:T(8,128)} collective-permute-done((f32[80,640]{1,0:T(8,128)}, f32[80,640]{1,0:T(8,128)}, u32[]{:S(2)}, u32[]{:S(2)}) %collective-permute-start.9) | collective-permute-done | bytes 204832 | tf_op jit(solution)/shard_map/ppermute | solution.py:173
  217.9 1.2 subtract_convert_fusion
  219.1 1.2 convolution_multiply_fusion
  220.3 4.0 %all-to-all-done.5 = bf16[8,80,768]{2,1,0:T(8,128)(2,1)} async-done(((bf16[8,80,768]{2,1,0:T(8,128)(2,1)}), bf16[8,80,768]{2,1,0:T(8,128)(2,1)}, u32[]{:S(2)}, u32[]{:S(2)}) %all-to-all-start.5) | async-done | bytes 983072 | tf_op jit(solution)/shard_map/all_to_all | solution.py:31
  224.2 1.4 convert_reduce_fusion
  225.6 0.7 broadcast_multiply_fusion
  (65 shorter events, 8.3 us)
Async XLA Ops:
  7.2 60.2 %copy-start = (bf16[256,5120]{1,0:T(8,128)(2,1)S(1)}, bf16[256,5120]{1,0:T(8,128)(2,1)}, u32[]{:S(2)}) copy-start(bf16[256,5120]{1,0:T(8,128)(2,1)} %param.6) | copy-start | bytes 7864324
  7.2 131.8 %all-gather.4.cloned.1.call-start = ((), (), s32[]{:S(2)}) async-start(), calls=%async_computation.6 | async-start | bytes 5324800 | tf_op jit(solution)/shard_map/all_gather | solution.py:71
  12.4 25.1 %all-to-all-start = ((bf16[8,96,256]{2,1,0:T(8,128)(2,1)}), bf16[8,96,256]{2,1,0:T(8,128)(2,1)S(1)}, u32[]{:S(2)}, u32[]{:S(2)}) async-start(bf16[8,96,256]{2,1,0:T(8,128)(2,1)} %broadcast_in_dim.134), calls=%async_computation | async-start | bytes 786432 | tf_op jit(solution)/shard_map/all_to_all | solution.py:31
  37.5 12.7 %collective-permute-start = (bf16[640,256]{1,0:T(8,128)(2,1)S(1)}, bf16[640,256]{1,0:T(8,128)(2,1)}, u32[]{:S(2)}, u32[]{:S(2)}) collective-permute-start(bf16[640,256]{1,0:T(8,128)(2,1)S(1)} %bitcast.110), channel_id=1, source_target_pairs={{0,448},{64,0},{128,64},{192,128},{256,192},{320,256},{384,320},{4... | collective-permute-start | bytes 983048 | tf_op jit(solution)/shard_map/ppermute | solution.py:39
  50.2 11.6 %collective-permute-start.1 = (bf16[640,256]{1,0:T(8,128)(2,1)}, bf16[640,256]{1,0:T(8,128)(2,1)}, u32[]{:S(2)}, u32[]{:S(2)}) collective-permute-start(bf16[640,256]{1,0:T(8,128)(2,1)} %collective-permute-done), channel_id=1, source_target_pairs={{0,448},{64,0},{128,64},{192,128},{256,192},{320,256},{384,320},{4... | collective-permute-start | bytes 983048 | tf_op jit(solution)/shard_map/ppermute | solution.py:39
  56.0 15.0 %collective-permute-start.4 = (bf16[640,256]{1,0:T(8,128)(2,1)S(1)}, bf16[640,256]{1,0:T(8,128)(2,1)}, u32[]{:S(2)}, u32[]{:S(2)}) collective-permute-start(bf16[640,256]{1,0:T(8,128)(2,1)S(1)} %bitcast.111), channel_id=1, source_target_pairs={{0,64},{64,128},{128,192},{192,256},{256,320},{320,384},{384,448},... | collective-permute-start | bytes 983048 | tf_op jit(solution)/shard_map/ppermute | solution.py:39
  61.8 13.9 %collective-permute-start.2 = (bf16[640,256]{1,0:T(8,128)(2,1)}, bf16[640,256]{1,0:T(8,128)(2,1)S(1)}, u32[]{:S(2)}, u32[]{:S(2)}) collective-permute-start(bf16[640,256]{1,0:T(8,128)(2,1)} %collective-permute-done.1), channel_id=1, source_target_pairs={{0,448},{64,0},{128,64},{192,128},{256,192},{320,256},{384,320},{4... | collective-permute-start | bytes 983048 | tf_op jit(solution)/shard_map/ppermute | solution.py:39
  71.0 18.9 %collective-permute-start.5 = (bf16[640,256]{1,0:T(8,128)(2,1)}, bf16[640,256]{1,0:T(8,128)(2,1)}, u32[]{:S(2)}, u32[]{:S(2)}) collective-permute-start(bf16[640,256]{1,0:T(8,128)(2,1)} %collective-permute-done.4), channel_id=1, source_target_pairs={{0,64},{64,128},{128,192},{192,256},{256,320},{320,384},{384,448},... | collective-permute-start | bytes 983048 | tf_op jit(solution)/shard_map/ppermute | solution.py:39
  75.7 0.7 copy-start.3
  76.4 15.4 %collective-permute-start.3 = (bf16[640,256]{1,0:T(8,128)(2,1)S(1)}, bf16[640,256]{1,0:T(8,128)(2,1)S(1)}, u32[]{:S(2)}, u32[]{:S(2)}) collective-permute-start(bf16[640,256]{1,0:T(8,128)(2,1)S(1)} %collective-permute-done.2), channel_id=1, source_target_pairs={{0,448},{64,0},{128,64},{192,128},{256,192},{320,256},{384,320},{4... | collective-permute-start | bytes 983048 | tf_op jit(solution)/shard_map/ppermute | solution.py:39
  89.9 30.9 %collective-permute-start.6 = (bf16[640,256]{1,0:T(8,128)(2,1)}, bf16[640,256]{1,0:T(8,128)(2,1)}, u32[]{:S(2)}, u32[]{:S(2)}) collective-permute-start(bf16[640,256]{1,0:T(8,128)(2,1)} %collective-permute-done.5), channel_id=1, source_target_pairs={{0,64},{64,128},{128,192},{192,256},{256,320},{320,384},{384,448},... | collective-permute-start | bytes 983048 | tf_op jit(solution)/shard_map/ppermute | solution.py:39
  91.8 22.2 %all-to-all-start.1 = ((bf16[8,16,640]{2,1,0:T(8,128)(2,1)}), bf16[8,16,640]{2,1,0:T(8,128)(2,1)S(1)}, u32[]{:S(2)}, u32[]{:S(2)}) async-start(bf16[8,16,640]{2,1,0:T(8,128)(2,1)} %bitcast.104), calls=%async_computation.1 | async-start | bytes 327680 | tf_op jit(solution)/shard_map/all_to_all | solution.py:31
  98.6 21.5 %copy-start.4 = (bf16[640,256]{1,0:T(8,128)(2,1)S(1)}, bf16[640,256]{1,0:T(8,128)(2,1)}, u32[]{:S(2)}) copy-start(bf16[640,256]{1,0:T(8,128)(2,1)} %copy-done.3) | copy-start | bytes 983044
  115.2 21.6 %all-to-all-start.2 = ((bf16[8,8,16,640]{3,1,2,0:T(8,128)(2,1)}), bf16[8,8,16,640]{3,1,2,0:T(8,128)(2,1)}, u32[]{:S(2)}, u32[]{:S(2)}) async-start(bf16[8,8,16,640]{3,1,2,0:T(8,128)(2,1)} %broadcast_in_dim.147), calls=%async_computation.2 | async-start | bytes 2621440 | tf_op jit(solution)/shard_map/all_to_all | solution.py:31
  143.0 10.9 %copy-start.5 = (s32[256]{0:T(256)S(1)}, s32[256]{0:T(256)}, u32[]{:S(2)}) copy-start(s32[256]{0:T(256)} %param.9) | copy-start | bytes 3076
  143.0 10.9 %copy-start.6 = (f32[256]{0:T(256)S(1)}, f32[256]{0:T(256)}, u32[]{:S(2)}) copy-start(f32[256]{0:T(256)} %param.11) | copy-start | bytes 3076
  143.0 10.9 %copy-start.7 = (f32[256]{0:T(256)S(1)}, f32[256]{0:T(256)}, u32[]{:S(2)}) copy-start(f32[256]{0:T(256)} %param.10) | copy-start | bytes 3076
  145.2 8.7 %all-to-all-start.3 = ((f32[8,4,256]{2,1,0:T(4,128)}), f32[8,4,256]{2,1,0:T(4,128)S(1)}, u32[]{:S(2)}, u32[]{:S(2)}) async-start(f32[8,4,256]{2,1,0:T(4,128)} %broadcast_in_dim.148), calls=%async_computation.3 | async-start | bytes 65536 | tf_op jit(solution)/shard_map/all_to_all | solution.py:31
  150.5 37.9 %all-gather.6.cloned.1.call-start = ((), (), s32[]{:S(2)}) async-start(), calls=%async_computation.7 | async-start | bytes 1216512 | tf_op jit(solution)/shard_map/all_gather | solution.py:117
  160.4 12.5 %all-to-all-start.4 = ((f32[8,8,128]{2,1,0:T(8,128)}), f32[8,8,128]{2,1,0:T(8,128)S(1)}, u32[]{:S(2)}, u32[]{:S(2)}) async-start(f32[8,8,128]{2,1,0:T(8,128)} %broadcast_in_dim.154), calls=%async_computation.4 | async-start | bytes 65536 | tf_op jit(solution)/shard_map/all_to_all | solution.py:31
  164.8 4.4 %copy-start.1 = (f32[88,5120]{1,0:T(8,128)S(1)}, f32[88,5120]{1,0:T(8,128)}, u32[]{:S(2)}) copy-start(f32[88,5120]{1,0:T(8,128)} %fusion.24) | copy-start | bytes 5406724
  173.0 0.9 copy-start.2
  173.9 3.8 %collective-permute-start.7 = (bf16[4,80,640]{2,1,0:T(8,128)(2,1)S(1)}, bf16[4,80,640]{2,1,0:T(8,128)(2,1)}, u32[]{:S(2)}, u32[]{:S(2)}) collective-permute-start(bf16[4,80,640]{2,1,0:T(8,128)(2,1)S(1)} %dynamic-slice_bitcast_fusion), channel_id=1, source_target_pairs={{0,1},{1,0},{2,3},{3,2},{4,5},{5,4},{6,7},{7,6},{8,9},{9,8},{10,11... | collective-permute-start | bytes 1228808 | tf_op jit(solution)/shard_map/ppermute | solution.py:159
  193.2 31.1 %all-to-all-start.5 = ((bf16[8,80,768]{2,1,0:T(8,128)(2,1)}), bf16[8,80,768]{2,1,0:T(8,128)(2,1)}, u32[]{:S(2)}, u32[]{:S(2)}) async-start(bf16[8,80,768]{2,1,0:T(8,128)(2,1)} %bitcast.113), calls=%async_computation.5 | async-start | bytes 1966080 | tf_op jit(solution)/shard_map/all_to_all | solution.py:31
  201.4 11.4 %collective-permute-start.10 = (f32[80,640]{1,0:T(8,128)}, f32[80,640]{1,0:T(8,128)}, u32[]{:S(2)}, u32[]{:S(2)}) collective-permute-start(f32[80,640]{1,0:T(8,128)} %get-tuple-element.37), channel_id=1, source_target_pairs={{0,6},{2,0},{4,2},{6,4},{1,7},{3,1},{5,3},{7,5},{8,14},{10,8},{12,... | collective-permute-start | bytes 614408 | tf_op jit(solution)/shard_map/ppermute | solution.py:173
  204.4 8.3 %collective-permute-start.8 = (f32[80,640]{1,0:T(8,128)}, f32[80,640]{1,0:T(8,128)}, u32[]{:S(2)}, u32[]{:S(2)}) collective-permute-start(f32[80,640]{1,0:T(8,128)} %get-tuple-element.36), channel_id=1, source_target_pairs={{0,2},{2,4},{4,6},{6,0},{1,3},{3,5},{5,7},{7,1},{8,10},{10,12},{12... | collective-permute-start | bytes 614408 | tf_op jit(solution)/shard_map/ppermute | solution.py:173
  208.4 9.5 %collective-permute-start.9 = (f32[80,640]{1,0:T(8,128)}, f32[80,640]{1,0:T(8,128)}, u32[]{:S(2)}, u32[]{:S(2)}) collective-permute-start(f32[80,640]{1,0:T(8,128)} %get-tuple-element.38), channel_id=1, source_target_pairs={{0,4},{2,6},{4,0},{6,2},{1,5},{3,7},{5,1},{7,3},{8,12},{10,14},{12... | collective-permute-start | bytes 614408 | tf_op jit(solution)/shard_map/ppermute | solution.py:173
Sparse Core Ops, SparseCore 0:
  11.1 105.4 all-gather.3
  154.0 34.3 all-gather.5

commit v15 on v13

--- a/solution.py
+++ b/solution.py
@@ -1,15 +1,19 @@
 import jax
 import jax.numpy as jnp
 from jax import lax
+from jax.experimental import pallas as pl
+from jax.experimental.pallas import tpu as pltpu
 from jax.sharding import Mesh, PartitionSpec as P
 
 Y, Z, X, C = 8, 8, 4, 2
 V = X * C
 KEEP_MOST = 80
-SPARE = 8
+SPARE = 16
 SLOTS = KEEP_MOST + SPARE
 SHARE = KEEP_MOST // V
 HELD = 16
+BLOCKS = 8
+GROUP = 32
 CLIP_EPS = 0.2
 LOSS_SCALE = 8192.0
 
@@ -38,6 +42,63 @@
     positions = lax.broadcasted_iota(jnp.int32, weights.shape, weights.ndim - 1).astype(jnp.float32)
     scale, entry, target = (factors[..., i, :, None] for i in range(3))
     return jnp.where(positions == target, entry, -scale * weights.astype(jnp.float32)).astype(jnp.bfloat16)
+
+
+def softmax_kernel(hidden, target, selector, head, compact, stats, held, total, weights_held, sems):
+    depth = held.shape[1]
+    copies = [
+        pltpu.make_async_copy(head.at[pl.ds(i * depth, depth)], held.at[i], sems.at[i]) for i in range(BLOCKS)
+    ]
+    for copy in copies:
+        copy.start()
+    for i, copy in enumerate(copies):
+        copy.wait()
+        part = jnp.dot(hidden[:, i * depth:(i + 1) * depth], held[i], preferred_element_type=jnp.float32)
+        total[...] = total[...] + part if i else part
+    tokens, cols = total.shape
+    positions = lax.broadcasted_iota(jnp.int32, (GROUP, cols), 1)
+    lane = lax.broadcasted_iota(jnp.int32, (GROUP, stats.shape[1]), 1)
+    for first in range(0, tokens, GROUP):
+        group = pl.ds(first, GROUP)
+        logits = total[group]
+        hit = positions == target[group]
+        top = jnp.max(logits, axis=1, keepdims=True)
+        shifted = logits - top
+        weights = jnp.exp(shifted)
+        weights_held[group] = jnp.where(hit, 0.0, weights).astype(jnp.bfloat16)
+        sums = [weights, weights * shifted, jnp.where(hit, logits, 0.0)]
+        sums = [jnp.sum(values, axis=1, keepdims=True) for values in sums]
+        stats[group] = jnp.where(
+            lane == 0, top, jnp.where(lane == 1, sums[0], jnp.where(lane == 2, sums[1], sums[2]))
+        )
+    compact[...] = jnp.dot(
+        selector[...], weights_held[...], preferred_element_type=jnp.float32
+    ).astype(jnp.bfloat16)
+
+
+def softmax_of(hidden, target, selector, head):
+    tokens, width = hidden.shape
+    cols = head.shape[1]
+    vmem, anywhere = pl.BlockSpec(memory_space=pltpu.VMEM), pl.BlockSpec(memory_space=pl.ANY)
+    return pl.pallas_call(
+        softmax_kernel,
+        out_shape=(
+            jax.ShapeDtypeStruct((SLOTS, cols), jnp.bfloat16),
+            jax.ShapeDtypeStruct((tokens, 128), jnp.float32),
+        ),
+        in_specs=[vmem, vmem, vmem, anywhere],
+        out_specs=(vmem, vmem),
+        scratch_shapes=[
+            pltpu.VMEM((BLOCKS, width // BLOCKS, cols), jnp.bfloat16),
+            pltpu.VMEM((tokens, cols), jnp.float32),
+            pltpu.VMEM((tokens, cols), jnp.bfloat16),
+            pltpu.SemaphoreType.DMA((BLOCKS,)),
+        ],
+        compiler_params=pltpu.CompilerParams(vmem_limit_bytes=58 * 1024 * 1024),
+        cost_estimate=pl.CostEstimate(
+            flops=2 * tokens * width * cols, bytes_accessed=width * (cols + tokens) * 2, transcendentals=tokens * cols
+        ),
+    )(hidden, target, selector, head)
 
 
 def per_device(hidden, head_weight, targets, kept_mask, old_logprob, advantage):
@@ -65,27 +126,13 @@
     scale = -(LOSS_SCALE / kept_total)
     hidden, kept_hidden, scale = lax.optimization_barrier((hidden, kept_hidden, scale))
 
-    logits = jnp.dot(hidden, head, preferred_element_type=jnp.float32)
     local_target = targets - offset
-    positions = jnp.arange(cols, dtype=jnp.int32)
-    hit = positions[None, :] == local_target[:, None]
-    local_top = jnp.max(logits, axis=1)
-    shifted = logits - local_top[:, None]
-    weights = jnp.exp(shifted)
-
-    compact = jnp.dot(
-        selector, jnp.where(hit, 0.0, weights).astype(jnp.bfloat16), preferred_element_type=jnp.float32
-    ).astype(jnp.bfloat16)
+    compact, stats = softmax_of(hidden, local_target[:, None], selector, head)
+    stats = stats[:, :4].T
+    local_top = stats[0]
+
     all_slots = lax.all_gather(compact, "y")
 
-    stats = jnp.stack(
-        [
-            local_top,
-            jnp.sum(weights, axis=1),
-            jnp.sum(weights * shifted, axis=1),
-            jnp.sum(jnp.where(hit, logits, 0.0), axis=1),
-        ]
-    )
     stats, compact = lax.optimization_barrier((stats, compact))
     stats = lax.all_gather(stats, ("x", "c"))
     tops, totals, moments, picks = (stats[:, i] for i in range(4))
@@ -119,13 +166,13 @@
     pair = mine.astype(jnp.float32) + lax.ppermute(other, "c", [(0, 1), (1, 0)]).astype(jnp.float32)
 
     all_rows = rows_of(all_slots[:, :KEEP_MOST], all_factors[:, :3, :KEEP_MOST])
-    part_head = lax.dot_general(
-        kept_hidden.reshape(Y * KEEP_MOST, Z * rows), all_rows.reshape(Y * KEEP_MOST, cols), (((0,), (0,)), ((), ())),
-        preferred_element_type=jnp.float32,
-    ).astype(jnp.bfloat16)
+    part_head = scale * lax.dot_general(
+        kept_hidden, all_rows, (((0, 1), (0, 1)), ((), ())), preferred_element_type=jnp.float32
+    )
+    part_head = part_head.astype(jnp.bfloat16)
     pair, part_head = lax.optimization_barrier((pair, part_head))
     sums = exchange(part_head.reshape(Z, rows, cols), "z")
-    grad_head = scale * jnp.sum(sums.astype(jnp.float32), axis=0)
+    grad_head = jnp.sum(sums.astype(jnp.float32), axis=0)
 
     total = lax.dynamic_index_in_dim(pair, at_x, 0, keepdims=False)
     for step in range(1, X):

time: 204 us -> 205 us (level)
  Pallas kernels: 0 us -> 8.38 us
  matrix products: 18.2 us -> 12.2 us
  other arithmetic: 8.98 us -> 5.57 us
  waiting for transfers between devices: 81.9 us -> 85.1 us
  local copies, waits for them, and re-layouts: 9.34 us -> 6.97 us
    pallas_call x0 -> x1, Pallas kernels: none -> 8.38 us  [softmax_of(): pl.pallas_call(softmax_kernel, out_shape=(jax.ShapeDtypeStruct((SLOTS, co...]
    dot_general x3 -> x1, matrix products: 10 us -> 2.37 us  [per_device(): lax.dot_general(kept_hidden, all_rows, (((0, 1), (0, 1)), ((), ())), pref...]
    all_gather x1, waiting for transfers between devices: 3.95 us -> 6.2 us  [per_device(): all_slots = lax.all_gather(compact, 'y')]
    slice x1 -> x2, local copies, waits for them, and re-layouts: 2.12 us -> 0.01 us  [per_device(): kept_hidden = to_all(kept_hidden, ('x', 'c'), V)[:, :, :SHARE]]
  transfers between devices with their start and end apart: 10 -> 10, of which waited for: 9 -> 9; matrix products, arithmetic and copies ran while one was open for 11% -> 9% of each run, Pallas kernels for 0% -> 0%
where the time goes in v15:
time: 205 us; the launch traced here: 204 us
  waiting for transfers between devices  85.1 us (42%)
  starting transfers between devices  41.2 us (20%)
  blocking collectives  29.5 us (14%)
  between operations  15 us (7%)
  matrix products  12.2 us (6%)
  Pallas kernels  8.38 us (4%)
  local copies, waits for them, and re-layouts  6.97 us (3%)
  other arithmetic  5.57 us (3%)
    all_gather x1, waiting for transfers between devices, per_device(): head = lax.all_gather(head_weight, ('y', 'z'), axis=0, tiled=True)  40.5 us
    all_to_all x4, waiting for transfers between devices, exchange(): return lax.all_to_all(parts, axes, split_axis=0, concat_axis=0)  32.4 us
    all_to_all x4, starting transfers between devices, exchange(): return lax.all_to_all(parts, axes, split_axis=0, concat_axis=0)  29.3 us
    all_to_all x1, blocking collectives, exchange(): return lax.all_to_all(parts, axes, split_axis=0, concat_axis=0)  16.7 us
    all_gather x1, blocking collectives, per_device(): stats = lax.all_gather(stats, ('x', 'c'))  12.8 us
    ppermute x3, starting transfers between devices, per_device(): lax.ppermute(sent, 'x', [(i, (i + step) % X) for i in range(X)])  9.8 us
    pallas_call x1, Pallas kernels, softmax_of(): pl.pallas_call(softmax_kernel, out_shape=(jax.ShapeDtypeStruct((SLOTS, co...  8.38 us
    all_gather x1, waiting for transfers between devices, per_device(): all_slots = lax.all_gather(compact, 'y')  6.2 us
  transfers between devices with their start and end apart: 10, of which 9 were waited for; matrix products, arithmetic and copies ran while one was open for 9% of the time, Pallas kernels for 0%

profile of v15, /device:TPU:6, one launch (start us, length us, event | category | flops | bytes accessed | tf_op | source)
XLA Modules:
  0.0 203.9 jit_solution(16032886886052819794)
XLA Ops:
  7.2 0.0 all-gather.6.cloned.1.call-start
  7.2 0.7 all-gather.6.cloned.1.call-update
  7.9 1.0 reduce-window.9
  8.9 0.1 slice.65
  9.0 1.3 convert_reduce_fusion.1
  10.3 0.1 slice_reduce_fusion.2
  10.4 0.7 broadcast_compare_fusion
  11.1 0.1 add_bitcast_fusion
  11.2 2.9 %fusion = bf16[16,5120]{1,0:T(8,128)(2,1)S(1)} fusion(bf16[256,5120]{1,0:T(8,128)(2,1)} %hidden, bf16[]{:T(256)} %convert_reduce_fusion.1, pred[16]{0:T(512)(128)(4,1)S(1)} %iota_compare_fusion.1, s32[256]{0:T(256)S(1)} %add_bitcast_fusion, s32[16]{0:T(128)S(1)} %iota_add_fusion, pred[256]{0:T(512)(128)(4,1)S(1)} %broadcast_compare_fusion), kind=kOutput, calls=%fused_computation.1 | convolution fusion | flops 42037248 | bytes 2786642 | tf_op jit(solution)/shard_map/dot_general | solution.py:119
  14.1 16.7 %all_to_all.25 = bf16[8,16,640]{2,1,0:T(8,128)(2,1)S(1)} all-to-all(bf16[8,16,640]{2,1,0:T(8,128)(2,1)S(1)} %bitcast.92), channel_id=1, replica_groups=mesh['y'=8,'z'=8,'x'=4,'c'=2] {'y'}, dimensions={0} | all-to-all | bytes 327680 | tf_op jit(solution)/shard_map/all_to_all | solution.py:34
  30.8 0.6 broadcast_in_dim_broadcast_in_dim_broadcast_in_dim.3
  31.4 10.4 %all-to-all-start.2 = ((f32[8,8,128]{2,1,0:T(8,128)}), f32[8,8,128]{2,1,0:T(8,128)S(1)}, u32[]{:S(2)}, u32[]{:S(2)}) async-start(f32[8,8,128]{2,1,0:T(8,128)} %broadcast_in_dim_broadcast_in_dim_broadcast_in_dim.3), calls=%async_computation.2 | async-start | bytes 65536 | tf_op jit(solution)/shard_map/all_to_all | solution.py:34
  41.8 0.0 copy-start.3
  41.8 8.0 %all-to-all-done.2 = f32[8,8,128]{2,1,0:T(8,128)S(1)} async-done(((f32[8,8,128]{2,1,0:T(8,128)}), f32[8,8,128]{2,1,0:T(8,128)S(1)}, u32[]{:S(2)}, u32[]{:S(2)}) %all-to-all-start.2) | async-done | bytes 32800 | tf_op jit(solution)/shard_map/all_to_all | solution.py:34
  49.8 1.3 broadcast_in_dim.79
  51.1 4.8 %all-to-all-start.1 = ((bf16[8,8,16,640]{3,1,2,0:T(8,128)(2,1)}), bf16[8,8,16,640]{3,1,2,0:T(8,128)(2,1)S(1)}, u32[]{:S(2)}, u32[]{:S(2)}) async-start(bf16[8,8,16,640]{3,1,2,0:T(8,128)(2,1)} %broadcast_in_dim.79), calls=%async_computation.1 | async-start | bytes 2621440 | tf_op jit(solution)/shard_map/all_to_all | solution.py:34
  55.9 0.0 all-gather.8.cloned.1.call-start
  55.9 0.0 copy-done.3
  55.9 0.8 copy.35.target
  56.7 0.6 fusion.17
  57.3 0.5 slice.69
  58.5 14.0 %all-to-all-done.1 = bf16[8,8,16,640]{3,1,2,0:T(8,128)(2,1)S(1)} async-done(((bf16[8,8,16,640]{3,1,2,0:T(8,128)(2,1)}), bf16[8,8,16,640]{3,1,2,0:T(8,128)(2,1)S(1)}, u32[]{:S(2)}, u32[]{:S(2)}) %all-to-all-start.1) | async-done | bytes 1310752 | tf_op jit(solution)/shard_map/all_to_all | solution.py:34
  72.6 40.5 %all-gather.6.cloned.1.call-done.head = bf16[5120,768]{1,0:T(8,128)(2,1)} async-done(((bf16[80,768]{1,0:T(8,128)(2,1)}), bf16[5120,768]{1,0:T(8,128)(2,1)}) %all-gather.6.cloned.1.call-update) | async-done | bytes 7864336 | tf_op jit(solution)/shard_map/all_gather | solution.py:108
  113.0 8.4 %shard_map.85 = (bf16[96,768]{1,0:T(8,128)(2,1)}, f32[256,128]{1,0:T(8,128)}) custom-call(bf16[256,5120]{1,0:T(8,128)(2,1)} %hidden, s32[256,1]{1,0:T(8,128)} %copy.35.target, bf16[96,256]{1,0:T(8,128)(2,1)} %get-tuple-element.49.selector, bf16[5120,768]{1,0:T(8,128)(2,1)} %all-gather.6.cloned.1.call-done.head), custom_call_target="tpu_custom_call" | custom-call | flops 2013265920 | bytes 10485760 | tf_op jit(solution)/shard_map/pallas_call | solution.py:83
  121.4 0.0 copy-done
  121.4 0.9 slice_bitcast_fusion
  122.3 0.1 slice_reduce_fusion
  122.5 0.0 all-gather.8.cloned.1.call-update
  122.5 0.1 copy.36
  122.6 12.8 %all-gather.2 = f32[8,4,256]{2,1,0:T(4,128)S(1)} all-gather(f32[1,4,256]{2,1,0:T(4,128)S(1)} %copy.36), channel_id=2, replica_groups=mesh['y'=8,'z'=8,'x'=4,'c'=2] {'x','c'}, dimensions={0}, use_global_device_ids=true | all-gather | bytes 36864 | tf_op jit(solution)/shard_map/all_gather | solution.py:137
  135.4 0.0 copy-done.2
  135.4 0.0 copy-done.4
  135.5 0.0 copy-done.5
  135.5 0.6 subtract_multiply_fusion
  136.1 0.1 select_reduce_fusion
  136.2 0.6 broadcast_in_dim.86
  136.9 6.4 %all-to-all-start.3 = ((f32[8,8,128]{2,1,0:T(8,128)}), f32[8,8,128]{2,1,0:T(8,128)S(1)}, u32[]{:S(2)}, u32[]{:S(2)}) async-start(f32[8,8,128]{2,1,0:T(8,128)} %broadcast_in_dim.86), calls=%async_computation.3 | async-start | bytes 65536 | tf_op jit(solution)/shard_map/all_to_all | solution.py:34
  143.3 5.8 %fusion.12 = bf16[96,5120]{1,0:T(8,128)(2,1)S(1)} fusion(bf16[5120,768]{1,0:T(8,128)(2,1)} %all-gather.6.cloned.1.call-done.head, bf16[96,768]{1,0:T(8,128)(2,1)} %get-tuple-element.19, f32[96]{0:T(128)S(1)} %get-tuple-element.47, bf16[96]{0:T(256)(128)(2,1)S(1)} %slice_bitcast_fusion.1, f32[768]{0:T(1024)S(1)} %iota_convert_fusion, ...), kind=kOutput, calls=%fused_computation.29 | convolution fusion | flops 755269632 | bytes 8998848 | tf_op jit(solution)/shard_map/dot_general | solution.py:156
  149.1 0.1 slice.108
  149.2 2.3 %all-to-all-done.3 = f32[8,8,128]{2,1,0:T(8,128)S(1)} async-done(((f32[8,8,128]{2,1,0:T(8,128)}), f32[8,8,128]{2,1,0:T(8,128)S(1)}, u32[]{:S(2)}, u32[]{:S(2)}) %all-to-all-start.3) | async-done | bytes 32800 | tf_op jit(solution)/shard_map/all_to_all | solution.py:34
  151.5 0.1 copy.77
  151.7 0.0 slice-start
  151.7 2.1 %collective-permute-start = (bf16[4,80,640]{2,1,0:T(8,128)(2,1)S(1)}, bf16[4,80,640]{2,1,0:T(8,128)(2,1)S(1)}, u32[]{:S(2)}, u32[]{:S(2)}) collective-permute-start(bf16[4,80,640]{2,1,0:T(8,128)(2,1)S(1)} %dynamic-slice_bitcast_fusion), channel_id=1, source_target_pairs={{0,1},{1,0},{2,3},{3,2},{4,5},{5,4},{6,7},{7,6},{8,9},{9,8},{10,11... | collective-permute-start | bytes 1228808 | tf_op jit(solution)/shard_map/ppermute | solution.py:166
  153.7 0.1 copy.43
  153.8 0.1 copy.42
  153.9 0.1 copy.41
  154.0 1.4 collective-permute-done
  155.4 0.1 convert_add_fusion
  155.5 6.2 %all-gather.8.cloned.1.call-done = bf16[768,768]{1,0:T(8,128)(2,1)} async-done(((bf16[96,768]{1,0:T(8,128)(2,1)}), bf16[768,768]{1,0:T(8,128)(2,1)}) %all-gather.8.cloned.1.call-update) | async-done | bytes 1179664 | tf_op jit(solution)/shard_map/all_gather | solution.py:134
  161.7 1.3 slice.94
  163.0 0.0 slice-done
  163.0 2.4 %fusion.1 = bf16[640,768]{1,0:T(8,128)(2,1)} fusion(bf16[8,80,640]{2,0,1:T(8,128)(2,1)S(1)} %bitcast.85, bf16[8,80,768]{2,1,0:T(8,128)(2,1)S(1)} %slice.94, f32[8,80]{0,1:T(8,128)S(1)} %copy.43, bf16[8,80]{0,1:T(8,128)(2,1)S(1)} %copy.42, f32[8,80]{0,1:T(8,128)S(1)} %copy.41, f32[768]{0:T(1024)S(1)} %iota_convert_fusion, f32[]{:T(128)} %bitcast.5), kind=kOutput, calls=%fused_computation.3 | convolution fusion | flops 632094720 | bytes 2794756 | tf_op jit(solution)/shard_map/dot_general | solution.py:169
  165.4 7.8 %all-to-all-start.4 = ((bf16[8,80,768]{2,1,0:T(8,128)(2,1)}), bf16[8,80,768]{2,1,0:T(8,128)(2,1)S(1)}, u32[]{:S(2)}, u32[]{:S(2)}) async-start(bf16[8,80,768]{2,1,0:T(8,128)(2,1)} %bitcast.32), calls=%async_computation.4 | async-start | bytes 1966080 | tf_op jit(solution)/shard_map/all_to_all | solution.py:34
  173.2 2.7 %collective-permute-start.3 = (f32[80,640]{1,0:T(8,128)S(1)}, f32[80,640]{1,0:T(8,128)S(1)}, u32[]{:S(2)}, u32[]{:S(2)}) collective-permute-start(f32[80,640]{1,0:T(8,128)S(1)} %get-tuple-element.36), channel_id=1, source_target_pairs={{0,6},{2,0},{4,2},{6,4},{1,7},{3,1},{5,3},{7,5},{8,14},{10,8},{12,... | collective-permute-start | bytes 614408 | tf_op jit(solution)/shard_map/ppermute | solution.py:180
  175.9 3.0 %collective-permute-start.2 = (f32[80,640]{1,0:T(8,128)S(1)}, f32[80,640]{1,0:T(8,128)S(1)}, u32[]{:S(2)}, u32[]{:S(2)}) collective-permute-start(f32[80,640]{1,0:T(8,128)S(1)} %get-tuple-element.37), channel_id=1, source_target_pairs={{0,4},{2,6},{4,0},{6,2},{1,5},{3,7},{5,1},{7,3},{8,12},{10,14},{12... | collective-permute-start | bytes 614408 | tf_op jit(solution)/shard_map/ppermute | solution.py:180
  178.9 4.1 %collective-permute-start.1 = (f32[80,640]{1,0:T(8,128)S(1)}, f32[80,640]{1,0:T(8,128)S(1)}, u32[]{:S(2)}, u32[]{:S(2)}) collective-permute-start(f32[80,640]{1,0:T(8,128)S(1)} %get-tuple-element.35), channel_id=1, source_target_pairs={{0,2},{2,4},{4,6},{6,0},{1,3},{3,5},{5,7},{7,1},{8,10},{10,12},{12... | collective-permute-start | bytes 614408 | tf_op jit(solution)/shard_map/ppermute | solution.py:180
  183.0 0.0 copy-done.1
  183.0 0.0 collective-permute-done.3
  183.0 2.0 collective-permute-done.2
  185.0 2.0 collective-permute-done.1
  187.0 0.1 subtract_convert_fusion
  187.1 1.1 convolution_multiply_fusion
  188.2 8.0 %all-to-all-done.4 = bf16[8,80,768]{2,1,0:T(8,128)(2,1)S(1)} async-done(((bf16[8,80,768]{2,1,0:T(8,128)(2,1)}), bf16[8,80,768]{2,1,0:T(8,128)(2,1)S(1)}, u32[]{:S(2)}, u32[]{:S(2)}) %all-to-all-start.4) | async-done | bytes 983072 | tf_op jit(solution)/shard_map/all_to_all | solution.py:34
  196.3 0.8 convert_reduce_fusion
  (25 shorter events, 0.4 us)
Async XLA Ops:
  7.2 105.9 %all-gather.6.cloned.1.call-start = ((), (), s32[]{:S(2)}) async-start(), calls=%async_computation.5 | async-start | bytes 7987200 | tf_op jit(solution)/shard_map/all_gather | solution.py:108
  31.4 18.4 %all-to-all-start.2 = ((f32[8,8,128]{2,1,0:T(8,128)}), f32[8,8,128]{2,1,0:T(8,128)S(1)}, u32[]{:S(2)}, u32[]{:S(2)}) async-start(f32[8,8,128]{2,1,0:T(8,128)} %broadcast_in_dim_broadcast_in_dim_broadcast_in_dim.3), calls=%async_computation.2 | async-start | bytes 65536 | tf_op jit(solution)/shard_map/all_to_all | solution.py:34
  41.8 14.1 %copy-start.3 = (s32[256]{0:T(256)S(1)}, s32[256]{0:T(256)}, u32[]{:S(2)}) copy-start(s32[256]{0:T(256)} %param.8) | copy-start | bytes 3076
  51.1 21.5 %all-to-all-start.1 = ((bf16[8,8,16,640]{3,1,2,0:T(8,128)(2,1)}), bf16[8,8,16,640]{3,1,2,0:T(8,128)(2,1)S(1)}, u32[]{:S(2)}, u32[]{:S(2)}) async-start(bf16[8,8,16,640]{3,1,2,0:T(8,128)(2,1)} %broadcast_in_dim.79), calls=%async_computation.1 | async-start | bytes 2621440 | tf_op jit(solution)/shard_map/all_to_all | solution.py:34
  55.9 105.9 %all-gather.8.cloned.1.call-start = ((), (), s32[]{:S(2)}) async-start(), calls=%async_computation.6 | async-start | bytes 1327104 | tf_op jit(solution)/shard_map/all_gather | solution.py:134
  72.6 48.9 %copy-start = (bf16[8,8,16,640]{3,1,2,0:T(8,128)(2,1)}, bf16[8,8,16,640]{3,1,2,0:T(8,128)(2,1)S(1)}, u32[]{:S(2)}) copy-start(bf16[8,8,16,640]{3,1,2,0:T(8,128)(2,1)S(1)} %all-to-all-done.1) | copy-start | bytes 3932164
  113.0 22.4 %copy-start.2 = (s32[256]{0:T(256)S(1)}, s32[256]{0:T(256)}, u32[]{:S(2)}) copy-start(s32[256]{0:T(256)} %param.9) | copy-start | bytes 3076
  113.0 22.4 %copy-start.4 = (f32[256]{0:T(256)S(1)}, f32[256]{0:T(256)}, u32[]{:S(2)}) copy-start(f32[256]{0:T(256)} %param.11) | copy-start | bytes 3076
  113.0 22.4 %copy-start.5 = (f32[256]{0:T(256)S(1)}, f32[256]{0:T(256)}, u32[]{:S(2)}) copy-start(f32[256]{0:T(256)} %param.10) | copy-start | bytes 3076
  136.9 14.7 %all-to-all-start.3 = ((f32[8,8,128]{2,1,0:T(8,128)}), f32[8,8,128]{2,1,0:T(8,128)S(1)}, u32[]{:S(2)}, u32[]{:S(2)}) async-start(f32[8,8,128]{2,1,0:T(8,128)} %broadcast_in_dim.86), calls=%async_computation.3 | async-start | bytes 65536 | tf_op jit(solution)/shard_map/all_to_all | solution.py:34
  151.7 11.3 %slice-start = ((bf16[8,8,16,640]{3,1,2,0:T(8,128)(2,1)}), bf16[8,8,10,640]{3,1,2,0:T(8,128)(2,1)S(1)}, s32[]{:S(2)}) async-start(bf16[8,8,16,640]{3,1,2,0:T(8,128)(2,1)} %copy-done), calls=%async_computation.7 | async-start | bytes 1638400 | tf_op jit(solution)/shard_map/slice | solution.py:123
  151.7 3.8 %collective-permute-start = (bf16[4,80,640]{2,1,0:T(8,128)(2,1)S(1)}, bf16[4,80,640]{2,1,0:T(8,128)(2,1)S(1)}, u32[]{:S(2)}, u32[]{:S(2)}) collective-permute-start(bf16[4,80,640]{2,1,0:T(8,128)(2,1)S(1)} %dynamic-slice_bitcast_fusion), channel_id=1, source_target_pairs={{0,1},{1,0},{2,3},{3,2},{4,5},{5,4},{6,7},{7,6},{8,9},{9,8},{10,11... | collective-permute-start | bytes 1228808 | tf_op jit(solution)/shard_map/ppermute | solution.py:166
  165.4 17.6 %copy-start.1 = (bf16[96,256]{1,0:T(8,128)(2,1)S(1)}, bf16[96,256]{1,0:T(8,128)(2,1)}, u32[]{:S(2)}) copy-start(bf16[96,256]{1,0:T(8,128)(2,1)} %get-tuple-element.49.selector) | copy-start | bytes 147460
  165.4 30.9 %all-to-all-start.4 = ((bf16[8,80,768]{2,1,0:T(8,128)(2,1)}), bf16[8,80,768]{2,1,0:T(8,128)(2,1)S(1)}, u32[]{:S(2)}, u32[]{:S(2)}) async-start(bf16[8,80,768]{2,1,0:T(8,128)(2,1)} %bitcast.32), calls=%async_computation.4 | async-start | bytes 1966080 | tf_op jit(solution)/shard_map/all_to_all | solution.py:34
  173.2 9.8 %collective-permute-start.3 = (f32[80,640]{1,0:T(8,128)S(1)}, f32[80,640]{1,0:T(8,128)S(1)}, u32[]{:S(2)}, u32[]{:S(2)}) collective-permute-start(f32[80,640]{1,0:T(8,128)S(1)} %get-tuple-element.36), channel_id=1, source_target_pairs={{0,6},{2,0},{4,2},{6,4},{1,7},{3,1},{5,3},{7,5},{8,14},{10,8},{12,... | collective-permute-start | bytes 614408 | tf_op jit(solution)/shard_map/ppermute | solution.py:180
  175.9 9.2 %collective-permute-start.2 = (f32[80,640]{1,0:T(8,128)S(1)}, f32[80,640]{1,0:T(8,128)S(1)}, u32[]{:S(2)}, u32[]{:S(2)}) collective-permute-start(f32[80,640]{1,0:T(8,128)S(1)} %get-tuple-element.37), channel_id=1, source_target_pairs={{0,4},{2,6},{4,0},{6,2},{1,5},{3,7},{5,1},{7,3},{8,12},{10,14},{12... | collective-permute-start | bytes 614408 | tf_op jit(solution)/shard_map/ppermute | solution.py:180
  178.9 8.1 %collective-permute-start.1 = (f32[80,640]{1,0:T(8,128)S(1)}, f32[80,640]{1,0:T(8,128)S(1)}, u32[]{:S(2)}, u32[]{:S(2)}) collective-permute-start(f32[80,640]{1,0:T(8,128)S(1)} %get-tuple-element.35), channel_id=1, source_target_pairs={{0,2},{2,4},{4,6},{6,0},{1,3},{3,5},{5,7},{7,1},{8,10},{10,12},{12... | collective-permute-start | bytes 614408 | tf_op jit(solution)/shard_map/ppermute | solution.py:180
Sparse Core Ops, SparseCore 0:
  11.1 101.9 all-gather.5
  122.6 39.0 all-gather.7

commit v16 on v13

--- a/solution.py
+++ b/solution.py
@@ -119,13 +119,13 @@
     pair = mine.astype(jnp.float32) + lax.ppermute(other, "c", [(0, 1), (1, 0)]).astype(jnp.float32)
 
     all_rows = rows_of(all_slots[:, :KEEP_MOST], all_factors[:, :3, :KEEP_MOST])
-    part_head = lax.dot_general(
-        kept_hidden.reshape(Y * KEEP_MOST, Z * rows), all_rows.reshape(Y * KEEP_MOST, cols), (((0,), (0,)), ((), ())),
-        preferred_element_type=jnp.float32,
-    ).astype(jnp.bfloat16)
+    part_head = scale * lax.dot_general(
+        kept_hidden, all_rows, (((0, 1), (0, 1)), ((), ())), preferred_element_type=jnp.float32
+    )
+    part_head = part_head.astype(jnp.bfloat16)
     pair, part_head = lax.optimization_barrier((pair, part_head))
     sums = exchange(part_head.reshape(Z, rows, cols), "z")
-    grad_head = scale * jnp.sum(sums.astype(jnp.float32), axis=0)
+    grad_head = jnp.sum(sums.astype(jnp.float32), axis=0)
 
     total = lax.dynamic_index_in_dim(pair, at_x, 0, keepdims=False)
     for step in range(1, X):

time: 204 us -> 204 us (level)
  no operation moved by 1% of the time
where the time goes in v16:
time: 204 us
  waiting for transfers between devices  81.9 us (40%)
  starting transfers between devices  40.7 us (20%)
  blocking collectives  29.5 us (14%)
  matrix products  18.2 us (9%)
  between operations  14.9 us (7%)
  local copies, waits for them, and re-layouts  9.34 us (5%)
  other arithmetic  8.95 us (4%)
    all_gather x1, waiting for transfers between devices, per_device(): head = lax.all_gather(head_weight, ('y', 'z'), axis=0, tiled=True)  39.9 us
    all_to_all x4, waiting for transfers between devices, exchange(): return lax.all_to_all(parts, axes, split_axis=0, concat_axis=0)  32.2 us
    all_to_all x4, starting transfers between devices, exchange(): return lax.all_to_all(parts, axes, split_axis=0, concat_axis=0)  29 us
    all_to_all x1, blocking collectives, exchange(): return lax.all_to_all(parts, axes, split_axis=0, concat_axis=0)  16.7 us
    all_gather x1, blocking collectives, per_device(): stats = lax.all_gather(stats, ('x', 'c'))  12.8 us
    ppermute x3, starting transfers between devices, per_device(): lax.ppermute(sent, 'x', [(i, (i + step) % X) for i in range(X)])  9.8 us
    dot_general x1, matrix products, per_device(): lax.dot_general(own_rows, head, (((1,), (1,)), ((), ())), preferred_eleme...  5.82 us
    dot_general x1, matrix products, per_device(): logits = jnp.dot(hidden, head, preferred_element_type=jnp.float32)  5.5 us
  transfers between devices with their start and end apart: 10, of which 9 were waited for; matrix products, arithmetic and copies ran while one was open for 11% of the time, Pallas kernels for 0%

profile of v16, /device:TPU:6, one launch (start us, length us, event | category | flops | bytes accessed | tf_op | source)
XLA Modules:
  0.0 203.6 jit_solution(17212741675626693340)
XLA Ops:
  7.2 0.0 copy-start
  7.2 0.0 all-gather.6.cloned.1.call-start
  7.2 0.7 all-gather.6.cloned.1.call-update
  7.9 1.0 reduce-window.9
  8.9 0.1 slice.60
  9.1 1.3 convert_reduce_fusion.1
  10.3 0.1 slice_reduce_fusion.1
  10.5 0.7 broadcast_compare_fusion
  11.1 0.1 add_bitcast_fusion
  11.2 0.0 copy-done
  11.2 1.1 fusion
  12.4 0.0 copy-start.3
  12.4 16.7 %all_to_all.25 = bf16[8,16,640]{2,1,0:T(8,128)(2,1)S(1)} all-to-all(bf16[8,16,640]{2,1,0:T(8,128)(2,1)S(1)} %bitcast.93), channel_id=1, replica_groups=mesh['y'=8,'z'=8,'x'=4,'c'=2] {'y'}, dimensions={0} | all-to-all | bytes 327680 | tf_op jit(solution)/shard_map/all_to_all | solution.py:30
  29.1 0.6 broadcast_in_dim_broadcast_in_dim_broadcast_in_dim.3
  29.7 10.3 %all-to-all-start.2 = ((f32[8,8,128]{2,1,0:T(8,128)}), f32[8,8,128]{2,1,0:T(8,128)S(1)}, u32[]{:S(2)}, u32[]{:S(2)}) async-start(f32[8,8,128]{2,1,0:T(8,128)} %broadcast_in_dim_broadcast_in_dim_broadcast_in_dim.3), calls=%async_computation.2 | async-start | bytes 65536 | tf_op jit(solution)/shard_map/all_to_all | solution.py:30
  40.1 8.0 %all-to-all-done.2 = f32[8,8,128]{2,1,0:T(8,128)S(1)} async-done(((f32[8,8,128]{2,1,0:T(8,128)}), f32[8,8,128]{2,1,0:T(8,128)S(1)}, u32[]{:S(2)}, u32[]{:S(2)}) %all-to-all-start.2) | async-done | bytes 32800 | tf_op jit(solution)/shard_map/all_to_all | solution.py:30
  48.1 1.2 broadcast_in_dim.85
  49.2 4.8 %all-to-all-start.1 = ((bf16[8,8,16,640]{3,1,2,0:T(8,128)(2,1)}), bf16[8,8,16,640]{3,1,2,0:T(8,128)(2,1)}, u32[]{:S(2)}, u32[]{:S(2)}) async-start(bf16[8,8,16,640]{3,1,2,0:T(8,128)(2,1)} %broadcast_in_dim.85), calls=%async_computation.1 | async-start | bytes 2621440 | tf_op jit(solution)/shard_map/all_to_all | solution.py:30
  54.0 0.0 all-gather.8.cloned.1.call-start
  54.0 0.0 copy-done.3
  54.1 0.5 slice.64
  55.3 15.5 %all-to-all-done.1 = bf16[8,8,16,640]{3,1,2,0:T(8,128)(2,1)} async-done(((bf16[8,8,16,640]{3,1,2,0:T(8,128)(2,1)}), bf16[8,8,16,640]{3,1,2,0:T(8,128)(2,1)}, u32[]{:S(2)}, u32[]{:S(2)}) %all-to-all-start.1) | async-done | bytes 1310752 | tf_op jit(solution)/shard_map/all_to_all | solution.py:30
  70.8 2.1 %slice.78 = bf16[8,8,10,640]{3,1,2,0:T(8,128)(2,1)} slice(bf16[8,8,16,640]{3,1,2,0:T(8,128)(2,1)} %all-to-all-done.1), slice={[0:8], [0:8], [0:10], [0:640]} | slice | bytes 1638400 | tf_op jit(solution)/shard_map/slice | solution.py:62
  73.0 0.0 copy-start.2
  73.0 39.9 %all-gather.6.cloned.1.call-done = bf16[5120,768]{1,0:T(8,128)(2,1)} async-done(((bf16[80,768]{1,0:T(8,128)(2,1)}), bf16[5120,768]{1,0:T(8,128)(2,1)}) %all-gather.6.cloned.1.call-update) | async-done | bytes 7864336 | tf_op jit(solution)/shard_map/all_gather | solution.py:47
  112.9 5.5 %fusion.48 = (f32[256]{0:T(256)S(1)}, f32[256,768]{1,0:T(8,128)S(1)}) fusion(bf16[256,5120]{1,0:T(8,128)(2,1)S(1)} %copy-done, bf16[5120,768]{1,0:T(8,128)(2,1)} %all-gather.6.cloned.1.call-done), kind=kOutput, calls=%fused_computation.95 | convolution fusion | flops 2013462272 | bytes 11273216 | tf_op jit(solution)/shard_map/dot_general | solution.py:68
  118.4 0.5 exponential_reduce_fusion
  118.8 1.0 convolution_convert_fusion
  119.9 0.0 all-gather.8.cloned.1.call-update
  119.9 12.8 %all-gather.2 = f32[8,4,256]{2,1,0:T(4,128)S(1)} all-gather(f32[1,4,256]{2,1,0:T(4,128)S(1)} %bitcast.94), channel_id=2, replica_groups=mesh['y'=8,'z'=8,'x'=4,'c'=2] {'x','c'}, dimensions={0}, use_global_device_ids=true | all-gather | bytes 36864 | tf_op jit(solution)/shard_map/all_gather | solution.py:90
  132.8 0.0 copy-done.2
  132.8 0.0 copy-done.4
  132.8 0.0 copy-done.5
  132.8 0.6 subtract_multiply_fusion
  133.4 0.1 select_reduce_fusion.1
  133.6 0.6 broadcast_in_dim.92
  134.2 6.4 %all-to-all-start.3 = ((f32[8,8,128]{2,1,0:T(8,128)}), f32[8,8,128]{2,1,0:T(8,128)S(1)}, u32[]{:S(2)}, u32[]{:S(2)}) async-start(f32[8,8,128]{2,1,0:T(8,128)} %broadcast_in_dim.92), calls=%async_computation.3 | async-start | bytes 65536 | tf_op jit(solution)/shard_map/all_to_all | solution.py:30
  140.6 5.8 %fusion.21 = bf16[88,5120]{1,0:T(8,128)(2,1)S(1)} fusion(bf16[5120,768]{1,0:T(8,128)(2,1)} %all-gather.6.cloned.1.call-done, bf16[88,768]{1,0:T(8,128)(2,1)} %convolution_convert_fusion, f32[88]{0:T(128)S(1)} %get-tuple-element.46, bf16[88]{0:T(256)(128)(2,1)S(1)} %slice_bitcast_fusion, f32[768]{0:T(1024)S(1)} %iota_convert_fusion, f32[88]{0:T(128)S(1)} %get-tuple-element.45), kind=kOutput, calls=%fused_computation.43 | convolution fusion | flops 692330496 | bytes 8904560 | tf_op jit(solution)/shard_map/dot_general | solution.py:109
  146.5 0.1 slice.98
  146.5 2.5 %all-to-all-done.3 = f32[8,8,128]{2,1,0:T(8,128)S(1)} async-done(((f32[8,8,128]{2,1,0:T(8,128)}), f32[8,8,128]{2,1,0:T(8,128)S(1)}, u32[]{:S(2)}, u32[]{:S(2)}) %all-to-all-start.3) | async-done | bytes 32800 | tf_op jit(solution)/shard_map/all_to_all | solution.py:30
  149.0 0.1 copy.63
  149.0 0.0 copy-start.1
  149.1 0.9 copy-done.1
  150.0 1.9 collective-permute-start
  151.9 0.1 copy.35
  152.0 0.7 copy.34
  152.7 0.1 copy.33
  152.8 1.0 collective-permute-done
  153.8 1.2 convert_add_fusion
  155.0 4.0 %all-gather.8.cloned.1.call-done = bf16[704,768]{1,0:T(8,128)(2,1)} async-done(((bf16[88,768]{1,0:T(8,128)(2,1)}), bf16[704,768]{1,0:T(8,128)(2,1)}) %all-gather.8.cloned.1.call-update) | async-done | bytes 1081360 | tf_op jit(solution)/shard_map/all_gather | solution.py:79
  158.9 1.3 slice.86
  160.2 3.5 %fusion.1 = bf16[640,768]{1,0:T(8,128)(2,1)} fusion(bf16[8,80,640]{2,0,1:T(8,128)(2,1)} %bitcast.91, bf16[8,80,768]{2,1,0:T(8,128)(2,1)S(1)} %slice.86, f32[8,80]{0,1:T(8,128)S(1)} %copy.35, bf16[8,80]{0,1:T(8,128)(2,1)} %copy.34, f32[8,80]{0,1:T(8,128)S(1)} %copy.33, f32[768]{0:T(1024)S(1)} %iota_convert_fusion, f32[]{:T(128)} %bitcast.5), kind=kOutput, calls=%fused_computation.3 | convolution fusion | flops 632094720 | bytes 2794756 | tf_op jit(solution)/shard_map/dot_general | solution.py:122
  163.7 7.5 %all-to-all-start.4 = ((bf16[8,80,768]{2,1,0:T(8,128)(2,1)}), bf16[8,80,768]{2,1,0:T(8,128)(2,1)}, u32[]{:S(2)}, u32[]{:S(2)}) async-start(bf16[8,80,768]{2,1,0:T(8,128)(2,1)} %bitcast.89), calls=%async_computation.4 | async-start | bytes 1966080 | tf_op jit(solution)/shard_map/all_to_all | solution.py:30
  171.2 0.8 dynamic-slice_bitcast_fusion.3
  172.0 2.7 %collective-permute-start.3 = (f32[80,640]{1,0:T(8,128)}, f32[80,640]{1,0:T(8,128)}, u32[]{:S(2)}, u32[]{:S(2)}) collective-permute-start(f32[80,640]{1,0:T(8,128)} %get-tuple-element.35), channel_id=1, source_target_pairs={{0,6},{2,0},{4,2},{6,4},{1,7},{3,1},{5,3},{7,5},{8,14},{10,8},{12,... | collective-permute-start | bytes 614408 | tf_op jit(solution)/shard_map/ppermute | solution.py:133
  174.7 2.9 %collective-permute-start.2 = (f32[80,640]{1,0:T(8,128)}, f32[80,640]{1,0:T(8,128)}, u32[]{:S(2)}, u32[]{:S(2)}) collective-permute-start(f32[80,640]{1,0:T(8,128)} %get-tuple-element.36), channel_id=1, source_target_pairs={{0,4},{2,6},{4,0},{6,2},{1,5},{3,7},{5,1},{7,3},{8,12},{10,14},{12... | collective-permute-start | bytes 614408 | tf_op jit(solution)/shard_map/ppermute | solution.py:133
  177.6 4.3 %collective-permute-start.1 = (f32[80,640]{1,0:T(8,128)}, f32[80,640]{1,0:T(8,128)}, u32[]{:S(2)}, u32[]{:S(2)}) collective-permute-start(f32[80,640]{1,0:T(8,128)} %get-tuple-element.34), channel_id=1, source_target_pairs={{0,2},{2,4},{4,6},{6,0},{1,3},{3,5},{5,7},{7,1},{8,10},{10,12},{12... | collective-permute-start | bytes 614408 | tf_op jit(solution)/shard_map/ppermute | solution.py:133
  181.9 0.0 collective-permute-done.3
  181.9 2.3 %collective-permute-done.2 = f32[80,640]{1,0:T(8,128)} collective-permute-done((f32[80,640]{1,0:T(8,128)}, f32[80,640]{1,0:T(8,128)}, u32[]{:S(2)}, u32[]{:S(2)}) %collective-permute-start.2) | collective-permute-done | bytes 204832 | tf_op jit(solution)/shard_map/ppermute | solution.py:133
  184.2 2.0 collective-permute-done.1
  186.2 1.2 subtract_convert_fusion
  187.4 1.2 convolution_multiply_fusion
  188.5 6.2 %all-to-all-done.4 = bf16[8,80,768]{2,1,0:T(8,128)(2,1)} async-done(((bf16[8,80,768]{2,1,0:T(8,128)(2,1)}), bf16[8,80,768]{2,1,0:T(8,128)(2,1)}, u32[]{:S(2)}, u32[]{:S(2)}) %all-to-all-start.4) | async-done | bytes 983072 | tf_op jit(solution)/shard_map/all_to_all | solution.py:30
  194.7 2.0 %convert_reduce_fusion = f32[80,768]{1,0:T(8,128)} fusion(bf16[8,80,768]{2,1,0:T(8,128)(2,1)} %all-to-all-done.4), kind=kLoop, calls=%fused_computation.4 | loop fusion | flops 921600 | bytes 1228800 | tf_op jit(solution)/shard_map/reduce_sum | solution.py:128
  (23 shorter events, 0.4 us)
Async XLA Ops:
  7.2 4.1 %copy-start = (bf16[256,5120]{1,0:T(8,128)(2,1)S(1)}, bf16[256,5120]{1,0:T(8,128)(2,1)}, u32[]{:S(2)}) copy-start(bf16[256,5120]{1,0:T(8,128)(2,1)} %param.6) | copy-start | bytes 7864324
  7.2 105.7 %all-gather.6.cloned.1.call-start = ((), (), s32[]{:S(2)}) async-start(), calls=%async_computation.5 | async-start | bytes 7987200 | tf_op jit(solution)/shard_map/all_gather | solution.py:47
  12.4 41.7 %copy-start.3 = (s32[256]{0:T(256)S(1)}, s32[256]{0:T(256)}, u32[]{:S(2)}) copy-start(s32[256]{0:T(256)} %param.8) | copy-start | bytes 3076
  29.7 18.4 %all-to-all-start.2 = ((f32[8,8,128]{2,1,0:T(8,128)}), f32[8,8,128]{2,1,0:T(8,128)S(1)}, u32[]{:S(2)}, u32[]{:S(2)}) async-start(f32[8,8,128]{2,1,0:T(8,128)} %broadcast_in_dim_broadcast_in_dim_broadcast_in_dim.3), calls=%async_computation.2 | async-start | bytes 65536 | tf_op jit(solution)/shard_map/all_to_all | solution.py:30
  49.2 21.6 %all-to-all-start.1 = ((bf16[8,8,16,640]{3,1,2,0:T(8,128)(2,1)}), bf16[8,8,16,640]{3,1,2,0:T(8,128)(2,1)}, u32[]{:S(2)}, u32[]{:S(2)}) async-start(bf16[8,8,16,640]{3,1,2,0:T(8,128)(2,1)} %broadcast_in_dim.85), calls=%async_computation.1 | async-start | bytes 2621440 | tf_op jit(solution)/shard_map/all_to_all | solution.py:30
  54.0 104.9 %all-gather.8.cloned.1.call-start = ((), (), s32[]{:S(2)}) async-start(), calls=%async_computation.6 | async-start | bytes 1216512 | tf_op jit(solution)/shard_map/all_gather | solution.py:79
  73.0 59.8 %copy-start.2 = (s32[256]{0:T(256)S(1)}, s32[256]{0:T(256)}, u32[]{:S(2)}) copy-start(s32[256]{0:T(256)} %param.9) | copy-start | bytes 3076
  73.0 59.8 %copy-start.4 = (f32[256]{0:T(256)S(1)}, f32[256]{0:T(256)}, u32[]{:S(2)}) copy-start(f32[256]{0:T(256)} %param.11) | copy-start | bytes 3076
  73.0 59.8 %copy-start.5 = (f32[256]{0:T(256)S(1)}, f32[256]{0:T(256)}, u32[]{:S(2)}) copy-start(f32[256]{0:T(256)} %param.10) | copy-start | bytes 3076
  134.2 14.8 %all-to-all-start.3 = ((f32[8,8,128]{2,1,0:T(8,128)}), f32[8,8,128]{2,1,0:T(8,128)S(1)}, u32[]{:S(2)}, u32[]{:S(2)}) async-start(f32[8,8,128]{2,1,0:T(8,128)} %broadcast_in_dim.92), calls=%async_computation.3 | async-start | bytes 65536 | tf_op jit(solution)/shard_map/all_to_all | solution.py:30
  149.0 0.9 copy-start.1
  150.0 3.8 %collective-permute-start = (bf16[4,80,640]{2,1,0:T(8,128)(2,1)S(1)}, bf16[4,80,640]{2,1,0:T(8,128)(2,1)}, u32[]{:S(2)}, u32[]{:S(2)}) collective-permute-start(bf16[4,80,640]{2,1,0:T(8,128)(2,1)S(1)} %dynamic-slice_bitcast_fusion), channel_id=1, source_target_pairs={{0,1},{1,0},{2,3},{3,2},{4,5},{5,4},{6,7},{7,6},{8,9},{9,8},{10,11... | collective-permute-start | bytes 1228808 | tf_op jit(solution)/shard_map/ppermute | solution.py:119
  163.7 31.0 %all-to-all-start.4 = ((bf16[8,80,768]{2,1,0:T(8,128)(2,1)}), bf16[8,80,768]{2,1,0:T(8,128)(2,1)}, u32[]{:S(2)}, u32[]{:S(2)}) async-start(bf16[8,80,768]{2,1,0:T(8,128)(2,1)} %bitcast.89), calls=%async_computation.4 | async-start | bytes 1966080 | tf_op jit(solution)/shard_map/all_to_all | solution.py:30
  172.0 9.8 %collective-permute-start.3 = (f32[80,640]{1,0:T(8,128)}, f32[80,640]{1,0:T(8,128)}, u32[]{:S(2)}, u32[]{:S(2)}) collective-permute-start(f32[80,640]{1,0:T(8,128)} %get-tuple-element.35), channel_id=1, source_target_pairs={{0,6},{2,0},{4,2},{6,4},{1,7},{3,1},{5,3},{7,5},{8,14},{10,8},{12,... | collective-permute-start | bytes 614408 | tf_op jit(solution)/shard_map/ppermute | solution.py:133
  174.7 9.5 %collective-permute-start.2 = (f32[80,640]{1,0:T(8,128)}, f32[80,640]{1,0:T(8,128)}, u32[]{:S(2)}, u32[]{:S(2)}) collective-permute-start(f32[80,640]{1,0:T(8,128)} %get-tuple-element.36), channel_id=1, source_target_pairs={{0,4},{2,6},{4,0},{6,2},{1,5},{3,7},{5,1},{7,3},{8,12},{10,14},{12... | collective-permute-start | bytes 614408 | tf_op jit(solution)/shard_map/ppermute | solution.py:133
  177.6 8.6 %collective-permute-start.1 = (f32[80,640]{1,0:T(8,128)}, f32[80,640]{1,0:T(8,128)}, u32[]{:S(2)}, u32[]{:S(2)}) collective-permute-start(f32[80,640]{1,0:T(8,128)} %get-tuple-element.34), channel_id=1, source_target_pairs={{0,2},{2,4},{4,6},{6,0},{1,3},{3,5},{5,7},{7,1},{8,10},{10,12},{12... | collective-permute-start | bytes 614408 | tf_op jit(solution)/shard_map/ppermute | solution.py:133
Sparse Core Ops, SparseCore 0:
  11.1 101.7 all-gather.5
  120.0 38.8 all-gather.7

commit v17 on v16

--- a/solution.py
+++ b/solution.py
@@ -1,12 +1,14 @@
 import jax
 import jax.numpy as jnp
 from jax import lax
+from jax.experimental import pallas as pl
+from jax.experimental.pallas import tpu as pltpu
 from jax.sharding import Mesh, PartitionSpec as P
 
 Y, Z, X, C = 8, 8, 4, 2
 V = X * C
 KEEP_MOST = 80
-SPARE = 8
+SPARE = 16
 SLOTS = KEEP_MOST + SPARE
 SHARE = KEEP_MOST // V
 HELD = 16
@@ -40,6 +42,33 @@
     return jnp.where(positions == target, entry, -scale * weights.astype(jnp.float32)).astype(jnp.bfloat16)
 
 
+def product_kernel(features, slots, factors, out, held):
+    positions = lax.broadcasted_iota(jnp.int32, (KEEP_MOST, slots.shape[2]), 1).astype(jnp.float32)
+    for y in range(Y):
+        scale, entry, target = (factors[y, :, i:i + 1] for i in range(3))
+        weights = slots[y, :KEEP_MOST, :].astype(jnp.float32)
+        held[y * KEEP_MOST:(y + 1) * KEEP_MOST, :] = jnp.where(
+            positions == target, entry, -scale * weights
+        ).astype(held.dtype)
+    out[...] = jnp.dot(features[...], held[...], preferred_element_type=jnp.float32).astype(out.dtype)
+
+
+def product_of(features, slots, factors):
+    rows, cols = features.shape[0], slots.shape[2]
+    vmem = pl.BlockSpec(memory_space=pltpu.VMEM)
+    return pl.pallas_call(
+        product_kernel,
+        out_shape=jax.ShapeDtypeStruct((rows, cols), jnp.bfloat16),
+        in_specs=[vmem] * 3,
+        out_specs=vmem,
+        scratch_shapes=[pltpu.VMEM((Y * KEEP_MOST, cols), jnp.bfloat16)],
+        compiler_params=pltpu.CompilerParams(vmem_limit_bytes=58 * 1024 * 1024),
+        cost_estimate=pl.CostEstimate(
+            flops=2 * rows * Y * KEEP_MOST * cols, bytes_accessed=2 * slots.size + 4 * rows * cols, transcendentals=0
+        ),
+    )(features, slots, factors)
+
+
 def per_device(hidden, head_weight, targets, kept_mask, old_logprob, advantage):
     tokens, width = hidden.shape
     rows, cols = head_weight.shape
@@ -60,7 +89,7 @@
     kept_hidden = exchange(kept_hidden.reshape(HELD, Y, Z * rows).transpose(1, 0, 2), "y")
     kept_y = jnp.sum(kept_hidden[:, SHARE, :128].astype(jnp.float32), axis=0)
     kept_hidden = to_all(kept_hidden, ("x", "c"), V)[:, :, :SHARE]
-    kept_hidden = kept_hidden.transpose(1, 0, 2, 3).reshape(Y, KEEP_MOST, Z * rows)
+    kept_hidden = kept_hidden.transpose(1, 0, 2, 3).reshape(Y * KEEP_MOST, Z * rows).T
     kept_total = jnp.sum(to_all(jnp.broadcast_to(kept_y, (8, 128)), "z", Z), axis=0)[0, 0]
     scale = -(LOSS_SCALE / kept_total)
     hidden, kept_hidden, scale = lax.optimization_barrier((hidden, kept_hidden, scale))
@@ -118,11 +147,8 @@
     other = lax.dynamic_index_in_dim(hidden_part, 1 - at_c, 1, keepdims=False)
     pair = mine.astype(jnp.float32) + lax.ppermute(other, "c", [(0, 1), (1, 0)]).astype(jnp.float32)
 
-    all_rows = rows_of(all_slots[:, :KEEP_MOST], all_factors[:, :3, :KEEP_MOST])
-    part_head = scale * lax.dot_general(
-        kept_hidden, all_rows, (((0, 1), (0, 1)), ((), ())), preferred_element_type=jnp.float32
-    )
-    part_head = part_head.astype(jnp.bfloat16)
+    factors = jnp.stack([scale * all_factors[:, 0], scale * all_factors[:, 1], all_factors[:, 2]], axis=2)
+    part_head = product_of(kept_hidden, all_slots, factors[:, :KEEP_MOST])
     pair, part_head = lax.optimization_barrier((pair, part_head))
     sums = exchange(part_head.reshape(Z, rows, cols), "z")
     grad_head = jnp.sum(sums.astype(jnp.float32), axis=0)

time: 204 us -> 204 us (level)
  blocking collectives: 29.5 us -> 47.8 us
  waiting for transfers between devices: 81.9 us -> 71 us
  starting transfers between devices: 40.7 us -> 30.6 us
  Pallas kernels: 0 us -> 3.76 us
  matrix products: 18.2 us -> 14.7 us
    all_to_all x1 -> x2, blocking collectives: 16.7 us -> 35 us  [exchange(): return lax.all_to_all(parts, axes, split_axis=0, concat_axis=0)]
    all_to_all x4 -> x3, starting transfers between devices: 29 us -> 18.8 us  [exchange(): return lax.all_to_all(parts, axes, split_axis=0, concat_axis=0)]
    all_to_all x4 -> x3, waiting for transfers between devices: 32.2 us -> 24.1 us  [exchange(): return lax.all_to_all(parts, axes, split_axis=0, concat_axis=0)]
    pallas_call x0 -> x1, Pallas kernels: none -> 3.76 us  [product_of(): pl.pallas_call(product_kernel, out_shape=jax.ShapeDtypeStruct((rows, cols...]
    dot_general x1 -> x0, matrix products: 3.52 us -> none  [per_device(): lax.dot_general(kept_hidden, all_rows, (((0, 1), (0, 1)), ((), ())), pref...]
    slice x3 -> x1, local copies, waits for them, and re-layouts: 3.46 us -> 0.07 us  [the longest x1 2.12 us: per_device(): kept_hidden = to_all(kept_hidden, ('x', 'c'), V)[:, :, :SHARE]]
    all_gather x1, waiting for transfers between devices: 39.9 us -> 36.9 us  [per_device(): head = lax.all_gather(head_weight, ('y', 'z'), axis=0, tiled=True)]
    transpose x0 -> x2, local copies, waits for them, and re-layouts: none -> 2.87 us  [per_device(): kept_hidden.transpose(1, 0, 2, 3).reshape(Y * KEEP_MOST, Z * rows)]
  transfers between devices with their start and end apart: 10 -> 9, of which waited for: 9 -> 8; matrix products, arithmetic and copies ran while one was open for 11% -> 12% of each run, Pallas kernels for 0% -> 0%
where the time goes in v17:
time: 204 us; the launch traced here: 203 us
  waiting for transfers between devices  71 us (35%)
  blocking collectives  47.8 us (23%)
  starting transfers between devices  30.6 us (15%)
  between operations  15 us (7%)
  matrix products  14.7 us (7%)
  local copies, waits for them, and re-layouts  11 us (5%)
  other arithmetic  8.95 us (4%)
  Pallas kernels  3.76 us (2%)
    all_gather x1, waiting for transfers between devices, per_device(): head = lax.all_gather(head_weight, ('y', 'z'), axis=0, tiled=True)  36.9 us
    all_to_all x2, blocking collectives, exchange(): return lax.all_to_all(parts, axes, split_axis=0, concat_axis=0)  35 us
    all_to_all x3, waiting for transfers between devices, exchange(): return lax.all_to_all(parts, axes, split_axis=0, concat_axis=0)  24.1 us
    all_to_all x3, starting transfers between devices, exchange(): return lax.all_to_all(parts, axes, split_axis=0, concat_axis=0)  18.8 us
    all_gather x1, blocking collectives, per_device(): stats = lax.all_gather(stats, ('x', 'c'))  12.8 us
    ppermute x3, starting transfers between devices, per_device(): lax.ppermute(sent, 'x', [(i, (i + step) % X) for i in range(X)])  9.82 us
    dot_general x1, matrix products, per_device(): lax.dot_general(own_rows, head, (((1,), (1,)), ((), ())), preferred_eleme...  5.83 us
    dot_general x1, matrix products, per_device(): logits = jnp.dot(hidden, head, preferred_element_type=jnp.float32)  5.5 us
  transfers between devices with their start and end apart: 9, of which 8 were waited for; matrix products, arithmetic and copies ran while one was open for 12% of the time, Pallas kernels for 0%

profile of v17, /device:TPU:6, one launch (start us, length us, event | category | flops | bytes accessed | tf_op | source)
XLA Modules:
  0.0 202.7 jit_solution(5404923973483889257)
XLA Ops:
  7.2 0.0 copy-start
  7.2 0.0 all-gather.6.cloned.1.call-start
  7.2 0.7 all-gather.6.cloned.1.call-update
  7.9 1.0 reduce-window.9
  8.9 0.1 slice.56
  9.1 1.3 convert_reduce_fusion.1
  10.3 0.1 slice_reduce_fusion.1
  10.5 0.7 broadcast_compare_fusion
  11.1 0.1 add_bitcast_fusion
  11.2 0.0 copy-done
  11.2 1.1 fusion
  12.4 0.0 copy-start.3
  12.4 16.7 %all_to_all.25 = bf16[8,16,640]{2,1,0:T(8,128)(2,1)S(1)} all-to-all(bf16[8,16,640]{2,1,0:T(8,128)(2,1)S(1)} %bitcast.91), channel_id=1, replica_groups=mesh['y'=8,'z'=8,'x'=4,'c'=2] {'y'}, dimensions={0} | all-to-all | bytes 327680 | tf_op jit(solution)/shard_map/all_to_all | solution.py:32
  29.1 18.3 %all_to_all.26 = f32[8,8,128]{2,1,0:T(8,128)S(1)} all-to-all(f32[8,8,128]{2,1,0:T(8,128)S(1)} %broadcast_in_dim_broadcast_in_dim_broadcast_in_dim.3), channel_id=1, replica_groups=mesh['y'=8,'z'=8,'x'=4,'c'=2] {'z'}, dimensions={0} | all-to-all | bytes 65536 | tf_op jit(solution)/shard_map/all_to_all | solution.py:32
  47.4 1.2 broadcast_in_dim.75
  48.6 4.9 %all-to-all-start.1 = ((bf16[8,8,16,640]{3,2,1,0:T(8,128)(2,1)}), bf16[8,8,16,640]{3,2,1,0:T(8,128)(2,1)}, u32[]{:S(2)}, u32[]{:S(2)}) async-start(bf16[8,8,16,640]{3,2,1,0:T(8,128)(2,1)} %broadcast_in_dim.75), calls=%async_computation.1 | async-start | bytes 2621440 | tf_op jit(solution)/shard_map/all_to_all | solution.py:32
  53.4 0.0 all-gather.8.cloned.1.call-start
  53.4 0.0 copy-done.3
  53.5 0.5 slice.60
  54.7 15.5 %all-to-all-done.1 = bf16[8,8,16,640]{3,2,1,0:T(8,128)(2,1)} async-done(((bf16[8,8,16,640]{3,2,1,0:T(8,128)(2,1)}), bf16[8,8,16,640]{3,2,1,0:T(8,128)(2,1)}, u32[]{:S(2)}, u32[]{:S(2)}) %all-to-all-start.1) | async-done | bytes 1310752 | tf_op jit(solution)/shard_map/all_to_all | solution.py:32
  70.3 1.6 slice_bitcast_fusion
  71.8 1.3 copy.46
  73.1 1.4 reshape.142
  74.6 1.3 copy.47
  75.9 0.0 copy-start.2
  75.9 0.0 copy-start.4
  75.9 0.0 copy-start.5
  75.9 36.9 %all-gather.6.cloned.1.call-done = bf16[5120,768]{1,0:T(8,128)(2,1)} async-done(((bf16[80,768]{1,0:T(8,128)(2,1)}), bf16[5120,768]{1,0:T(8,128)(2,1)}) %all-gather.6.cloned.1.call-update) | async-done | bytes 7864336 | tf_op jit(solution)/shard_map/all_gather | solution.py:76
  112.8 5.5 %fusion.43 = (f32[256]{0:T(256)S(1)}, f32[256,768]{1,0:T(8,128)S(1)}) fusion(bf16[256,5120]{1,0:T(8,128)(2,1)S(1)} %copy-done, bf16[5120,768]{1,0:T(8,128)(2,1)} %all-gather.6.cloned.1.call-done), kind=kOutput, calls=%fused_computation.93 | convolution fusion | flops 2013462272 | bytes 11273216 | tf_op jit(solution)/shard_map/dot_general | solution.py:97
  118.3 0.5 exponential_reduce_fusion
  118.8 1.0 convolution_convert_fusion
  119.8 0.0 all-gather.8.cloned.1.call-update
  119.9 12.8 %all-gather.2 = f32[8,4,256]{2,1,0:T(4,128)S(1)} all-gather(f32[1,4,256]{2,1,0:T(4,128)S(1)} %bitcast.92), channel_id=2, replica_groups=mesh['y'=8,'z'=8,'x'=4,'c'=2] {'x','c'}, dimensions={0}, use_global_device_ids=true | all-gather | bytes 36864 | tf_op jit(solution)/shard_map/all_gather | solution.py:119
  132.7 0.0 copy-done.2
  132.7 0.0 copy-done.4
  132.8 0.0 copy-done.5
  132.8 0.6 subtract_multiply_fusion
  133.4 0.1 select_reduce_fusion.1
  133.5 0.6 broadcast_in_dim.82
  134.2 6.4 %all-to-all-start.3 = ((f32[8,8,128]{2,1,0:T(8,128)}), f32[8,8,128]{2,1,0:T(8,128)S(1)}, u32[]{:S(2)}, u32[]{:S(2)}) async-start(f32[8,8,128]{2,1,0:T(8,128)} %broadcast_in_dim.82), calls=%async_computation.3 | async-start | bytes 65536 | tf_op jit(solution)/shard_map/all_to_all | solution.py:32
  140.6 5.8 %fusion.15 = bf16[96,5120]{1,0:T(8,128)(2,1)S(1)} fusion(bf16[5120,768]{1,0:T(8,128)(2,1)} %all-gather.6.cloned.1.call-done, bf16[96,768]{1,0:T(8,128)(2,1)} %convolution_convert_fusion, f32[96]{0:T(128)S(1)} %get-tuple-element.46, bf16[96]{0:T(256)(128)(2,1)S(1)} %slice_bitcast_fusion.2, f32[768]{0:T(1024)S(1)} %iota_convert_fusion, ...), kind=kOutput, calls=%fused_computation.36 | convolution fusion | flops 755269632 | bytes 8998848 | tf_op jit(solution)/shard_map/dot_general | solution.py:138
  146.4 0.1 slice.103
  146.5 2.4 %all-to-all-done.3 = f32[8,8,128]{2,1,0:T(8,128)S(1)} async-done(((f32[8,8,128]{2,1,0:T(8,128)}), f32[8,8,128]{2,1,0:T(8,128)S(1)}, u32[]{:S(2)}, u32[]{:S(2)}) %all-to-all-start.3) | async-done | bytes 32800 | tf_op jit(solution)/shard_map/all_to_all | solution.py:32
  148.9 0.1 copy.77
  149.0 0.0 copy-start.1
  149.0 0.9 copy-done.1
  149.9 1.9 collective-permute-start
  151.9 0.9 copy.58.factors
  152.8 0.9 collective-permute-done
  153.7 1.2 convert_add_fusion
  154.9 4.2 %all-gather.8.cloned.1.call-done = bf16[768,768]{1,0:T(8,128)(2,1)} async-done(((bf16[96,768]{1,0:T(8,128)(2,1)}), bf16[768,768]{1,0:T(8,128)(2,1)}) %all-gather.8.cloned.1.call-update) | async-done | bytes 1179664 | tf_op jit(solution)/shard_map/all_gather | solution.py:108
  159.0 3.8 %shard_map.85 = bf16[640,768]{1,0:T(8,128)(2,1)} custom-call(bf16[640,640]{1,0:T(8,128)(2,1)} %bitcast.85, bf16[8,96,768]{2,1,0:T(8,128)(2,1)} %bitcast.89, f32[8,80,3]{2,1,0:T(8,128)} %copy.58.factors), custom_call_target="tpu_custom_call" | custom-call | flops 629145600 | bytes 3145728 | tf_op jit(solution)/shard_map/pallas_call | solution.py:59
  162.8 7.5 %all-to-all-start.4 = ((bf16[8,80,768]{2,1,0:T(8,128)(2,1)}), bf16[8,80,768]{2,1,0:T(8,128)(2,1)}, u32[]{:S(2)}, u32[]{:S(2)}) async-start(bf16[8,80,768]{2,1,0:T(8,128)(2,1)} %bitcast.84), calls=%async_computation.4 | async-start | bytes 1966080 | tf_op jit(solution)/shard_map/all_to_all | solution.py:32
  170.3 0.8 dynamic-slice_bitcast_fusion.3
  171.2 2.8 %collective-permute-start.3 = (f32[80,640]{1,0:T(8,128)}, f32[80,640]{1,0:T(8,128)}, u32[]{:S(2)}, u32[]{:S(2)}) collective-permute-start(f32[80,640]{1,0:T(8,128)} %get-tuple-element.35), channel_id=1, source_target_pairs={{0,6},{2,0},{4,2},{6,4},{1,7},{3,1},{5,3},{7,5},{8,14},{10,8},{12,... | collective-permute-start | bytes 614408 | tf_op jit(solution)/shard_map/ppermute | solution.py:159
  174.0 3.2 %collective-permute-start.2 = (f32[80,640]{1,0:T(8,128)}, f32[80,640]{1,0:T(8,128)}, u32[]{:S(2)}, u32[]{:S(2)}) collective-permute-start(f32[80,640]{1,0:T(8,128)} %get-tuple-element.36), channel_id=1, source_target_pairs={{0,4},{2,6},{4,0},{6,2},{1,5},{3,7},{5,1},{7,3},{8,12},{10,14},{12... | collective-permute-start | bytes 614408 | tf_op jit(solution)/shard_map/ppermute | solution.py:159
  177.2 3.8 %collective-permute-start.1 = (f32[80,640]{1,0:T(8,128)}, f32[80,640]{1,0:T(8,128)}, u32[]{:S(2)}, u32[]{:S(2)}) collective-permute-start(f32[80,640]{1,0:T(8,128)} %get-tuple-element.34), channel_id=1, source_target_pairs={{0,2},{2,4},{4,6},{6,0},{1,3},{3,5},{5,7},{7,1},{8,10},{10,12},{12... | collective-permute-start | bytes 614408 | tf_op jit(solution)/shard_map/ppermute | solution.py:159
  181.0 0.0 collective-permute-done.3
  181.0 2.4 %collective-permute-done.2 = f32[80,640]{1,0:T(8,128)} collective-permute-done((f32[80,640]{1,0:T(8,128)}, f32[80,640]{1,0:T(8,128)}, u32[]{:S(2)}, u32[]{:S(2)}) %collective-permute-start.2) | collective-permute-done | bytes 204832 | tf_op jit(solution)/shard_map/ppermute | solution.py:159
  183.5 1.8 collective-permute-done.1
  185.3 1.2 subtract_convert_fusion
  186.5 1.2 convolution_multiply_fusion
  187.7 6.2 %all-to-all-done.4 = bf16[8,80,768]{2,1,0:T(8,128)(2,1)} async-done(((bf16[8,80,768]{2,1,0:T(8,128)(2,1)}), bf16[8,80,768]{2,1,0:T(8,128)(2,1)}, u32[]{:S(2)}, u32[]{:S(2)}) %all-to-all-start.4) | async-done | bytes 983072 | tf_op jit(solution)/shard_map/all_to_all | solution.py:32
  193.8 2.0 %convert_reduce_fusion = f32[80,768]{1,0:T(8,128)} fusion(bf16[8,80,768]{2,1,0:T(8,128)(2,1)} %all-to-all-done.4), kind=kLoop, calls=%fused_computation.2 | loop fusion | flops 921600 | bytes 1228800 | tf_op jit(solution)/shard_map/reduce_sum | solution.py:154
  (23 shorter events, 0.3 us)
Async XLA Ops:
  7.2 4.1 %copy-start = (bf16[256,5120]{1,0:T(8,128)(2,1)S(1)}, bf16[256,5120]{1,0:T(8,128)(2,1)}, u32[]{:S(2)}) copy-start(bf16[256,5120]{1,0:T(8,128)(2,1)} %param.6) | copy-start | bytes 7864324
  7.2 105.6 %all-gather.6.cloned.1.call-start = ((), (), s32[]{:S(2)}) async-start(), calls=%async_computation.5 | async-start | bytes 7987200 | tf_op jit(solution)/shard_map/all_gather | solution.py:76
  12.4 41.1 %copy-start.3 = (s32[256]{0:T(256)S(1)}, s32[256]{0:T(256)}, u32[]{:S(2)}) copy-start(s32[256]{0:T(256)} %param.8) | copy-start | bytes 3076
  48.6 21.7 %all-to-all-start.1 = ((bf16[8,8,16,640]{3,2,1,0:T(8,128)(2,1)}), bf16[8,8,16,640]{3,2,1,0:T(8,128)(2,1)}, u32[]{:S(2)}, u32[]{:S(2)}) async-start(bf16[8,8,16,640]{3,2,1,0:T(8,128)(2,1)} %broadcast_in_dim.75), calls=%async_computation.1 | async-start | bytes 2621440 | tf_op jit(solution)/shard_map/all_to_all | solution.py:32
  53.4 105.6 %all-gather.8.cloned.1.call-start = ((), (), s32[]{:S(2)}) async-start(), calls=%async_computation.6 | async-start | bytes 1327104 | tf_op jit(solution)/shard_map/all_gather | solution.py:108
  75.9 56.8 %copy-start.2 = (s32[256]{0:T(256)S(1)}, s32[256]{0:T(256)}, u32[]{:S(2)}) copy-start(s32[256]{0:T(256)} %param.9) | copy-start | bytes 3076
  75.9 56.8 %copy-start.4 = (f32[256]{0:T(256)S(1)}, f32[256]{0:T(256)}, u32[]{:S(2)}) copy-start(f32[256]{0:T(256)} %param.11) | copy-start | bytes 3076
  75.9 56.9 %copy-start.5 = (f32[256]{0:T(256)S(1)}, f32[256]{0:T(256)}, u32[]{:S(2)}) copy-start(f32[256]{0:T(256)} %param.10) | copy-start | bytes 3076
  134.2 14.7 %all-to-all-start.3 = ((f32[8,8,128]{2,1,0:T(8,128)}), f32[8,8,128]{2,1,0:T(8,128)S(1)}, u32[]{:S(2)}, u32[]{:S(2)}) async-start(f32[8,8,128]{2,1,0:T(8,128)} %broadcast_in_dim.82), calls=%async_computation.3 | async-start | bytes 65536 | tf_op jit(solution)/shard_map/all_to_all | solution.py:32
  149.0 0.9 copy-start.1
  149.9 3.8 %collective-permute-start = (bf16[4,80,640]{2,1,0:T(8,128)(2,1)S(1)}, bf16[4,80,640]{2,1,0:T(8,128)(2,1)}, u32[]{:S(2)}, u32[]{:S(2)}) collective-permute-start(bf16[4,80,640]{2,1,0:T(8,128)(2,1)S(1)} %dynamic-slice_bitcast_fusion), channel_id=1, source_target_pairs={{0,1},{1,0},{2,3},{3,2},{4,5},{5,4},{6,7},{7,6},{8,9},{9,8},{10,11... | collective-permute-start | bytes 1228808 | tf_op jit(solution)/shard_map/ppermute | solution.py:148
  162.8 31.0 %all-to-all-start.4 = ((bf16[8,80,768]{2,1,0:T(8,128)(2,1)}), bf16[8,80,768]{2,1,0:T(8,128)(2,1)}, u32[]{:S(2)}, u32[]{:S(2)}) async-start(bf16[8,80,768]{2,1,0:T(8,128)(2,1)} %bitcast.84), calls=%async_computation.4 | async-start | bytes 1966080 | tf_op jit(solution)/shard_map/all_to_all | solution.py:32
  171.2 9.9 %collective-permute-start.3 = (f32[80,640]{1,0:T(8,128)}, f32[80,640]{1,0:T(8,128)}, u32[]{:S(2)}, u32[]{:S(2)}) collective-permute-start(f32[80,640]{1,0:T(8,128)} %get-tuple-element.35), channel_id=1, source_target_pairs={{0,6},{2,0},{4,2},{6,4},{1,7},{3,1},{5,3},{7,5},{8,14},{10,8},{12,... | collective-permute-start | bytes 614408 | tf_op jit(solution)/shard_map/ppermute | solution.py:159
  174.0 9.5 %collective-permute-start.2 = (f32[80,640]{1,0:T(8,128)}, f32[80,640]{1,0:T(8,128)}, u32[]{:S(2)}, u32[]{:S(2)}) collective-permute-start(f32[80,640]{1,0:T(8,128)} %get-tuple-element.36), channel_id=1, source_target_pairs={{0,4},{2,6},{4,0},{6,2},{1,5},{3,7},{5,1},{7,3},{8,12},{10,14},{12... | collective-permute-start | bytes 614408 | tf_op jit(solution)/shard_map/ppermute | solution.py:159
  177.2 8.1 %collective-permute-start.1 = (f32[80,640]{1,0:T(8,128)}, f32[80,640]{1,0:T(8,128)}, u32[]{:S(2)}, u32[]{:S(2)}) collective-permute-start(f32[80,640]{1,0:T(8,128)} %get-tuple-element.34), channel_id=1, source_target_pairs={{0,2},{2,4},{4,6},{6,0},{1,3},{3,5},{5,7},{7,1},{8,10},{10,12},{12... | collective-permute-start | bytes 614408 | tf_op jit(solution)/shard_map/ppermute | solution.py:159
Sparse Core Ops, SparseCore 0:
  11.1 101.6 all-gather.5
  120.0 39.0 all-gather.7

commit v18 on v17

--- a/solution.py
+++ b/solution.py
@@ -67,6 +67,27 @@
             flops=2 * rows * Y * KEEP_MOST * cols, bytes_accessed=2 * slots.size + 4 * rows * cols, transcendentals=0
         ),
     )(features, slots, factors)
+
+
+def sum_kernel(parts, out):
+    total = parts[0].astype(jnp.float32)
+    for i in range(1, parts.shape[0]):
+        total = total + parts[i].astype(jnp.float32)
+    out[...] = total
+
+
+def sum_of(parts):
+    n, rows, cols = parts.shape
+    half = cols // 2
+    return pl.pallas_call(
+        sum_kernel,
+        out_shape=jax.ShapeDtypeStruct((rows, cols), jnp.float32),
+        grid=(2,),
+        in_specs=[pl.BlockSpec((n, rows, half), lambda i: (0, 0, i))],
+        out_specs=pl.BlockSpec((rows, half), lambda i: (0, i)),
+        compiler_params=pltpu.CompilerParams(vmem_limit_bytes=58 * 1024 * 1024),
+        cost_estimate=pl.CostEstimate(flops=parts.size, bytes_accessed=2 * parts.size + 4 * rows * cols, transcendentals=0),
+    )(parts)
 
 
 def per_device(hidden, head_weight, targets, kept_mask, old_logprob, advantage):
@@ -151,7 +172,7 @@
     part_head = product_of(kept_hidden, all_slots, factors[:, :KEEP_MOST])
     pair, part_head = lax.optimization_barrier((pair, part_head))
     sums = exchange(part_head.reshape(Z, rows, cols), "z")
-    grad_head = jnp.sum(sums.astype(jnp.float32), axis=0)
+    grad_head = sum_of(sums)
 
     total = lax.dynamic_index_in_dim(pair, at_x, 0, keepdims=False)
     for step in range(1, X):

time: 204 us -> 204 us (level)
  other arithmetic: 8.95 us -> 6.9 us
    reduce_sum x1 -> x0, other arithmetic: 2.05 us -> none  [per_device(): grad_head = jnp.sum(sums.astype(jnp.float32), axis=0)]
where the time goes in v18:
time: 204 us; the launch traced here: 203 us
  waiting for transfers between devices  71 us (35%)
  blocking collectives  47.8 us (23%)
  starting transfers between devices  30.6 us (15%)
  between operations  15 us (7%)
  matrix products  14.7 us (7%)
  local copies, waits for them, and re-layouts  11 us (5%)
  other arithmetic  6.9 us (3%)
  Pallas kernels  5.65 us (3%)
    all_gather x1, waiting for transfers between devices, per_device(): head = lax.all_gather(head_weight, ('y', 'z'), axis=0, tiled=True)  36.9 us
    all_to_all x2, blocking collectives, exchange(): return lax.all_to_all(parts, axes, split_axis=0, concat_axis=0)  35 us
    all_to_all x3, waiting for transfers between devices, exchange(): return lax.all_to_all(parts, axes, split_axis=0, concat_axis=0)  24.1 us
    all_to_all x3, starting transfers between devices, exchange(): return lax.all_to_all(parts, axes, split_axis=0, concat_axis=0)  18.8 us
    all_gather x1, blocking collectives, per_device(): stats = lax.all_gather(stats, ('x', 'c'))  12.8 us
    ppermute x3, starting transfers between devices, per_device(): lax.ppermute(sent, 'x', [(i, (i + step) % X) for i in range(X)])  9.82 us
    dot_general x1, matrix products, per_device(): lax.dot_general(own_rows, head, (((1,), (1,)), ((), ())), preferred_eleme...  5.83 us
    dot_general x1, matrix products, per_device(): logits = jnp.dot(hidden, head, preferred_element_type=jnp.float32)  5.5 us
  transfers between devices with their start and end apart: 9, of which 8 were waited for; matrix products, arithmetic and copies ran while one was open for 12% of the time, Pallas kernels for 0%

profile of v18, /device:TPU:6, one launch (start us, length us, event | category | flops | bytes accessed | tf_op | source)
XLA Modules:
  0.0 202.6 jit_solution(14586591420350750153)
XLA Ops:
  7.2 0.0 copy-start
  7.2 0.0 all-gather.6.cloned.1.call-start
  7.2 0.7 all-gather.6.cloned.1.call-update
  7.9 1.0 reduce-window.9
  8.9 0.1 slice.56
  9.1 1.3 convert_reduce_fusion
  10.3 0.1 slice_reduce_fusion.1
  10.5 0.7 broadcast_compare_fusion
  11.1 0.1 add_bitcast_fusion
  11.2 0.0 copy-done
  11.2 1.1 fusion
  12.4 0.0 copy-start.3
  12.4 16.7 %all_to_all.25 = bf16[8,16,640]{2,1,0:T(8,128)(2,1)S(1)} all-to-all(bf16[8,16,640]{2,1,0:T(8,128)(2,1)S(1)} %bitcast.91), channel_id=1, replica_groups=mesh['y'=8,'z'=8,'x'=4,'c'=2] {'y'}, dimensions={0} | all-to-all | bytes 327680 | tf_op jit(solution)/shard_map/all_to_all | solution.py:32
  29.1 18.3 %all_to_all.26 = f32[8,8,128]{2,1,0:T(8,128)S(1)} all-to-all(f32[8,8,128]{2,1,0:T(8,128)S(1)} %broadcast_in_dim_broadcast_in_dim_broadcast_in_dim.3), channel_id=1, replica_groups=mesh['y'=8,'z'=8,'x'=4,'c'=2] {'z'}, dimensions={0} | all-to-all | bytes 65536 | tf_op jit(solution)/shard_map/all_to_all | solution.py:32
  47.4 1.2 broadcast_in_dim.75
  48.6 4.9 %all-to-all-start.1 = ((bf16[8,8,16,640]{3,2,1,0:T(8,128)(2,1)}), bf16[8,8,16,640]{3,2,1,0:T(8,128)(2,1)}, u32[]{:S(2)}, u32[]{:S(2)}) async-start(bf16[8,8,16,640]{3,2,1,0:T(8,128)(2,1)} %broadcast_in_dim.75), calls=%async_computation.1 | async-start | bytes 2621440 | tf_op jit(solution)/shard_map/all_to_all | solution.py:32
  53.4 0.0 all-gather.8.cloned.1.call-start
  53.4 0.0 copy-done.3
  53.5 0.5 slice.60
  54.7 15.5 %all-to-all-done.1 = bf16[8,8,16,640]{3,2,1,0:T(8,128)(2,1)} async-done(((bf16[8,8,16,640]{3,2,1,0:T(8,128)(2,1)}), bf16[8,8,16,640]{3,2,1,0:T(8,128)(2,1)}, u32[]{:S(2)}, u32[]{:S(2)}) %all-to-all-start.1) | async-done | bytes 1310752 | tf_op jit(solution)/shard_map/all_to_all | solution.py:32
  70.3 1.6 slice_bitcast_fusion
  71.8 1.3 copy.46
  73.1 1.4 reshape.142
  74.6 1.3 copy.47
  75.9 0.0 copy-start.2
  75.9 0.0 copy-start.4
  75.9 0.0 copy-start.5
  75.9 36.9 %all-gather.6.cloned.1.call-done = bf16[5120,768]{1,0:T(8,128)(2,1)} async-done(((bf16[80,768]{1,0:T(8,128)(2,1)}), bf16[5120,768]{1,0:T(8,128)(2,1)}) %all-gather.6.cloned.1.call-update) | async-done | bytes 7864336 | tf_op jit(solution)/shard_map/all_gather | solution.py:97
  112.8 5.5 %fusion.43 = (f32[256]{0:T(256)S(1)}, f32[256,768]{1,0:T(8,128)S(1)}) fusion(bf16[256,5120]{1,0:T(8,128)(2,1)S(1)} %copy-done, bf16[5120,768]{1,0:T(8,128)(2,1)} %all-gather.6.cloned.1.call-done), kind=kOutput, calls=%fused_computation.92 | convolution fusion | flops 2013462272 | bytes 11273216 | tf_op jit(solution)/shard_map/dot_general | solution.py:118
  118.3 0.5 exponential_reduce_fusion
  118.8 1.0 convolution_convert_fusion
  119.8 0.0 all-gather.8.cloned.1.call-update
  119.9 12.8 %all-gather.2 = f32[8,4,256]{2,1,0:T(4,128)S(1)} all-gather(f32[1,4,256]{2,1,0:T(4,128)S(1)} %bitcast.92), channel_id=2, replica_groups=mesh['y'=8,'z'=8,'x'=4,'c'=2] {'x','c'}, dimensions={0}, use_global_device_ids=true | all-gather | bytes 36864 | tf_op jit(solution)/shard_map/all_gather | solution.py:140
  132.7 0.0 copy-done.2
  132.7 0.0 copy-done.4
  132.8 0.0 copy-done.5
  132.8 0.6 subtract_multiply_fusion
  133.4 0.1 select_reduce_fusion.1
  133.5 0.6 broadcast_in_dim.82
  134.2 6.4 %all-to-all-start.3 = ((f32[8,8,128]{2,1,0:T(8,128)}), f32[8,8,128]{2,1,0:T(8,128)S(1)}, u32[]{:S(2)}, u32[]{:S(2)}) async-start(f32[8,8,128]{2,1,0:T(8,128)} %broadcast_in_dim.82), calls=%async_computation.3 | async-start | bytes 65536 | tf_op jit(solution)/shard_map/all_to_all | solution.py:32
  140.6 5.8 %fusion.15 = bf16[96,5120]{1,0:T(8,128)(2,1)S(1)} fusion(bf16[5120,768]{1,0:T(8,128)(2,1)} %all-gather.6.cloned.1.call-done, bf16[96,768]{1,0:T(8,128)(2,1)} %convolution_convert_fusion, f32[96]{0:T(128)S(1)} %get-tuple-element.46, bf16[96]{0:T(256)(128)(2,1)S(1)} %slice_bitcast_fusion.2, f32[768]{0:T(1024)S(1)} %iota_convert_fusion, ...), kind=kOutput, calls=%fused_computation.35 | convolution fusion | flops 755269632 | bytes 8998848 | tf_op jit(solution)/shard_map/dot_general | solution.py:159
  146.4 0.1 slice.103
  146.5 2.4 %all-to-all-done.3 = f32[8,8,128]{2,1,0:T(8,128)S(1)} async-done(((f32[8,8,128]{2,1,0:T(8,128)}), f32[8,8,128]{2,1,0:T(8,128)S(1)}, u32[]{:S(2)}, u32[]{:S(2)}) %all-to-all-start.3) | async-done | bytes 32800 | tf_op jit(solution)/shard_map/all_to_all | solution.py:32
  148.9 0.1 copy.77
  149.0 0.0 copy-start.1
  149.0 0.9 copy-done.1
  149.9 1.9 collective-permute-start
  151.9 0.9 copy.58.factors
  152.8 0.9 collective-permute-done
  153.7 1.2 convert_add_fusion
  154.9 4.2 %all-gather.8.cloned.1.call-done = bf16[768,768]{1,0:T(8,128)(2,1)} async-done(((bf16[96,768]{1,0:T(8,128)(2,1)}), bf16[768,768]{1,0:T(8,128)(2,1)}) %all-gather.8.cloned.1.call-update) | async-done | bytes 1179664 | tf_op jit(solution)/shard_map/all_gather | solution.py:129
  159.0 3.8 %shard_map.85 = bf16[640,768]{1,0:T(8,128)(2,1)} custom-call(bf16[640,640]{1,0:T(8,128)(2,1)} %bitcast.85, bf16[8,96,768]{2,1,0:T(8,128)(2,1)} %bitcast.89, f32[8,80,3]{2,1,0:T(8,128)} %copy.58.factors), custom_call_target="tpu_custom_call" | custom-call | flops 629145600 | bytes 3145728 | tf_op jit(solution)/shard_map/pallas_call | solution.py:59
  162.8 7.5 %all-to-all-start.4 = ((bf16[8,80,768]{2,1,0:T(8,128)(2,1)}), bf16[8,80,768]{2,1,0:T(8,128)(2,1)}, u32[]{:S(2)}, u32[]{:S(2)}) async-start(bf16[8,80,768]{2,1,0:T(8,128)(2,1)} %bitcast.84), calls=%async_computation.4 | async-start | bytes 1966080 | tf_op jit(solution)/shard_map/all_to_all | solution.py:32
  170.3 0.8 dynamic-slice_bitcast_fusion.3
  171.2 2.8 %collective-permute-start.3 = (f32[80,640]{1,0:T(8,128)}, f32[80,640]{1,0:T(8,128)}, u32[]{:S(2)}, u32[]{:S(2)}) collective-permute-start(f32[80,640]{1,0:T(8,128)} %get-tuple-element.35), channel_id=1, source_target_pairs={{0,6},{2,0},{4,2},{6,4},{1,7},{3,1},{5,3},{7,5},{8,14},{10,8},{12,... | collective-permute-start | bytes 614408 | tf_op jit(solution)/shard_map/ppermute | solution.py:180
  174.0 3.2 %collective-permute-start.2 = (f32[80,640]{1,0:T(8,128)}, f32[80,640]{1,0:T(8,128)}, u32[]{:S(2)}, u32[]{:S(2)}) collective-permute-start(f32[80,640]{1,0:T(8,128)} %get-tuple-element.36), channel_id=1, source_target_pairs={{0,4},{2,6},{4,0},{6,2},{1,5},{3,7},{5,1},{7,3},{8,12},{10,14},{12... | collective-permute-start | bytes 614408 | tf_op jit(solution)/shard_map/ppermute | solution.py:180
  177.2 3.8 %collective-permute-start.1 = (f32[80,640]{1,0:T(8,128)}, f32[80,640]{1,0:T(8,128)}, u32[]{:S(2)}, u32[]{:S(2)}) collective-permute-start(f32[80,640]{1,0:T(8,128)} %get-tuple-element.34), channel_id=1, source_target_pairs={{0,2},{2,4},{4,6},{6,0},{1,3},{3,5},{5,7},{7,1},{8,10},{10,12},{12... | collective-permute-start | bytes 614408 | tf_op jit(solution)/shard_map/ppermute | solution.py:180
  181.0 0.0 collective-permute-done.3
  181.0 2.4 %collective-permute-done.2 = f32[80,640]{1,0:T(8,128)} collective-permute-done((f32[80,640]{1,0:T(8,128)}, f32[80,640]{1,0:T(8,128)}, u32[]{:S(2)}, u32[]{:S(2)}) %collective-permute-start.2) | collective-permute-done | bytes 204832 | tf_op jit(solution)/shard_map/ppermute | solution.py:180
  183.5 1.8 collective-permute-done.1
  185.3 1.2 subtract_convert_fusion
  186.5 1.2 convolution_multiply_fusion
  187.7 6.2 %all-to-all-done.4.parts = bf16[8,80,768]{2,1,0:T(8,128)(2,1)} async-done(((bf16[8,80,768]{2,1,0:T(8,128)(2,1)}), bf16[8,80,768]{2,1,0:T(8,128)(2,1)}, u32[]{:S(2)}, u32[]{:S(2)}) %all-to-all-start.4) | async-done | bytes 983072 | tf_op jit(solution)/shard_map/all_to_all | solution.py:32
  193.8 1.9 shard_map.86
  (23 shorter events, 0.3 us)
Async XLA Ops:
  7.2 4.1 %copy-start = (bf16[256,5120]{1,0:T(8,128)(2,1)S(1)}, bf16[256,5120]{1,0:T(8,128)(2,1)}, u32[]{:S(2)}) copy-start(bf16[256,5120]{1,0:T(8,128)(2,1)} %param.6) | copy-start | bytes 7864324
  7.2 105.6 %all-gather.6.cloned.1.call-start = ((), (), s32[]{:S(2)}) async-start(), calls=%async_computation.5 | async-start | bytes 7987200 | tf_op jit(solution)/shard_map/all_gather | solution.py:97
  12.4 41.1 %copy-start.3 = (s32[256]{0:T(256)S(1)}, s32[256]{0:T(256)}, u32[]{:S(2)}) copy-start(s32[256]{0:T(256)} %param.8) | copy-start | bytes 3076
  48.6 21.7 %all-to-all-start.1 = ((bf16[8,8,16,640]{3,2,1,0:T(8,128)(2,1)}), bf16[8,8,16,640]{3,2,1,0:T(8,128)(2,1)}, u32[]{:S(2)}, u32[]{:S(2)}) async-start(bf16[8,8,16,640]{3,2,1,0:T(8,128)(2,1)} %broadcast_in_dim.75), calls=%async_computation.1 | async-start | bytes 2621440 | tf_op jit(solution)/shard_map/all_to_all | solution.py:32
  53.4 105.6 %all-gather.8.cloned.1.call-start = ((), (), s32[]{:S(2)}) async-start(), calls=%async_computation.6 | async-start | bytes 1327104 | tf_op jit(solution)/shard_map/all_gather | solution.py:129
  75.9 56.8 %copy-start.2 = (s32[256]{0:T(256)S(1)}, s32[256]{0:T(256)}, u32[]{:S(2)}) copy-start(s32[256]{0:T(256)} %param.9) | copy-start | bytes 3076
  75.9 56.8 %copy-start.4 = (f32[256]{0:T(256)S(1)}, f32[256]{0:T(256)}, u32[]{:S(2)}) copy-start(f32[256]{0:T(256)} %param.11) | copy-start | bytes 3076
  75.9 56.9 %copy-start.5 = (f32[256]{0:T(256)S(1)}, f32[256]{0:T(256)}, u32[]{:S(2)}) copy-start(f32[256]{0:T(256)} %param.10) | copy-start | bytes 3076
  134.2 14.7 %all-to-all-start.3 = ((f32[8,8,128]{2,1,0:T(8,128)}), f32[8,8,128]{2,1,0:T(8,128)S(1)}, u32[]{:S(2)}, u32[]{:S(2)}) async-start(f32[8,8,128]{2,1,0:T(8,128)} %broadcast_in_dim.82), calls=%async_computation.3 | async-start | bytes 65536 | tf_op jit(solution)/shard_map/all_to_all | solution.py:32
  149.0 0.9 copy-start.1
  149.9 3.8 %collective-permute-start = (bf16[4,80,640]{2,1,0:T(8,128)(2,1)S(1)}, bf16[4,80,640]{2,1,0:T(8,128)(2,1)}, u32[]{:S(2)}, u32[]{:S(2)}) collective-permute-start(bf16[4,80,640]{2,1,0:T(8,128)(2,1)S(1)} %dynamic-slice_bitcast_fusion), channel_id=1, source_target_pairs={{0,1},{1,0},{2,3},{3,2},{4,5},{5,4},{6,7},{7,6},{8,9},{9,8},{10,11... | collective-permute-start | bytes 1228808 | tf_op jit(solution)/shard_map/ppermute | solution.py:169
  162.8 31.0 %all-to-all-start.4 = ((bf16[8,80,768]{2,1,0:T(8,128)(2,1)}), bf16[8,80,768]{2,1,0:T(8,128)(2,1)}, u32[]{:S(2)}, u32[]{:S(2)}) async-start(bf16[8,80,768]{2,1,0:T(8,128)(2,1)} %bitcast.84), calls=%async_computation.4 | async-start | bytes 1966080 | tf_op jit(solution)/shard_map/all_to_all | solution.py:32
  171.2 9.9 %collective-permute-start.3 = (f32[80,640]{1,0:T(8,128)}, f32[80,640]{1,0:T(8,128)}, u32[]{:S(2)}, u32[]{:S(2)}) collective-permute-start(f32[80,640]{1,0:T(8,128)} %get-tuple-element.35), channel_id=1, source_target_pairs={{0,6},{2,0},{4,2},{6,4},{1,7},{3,1},{5,3},{7,5},{8,14},{10,8},{12,... | collective-permute-start | bytes 614408 | tf_op jit(solution)/shard_map/ppermute | solution.py:180
  174.0 9.5 %collective-permute-start.2 = (f32[80,640]{1,0:T(8,128)}, f32[80,640]{1,0:T(8,128)}, u32[]{:S(2)}, u32[]{:S(2)}) collective-permute-start(f32[80,640]{1,0:T(8,128)} %get-tuple-element.36), channel_id=1, source_target_pairs={{0,4},{2,6},{4,0},{6,2},{1,5},{3,7},{5,1},{7,3},{8,12},{10,14},{12... | collective-permute-start | bytes 614408 | tf_op jit(solution)/shard_map/ppermute | solution.py:180
  177.2 8.1 %collective-permute-start.1 = (f32[80,640]{1,0:T(8,128)}, f32[80,640]{1,0:T(8,128)}, u32[]{:S(2)}, u32[]{:S(2)}) collective-permute-start(f32[80,640]{1,0:T(8,128)} %get-tuple-element.34), channel_id=1, source_target_pairs={{0,2},{2,4},{4,6},{6,0},{1,3},{3,5},{5,7},{7,1},{8,10},{10,12},{12... | collective-permute-start | bytes 614408 | tf_op jit(solution)/shard_map/ppermute | solution.py:180
Sparse Core Ops, SparseCore 0:
  11.1 101.6 all-gather.5
  120.0 39.0 all-gather.7
